TPU v7x, 512 devices: a whole 4x8x8 slice. The times are simulated.
512 devices in a mesh: dp: 32 (over x_lo, y, core), tensor: 16 (over x_hi, z).
Axes of the slice: x: 4 (x_hi: 2, x_lo: 2; x = x_hi * 2 + x_lo), y: 8, z: 8, core: 2. Of those that a mesh axis runs over, the one named last changes fastest.
Arguments:
- hidden_rows: bfloat16 [4096, 4096], P(('dp', 'tensor')), may hold values from -3 to 3
- queries: bfloat16 [4096, 8192], P('dp', 'tensor'), may hold values from -8 to 8
- keys: bfloat16 [36864, 2048], P('dp', 'tensor'), may hold values from -8 to 8, as said below
- values: bfloat16 [36864, 2048], P('dp', 'tensor'), may hold values from -6 to 6, as said below
- slab_start: int32 [32], P('dp'), may hold values from 512 to 1024
- out_weight: bfloat16 [8192, 4096], P('tensor', 'dp'), may hold values from -0.1875 to 0.1875
- norm_gain: bfloat16 [4096], replicated, may hold values from 0.5 to 1.5
- route_ids: int32 [4096, 8], P('dp'), may hold values from 0 to 127, as said below
- route_weights: int32 [4096, 8], P('dp'), may hold values from 4096 to 32767
- flight_experts: int32 [4], replicated, may hold values from 0 to 127, as said below
- gate_weight: bfloat16 [4096, 6144], P('dp', 'tensor'), may hold values from -0.09375 to 0.09375
- up_weight: bfloat16 [4096, 6144], P('dp', 'tensor'), may hold values from -0.09375 to 0.09375
- down_weight: bfloat16 [6144, 4096], P('tensor', 'dp'), may hold values from -0.3125 to 0.3125
Outputs:
- mixed: bfloat16 [4096, 4096], P(('dp', 'tensor'))
Inputs may be any that keep to these rules, and one draw needn't show every extreme that they name: Column blocks t and u of keys are equal where t // 4 == u // 4. Column blocks t and u of values are equal where t // 4 == u // 4. `flight_experts`: 4 different expert numbers. `route_ids`: each row names 8 different experts. In the 8 rows of one tensor index (aligned blocks of each slab), each expert of flight_experts is named by at most 4 rows; in every slab some expert of flight_experts is named by exactly 4 rows in every block. `route_weights`: gate weights in units of 1/65536.
All inputs are finite; a program needn't handle non-finite values.
Results may differ from a plain program's by a relative error of at most 0.022.
Values may be sent and summed in bfloat16 or wider, within the bound.
No kernel may reach another device: no remote copies, remote signals or barrier semaphores. Data moves between devices by JAX's collectives and lax.ppermute only.
A program may use at most 64 MiB of HBM per device.

v0:
```python
import jax
import jax.numpy as jnp
from jax import lax
from jax.sharding import PartitionSpec as P


def attend(q_dev, keys_dev, values_dev, first_pos):
    slab_rows = q_dev.shape[0]
    head_size = keys_dev.shape[1]
    head_count = q_dev.shape[1] // head_size
    pair_count = head_count // 2
    grouped = (
        q_dev.reshape(slab_rows, pair_count, 2, head_size)
        .transpose(1, 2, 0, 3)
        .reshape(pair_count, 2 * slab_rows, head_size)
    )
    position = first_pos + jnp.arange(2 * slab_rows, dtype=jnp.int32) % slab_rows
    visible = jnp.arange(keys_dev.shape[0], dtype=jnp.int32)[None, :] <= position[:, None]

    def one_pair(q_block):
        scores = lax.dot_general(
            q_block, keys_dev, (((1,), (1,)), ((), ())), preferred_element_type=jnp.float32
        ) * head_size ** (-0.5)
        scores = jnp.where(visible, scores, -1e30)
        maxima = jnp.max(scores, axis=1, keepdims=True)
        exp_scores = jnp.exp(scores - maxima)
        totals = jnp.sum(exp_scores, axis=1, keepdims=True)
        context = (
            jnp.dot(exp_scores.astype(jnp.bfloat16), values_dev, preferred_element_type=jnp.float32)
            / totals
        )
        return context.astype(jnp.bfloat16)

    result = lax.map(one_pair, grouped)
    return (
        result.reshape(pair_count, 2, slab_rows, head_size)
        .transpose(2, 0, 1, 3)
        .reshape(slab_rows, head_count * head_size)
    )


def rms_norm(residual, norm_gain):
    values32 = residual.astype(jnp.float32)
    inverse = lax.rsqrt(jnp.mean(values32 * values32, axis=1, keepdims=True) + 1e-06)
    return (values32 * inverse * norm_gain.astype(jnp.float32)).astype(jnp.bfloat16)


def per_device(
    hidden_rows,
    queries,
    keys,
    values,
    slab_start,
    out_weight,
    norm_gain,
    route_ids,
    route_weights,
    flight_experts,
    gate_weight,
    up_weight,
    down_weight,
):
    tensor_idx = lax.axis_index("tensor")
    groups = lax.axis_size("tensor")
    own_rows = hidden_rows.shape[0]
    width = hidden_rows.shape[1]
    flight = flight_experts.shape[0]
    per_expert = groups // flight
    capacity = min(4, own_rows)
    context = attend(queries, keys, values, slab_start[0])
    projected = jnp.dot(
        context,
        lax.all_gather(out_weight, "dp", axis=1, tiled=True),
        preferred_element_type=jnp.float32,
    )
    matches = route_ids[:, None, :] == flight_experts[None, :, None]
    hits = jnp.sum(matches.astype(jnp.int32), axis=2, dtype=jnp.int32).reshape(
        groups, own_rows, flight
    )
    gate_coef = (
        jnp.sum(jnp.where(matches, route_weights[:, None, :], 0), axis=2, dtype=jnp.int32).astype(
            jnp.float32
        )
        / 65536.0
    )
    slot_number = jnp.cumsum(hits, axis=1) - 1
    placing = jnp.logical_and(
        hits[..., None] == 1, slot_number[..., None] == jnp.arange(capacity, dtype=jnp.int32)
    )
    own_place = lax.dynamic_index_in_dim(placing, tensor_idx, 0, keepdims=False)
    own_coef = lax.dynamic_slice_in_dim(gate_coef, tensor_idx * own_rows, own_rows, 0)
    attention = lax.psum_scatter(
        projected.astype(jnp.bfloat16), "tensor", scatter_dimension=0, tiled=True
    ).astype(jnp.float32)
    residual = (hidden_rows.astype(jnp.float32) + attention).astype(jnp.bfloat16)
    normed = rms_norm(residual, norm_gain)
    packed = jnp.einsum(
        "rfc,rd->fcd", own_place.astype(jnp.bfloat16), normed, preferred_element_type=jnp.float32
    ).astype(jnp.bfloat16)
    rows_in = lax.all_to_all(
        jnp.repeat(packed, per_expert, axis=0), "tensor", split_axis=0, concat_axis=0, tiled=True
    )
    flat_rows = rows_in.reshape(groups * capacity, width)
    gate_pre = jnp.dot(
        flat_rows,
        lax.all_gather(gate_weight, "dp", axis=0, tiled=True),
        preferred_element_type=jnp.float32,
    )
    up_pre = jnp.dot(
        flat_rows,
        lax.all_gather(up_weight, "dp", axis=0, tiled=True),
        preferred_element_type=jnp.float32,
    )
    activated = (jax.nn.silu(gate_pre) * up_pre).astype(jnp.bfloat16)
    expert_out = jnp.dot(
        activated,
        lax.all_gather(down_weight, "dp", axis=1, tiled=True),
        preferred_element_type=jnp.float32,
    )
    slice_parts = expert_out.astype(jnp.bfloat16).reshape(groups, capacity, width)
    returned = lax.all_to_all(slice_parts, "tensor", split_axis=0, concat_axis=0, tiled=True)
    weighted = own_place.astype(jnp.float32) * own_coef[:, :, None]
    weighted = jnp.repeat(weighted, per_expert, axis=1)
    expert_sum = jnp.einsum(
        "rtc,tcd->rd", weighted, returned.astype(jnp.float32), precision=lax.Precision.HIGHEST
    )
    return (residual.astype(jnp.float32) + expert_sum).astype(jnp.bfloat16)


def solution(mesh):
    placed = (
        P(("dp", "tensor"), None),
        P("dp", "tensor"),
        P("dp", "tensor"),
        P("dp", "tensor"),
        P("dp"),
        P("tensor", "dp"),
        P(),
        P("dp", None),
        P("dp", None),
        P(),
        P("dp", "tensor"),
        P("dp", "tensor"),
        P("tensor", "dp"),
    )
    return jax.shard_map(
        per_device, mesh=mesh, in_specs=placed, out_specs=P(("dp", "tensor"), None), check_vma=False
    )
```

profile of v0, /device:TPU:2, one launch (start us, length us, event | category | flops | bytes accessed | tf_op | source)
XLA Modules:
  0.0 547.6 jit_solution(3616328736121962919)
XLA Ops:
  6.5 0.7 all-gather.5.cloned.1.call-update
  7.3 0.9 reshape.65
  8.9 4.5 while.11
  9.0 1.4 fusion.61
  10.4 0.3 fusion.62
  10.8 0.4 fusion.63
  11.2 1.4 fusion.61
  12.7 0.3 fusion.62
  13.0 0.4 fusion.63
  13.4 0.1 copy.46
  13.6 75.3 %all-gather.5.cloned.1.call-done = bf16[512,4096]{1,0:T(8,128)(2,1)} async-done(((bf16[512,128]{1,0:T(8,128)(2,1)}), bf16[512,4096]{1,0:T(8,128)(2,1)}) %all-gather.5.cloned.1.call-update) | async-done | bytes 4194320 | tf_op jit(solution)/shard_map/all_gather | solution.py:73
  88.9 4.0 convolution_convert_fusion
  93.0 0.7 all-gather.7.cloned.1.call-update
  93.7 0.5 all-gather.11.cloned.1.call-update
  94.3 0.5 all-gather.9.cloned.1.call-update
  94.8 0.1 fusion.31
  95.0 0.7 reduce_window_sum.11
  95.8 200.7 %reduce-scatter.2.cloned.1.call-done = bf16[8,4096]{1,0:T(8,128)(2,1)} async-done(((bf16[128,4096]{1,0:T(8,128)(2,1)}), bf16[8,4096]{1,0:T(8,128)(2,1)}) %reduce-scatter.2.cloned.1.call-update) | async-done | bytes 65552 | tf_op jit(solution)/shard_map/reduce_scatter | solution.py:92
  296.5 1.0 fusion.17
  297.5 1.1 convolution_convert_fusion.2
  298.6 0.2 broadcast_in_dim.45
  298.8 19.3 %all_to_all.10 = bf16[16,4,4096]{2,1,0:T(4,128)(2,1)S(1)} all-to-all(bf16[16,4,4096]{2,1,0:T(4,128)(2,1)S(1)} %bitcast.54), channel_id=1, replica_groups=mesh['dp'=32,'tensor'=16] {'tensor'}, dimensions={0} | all-to-all | bytes 1048576 | tf_op jit(solution)/shard_map/all_to_all | solution.py:100
  318.1 0.1 reshape.71
  318.2 46.5 %all-gather.7.cloned.1.call-done = bf16[4096,384]{1,0:T(8,128)(2,1)} async-done(((bf16[128,384]{1,0:T(8,128)(2,1)}), bf16[4096,384]{1,0:T(8,128)(2,1)}) %all-gather.7.cloned.1.call-update) | async-done | bytes 3145744 | tf_op jit(solution)/shard_map/all_gather | solution.py:106
  364.7 2.5 fusion.41
  367.2 71.9 %all-gather.11.cloned.1.call-done = bf16[384,4096]{1,0:T(8,128)(2,1)} async-done(((bf16[384,128]{1,0:T(8,128)(2,1)}), bf16[384,4096]{1,0:T(8,128)(2,1)}) %all-gather.11.cloned.1.call-update) | async-done | bytes 3145744 | tf_op jit(solution)/shard_map/all_gather | solution.py:117
  439.2 68.9 %all-gather.9.cloned.1.call-done = bf16[4096,384]{1,0:T(8,128)(2,1)} async-done(((bf16[128,384]{1,0:T(8,128)(2,1)}), bf16[4096,384]{1,0:T(8,128)(2,1)}) %all-gather.9.cloned.1.call-update) | async-done | bytes 3145744 | tf_op jit(solution)/shard_map/all_gather | solution.py:111
  508.1 4.4 convolution_convert_fusion.1
  512.4 1.0 reshape.72
  513.4 9.1 %all-to-all-start.1 = ((bf16[16,4,4096]{2,1,0:T(4,128)(2,1)}), bf16[16,4,4096]{2,1,0:T(4,128)(2,1)S(1)}, u32[]{:S(2)}, u32[]{:S(2)}) async-start(bf16[16,4,4096]{2,1,0:T(4,128)(2,1)} %reshape.72), calls=%async_computation.2 | async-start | bytes 1048576 | tf_op jit(solution)/shard_map/all_to_all | solution.py:121
  522.6 17.3 %all-to-all-done.1 = bf16[16,4,4096]{2,1,0:T(4,128)(2,1)S(1)} async-done(((bf16[16,4,4096]{2,1,0:T(4,128)(2,1)}), bf16[16,4,4096]{2,1,0:T(4,128)(2,1)S(1)}, u32[]{:S(2)}, u32[]{:S(2)}) %all-to-all-start.1) | async-done | bytes 524320 | tf_op jit(solution)/shard_map/all_to_all | solution.py:121
  539.9 1.2 fusion.14
  (39 shorter events, 0.5 us)
Async XLA Ops:
  6.5 82.4 %all-gather.5.cloned.1.call-start = ((), (), s32[]{:S(2)}) async-start(), calls=%async_computation.3 | async-start | bytes 4325376 | tf_op jit(solution)/shard_map/all_gather | solution.py:73
  7.3 289.3 %reduce-scatter.2.cloned.1.call-start = ((), (), s32[]{:S(2)}) async-start(), calls=%async_computation.4 | async-start | bytes 1114112 | tf_op jit(solution)/shard_map/reduce_scatter | solution.py:92
  9.0 1.8 copy-start.6
  11.2 1.8 copy-start.6
  88.9 5.9 %copy-start.3 = (s32[128,8]{0,1:T(8,128)S(1)}, s32[128,8]{0,1:T(8,128)}, u32[]{:S(2)}) copy-start(s32[128,8]{0,1:T(8,128)} %param.23) | copy-start | bytes 12292
  88.9 5.9 %copy-start.4 = (s32[128,8]{0,1:T(8,128)S(1)}, s32[128,8]{0,1:T(8,128)}, u32[]{:S(2)}) copy-start(s32[128,8]{0,1:T(8,128)} %param.22) | copy-start | bytes 12292
  88.9 5.9 %copy-start.5 = (s32[4]{0:T(128)S(1)}, s32[4]{0:T(128)}, u32[]{:S(2)}) copy-start(s32[4]{0:T(128)} %param.24) | copy-start | bytes 52
  88.9 6.9 %copy-start.2 = (bf16[4096]{0:T(1024)(128)(2,1)S(1)}, bf16[4096]{0:T(1024)(128)(2,1)}, u32[]{:S(2)}) copy-start(bf16[4096]{0:T(1024)(128)(2,1)} %param.21) | copy-start | bytes 24580
  88.9 207.6 %copy-start = (bf16[8,4096]{1,0:T(8,128)(2,1)S(1)}, bf16[8,4096]{1,0:T(8,128)(2,1)}, u32[]{:S(2)}) copy-start(bf16[8,4096]{1,0:T(8,128)(2,1)} %param.15) | copy-start | bytes 196612
  92.9 271.8 %all-gather.7.cloned.1.call-start = ((), (), s32[]{:S(2)}) async-start(), calls=%async_computation.5 | async-start | bytes 3244032 | tf_op jit(solution)/shard_map/all_gather | solution.py:106
  93.6 345.5 %all-gather.11.cloned.1.call-start = ((), (), s32[]{:S(2)}) async-start(), calls=%async_computation.7 | async-start | bytes 3244032 | tf_op jit(solution)/shard_map/all_gather | solution.py:117
  94.2 413.8 %all-gather.9.cloned.1.call-start = ((), (), s32[]{:S(2)}) async-start(), calls=%async_computation.6 | async-start | bytes 3244032 | tf_op jit(solution)/shard_map/all_gather | solution.py:111
  512.4 27.5 %copy-start.1 = (bf16[8,4096]{1,0:T(8,128)(2,1)S(1)}, bf16[8,4096]{1,0:T(8,128)(2,1)}, u32[]{:S(2)}) copy-start(bf16[8,4096]{1,0:T(8,128)(2,1)} %reduce-scatter.2.cloned.1.call-done) | copy-start | bytes 196612
  513.4 26.5 %all-to-all-start.1 = ((bf16[16,4,4096]{2,1,0:T(4,128)(2,1)}), bf16[16,4,4096]{2,1,0:T(4,128)(2,1)S(1)}, u32[]{:S(2)}, u32[]{:S(2)}) async-start(bf16[16,4,4096]{2,1,0:T(4,128)(2,1)} %reshape.72), calls=%async_computation.2 | async-start | bytes 1048576 | tf_op jit(solution)/shard_map/all_to_all | solution.py:121
Sparse Core Ops, SparseCore 0:
  9.4 79.4 all-gather.4
  93.3 203.1 reduce-scatter.1
  298.7 66.0 all-gather.6
  366.7 72.4 all-gather.10
  441.1 66.8 all-gather.8
where the time goes:
time: 549 us; the launch traced here: 548 us
  waiting for transfers between devices  483 us (88%)
  blocking collectives  19.3 us (4%)
  matrix products  16.8 us (3%)
  between operations  14 us (3%)
  starting transfers between devices  9.24 us (2%)
    reduce_scatter x1, waiting for transfers between devices, per_device(): lax.psum_scatter(projected.astype(jnp.bfloat16), 'tensor', scatter_dimens...  201 us
    all_gather x1, waiting for transfers between devices, per_device(): lax.all_gather(out_weight, 'dp', axis=1, tiled=True)  75.3 us
    all_gather x1, waiting for transfers between devices, per_device(): lax.all_gather(down_weight, 'dp', axis=1, tiled=True)  71.9 us
    all_gather x1, waiting for transfers between devices, per_device(): lax.all_gather(up_weight, 'dp', axis=0, tiled=True)  68.9 us
    all_gather x1, waiting for transfers between devices, per_device(): lax.all_gather(gate_weight, 'dp', axis=0, tiled=True)  46.5 us
    all_to_all x1, blocking collectives, per_device(): lax.all_to_all(jnp.repeat(packed, per_expert, axis=0), 'tensor', split_ax...  19.3 us
    all_to_all x1, waiting for transfers between devices, per_device(): lax.all_to_all(slice_parts, 'tensor', split_axis=0, concat_axis=0, tiled=...  17.3 us
  transfers between devices with their start and end apart: 6, of which 6 were waited for; matrix products, arithmetic and copies ran while one was open for 2% of the time, Pallas kernels for 0%

commit v1 on v0

v1 whole, which is shorter than its diff:
```python
import jax
import jax.numpy as jnp
from jax import lax
from jax.experimental import pallas as pl
from jax.experimental.pallas import tpu as pltpu
from jax.sharding import Mesh
from jax.sharding import PartitionSpec as P

DP = ("xl", "y", "core")
TENSOR = ("xh", "z")
RING = 8
FIRST = (0, -1, 1, -2, 2)
SECOND = (-3, 3, 4)
VMEM_BYTES = 48 * 1024 * 1024


def attend(q_dev, keys_dev, values_dev, first_pos):
    slab_rows = q_dev.shape[0]
    head_size = keys_dev.shape[1]
    head_count = q_dev.shape[1] // head_size
    pair_count = head_count // 2
    grouped = (
        q_dev.reshape(slab_rows, pair_count, 2, head_size)
        .transpose(1, 2, 0, 3)
        .reshape(pair_count, 2 * slab_rows, head_size)
    )
    position = first_pos + jnp.arange(2 * slab_rows, dtype=jnp.int32) % slab_rows
    visible = jnp.arange(keys_dev.shape[0], dtype=jnp.int32)[None, :] <= position[:, None]

    def one_pair(q_block):
        scores = lax.dot_general(
            q_block, keys_dev, (((1,), (1,)), ((), ())), preferred_element_type=jnp.float32
        ) * head_size ** (-0.5)
        scores = jnp.where(visible, scores, -1e30)
        maxima = jnp.max(scores, axis=1, keepdims=True)
        exp_scores = jnp.exp(scores - maxima)
        totals = jnp.sum(exp_scores, axis=1, keepdims=True)
        context = (
            jnp.dot(exp_scores.astype(jnp.bfloat16), values_dev, preferred_element_type=jnp.float32)
            / totals
        )
        return context.astype(jnp.bfloat16)

    result = lax.map(one_pair, grouped)
    return (
        result.reshape(pair_count, 2, slab_rows, head_size)
        .transpose(2, 0, 1, 3)
        .reshape(slab_rows, head_count * head_size)
    )


def rms_norm(residual, norm_gain):
    values32 = residual.astype(jnp.float32)
    inverse = lax.rsqrt(jnp.mean(values32 * values32, axis=1, keepdims=True) + 1e-06)
    return (values32 * inverse * norm_gain.astype(jnp.float32)).astype(jnp.bfloat16)


def along_y(block, step):
    return lax.ppermute(block, "y", [(i, (i + step) % RING) for i in range(RING)])


def swap(block, axis):
    return lax.ppermute(block, axis, [(0, 1), (1, 0)])


def ring_gather(weight):
    pair = jnp.stack([weight, swap(weight, "xl")])
    up1, down1 = along_y(pair, 1), along_y(pair, -1)
    up2, down2 = along_y(up1, 1), along_y(down1, -1)
    first = jnp.stack([pair, up1, down1, up2, down2])
    up3, down3 = along_y(up2, 1), along_y(down2, -1)
    other_first = swap(first, "core")
    up4, down4 = along_y(up3[:1], 1), along_y(down3[1:], -1)
    second = jnp.stack([up3, down3, jnp.concatenate([up4, down4])])
    other_second = swap(second, "core")
    return first, second, other_first, other_second


def project_kernel(place_ref, context_ref, first_ref, second_ref, other_first_ref, other_second_ref, out_ref):
    xl, y, core = place_ref[0], place_ref[1], place_ref[2]
    context = context_ref[...]
    for blocks_ref, steps, own in (
        (first_ref, FIRST, 0),
        (other_first_ref, FIRST, 1),
        (second_ref, SECOND, 0),
        (other_second_ref, SECOND, 1),
    ):
        for k, step in enumerate(steps):
            for side in range(2):
                chip = (xl ^ side) * RING + ((y + (step + RING)) & (RING - 1))
                column = pl.multiple_of((chip * 2 + (core ^ own)) * 128, 128)
                out_ref[:, pl.ds(column, 128)] = jnp.dot(
                    context, blocks_ref[k, side], preferred_element_type=jnp.float32
                ).astype(out_ref.dtype)


def project(context, blocks, width):
    place = jnp.stack([lax.axis_index("xl"), lax.axis_index("y"), lax.axis_index("core")]).astype(jnp.int32)
    rows = context.shape[0]
    vmem = pl.BlockSpec(memory_space=pltpu.VMEM)
    return pl.pallas_call(
        project_kernel,
        out_shape=jax.ShapeDtypeStruct((rows, width), jnp.bfloat16),
        in_specs=[pl.BlockSpec(memory_space=pltpu.SMEM)] + [vmem] * 5,
        out_specs=vmem,
        compiler_params=pltpu.CompilerParams(vmem_limit_bytes=VMEM_BYTES),
        cost_estimate=pl.CostEstimate(
            flops=2 * rows * context.shape[1] * width,
            bytes_accessed=2 * context.shape[1] * width,
            transcendentals=0,
        ),
        name="project",
    )(place, context, *blocks)


CHUNKS = 8


def expert_kernel(rows_ref, weights_hbm, out_ref, weights, sems):
    width, hidden = rows_ref.shape[1], weights.shape[1] // 3
    part = width // CHUNKS

    def copy(i):
        at = pl.ds(i * part, part)
        return pltpu.make_async_copy(weights_hbm.at[at], weights.at[at], sems.at[i])

    for i in range(CHUNKS):
        copy(i).start()
    total = jnp.zeros((rows_ref.shape[0], 2 * hidden), jnp.float32)
    for i in range(CHUNKS):
        copy(i).wait()
        total += jnp.dot(
            rows_ref[:, i * part : (i + 1) * part],
            weights[i * part : (i + 1) * part, : 2 * hidden],
            preferred_element_type=jnp.float32,
        )
    gate, up = total[:, :hidden], total[:, hidden:]
    activated = (gate / (1.0 + jnp.exp(-gate)) * up).astype(jnp.bfloat16)
    for d in range(width // 128):
        down = jnp.concatenate(
            [
                weights[d * 128 : (d + 1) * 128, 2 * hidden + j * 128 : 2 * hidden + (j + 1) * 128]
                for j in range(hidden // 128)
            ]
        )
        out_ref[:, d * 128 : (d + 1) * 128] = jnp.dot(
            activated, down, preferred_element_type=jnp.float32
        ).astype(out_ref.dtype)


def expert(rows, weights):
    vmem = pl.BlockSpec(memory_space=pltpu.VMEM)
    return pl.pallas_call(
        expert_kernel,
        out_shape=jax.ShapeDtypeStruct(rows.shape, jnp.bfloat16),
        in_specs=[vmem, pl.BlockSpec(memory_space=pl.ANY)],
        out_specs=vmem,
        scratch_shapes=[
            pltpu.VMEM(weights.shape, jnp.bfloat16),
            pltpu.SemaphoreType.DMA((CHUNKS,)),
        ],
        compiler_params=pltpu.CompilerParams(vmem_limit_bytes=VMEM_BYTES),
        cost_estimate=pl.CostEstimate(
            flops=2 * rows.shape[0] * weights.size, bytes_accessed=2 * weights.size, transcendentals=0
        ),
        name="expert",
    )(rows, weights)


def per_device(
    hidden_rows,
    queries,
    keys,
    values,
    slab_start,
    out_weight,
    norm_gain,
    route_ids,
    route_weights,
    flight_experts,
    gate_weight,
    up_weight,
    down_weight,
):
    tensor_idx = lax.axis_index(TENSOR)
    groups = lax.axis_size(TENSOR)
    own_rows = hidden_rows.shape[0]
    width = hidden_rows.shape[1]
    flight = flight_experts.shape[0]
    per_expert = groups // flight
    capacity = min(4, own_rows)
    hidden = gate_weight.shape[1]

    down_wide = down_weight.reshape(hidden // 128, 128, 128).transpose(1, 0, 2).reshape(128, hidden)
    expert_weights = lax.all_gather(
        jnp.concatenate([gate_weight, up_weight, down_wide], axis=1), DP, axis=0, tiled=True
    )
    blocks = ring_gather(out_weight)
    context = attend(queries, keys, values, slab_start[0])

    matches = route_ids[:, None, :] == flight_experts[None, :, None]
    hits = jnp.sum(matches.astype(jnp.int32), axis=2, dtype=jnp.int32).reshape(
        groups, own_rows, flight
    )
    gate_coef = (
        jnp.sum(jnp.where(matches, route_weights[:, None, :], 0), axis=2, dtype=jnp.int32).astype(
            jnp.float32
        )
        / 65536.0
    )
    own_hits = lax.dynamic_index_in_dim(hits, tensor_idx, 0, keepdims=False)
    slot_number = jnp.cumsum(own_hits, axis=0) - 1
    own_place = jnp.logical_and(
        own_hits[..., None] == 1, slot_number[..., None] == jnp.arange(capacity, dtype=jnp.int32)
    )
    own_coef = lax.dynamic_slice_in_dim(gate_coef, tensor_idx * own_rows, own_rows, 0)

    projected = project(context, blocks, width)
    head_parts = lax.all_to_all(
        projected.reshape(groups, own_rows, width), TENSOR, split_axis=0, concat_axis=0, tiled=True
    )
    attention = jnp.sum(head_parts.astype(jnp.float32), axis=0)
    residual = (hidden_rows.astype(jnp.float32) + attention).astype(jnp.bfloat16)
    normed = rms_norm(residual, norm_gain)
    packed = jnp.einsum(
        "rfc,rd->fcd", own_place.astype(jnp.bfloat16), normed, preferred_element_type=jnp.float32
    ).astype(jnp.bfloat16)
    rows_in = lax.all_to_all(
        jnp.repeat(packed, per_expert, axis=0), TENSOR, split_axis=0, concat_axis=0, tiled=True
    )
    expert_out = expert(rows_in.reshape(groups * capacity, width), expert_weights)
    slice_parts = expert_out.reshape(groups, capacity, width)
    returned = lax.all_to_all(slice_parts, TENSOR, split_axis=0, concat_axis=0, tiled=True)
    weighted = own_place.astype(jnp.float32) * own_coef[:, :, None]
    weighted = jnp.repeat(weighted, per_expert, axis=1)
    expert_sum = jnp.einsum(
        "rtc,tcd->rd", weighted, returned.astype(jnp.float32), precision=lax.Precision.HIGHEST
    )
    return (residual.astype(jnp.float32) + expert_sum).astype(jnp.bfloat16)


def solution(mesh):
    fine = Mesh(mesh.devices.reshape(2, RING, 2, 2, 8), DP + TENSOR)
    placed = (
        P(DP + TENSOR, None),
        P(DP, TENSOR),
        P(DP, TENSOR),
        P(DP, TENSOR),
        P(DP),
        P(TENSOR, DP),
        P(),
        P(DP, None),
        P(DP, None),
        P(),
        P(DP, TENSOR),
        P(DP, TENSOR),
        P(TENSOR, DP),
    )
    return jax.shard_map(
        per_device, mesh=fine, in_specs=placed, out_specs=P(DP + TENSOR, None), check_vma=False
    )
```

time: 549 us -> 196 us (0.36)
  the two profiles are of different devices: /device:TPU:2 before, /device:TPU:24 now
where the time goes in v1:
time: 196 us; the launch traced here: 195 us
  waiting for transfers between devices  75.7 us (39%)
  starting transfers between devices  60.4 us (31%)
  blocking collectives  21.2 us (11%)
  between operations  14.4 us (7%)
  Pallas kernels  8.38 us (4%)
  matrix products  6.36 us (3%)
  local copies, waits for them, and re-layouts  5.6 us (3%)
  other arithmetic  3.19 us (2%)
    ppermute x8, starting transfers between devices, along_y(): lax.ppermute(block, 'y', [(i, (i + step) % RING) for i in range(RING)])  29.1 us
    all_to_all x1, waiting for transfers between devices, per_device(): lax.all_to_all(projected.reshape(groups, own_rows, width), TENSOR, split_...  28.9 us
    ppermute x8, waiting for transfers between devices, along_y(): lax.ppermute(block, 'y', [(i, (i + step) % RING) for i in range(RING)])  26.7 us
    all_to_all x1, blocking collectives, per_device(): lax.all_to_all(jnp.repeat(packed, per_expert, axis=0), TENSOR, split_axis...  21.2 us
    all_to_all x1, starting transfers between devices, per_device(): lax.all_to_all(projected.reshape(groups, own_rows, width), TENSOR, split_...  19.3 us
    all_to_all x1, waiting for transfers between devices, per_device(): lax.all_to_all(slice_parts, TENSOR, split_axis=0, concat_axis=0, tiled=True)  16.1 us
    ppermute x3, starting transfers between devices, swap(): return lax.ppermute(block, axis, [(0, 1), (1, 0)])  7.24 us
    pallas_call x1, Pallas kernels, expert(): pl.pallas_call(expert_kernel, out_shape=jax.ShapeDtypeStruct(rows.shape,...  5.02 us
  transfers between devices with their start and end apart: 14, of which 9 were waited for; matrix products, arithmetic and copies ran while one was open for 5% of the time, Pallas kernels for 2%

profile of v1, /device:TPU:24, one launch (start us, length us, event | category | flops | bytes accessed | tf_op | source)
XLA Modules:
  0.0 195.3 jit_solution(16790297347135508321)
XLA Ops:
  6.5 1.0 copy.50
  7.7 1.7 pad_maximum_fusion.1
  9.4 3.4 %collective-permute-start = (bf16[512,128]{1,0:T(8,128)(2,1)}, bf16[512,128]{1,0:T(8,128)(2,1)S(1)}, u32[]{:S(2)}, u32[]{:S(2)}) collective-permute-start(bf16[512,128]{1,0:T(8,128)(2,1)} %param.20), channel_id=1, source_target_pairs={{0,256},{256,0},{1,257},{257,1},{2,258},{258,2},{3,259},{259,3},{4... | collective-permute-start | bytes 393224 | tf_op jit(solution)/shard_map/ppermute | solution.py:63
  12.8 3.9 %collective-permute-done = bf16[512,128]{1,0:T(8,128)(2,1)S(1)} collective-permute-done((bf16[512,128]{1,0:T(8,128)(2,1)}, bf16[512,128]{1,0:T(8,128)(2,1)S(1)}, u32[]{:S(2)}, u32[]{:S(2)}) %collective-permute-start) | collective-permute-done | bytes 131104 | tf_op jit(solution)/shard_map/ppermute | solution.py:63
  16.8 4.7 %collective-permute-start.1 = (bf16[2,512,128]{2,1,0:T(8,128)(2,1)S(1)}, bf16[2,512,128]{2,1,0:T(8,128)(2,1)S(1)}, u32[]{:S(2)}, u32[]{:S(2)}) collective-permute-start(bf16[2,512,128]{2,1,0:T(8,128)(2,1)S(1)} %pad_maximum_fusion.2), channel_id=1, source_target_pairs={{0,32},{32,64},{64,96},{96,128},{128,160},{160,192},{192,224},{224... | collective-permute-start | bytes 786440 | tf_op jit(solution)/shard_map/ppermute | solution.py:59
  21.5 1.9 collective-permute-start.2
  24.2 2.0 %collective-permute-done.1 = bf16[2,512,128]{2,1,0:T(8,128)(2,1)S(1)} collective-permute-done((bf16[2,512,128]{2,1,0:T(8,128)(2,1)S(1)}, bf16[2,512,128]{2,1,0:T(8,128)(2,1)S(1)}, u32[]{:S(2)}, u32[]{:S(2)}) %collective-permute-start.1) | collective-permute-done | bytes 262176 | tf_op jit(solution)/shard_map/ppermute | solution.py:59
  26.2 5.6 %collective-permute-start.3 = (bf16[2,512,128]{2,1,0:T(8,128)(2,1)S(1)}, bf16[2,512,128]{2,1,0:T(8,128)(2,1)S(1)}, u32[]{:S(2)}, u32[]{:S(2)}) collective-permute-start(bf16[2,512,128]{2,1,0:T(8,128)(2,1)S(1)} %collective-permute-done.1), channel_id=1, source_target_pairs={{0,32},{32,64},{64,96},{96,128},{128,160},{160,192},{192,224},{224... | collective-permute-start | bytes 786440 | tf_op jit(solution)/shard_map/ppermute | solution.py:59
  31.8 1.9 collective-permute-start.4
  33.8 8.6 %collective-permute-done.3 = bf16[2,512,128]{2,1,0:T(8,128)(2,1)S(1)} collective-permute-done((bf16[2,512,128]{2,1,0:T(8,128)(2,1)S(1)}, bf16[2,512,128]{2,1,0:T(8,128)(2,1)S(1)}, u32[]{:S(2)}, u32[]{:S(2)}) %collective-permute-start.3) | collective-permute-done | bytes 262176 | tf_op jit(solution)/shard_map/ppermute | solution.py:59
  42.3 5.6 %collective-permute-start.5 = (bf16[2,512,128]{2,1,0:T(8,128)(2,1)S(1)}, bf16[2,512,128]{2,1,0:T(8,128)(2,1)S(1)}, u32[]{:S(2)}, u32[]{:S(2)}) collective-permute-start(bf16[2,512,128]{2,1,0:T(8,128)(2,1)S(1)} %collective-permute-done.3), channel_id=1, source_target_pairs={{0,32},{32,64},{64,96},{96,128},{128,160},{160,192},{192,224},{224... | collective-permute-start | bytes 786440 | tf_op jit(solution)/shard_map/ppermute | solution.py:59
  48.5 1.9 collective-permute-start.6
  50.5 7.9 %collective-permute-done.5 = bf16[2,512,128]{2,1,0:T(8,128)(2,1)S(1)} collective-permute-done((bf16[2,512,128]{2,1,0:T(8,128)(2,1)S(1)}, bf16[2,512,128]{2,1,0:T(8,128)(2,1)S(1)}, u32[]{:S(2)}, u32[]{:S(2)}) %collective-permute-start.5) | collective-permute-done | bytes 262176 | tf_op jit(solution)/shard_map/ppermute | solution.py:59
  58.4 5.6 %collective-permute-start.7 = (bf16[1,512,128]{2,1,0:T(8,128)(2,1)S(1)}, bf16[1,512,128]{2,1,0:T(8,128)(2,1)S(1)}, u32[]{:S(2)}, u32[]{:S(2)}) collective-permute-start(bf16[1,512,128]{2,1,0:T(8,128)(2,1)S(1)} %slice.8), channel_id=1, source_target_pairs={{0,32},{32,64},{64,96},{96,128},{128,160},{160,192},{192,224},{224... | collective-permute-start | bytes 393224 | tf_op jit(solution)/shard_map/ppermute | solution.py:59
  65.0 1.9 collective-permute-start.8
  66.9 1.9 collective-permute-start.9
  68.9 6.7 %collective-permute-done.8 = bf16[1,512,128]{2,1,0:T(8,128)(2,1)S(1)} collective-permute-done((bf16[1,512,128]{2,1,0:T(8,128)(2,1)S(1)}, bf16[1,512,128]{2,1,0:T(8,128)(2,1)S(1)}, u32[]{:S(2)}, u32[]{:S(2)}) %collective-permute-start.8) | collective-permute-done | bytes 131104 | tf_op jit(solution)/shard_map/ppermute | solution.py:59
  75.7 1.9 collective-permute-start.10
  77.7 5.7 %while.11 = (s32[]{:T(128)}, bf16[2,256,128]{2,1,0:T(8,128)(2,1)}, bf16[2,256,128]{2,1,0:T(8,128)(2,1)S(1)}, bf16[1152,128]{1,0:T(8,128)(2,1)}, bf16[1152,128]{1,0:T(8,128)(2,1)}, /*index=5*/s32[256]{0:T(256)S(1)}, s32[]{:T(128)}) while((s32[]{:T(128)}, bf16[2,256,128]{2,1,0:T(8,128)(2,1)}, bf16[2,256,128]{2,1,0:T(8,128)(2,1)S(1)}, ...), condition=%wide.region_3.4_spmd.clone, body=%wide.region_0.3_spmd.clone.sunk | while | flops 153419264 | bytes 5446253 | solution.py:44
  77.7 1.4 fusion.44
  79.5 1.0 fusion.46
  80.5 1.4 fusion.44
  82.3 1.0 fusion.46
  83.3 1.7 copy.58
  86.1 3.4 %project.1 = bf16[128,4096]{1,0:T(8,128)(2,1)} custom-call(s32[3]{0:T(128)S(1)} %pad_add_fusion.place_ref, bf16[128,512]{1,0:T(8,128)(2,1)S(1)} %reshape.80.context_ref, bf16[5,2,512,128]{3,2,1,0:T(8,128)(2,1)S(1)} %bitcast_dynamic-update-slice_fusion.first_ref, bf16[3,2,512,128]{3,2,1,0:T(8,128)(2,1)S(1)} %pad_maximum_fusion.second_ref, ...), custom_call_target="tpu_custom_call" | custom-call | flops 536870912 | bytes 4194304 | tf_op jit(solution)/shard_map/project/pallas_call | solution.py:101
  89.5 19.3 %all-to-all-start = ((bf16[16,8,4096]{2,1,0:T(8,128)(2,1)}), bf16[16,8,4096]{2,1,0:T(8,128)(2,1)S(1)}, u32[]{:S(2)}, u32[]{:S(2)}) async-start(bf16[16,8,4096]{2,1,0:T(8,128)(2,1)} %bitcast.18), calls=%async_computation | async-start | bytes 2097152 | tf_op jit(solution)/shard_map/all_to_all | solution.py:219
  109.2 28.9 %all-to-all-done = bf16[16,8,4096]{2,1,0:T(8,128)(2,1)S(1)} async-done(((bf16[16,8,4096]{2,1,0:T(8,128)(2,1)}), bf16[16,8,4096]{2,1,0:T(8,128)(2,1)S(1)}, u32[]{:S(2)}, u32[]{:S(2)}) %all-to-all-start) | async-done | bytes 1048608 | tf_op jit(solution)/shard_map/all_to_all | solution.py:219
  138.8 21.2 %all_to_all.15 = bf16[16,4,4096]{2,1,0:T(4,128)(2,1)S(1)} all-to-all(bf16[16,4,4096]{2,1,0:T(4,128)(2,1)S(1)} %bitcast.67), channel_id=1, replica_groups=mesh['xl'=2,'y'=8,'core'=2,'xh'=2,'z'=8] {'xh','z'}, dimensions={0} | all-to-all | bytes 1048576 | tf_op jit(solution)/shard_map/all_to_all | solution.py:228
  160.2 5.0 %expert.1 = bf16[64,4096]{1,0:T(8,128)(2,1)S(1)} custom-call(bf16[64,4096]{1,0:T(8,128)(2,1)S(1)} %reshape.85.rows_ref, bf16[4096,1152]{1,0:T(8,128)(2,1)} %all-gather.2.cloned.1.call-done.weights_hbm), custom_call_target="tpu_custom_call" | custom-call | flops 603979776 | bytes 9437184 | tf_op jit(solution)/shard_map/expert/pallas_call | solution.py:153
  166.2 4.8 %all-to-all-start.2 = ((bf16[16,4,4096]{2,1,0:T(4,128)(2,1)}), bf16[16,4,4096]{2,1,0:T(4,128)(2,1)S(1)}, u32[]{:S(2)}, u32[]{:S(2)}) async-start(bf16[16,4,4096]{2,1,0:T(4,128)(2,1)} %reshape.88), calls=%async_computation.2 | async-start | bytes 1048576 | tf_op jit(solution)/shard_map/all_to_all | solution.py:233
  171.1 16.1 %all-to-all-done.2 = bf16[16,4,4096]{2,1,0:T(4,128)(2,1)S(1)} async-done(((bf16[16,4,4096]{2,1,0:T(4,128)(2,1)}), bf16[16,4,4096]{2,1,0:T(4,128)(2,1)S(1)}, u32[]{:S(2)}, u32[]{:S(2)}) %all-to-all-start.2) | async-done | bytes 524320 | tf_op jit(solution)/shard_map/all_to_all | solution.py:233
  187.3 1.2 fusion.14
  (65 shorter events, 6.2 us)
Async XLA Ops:
  6.5 10.2 %copy-start = (bf16[512,128]{1,0:T(8,128)(2,1)S(1)}, bf16[512,128]{1,0:T(8,128)(2,1)}, u32[]{:S(2)}) copy-start(bf16[512,128]{1,0:T(8,128)(2,1)} %param.20) | copy-start | bytes 393220
  6.5 16.9 %copy-start.1 = (bf16[128,512]{1,0:T(8,128)(2,1)S(1)}, bf16[128,512]{1,0:T(8,128)(2,1)}, u32[]{:S(2)}) copy-start(bf16[128,512]{1,0:T(8,128)(2,1)} %param.16) | copy-start | bytes 393220
  6.5 153.6 %all-gather.2.cloned.1.call-start = ((), (), s32[]{:S(2)}) async-start(), calls=%async_computation.3 | async-start | bytes 9732096 | tf_op jit(solution)/shard_map/all_gather | solution.py:195
  9.4 7.3 %collective-permute-start = (bf16[512,128]{1,0:T(8,128)(2,1)}, bf16[512,128]{1,0:T(8,128)(2,1)S(1)}, u32[]{:S(2)}, u32[]{:S(2)}) collective-permute-start(bf16[512,128]{1,0:T(8,128)(2,1)} %param.20), channel_id=1, source_target_pairs={{0,256},{256,0},{1,257},{257,1},{2,258},{258,2},{3,259},{259,3},{4... | collective-permute-start | bytes 393224 | tf_op jit(solution)/shard_map/ppermute | solution.py:63
  16.8 9.4 %collective-permute-start.1 = (bf16[2,512,128]{2,1,0:T(8,128)(2,1)S(1)}, bf16[2,512,128]{2,1,0:T(8,128)(2,1)S(1)}, u32[]{:S(2)}, u32[]{:S(2)}) collective-permute-start(bf16[2,512,128]{2,1,0:T(8,128)(2,1)S(1)} %pad_maximum_fusion.2), channel_id=1, source_target_pairs={{0,32},{32,64},{64,96},{96,128},{128,160},{160,192},{192,224},{224... | collective-permute-start | bytes 786440 | tf_op jit(solution)/shard_map/ppermute | solution.py:59
  21.5 10.3 %collective-permute-start.2 = (bf16[2,512,128]{2,1,0:T(8,128)(2,1)S(1)}, bf16[2,512,128]{2,1,0:T(8,128)(2,1)S(1)}, u32[]{:S(2)}, u32[]{:S(2)}) collective-permute-start(bf16[2,512,128]{2,1,0:T(8,128)(2,1)S(1)} %pad_maximum_fusion.2), channel_id=1, source_target_pairs={{0,224},{32,0},{64,32},{96,64},{128,96},{160,128},{192,160},{224,1... | collective-permute-start | bytes 786440 | tf_op jit(solution)/shard_map/ppermute | solution.py:59
  26.2 16.2 %collective-permute-start.3 = (bf16[2,512,128]{2,1,0:T(8,128)(2,1)S(1)}, bf16[2,512,128]{2,1,0:T(8,128)(2,1)S(1)}, u32[]{:S(2)}, u32[]{:S(2)}) collective-permute-start(bf16[2,512,128]{2,1,0:T(8,128)(2,1)S(1)} %collective-permute-done.1), channel_id=1, source_target_pairs={{0,32},{32,64},{64,96},{96,128},{128,160},{160,192},{192,224},{224... | collective-permute-start | bytes 786440 | tf_op jit(solution)/shard_map/ppermute | solution.py:59
  31.8 16.7 %collective-permute-start.4 = (bf16[2,512,128]{2,1,0:T(8,128)(2,1)S(1)}, bf16[2,512,128]{2,1,0:T(8,128)(2,1)S(1)}, u32[]{:S(2)}, u32[]{:S(2)}) collective-permute-start(bf16[2,512,128]{2,1,0:T(8,128)(2,1)S(1)} %collective-permute-done.2), channel_id=1, source_target_pairs={{0,224},{32,0},{64,32},{96,64},{128,96},{160,128},{192,160},{224,1... | collective-permute-start | bytes 786440 | tf_op jit(solution)/shard_map/ppermute | solution.py:59
  42.3 16.1 %collective-permute-start.5 = (bf16[2,512,128]{2,1,0:T(8,128)(2,1)S(1)}, bf16[2,512,128]{2,1,0:T(8,128)(2,1)S(1)}, u32[]{:S(2)}, u32[]{:S(2)}) collective-permute-start(bf16[2,512,128]{2,1,0:T(8,128)(2,1)S(1)} %collective-permute-done.3), channel_id=1, source_target_pairs={{0,32},{32,64},{64,96},{96,128},{128,160},{160,192},{192,224},{224... | collective-permute-start | bytes 786440 | tf_op jit(solution)/shard_map/ppermute | solution.py:59
  48.5 16.4 %collective-permute-start.6 = (bf16[2,512,128]{2,1,0:T(8,128)(2,1)S(1)}, bf16[2,512,128]{2,1,0:T(8,128)(2,1)S(1)}, u32[]{:S(2)}, u32[]{:S(2)}) collective-permute-start(bf16[2,512,128]{2,1,0:T(8,128)(2,1)S(1)} %collective-permute-done.4), channel_id=1, source_target_pairs={{0,224},{32,0},{64,32},{96,64},{128,96},{160,128},{192,160},{224,1... | collective-permute-start | bytes 786440 | tf_op jit(solution)/shard_map/ppermute | solution.py:59
  58.4 10.5 %collective-permute-start.7 = (bf16[1,512,128]{2,1,0:T(8,128)(2,1)S(1)}, bf16[1,512,128]{2,1,0:T(8,128)(2,1)S(1)}, u32[]{:S(2)}, u32[]{:S(2)}) collective-permute-start(bf16[1,512,128]{2,1,0:T(8,128)(2,1)S(1)} %slice.8), channel_id=1, source_target_pairs={{0,32},{32,64},{64,96},{96,128},{128,160},{160,192},{192,224},{224... | collective-permute-start | bytes 393224 | tf_op jit(solution)/shard_map/ppermute | solution.py:59
  65.0 10.6 %collective-permute-start.8 = (bf16[1,512,128]{2,1,0:T(8,128)(2,1)S(1)}, bf16[1,512,128]{2,1,0:T(8,128)(2,1)S(1)}, u32[]{:S(2)}, u32[]{:S(2)}) collective-permute-start(bf16[1,512,128]{2,1,0:T(8,128)(2,1)S(1)} %slice.9), channel_id=1, source_target_pairs={{0,224},{32,0},{64,32},{96,64},{128,96},{160,128},{192,160},{224,1... | collective-permute-start | bytes 393224 | tf_op jit(solution)/shard_map/ppermute | solution.py:59
  66.9 19.1 %collective-permute-start.9 = (bf16[5,2,512,128]{3,2,1,0:T(8,128)(2,1)S(1)}, bf16[5,2,512,128]{3,2,1,0:T(8,128)(2,1)S(1)}, u32[]{:S(2)}, u32[]{:S(2)}) collective-permute-start(bf16[5,2,512,128]{3,2,1,0:T(8,128)(2,1)S(1)} %bitcast_dynamic-update-slice_fusion.first_ref), channel_id=1, source_target_pairs={{0,16},{16,0},{1,17},{17,1},{2,18},{18,2},{3,19},{19,3},{4,20},{20... | collective-permute-start | bytes 3932168 | tf_op jit(solution)/shard_map/ppermute | solution.py:63
  75.7 10.3 %collective-permute-start.10 = (bf16[3,2,512,128]{3,2,1,0:T(8,128)(2,1)S(1)}, bf16[3,2,512,128]{3,2,1,0:T(8,128)(2,1)}, u32[]{:S(2)}, u32[]{:S(2)}) collective-permute-start(bf16[3,2,512,128]{3,2,1,0:T(8,128)(2,1)S(1)} %pad_maximum_fusion.second_ref), channel_id=1, source_target_pairs={{0,16},{16,0},{1,17},{17,1},{2,18},{18,2},{3,19},{19,3},{4,20},{20... | collective-permute-start | bytes 2359304 | tf_op jit(solution)/shard_map/ppermute | solution.py:63
  77.7 1.8 copy-start.7
  80.5 1.8 copy-start.7
  89.4 19.3 %copy-start.4 = (s32[128,8]{0,1:T(8,128)S(1)}, s32[128,8]{0,1:T(8,128)}, u32[]{:S(2)}) copy-start(s32[128,8]{0,1:T(8,128)} %param.22) | copy-start | bytes 12292
  89.4 19.3 %copy-start.5 = (s32[128,8]{0,1:T(8,128)S(1)}, s32[128,8]{0,1:T(8,128)}, u32[]{:S(2)}) copy-start(s32[128,8]{0,1:T(8,128)} %param.23) | copy-start | bytes 12292
  89.4 19.3 %copy-start.6 = (s32[4]{0:T(128)S(1)}, s32[4]{0:T(128)}, u32[]{:S(2)}) copy-start(s32[4]{0:T(128)} %param.24) | copy-start | bytes 52
  89.4 19.7 %copy-start.3 = (bf16[4096]{0:T(1024)(128)(2,1)S(1)}, bf16[4096]{0:T(1024)(128)(2,1)}, u32[]{:S(2)}) copy-start(bf16[4096]{0:T(1024)(128)(2,1)} %param.21) | copy-start | bytes 24580
  89.5 48.7 %copy-start.2 = (bf16[8,4096]{1,0:T(8,128)(2,1)S(1)}, bf16[8,4096]{1,0:T(8,128)(2,1)}, u32[]{:S(2)}) copy-start(bf16[8,4096]{1,0:T(8,128)(2,1)} %param.15) | copy-start | bytes 196612
  89.5 48.6 %all-to-all-start = ((bf16[16,8,4096]{2,1,0:T(8,128)(2,1)}), bf16[16,8,4096]{2,1,0:T(8,128)(2,1)S(1)}, u32[]{:S(2)}, u32[]{:S(2)}) async-start(bf16[16,8,4096]{2,1,0:T(8,128)(2,1)} %bitcast.18), calls=%async_computation | async-start | bytes 2097152 | tf_op jit(solution)/shard_map/all_to_all | solution.py:219
  166.2 21.1 %all-to-all-start.2 = ((bf16[16,4,4096]{2,1,0:T(4,128)(2,1)}), bf16[16,4,4096]{2,1,0:T(4,128)(2,1)S(1)}, u32[]{:S(2)}, u32[]{:S(2)}) async-start(bf16[16,4,4096]{2,1,0:T(4,128)(2,1)} %reshape.88), calls=%async_computation.2 | async-start | bytes 1048576 | tf_op jit(solution)/shard_map/all_to_all | solution.py:233
Sparse Core Ops, SparseCore 0:
  9.5 88.3 all-gather.1

commit v2 on v0

v2 whole, which is shorter than its diff:
```python
import jax
import jax.numpy as jnp
from jax import lax
from jax.experimental import pallas as pl
from jax.experimental.pallas import tpu as pltpu
from jax.sharding import Mesh
from jax.sharding import PartitionSpec as P

DP = ("xl", "y", "core")
TENSOR = ("xh", "z")
RING = 8
STEPS = (0, -1, 1, -2, 2, -3, 3)
SLAB = 128
HALF = 2048
COLS = 256
HIDDEN = 384
HEADS_WIDE = 512
CAP = 4
FLIGHT = 4
GROUP = 4
BLOCKS = 16
ROWS = 8
VMEM_BYTES = 48 * 1024 * 1024
F32, BF16 = jnp.float32, jnp.bfloat16


def attend(q_dev, keys_dev, values_dev, first_pos):
    slab_rows = q_dev.shape[0]
    head_size = keys_dev.shape[1]
    head_count = q_dev.shape[1] // head_size
    pair_count = head_count // 2
    grouped = (
        q_dev.reshape(slab_rows, pair_count, 2, head_size)
        .transpose(1, 2, 0, 3)
        .reshape(pair_count, 2 * slab_rows, head_size)
    )
    position = first_pos + jnp.arange(2 * slab_rows, dtype=jnp.int32) % slab_rows
    visible = jnp.arange(keys_dev.shape[0], dtype=jnp.int32)[None, :] <= position[:, None]

    def one_pair(q_block):
        scores = lax.dot_general(
            q_block, keys_dev, (((1,), (1,)), ((), ())), preferred_element_type=jnp.float32
        ) * head_size ** (-0.5)
        scores = jnp.where(visible, scores, -1e30)
        maxima = jnp.max(scores, axis=1, keepdims=True)
        exp_scores = jnp.exp(scores - maxima)
        totals = jnp.sum(exp_scores, axis=1, keepdims=True)
        context = (
            jnp.dot(exp_scores.astype(jnp.bfloat16), values_dev, preferred_element_type=jnp.float32)
            / totals
        )
        return context.astype(jnp.bfloat16)

    result = lax.map(one_pair, grouped)
    return (
        result.reshape(pair_count, 2, slab_rows, head_size)
        .transpose(2, 0, 1, 3)
        .reshape(slab_rows, head_count * head_size)
    )


def swap(block, axis):
    return lax.ppermute(block, axis, [(0, 1), (1, 0)])


def along_z(block, step):
    return lax.ppermute(block, "z", [(i, (i + step) % RING) for i in range(RING)])


def by_slab(own, other, xl):
    return jnp.where(xl == 0, jnp.stack([own, other]), jnp.stack([other, own]))


def kernel_call(body, out_shapes, operands, spaces, flops, moved, name, scratch=()):
    kinds = {
        "v": pl.BlockSpec(memory_space=pltpu.VMEM),
        "s": pl.BlockSpec(memory_space=pltpu.SMEM),
        "h": pl.BlockSpec(memory_space=pl.ANY),
    }
    return pl.pallas_call(
        body,
        out_shape=[jax.ShapeDtypeStruct(shape, dtype) for shape, dtype in out_shapes],
        in_specs=[kinds[s] for s in spaces],
        out_specs=[kinds["v"]] * len(out_shapes),
        scratch_shapes=list(scratch),
        compiler_params=pltpu.CompilerParams(vmem_limit_bytes=VMEM_BYTES),
        cost_estimate=pl.CostEstimate(flops=flops, bytes_accessed=moved, transcendentals=0),
        name=name,
    )(*operands)


def pack_weights_kernel(gate_ref, up_ref, down_ref, out_weight_ref, packed_ref):
    packed_ref[:, :HIDDEN] = gate_ref[...]
    packed_ref[:, HIDDEN : 2 * HIDDEN] = up_ref[...]
    at = 2 * HIDDEN
    for ref in (down_ref, out_weight_ref):
        for j in range(ref.shape[0] // 128):
            packed_ref[:, at : at + 128] = ref[j * 128 : (j + 1) * 128, :]
            at += 128


def project_kernel(place_ref, hidden_ref, *refs):
    contexts, (weights_hbm, keep_ref, send_ref, weights, sems) = refs[:9], refs[9:]
    xh, z = place_ref[3], place_ref[4]

    def copy(k):
        at = pl.ds(k * 2 * 128, 2 * 128)
        return pltpu.make_async_copy(
            weights_hbm.at[at, pl.ds(3 * HIDDEN, HEADS_WIDE)], weights.at[at], sems.at[k]
        )

    for k in range(RING):
        copy(k).start()
    for k in range(RING):
        copy(k).wait()
    total = jnp.zeros((2 * SLAB, COLS), F32)
    for k in range(RING):
        if k < len(STEPS):
            step, context = STEPS[k], contexts[k][...]
        else:
            step, context = 4, jnp.concatenate([contexts[k][...], contexts[k + 1][...]])
        first = pl.multiple_of(((z + (step + RING)) & (RING - 1)) * 256, 256)
        block = weights[pl.ds(first, 256), :]
        for half in range(2):
            rhs = jnp.concatenate(
                [
                    jnp.concatenate([block[:128, q * 128 : (q + 1) * 128], block[128:, q * 128 : (q + 1) * 128]], axis=1)
                    for q in (2 * half, 2 * half + 1)
                ]
            )
            total += jnp.dot(context[:, half * 256 : (half + 1) * 256], rhs, preferred_element_type=F32)
    low, high = total[:SLAB], total[SLAB:]
    keep_ref[...] = jnp.where(xh == 0, low, high) + hidden_ref[...].astype(F32)
    send_ref[...] = jnp.where(xh == 0, high, low).astype(BF16)


def residual_kernel(keep_ref, recv_ref, place_ref, residual_ref, rows_ref):
    residual = (keep_ref[...] + recv_ref[...].astype(F32)).astype(BF16)
    residual_ref[...] = residual
    picked = jnp.dot(place_ref[...], residual, preferred_element_type=F32).astype(BF16)
    per_expert = BLOCKS * CAP
    for f in range(FLIGHT):
        for j in range(GROUP):
            at = (f * GROUP + j) * per_expert
            rows_ref[at : at + per_expert, :] = picked[f * per_expert : (f + 1) * per_expert]


def gate_up_kernel(rows_ref, gain_ref, weights_hbm, own_ref, send_ref, weights, sems):
    part = HALF // RING

    def copy(k):
        at = pl.ds(k * part, part)
        return pltpu.make_async_copy(
            weights_hbm.at[at, pl.ds(0, 2 * HIDDEN)], weights.at[at], sems.at[k]
        )

    for k in range(RING):
        copy(k).start()
    slots = BLOCKS * CAP
    total = jnp.zeros((2 * slots, 2 * HIDDEN), F32)
    squares = jnp.zeros((2 * slots, 1), F32)
    for k in range(RING):
        rows = jnp.concatenate(
            [rows_ref[k * slots : (k + 1) * slots, :], rows_ref[(RING + k) * slots : (RING + k + 1) * slots, :]]
        ).astype(F32)
        squares += jnp.sum(rows * rows, axis=1, keepdims=True)
        scaled = (rows * gain_ref[:, k * part : (k + 1) * part].astype(F32)).astype(BF16)
        copy(k).wait()
        total += jnp.dot(scaled, weights[k * part : (k + 1) * part, :], preferred_element_type=F32)
    own_ref[:, : 2 * HIDDEN] = total
    own_ref[:, 2 * HIDDEN :] = jnp.broadcast_to(squares, (2 * slots, 128))
    send_ref[:, : 2 * HIDDEN] = total.astype(BF16)
    high = squares.astype(BF16)
    rest = squares - high.astype(F32)
    middle = rest.astype(BF16)
    low = (rest - middle.astype(F32)).astype(BF16)
    lane = lax.broadcasted_iota(jnp.int32, (2 * slots, 128), 1)
    tail = jnp.where(lane == 0, high.astype(F32), 0.0)
    tail = jnp.where(lane == 1, middle.astype(F32), tail)
    tail = jnp.where(lane == 2, low.astype(F32), tail)
    send_ref[:, 2 * HIDDEN :] = tail.astype(BF16)


def down_kernel(own_ref, recv_ref, residual_ref, weights_hbm, out_ref, weights, sem):
    copy = pltpu.make_async_copy(weights_hbm.at[:, pl.ds(2 * HIDDEN, HIDDEN)], weights, sem)
    copy.start()
    slots = 2 * BLOCKS * CAP
    other = recv_ref[:, 2 * HIDDEN :].astype(F32)
    squares = own_ref[:, 2 * HIDDEN : 2 * HIDDEN + 1] + jnp.sum(other, axis=1, keepdims=True)
    inverse = lax.rsqrt(squares / (2 * HALF) + 1e-06)
    total = (own_ref[:, : 2 * HIDDEN] + recv_ref[:, : 2 * HIDDEN].astype(F32)) * inverse
    gate, up = total[:, :HIDDEN], total[:, HIDDEN:]
    activated = (gate / (1.0 + jnp.exp(-gate)) * up).astype(BF16)
    to = lax.broadcasted_iota(jnp.int32, (slots, slots), 0)
    source = lax.broadcasted_iota(jnp.int32, (slots, slots), 1)
    wanted = ((to >> 2) & 1) * (BLOCKS * CAP) + (to >> 3) * CAP + (to & 3)
    order = jnp.where(source == wanted, 1.0, 0.0).astype(BF16)
    activated = jnp.dot(order, activated, preferred_element_type=F32).astype(BF16)
    copy.wait()
    for d in range(HALF // 256):
        rhs = jnp.concatenate(
            [
                jnp.concatenate(
                    [
                        weights[(2 * d + e) * 128 : (2 * d + e + 1) * 128, j * 128 : (j + 1) * 128]
                        for j in range(HIDDEN // 128)
                    ]
                )
                for e in range(2)
            ],
            axis=1,
        )
        out_ref[:, d * 256 : (d + 1) * 256] = jnp.dot(
            activated, rhs, preferred_element_type=F32
        ).astype(BF16)
    out_ref[:, HALF:] = residual_ref[...]


def combine_kernel(place_ref, coefs_ref, returned_ref, keep_ref, send_ref):
    xl = place_ref[0]
    coefs = coefs_ref[...]
    high = coefs.astype(BF16)
    rest = coefs - high.astype(F32)
    middle = rest.astype(BF16)
    low = (rest - middle.astype(F32)).astype(BF16)
    slots = BLOCKS * ROWS
    to = lax.broadcasted_iota(jnp.int32, (slots, slots), 0)
    source = lax.broadcasted_iota(jnp.int32, (slots, slots), 1)
    wanted = ((to >> 3) & 1) * (RING * ROWS) + (to >> 4) * ROWS + (to & 7)
    order = jnp.where(source == wanted, 1.0, 0.0).astype(BF16)
    residual = jnp.dot(order, returned_ref[:, HALF:], preferred_element_type=F32)
    for k in range(RING):
        at = slice(k * COLS, (k + 1) * COLS)
        parts = returned_ref[:, at]
        mixed = (
            residual[k * 16 : (k + 1) * 16]
            + jnp.dot(high, parts, preferred_element_type=F32)
            + (
                jnp.dot(middle, parts, preferred_element_type=F32)
                + jnp.dot(low, parts, preferred_element_type=F32)
            )
        )
        keep_ref[:, at] = jnp.where(xl == 0, mixed[:ROWS], mixed[ROWS:]).astype(BF16)
        send_ref[:, at] = jnp.where(xl == 0, mixed[ROWS:], mixed[:ROWS]).astype(BF16)


def per_device(
    hidden_rows,
    queries,
    keys,
    values,
    slab_start,
    out_weight,
    norm_gain,
    route_ids,
    route_weights,
    flight_experts,
    gate_weight,
    up_weight,
    down_weight,
):
    xl, xh = lax.axis_index("xl"), lax.axis_index("xh")
    tensor_idx = lax.axis_index(TENSOR)
    place = jnp.stack([lax.axis_index(a) for a in DP + TENSOR]).astype(jnp.int32)

    swapped = lax.ppermute(
        out_weight, ("y", "z"), [(a * RING + b, b * RING + a) for a in range(RING) for b in range(RING)]
    )
    context = attend(queries, keys, values, slab_start[0])
    swapped, context = lax.optimization_barrier((swapped, context))
    (packed,) = kernel_call(
        pack_weights_kernel,
        [((128, 3 * HIDDEN + HEADS_WIDE), BF16)],
        (gate_weight, up_weight, down_weight, swapped),
        "vvvv",
        0,
        4 * 128 * 1664,
        "pack_weights",
    )
    weights = lax.all_gather(packed, ("y", "core"), axis=0, tiled=True)

    hidden_own = lax.dynamic_slice(hidden_rows, (0, xl * HALF), (ROWS, HALF))
    hidden_other = swap(lax.dynamic_slice(hidden_rows, (0, (1 - xl) * HALF), (ROWS, HALF)), "xl")
    hidden_both = by_slab(hidden_own, hidden_other, xl)
    hidden_cols = lax.all_to_all(
        hidden_both.reshape(2, ROWS, RING, COLS).transpose(0, 2, 1, 3).reshape(BLOCKS, ROWS, COLS),
        TENSOR,
        split_axis=0,
        concat_axis=0,
        tiled=True,
    ).reshape(SLAB, COLS)

    matches = route_ids[:, None, :] == flight_experts[None, :, None]
    hits = jnp.sum(matches.astype(jnp.int32), axis=2, dtype=jnp.int32)
    units = jnp.sum(jnp.where(matches, route_weights[:, None, :], 0), axis=2, dtype=jnp.int32)
    table = jnp.concatenate([hits, units], axis=1).T
    tables = by_slab(table, swap(table, "xl"), xl)
    tables = tables.transpose(0, 2, 1).reshape(2, BLOCKS, ROWS, 2 * FLIGHT)
    hits, units = tables[..., :FLIGHT], tables[..., FLIGHT:]
    slot = jnp.cumsum(hits, axis=2) - 1
    placing = jnp.logical_and(
        hits[..., None] == 1, slot[..., None] == jnp.arange(CAP, dtype=jnp.int32)
    )
    coef = units.astype(F32) / 65536.0
    here = lax.dynamic_index_in_dim(placing, xh, 0, keepdims=False).astype(BF16)
    same = jnp.eye(BLOCKS, dtype=BF16)
    picker = (
        here.transpose(2, 0, 3, 1)[:, :, :, None, :] * same[None, :, None, :, None]
    ).reshape(FLIGHT * BLOCKS * CAP, SLAB)
    mine = lax.dynamic_index_in_dim(placing, tensor_idx, 1, keepdims=False).astype(F32)
    mine = mine * lax.dynamic_index_in_dim(coef, tensor_idx, 1, keepdims=False)[..., None]
    coefs = mine[:, :, :, None, None, :] * jnp.eye(2, dtype=F32)[:, None, None, None, :, None]
    coefs = jnp.broadcast_to(coefs, (2, ROWS, FLIGHT, GROUP, 2, CAP)).reshape(
        2 * ROWS, BLOCKS * 2 * CAP
    )

    both = by_slab(context, swap(context, "xl"), xl).reshape(2 * SLAB, HEADS_WIDE)
    up1, down1 = along_z(both, 1), along_z(both, -1)
    up2, down2 = along_z(up1, 1), along_z(down1, -1)
    up3, down3 = along_z(up2, 1), along_z(down2, -1)
    up4, down4 = along_z(up3[:SLAB], 1), along_z(down3[SLAB:], -1)

    keep, send = kernel_call(
        project_kernel,
        [((SLAB, COLS), F32), ((SLAB, COLS), BF16)],
        (place, hidden_cols, both, up1, down1, up2, down2, up3, down3, up4, down4, weights),
        "sv" + "v" * 9 + "h",
        2 * 256 * 4096 * 256,
        2 * 2048 * 1024,
        "project",
        [pltpu.VMEM((HALF, HEADS_WIDE), BF16), pltpu.SemaphoreType.DMA((RING,))],
    )
    residual, rows_out = kernel_call(
        residual_kernel,
        [((SLAB, COLS), BF16), ((FLIGHT * GROUP * BLOCKS * CAP, COLS), BF16)],
        (keep, swap(send, "xh"), picker),
        "vvv",
        2 * 256 * 128 * 256,
        1 << 20,
        "residual",
    )
    rows_in = lax.all_to_all(
        rows_out.reshape(BLOCKS, BLOCKS * CAP, COLS), TENSOR, split_axis=0, concat_axis=0, tiled=True
    ).reshape(BLOCKS * BLOCKS * CAP, COLS)
    gain = lax.dynamic_slice(norm_gain, (xl * HALF,), (HALF,)).reshape(1, HALF)
    own, part = kernel_call(
        gate_up_kernel,
        [((2 * BLOCKS * CAP, 2 * HIDDEN + 128), F32), ((2 * BLOCKS * CAP, 2 * HIDDEN + 128), BF16)],
        (rows_in, gain, weights),
        "vvh",
        2 * 128 * 2048 * 768,
        3 << 20,
        "gate_up",
        [pltpu.VMEM((HALF, 2 * HIDDEN), BF16), pltpu.SemaphoreType.DMA((RING,))],
    )
    (outward,) = kernel_call(
        down_kernel,
        [((2 * BLOCKS * CAP, HALF + COLS), BF16)],
        (own, swap(part, "xl"), residual, weights),
        "vvvh",
        2 * 128 * 384 * 2048,
        2 << 20,
        "down",
        [pltpu.VMEM((HALF, HIDDEN), BF16), pltpu.SemaphoreType.DMA],
    )
    returned = lax.all_to_all(
        outward.reshape(BLOCKS, 2 * CAP, HALF + COLS), TENSOR, split_axis=0, concat_axis=0, tiled=True
    ).reshape(BLOCKS * 2 * CAP, HALF + COLS)
    kept, sent = kernel_call(
        combine_kernel,
        [((ROWS, HALF), BF16), ((ROWS, HALF), BF16)],
        (place, coefs, returned),
        "svv",
        2 * 48 * 128 * 2304,
        1 << 20,
        "combine",
    )
    arrived = swap(sent, "xl")
    return jnp.where(
        xl == 0, jnp.concatenate([kept, arrived], axis=1), jnp.concatenate([arrived, kept], axis=1)
    )


def solution(mesh):
    fine = Mesh(mesh.devices.reshape(2, RING, 2, 2, RING), DP + TENSOR)
    placed = (
        P(DP + TENSOR, None),
        P(DP, TENSOR),
        P(DP, TENSOR),
        P(DP, TENSOR),
        P(DP),
        P(TENSOR, DP),
        P(),
        P(DP, None),
        P(DP, None),
        P(),
        P(DP, TENSOR),
        P(DP, TENSOR),
        P(TENSOR, DP),
    )
    return jax.shard_map(
        per_device, mesh=fine, in_specs=placed, out_specs=P(DP + TENSOR, None), check_vma=False
    )
```

time: 549 us -> 170 us (0.31)
  the two profiles are of different devices: /device:TPU:2 before, /device:TPU:24 now
where the time goes in v2:
time: 170 us; the launch traced here: 169 us
  starting transfers between devices  88.4 us (52%)
  waiting for transfers between devices  46 us (27%)
  between operations  14.6 us (9%)
  Pallas kernels  10.5 us (6%)
  matrix products  3.74 us (2%)
  local copies, waits for them, and re-layouts  3.02 us (2%)
  other arithmetic  2.71 us (2%)
    ppermute x8, starting transfers between devices, along_z(): lax.ppermute(block, 'z', [(i, (i + step) % RING) for i in range(RING)])  36.6 us
    ppermute x6, starting transfers between devices, swap(): return lax.ppermute(block, axis, [(0, 1), (1, 0)])  19 us
    ppermute x6, waiting for transfers between devices, swap(): return lax.ppermute(block, axis, [(0, 1), (1, 0)])  14.2 us
    all_to_all x1, waiting for transfers between devices, per_device(): lax.all_to_all(outward.reshape(BLOCKS, 2 * CAP, HALF + COLS), TENSOR, spl...  13.1 us
    all_to_all x1, waiting for transfers between devices, per_device(): lax.all_to_all(rows_out.reshape(BLOCKS, BLOCKS * CAP, COLS), TENSOR, spli...  12.9 us
    all_to_all x1, starting transfers between devices, per_device(): lax.all_to_all(hidden_both.reshape(2, ROWS, RING, COLS).transpose(0, 2, 1...  11.6 us
    pallas_call x6, Pallas kernels, kernel_call(): pl.pallas_call(body, out_shape=[jax.ShapeDtypeStruct(shape, dtype) for sh...  10.5 us
    all_to_all x1, starting transfers between devices, per_device(): lax.all_to_all(rows_out.reshape(BLOCKS, BLOCKS * CAP, COLS), TENSOR, spli...  10.1 us
  transfers between devices with their start and end apart: 19, of which 10 were waited for; matrix products, arithmetic and copies ran while one was open for 5% of the time, Pallas kernels for 0%

profile of v2, /device:TPU:24, one launch (start us, length us, event | category | flops | bytes accessed | tf_op | source)
XLA Modules:
  0.0 169.1 jit_solution(4663145324844334748)
XLA Ops:
  6.5 7.5 %collective-permute-start.2 = (bf16[512,128]{1,0:T(8,128)(2,1)}, bf16[512,128]{1,0:T(8,128)(2,1)S(1)}, u32[]{:S(2)}, u32[]{:S(2)}) collective-permute-start(bf16[512,128]{1,0:T(8,128)(2,1)} %param.20), channel_id=1, source_target_pairs={{0,0},{1,32},{2,64},{3,96},{4,128},{5,160},{6,192},{7,224},{32,1},... | collective-permute-start | bytes 393224 | tf_op jit(solution)/shard_map/ppermute | solution.py:266
  15.8 4.5 %while.11 = (s32[]{:T(128)}, bf16[2,256,128]{2,1,0:T(8,128)(2,1)S(1)}, bf16[2,256,128]{2,1,0:T(8,128)(2,1)S(1)}, bf16[1152,128]{1,0:T(8,128)(2,1)}, bf16[1152,128]{1,0:T(8,128)(2,1)}, /*index=5*/s32[256]{0:T(256)S(1)}, s32[]{:T(128)}) while((s32[]{:T(128)}, bf16[2,256,128]{2,1,0:T(8,128)(2,1)S(1)}, ...), condition=%wide.region_6.7_spmd.clone, body=%wide.region_3.6_spmd.clone.sunk | while | flops 153419264 | bytes 5445745 | solution.py:54
  15.8 1.5 fusion.39
  18.1 1.4 fusion.39
  21.4 3.4 %collective-permute-start.3 = (bf16[128,512]{1,0:T(8,128)(2,1)S(1)}, bf16[128,512]{1,0:T(8,128)(2,1)S(1)}, u32[]{:S(2)}, u32[]{:S(2)}) collective-permute-start(bf16[128,512]{1,0:T(8,128)(2,1)S(1)} %reshape.120), channel_id=1, source_target_pairs={{0,256},{256,0},{1,257},{257,1},{2,258},{258,2},{3,259},{259,3},{4... | collective-permute-start | bytes 393224 | tf_op jit(solution)/shard_map/ppermute | solution.py:63
  24.9 2.4 %collective-permute-start.1 = (bf16[8,2048]{1,0:T(8,128)(2,1)S(1)}, bf16[8,2048]{1,0:T(8,128)(2,1)S(1)}, u32[]{:S(2)}, u32[]{:S(2)}) collective-permute-start(bf16[8,2048]{1,0:T(8,128)(2,1)S(1)} %get-tuple-element.92), channel_id=1, source_target_pairs={{0,256},{256,0},{1,257},{257,1},{2,258},{258,2},{3,259},{259,3},{4... | collective-permute-start | bytes 98312 | tf_op jit(solution)/shard_map/ppermute | solution.py:63
  28.3 3.6 %collective-permute-start.4 = (bf16[256,512]{1,0:T(8,128)(2,1)S(1)}, bf16[256,512]{1,0:T(8,128)(2,1)S(1)}, u32[]{:S(2)}, u32[]{:S(2)}) collective-permute-start(bf16[256,512]{1,0:T(8,128)(2,1)S(1)} %bitcast.70), channel_id=1, source_target_pairs={{0,1},{1,2},{2,3},{3,4},{4,5},{5,6},{6,7},{7,0},{8,9},{9,10},{10,1... | collective-permute-start | bytes 786440 | tf_op jit(solution)/shard_map/ppermute | solution.py:67
  31.9 11.9 %collective-permute-start.5 = (bf16[256,512]{1,0:T(8,128)(2,1)S(1)}, bf16[256,512]{1,0:T(8,128)(2,1)S(1)}, u32[]{:S(2)}, u32[]{:S(2)}) collective-permute-start(bf16[256,512]{1,0:T(8,128)(2,1)S(1)} %bitcast.71), channel_id=1, source_target_pairs={{0,7},{1,0},{2,1},{3,2},{4,3},{5,4},{6,5},{7,6},{8,15},{9,8},{10,9... | collective-permute-start | bytes 786440 | tf_op jit(solution)/shard_map/ppermute | solution.py:67
  43.8 3.4 %collective-permute-start = (s32[8,128]{1,0:T(8,128)S(1)}, s32[8,128]{1,0:T(8,128)S(1)}, u32[]{:S(2)}, u32[]{:S(2)}) collective-permute-start(s32[8,128]{1,0:T(8,128)S(1)} %get-tuple-element.94), channel_id=1, source_target_pairs={{0,256},{256,0},{1,257},{257,1},{2,258},{258,2},{3,259},{259,3},{4... | collective-permute-start | bytes 12296 | tf_op jit(solution)/shard_map/ppermute | solution.py:63
  47.3 2.0 %collective-permute-done = s32[8,128]{1,0:T(8,128)S(1)} collective-permute-done((s32[8,128]{1,0:T(8,128)S(1)}, s32[8,128]{1,0:T(8,128)S(1)}, u32[]{:S(2)}, u32[]{:S(2)}) %collective-permute-start) | collective-permute-done | bytes 4128 | tf_op jit(solution)/shard_map/ppermute | solution.py:63
  49.4 1.9 %collective-permute-start.6 = (bf16[256,512]{1,0:T(8,128)(2,1)S(1)}, bf16[256,512]{1,0:T(8,128)(2,1)S(1)}, u32[]{:S(2)}, u32[]{:S(2)}) collective-permute-start(bf16[256,512]{1,0:T(8,128)(2,1)S(1)} %collective-permute-done.4.refs_1_), channel_id=1, source_target_pairs={{0,1},{1,2},{2,3},{3,4},{4,5},{5,6},{6,7},{7,0},{8,9},{9,10},{10,1... | collective-permute-start | bytes 786440 | tf_op jit(solution)/shard_map/ppermute | solution.py:67
  51.4 5.1 %collective-permute-start.7 = (bf16[256,512]{1,0:T(8,128)(2,1)S(1)}, bf16[256,512]{1,0:T(8,128)(2,1)S(1)}, u32[]{:S(2)}, u32[]{:S(2)}) collective-permute-start(bf16[256,512]{1,0:T(8,128)(2,1)S(1)} %collective-permute-done.5.refs_2_), channel_id=1, source_target_pairs={{0,7},{1,0},{2,1},{3,2},{4,3},{5,4},{6,5},{7,6},{8,15},{9,8},{10,9... | collective-permute-start | bytes 786440 | tf_op jit(solution)/shard_map/ppermute | solution.py:67
  56.7 2.2 %collective-permute-done.6.refs_3_ = bf16[256,512]{1,0:T(8,128)(2,1)S(1)} collective-permute-done((bf16[256,512]{1,0:T(8,128)(2,1)S(1)}, bf16[256,512]{1,0:T(8,128)(2,1)S(1)}, u32[]{:S(2)}, u32[]{:S(2)}) %collective-permute-start.6) | collective-permute-done | bytes 262176 | tf_op jit(solution)/shard_map/ppermute | solution.py:67
  58.9 1.9 %collective-permute-start.8 = (bf16[256,512]{1,0:T(8,128)(2,1)S(1)}, bf16[256,512]{1,0:T(8,128)(2,1)S(1)}, u32[]{:S(2)}, u32[]{:S(2)}) collective-permute-start(bf16[256,512]{1,0:T(8,128)(2,1)S(1)} %collective-permute-done.6.refs_3_), channel_id=1, source_target_pairs={{0,1},{1,2},{2,3},{3,4},{4,5},{5,6},{6,7},{7,0},{8,9},{9,10},{10,1... | collective-permute-start | bytes 786440 | tf_op jit(solution)/shard_map/ppermute | solution.py:67
  60.8 5.1 %collective-permute-start.9 = (bf16[256,512]{1,0:T(8,128)(2,1)S(1)}, bf16[256,512]{1,0:T(8,128)(2,1)S(1)}, u32[]{:S(2)}, u32[]{:S(2)}) collective-permute-start(bf16[256,512]{1,0:T(8,128)(2,1)S(1)} %collective-permute-done.7.refs_4_), channel_id=1, source_target_pairs={{0,7},{1,0},{2,1},{3,2},{4,3},{5,4},{6,5},{7,6},{8,15},{9,8},{10,9... | collective-permute-start | bytes 786440 | tf_op jit(solution)/shard_map/ppermute | solution.py:67
  66.8 11.6 %all-to-all-start = ((bf16[16,8,256]{2,1,0:T(8,128)(2,1)}), bf16[16,8,256]{2,1,0:T(8,128)(2,1)S(1)}, u32[]{:S(2)}, u32[]{:S(2)}) async-start(bf16[16,8,256]{2,1,0:T(8,128)(2,1)} %bitcast.15), calls=%async_computation | async-start | bytes 131072 | tf_op jit(solution)/shard_map/all_to_all | solution.py:285
  78.4 3.8 %collective-permute-start.10 = (bf16[128,512]{1,0:T(8,128)(2,1)S(1)}, bf16[128,512]{1,0:T(8,128)(2,1)S(1)}, u32[]{:S(2)}, u32[]{:S(2)}) collective-permute-start(bf16[128,512]{1,0:T(8,128)(2,1)S(1)} %slice.18), channel_id=1, source_target_pairs={{0,1},{1,2},{2,3},{3,4},{4,5},{5,6},{6,7},{7,0},{8,9},{9,10},{10,1... | collective-permute-start | bytes 393224 | tf_op jit(solution)/shard_map/ppermute | solution.py:67
  82.3 3.2 %collective-permute-start.11 = (bf16[128,512]{1,0:T(8,128)(2,1)S(1)}, bf16[128,512]{1,0:T(8,128)(2,1)S(1)}, u32[]{:S(2)}, u32[]{:S(2)}) collective-permute-start(bf16[128,512]{1,0:T(8,128)(2,1)S(1)} %slice.19), channel_id=1, source_target_pairs={{0,7},{1,0},{2,1},{3,2},{4,3},{5,4},{6,5},{7,6},{8,15},{9,8},{10,9... | collective-permute-start | bytes 393224 | tf_op jit(solution)/shard_map/ppermute | solution.py:67
  85.7 3.0 %all-to-all-done = bf16[16,8,256]{2,1,0:T(8,128)(2,1)S(1)} async-done(((bf16[16,8,256]{2,1,0:T(8,128)(2,1)}), bf16[16,8,256]{2,1,0:T(8,128)(2,1)S(1)}, u32[]{:S(2)}, u32[]{:S(2)}) %all-to-all-start) | async-done | bytes 65568 | tf_op jit(solution)/shard_map/all_to_all | solution.py:285
  89.2 2.8 %project.1 = (f32[128,256]{1,0:T(8,128)S(1)}, bf16[128,256]{1,0:T(8,128)(2,1)S(1)}) custom-call(s32[5]{0:T(128)S(1)} %stack.65.place_ref, bf16[128,256]{1,0:T(8,128)(2,1)S(1)} %bitcast.73, bf16[256,512]{1,0:T(8,128)(2,1)S(1)} %bitcast.72, bf16[256,512]{1,0:T(8,128)(2,1)S(1)} %collective-permute-done.4.refs_1_, ...), custom_call_target="tpu_custom_call" | custom-call | flops 536870912 | bytes 4194304 | tf_op jit(solution)/shard_map/project/pallas_call | solution.py:80
  92.0 4.9 %collective-permute-start.12 = (bf16[128,256]{1,0:T(8,128)(2,1)S(1)}, bf16[128,256]{1,0:T(8,128)(2,1)S(1)}, u32[]{:S(2)}, u32[]{:S(2)}) collective-permute-start(bf16[128,256]{1,0:T(8,128)(2,1)S(1)} %get-tuple-element.51), channel_id=1, source_target_pairs={{0,8},{8,0},{1,9},{9,1},{2,10},{10,2},{3,11},{11,3},{4,12},{12,4},... | collective-permute-start | bytes 196616 | tf_op jit(solution)/shard_map/ppermute | solution.py:63
  98.3 1.3 collective-permute-done.12.recv_ref
  100.7 10.1 %all-to-all-start.1 = ((bf16[16,64,256]{2,1,0:T(8,128)(2,1)}), bf16[16,64,256]{2,1,0:T(8,128)(2,1)S(1)}, u32[]{:S(2)}, u32[]{:S(2)}) async-start(bf16[16,64,256]{2,1,0:T(8,128)(2,1)} %bitcast.27), calls=%async_computation.1 | async-start | bytes 1048576 | tf_op jit(solution)/shard_map/all_to_all | solution.py:342
  110.8 12.9 %all-to-all-done.1 = bf16[16,64,256]{2,1,0:T(8,128)(2,1)S(1)} async-done(((bf16[16,64,256]{2,1,0:T(8,128)(2,1)}), bf16[16,64,256]{2,1,0:T(8,128)(2,1)S(1)}, u32[]{:S(2)}, u32[]{:S(2)}) %all-to-all-start.1) | async-done | bytes 524320 | tf_op jit(solution)/shard_map/all_to_all | solution.py:342
  123.8 2.3 %gate_up.1 = (f32[128,896]{1,0:T(8,128)S(1)}, bf16[128,896]{1,0:T(8,128)(2,1)S(1)}) custom-call(bf16[1024,256]{1,0:T(8,128)(2,1)S(1)} %bitcast.69, bf16[1,2048]{1,0:T(2,128)(2,1)S(1)} %reshape.123.gain_ref, bf16[2048,1664]{1,0:T(8,128)(2,1)} %all-gather.2.cloned.1.call-done.refs_9_.weights_hbm), custom_call_target="tpu_custom_call" | custom-call | flops 402653184 | bytes 3145728 | tf_op jit(solution)/shard_map/gate_up/pallas_call | solution.py:80
  126.1 2.5 %collective-permute-start.13 = (bf16[128,896]{1,0:T(8,128)(2,1)S(1)}, bf16[128,896]{1,0:T(8,128)(2,1)S(1)}, u32[]{:S(2)}, u32[]{:S(2)}) collective-permute-start(bf16[128,896]{1,0:T(8,128)(2,1)S(1)} %get-tuple-element.54), channel_id=1, source_target_pairs={{0,256},{256,0},{1,257},{257,1},{2,258},{258,2},{3,259},{259,3},{4... | collective-permute-start | bytes 688136 | tf_op jit(solution)/shard_map/ppermute | solution.py:63
  128.6 6.6 %collective-permute-done.13.recv_ref = bf16[128,896]{1,0:T(8,128)(2,1)S(1)} collective-permute-done((bf16[128,896]{1,0:T(8,128)(2,1)S(1)}, bf16[128,896]{1,0:T(8,128)(2,1)S(1)}, u32[]{:S(2)}, u32[]{:S(2)}) %collective-permute-start.13) | collective-permute-done | bytes 229408 | tf_op jit(solution)/shard_map/ppermute | solution.py:63
  135.2 2.7 %down.1 = bf16[128,2304]{1,0:T(8,128)(2,1)} custom-call(f32[128,896]{1,0:T(8,128)S(1)} %get-tuple-element.53.own_ref, bf16[128,896]{1,0:T(8,128)(2,1)S(1)} %collective-permute-done.13.recv_ref, bf16[128,256]{1,0:T(8,128)(2,1)S(1)} %get-tuple-element.55.residual_ref, bf16[2048,1664]{1,0:T(8,128)(2,1)} %all-gather.2.cloned.1.call-done.refs_9_.weights_hbm), custom_call_target="tpu_custom_call" | custom-call | flops 201326592 | bytes 2097152 | tf_op jit(solution)/shard_map/down/pallas_call | solution.py:80
  137.9 3.6 %all-to-all-start.2 = ((bf16[16,8,2304]{2,1,0:T(8,128)(2,1)}), bf16[16,8,2304]{2,1,0:T(8,128)(2,1)S(1)}, u32[]{:S(2)}, u32[]{:S(2)}) async-start(bf16[16,8,2304]{2,1,0:T(8,128)(2,1)} %bitcast.29), calls=%async_computation.2 | async-start | bytes 1179648 | tf_op jit(solution)/shard_map/all_to_all | solution.py:366
  141.9 13.1 %all-to-all-done.2 = bf16[16,8,2304]{2,1,0:T(8,128)(2,1)S(1)} async-done(((bf16[16,8,2304]{2,1,0:T(8,128)(2,1)}), bf16[16,8,2304]{2,1,0:T(8,128)(2,1)S(1)}, u32[]{:S(2)}, u32[]{:S(2)}) %all-to-all-start.2) | async-done | bytes 589856 | tf_op jit(solution)/shard_map/all_to_all | solution.py:366
  155.8 2.4 %collective-permute-start.14 = (bf16[8,2048]{1,0:T(8,128)(2,1)S(1)}, bf16[8,2048]{1,0:T(8,128)(2,1)S(1)}, u32[]{:S(2)}, u32[]{:S(2)}) collective-permute-start(bf16[8,2048]{1,0:T(8,128)(2,1)S(1)} %get-tuple-element.57), channel_id=1, source_target_pairs={{0,256},{256,0},{1,257},{257,1},{2,258},{258,2},{3,259},{259,3},{4... | collective-permute-start | bytes 98312 | tf_op jit(solution)/shard_map/ppermute | solution.py:63
  158.2 3.4 %collective-permute-done.14 = bf16[8,2048]{1,0:T(8,128)(2,1)S(1)} collective-permute-done((bf16[8,2048]{1,0:T(8,128)(2,1)S(1)}, bf16[8,2048]{1,0:T(8,128)(2,1)S(1)}, u32[]{:S(2)}, u32[]{:S(2)}) %collective-permute-start.14) | collective-permute-done | bytes 32800 | tf_op jit(solution)/shard_map/ppermute | solution.py:63
  (77 shorter events, 10.6 us)
Async XLA Ops:
  6.5 82.6 %all-gather.2.cloned.1.call-start = ((), (), s32[]{:S(2)}) async-start(), calls=%async_computation.3 | async-start | bytes 7241728 | tf_op jit(solution)/shard_map/all_gather | solution.py:280
  6.5 14.0 %collective-permute-start.2 = (bf16[512,128]{1,0:T(8,128)(2,1)}, bf16[512,128]{1,0:T(8,128)(2,1)S(1)}, u32[]{:S(2)}, u32[]{:S(2)}) collective-permute-start(bf16[512,128]{1,0:T(8,128)(2,1)} %param.20), channel_id=1, source_target_pairs={{0,0},{1,32},{2,64},{3,96},{4,128},{5,160},{6,192},{7,224},{32,1},... | collective-permute-start | bytes 393224 | tf_op jit(solution)/shard_map/ppermute | solution.py:266
  15.7 4.8 %copy-start = (bf16[128,384]{1,0:T(8,128)(2,1)S(1)}, bf16[128,384]{1,0:T(8,128)(2,1)}, u32[]{:S(2)}) copy-start(bf16[128,384]{1,0:T(8,128)(2,1)} %gate_ref.1) | copy-start | bytes 294916
  15.7 4.8 %copy-start.1 = (bf16[128,384]{1,0:T(8,128)(2,1)S(1)}, bf16[128,384]{1,0:T(8,128)(2,1)}, u32[]{:S(2)}) copy-start(bf16[128,384]{1,0:T(8,128)(2,1)} %up_ref.1) | copy-start | bytes 294916
  15.8 4.8 %copy-start.2 = (bf16[384,128]{1,0:T(8,128)(2,1)S(1)}, bf16[384,128]{1,0:T(8,128)(2,1)}, u32[]{:S(2)}) copy-start(bf16[384,128]{1,0:T(8,128)(2,1)} %down_ref.1) | copy-start | bytes 294916
  15.8 1.8 %copy-start.7 = (bf16[1152,128]{1,0:T(8,128)(2,1)S(1)}, bf16[1152,128]{1,0:T(8,128)(2,1)}, u32[]{:S(2)}) copy-start(bf16[1152,128]{1,0:T(8,128)(2,1)} %get-tuple-element.154) | copy-start | bytes 884740 | tf_op jit(solution)/shard_map/while
  18.0 1.8 %copy-start.7 = (bf16[1152,128]{1,0:T(8,128)(2,1)S(1)}, bf16[1152,128]{1,0:T(8,128)(2,1)}, u32[]{:S(2)}) copy-start(bf16[1152,128]{1,0:T(8,128)(2,1)} %get-tuple-element.154) | copy-start | bytes 884740 | tf_op jit(solution)/shard_map/while
  20.3 4.6 %copy-start.3 = (bf16[8,4096]{1,0:T(8,128)(2,1)S(1)}, bf16[8,4096]{1,0:T(8,128)(2,1)}, u32[]{:S(2)}) copy-start(bf16[8,4096]{1,0:T(8,128)(2,1)} %param.15) | copy-start | bytes 196612
  20.3 7.0 %copy-start.4 = (s32[128,8]{0,1:T(8,128)S(1)}, s32[128,8]{0,1:T(8,128)}, u32[]{:S(2)}) copy-start(s32[128,8]{0,1:T(8,128)} %param.22) | copy-start | bytes 12292
  20.3 7.0 %copy-start.5 = (s32[128,8]{0,1:T(8,128)S(1)}, s32[128,8]{0,1:T(8,128)}, u32[]{:S(2)}) copy-start(s32[128,8]{0,1:T(8,128)} %param.23) | copy-start | bytes 12292
  20.3 7.0 %copy-start.6 = (s32[4]{0:T(128)S(1)}, s32[4]{0:T(128)}, u32[]{:S(2)}) copy-start(s32[4]{0:T(128)} %param.24) | copy-start | bytes 52
  21.4 6.9 %collective-permute-start.3 = (bf16[128,512]{1,0:T(8,128)(2,1)S(1)}, bf16[128,512]{1,0:T(8,128)(2,1)S(1)}, u32[]{:S(2)}, u32[]{:S(2)}) collective-permute-start(bf16[128,512]{1,0:T(8,128)(2,1)S(1)} %reshape.120), channel_id=1, source_target_pairs={{0,256},{256,0},{1,257},{257,1},{2,258},{258,2},{3,259},{259,3},{4... | collective-permute-start | bytes 393224 | tf_op jit(solution)/shard_map/ppermute | solution.py:63
  24.9 41.3 %collective-permute-start.1 = (bf16[8,2048]{1,0:T(8,128)(2,1)S(1)}, bf16[8,2048]{1,0:T(8,128)(2,1)S(1)}, u32[]{:S(2)}, u32[]{:S(2)}) collective-permute-start(bf16[8,2048]{1,0:T(8,128)(2,1)S(1)} %get-tuple-element.92), channel_id=1, source_target_pairs={{0,256},{256,0},{1,257},{257,1},{2,258},{258,2},{3,259},{259,3},{4... | collective-permute-start | bytes 98312 | tf_op jit(solution)/shard_map/ppermute | solution.py:63
  28.3 21.1 %collective-permute-start.4 = (bf16[256,512]{1,0:T(8,128)(2,1)S(1)}, bf16[256,512]{1,0:T(8,128)(2,1)S(1)}, u32[]{:S(2)}, u32[]{:S(2)}) collective-permute-start(bf16[256,512]{1,0:T(8,128)(2,1)S(1)} %bitcast.70), channel_id=1, source_target_pairs={{0,1},{1,2},{2,3},{3,4},{4,5},{5,6},{6,7},{7,0},{8,9},{9,10},{10,1... | collective-permute-start | bytes 786440 | tf_op jit(solution)/shard_map/ppermute | solution.py:67
  31.9 19.5 %collective-permute-start.5 = (bf16[256,512]{1,0:T(8,128)(2,1)S(1)}, bf16[256,512]{1,0:T(8,128)(2,1)S(1)}, u32[]{:S(2)}, u32[]{:S(2)}) collective-permute-start(bf16[256,512]{1,0:T(8,128)(2,1)S(1)} %bitcast.71), channel_id=1, source_target_pairs={{0,7},{1,0},{2,1},{3,2},{4,3},{5,4},{6,5},{7,6},{8,15},{9,8},{10,9... | collective-permute-start | bytes 786440 | tf_op jit(solution)/shard_map/ppermute | solution.py:67
  43.8 5.5 %collective-permute-start = (s32[8,128]{1,0:T(8,128)S(1)}, s32[8,128]{1,0:T(8,128)S(1)}, u32[]{:S(2)}, u32[]{:S(2)}) collective-permute-start(s32[8,128]{1,0:T(8,128)S(1)} %get-tuple-element.94), channel_id=1, source_target_pairs={{0,256},{256,0},{1,257},{257,1},{2,258},{258,2},{3,259},{259,3},{4... | collective-permute-start | bytes 12296 | tf_op jit(solution)/shard_map/ppermute | solution.py:63
  49.4 9.5 %collective-permute-start.6 = (bf16[256,512]{1,0:T(8,128)(2,1)S(1)}, bf16[256,512]{1,0:T(8,128)(2,1)S(1)}, u32[]{:S(2)}, u32[]{:S(2)}) collective-permute-start(bf16[256,512]{1,0:T(8,128)(2,1)S(1)} %collective-permute-done.4.refs_1_), channel_id=1, source_target_pairs={{0,1},{1,2},{2,3},{3,4},{4,5},{5,6},{6,7},{7,0},{8,9},{9,10},{10,1... | collective-permute-start | bytes 786440 | tf_op jit(solution)/shard_map/ppermute | solution.py:67
  51.4 9.5 %collective-permute-start.7 = (bf16[256,512]{1,0:T(8,128)(2,1)S(1)}, bf16[256,512]{1,0:T(8,128)(2,1)S(1)}, u32[]{:S(2)}, u32[]{:S(2)}) collective-permute-start(bf16[256,512]{1,0:T(8,128)(2,1)S(1)} %collective-permute-done.5.refs_2_), channel_id=1, source_target_pairs={{0,7},{1,0},{2,1},{3,2},{4,3},{5,4},{6,5},{7,6},{8,15},{9,8},{10,9... | collective-permute-start | bytes 786440 | tf_op jit(solution)/shard_map/ppermute | solution.py:67
  58.9 19.5 %collective-permute-start.8 = (bf16[256,512]{1,0:T(8,128)(2,1)S(1)}, bf16[256,512]{1,0:T(8,128)(2,1)S(1)}, u32[]{:S(2)}, u32[]{:S(2)}) collective-permute-start(bf16[256,512]{1,0:T(8,128)(2,1)S(1)} %collective-permute-done.6.refs_3_), channel_id=1, source_target_pairs={{0,1},{1,2},{2,3},{3,4},{4,5},{5,6},{6,7},{7,0},{8,9},{9,10},{10,1... | collective-permute-start | bytes 786440 | tf_op jit(solution)/shard_map/ppermute | solution.py:67
  60.8 21.5 %collective-permute-start.9 = (bf16[256,512]{1,0:T(8,128)(2,1)S(1)}, bf16[256,512]{1,0:T(8,128)(2,1)S(1)}, u32[]{:S(2)}, u32[]{:S(2)}) collective-permute-start(bf16[256,512]{1,0:T(8,128)(2,1)S(1)} %collective-permute-done.7.refs_4_), channel_id=1, source_target_pairs={{0,7},{1,0},{2,1},{3,2},{4,3},{5,4},{6,5},{7,6},{8,15},{9,8},{10,9... | collective-permute-start | bytes 786440 | tf_op jit(solution)/shard_map/ppermute | solution.py:67
  66.8 21.8 %all-to-all-start = ((bf16[16,8,256]{2,1,0:T(8,128)(2,1)}), bf16[16,8,256]{2,1,0:T(8,128)(2,1)S(1)}, u32[]{:S(2)}, u32[]{:S(2)}) async-start(bf16[16,8,256]{2,1,0:T(8,128)(2,1)} %bitcast.15), calls=%async_computation | async-start | bytes 131072 | tf_op jit(solution)/shard_map/all_to_all | solution.py:285
  78.4 10.2 %collective-permute-start.10 = (bf16[128,512]{1,0:T(8,128)(2,1)S(1)}, bf16[128,512]{1,0:T(8,128)(2,1)S(1)}, u32[]{:S(2)}, u32[]{:S(2)}) collective-permute-start(bf16[128,512]{1,0:T(8,128)(2,1)S(1)} %slice.18), channel_id=1, source_target_pairs={{0,1},{1,2},{2,3},{3,4},{4,5},{5,6},{6,7},{7,0},{8,9},{9,10},{10,1... | collective-permute-start | bytes 393224 | tf_op jit(solution)/shard_map/ppermute | solution.py:67
  82.3 6.9 %collective-permute-start.11 = (bf16[128,512]{1,0:T(8,128)(2,1)S(1)}, bf16[128,512]{1,0:T(8,128)(2,1)S(1)}, u32[]{:S(2)}, u32[]{:S(2)}) collective-permute-start(bf16[128,512]{1,0:T(8,128)(2,1)S(1)} %slice.19), channel_id=1, source_target_pairs={{0,7},{1,0},{2,1},{3,2},{4,3},{5,4},{6,5},{7,6},{8,15},{9,8},{10,9... | collective-permute-start | bytes 393224 | tf_op jit(solution)/shard_map/ppermute | solution.py:67
  92.0 7.7 %collective-permute-start.12 = (bf16[128,256]{1,0:T(8,128)(2,1)S(1)}, bf16[128,256]{1,0:T(8,128)(2,1)S(1)}, u32[]{:S(2)}, u32[]{:S(2)}) collective-permute-start(bf16[128,256]{1,0:T(8,128)(2,1)S(1)} %get-tuple-element.51), channel_id=1, source_target_pairs={{0,8},{8,0},{1,9},{9,1},{2,10},{10,2},{3,11},{11,3},{4,12},{12,4},... | collective-permute-start | bytes 196616 | tf_op jit(solution)/shard_map/ppermute | solution.py:63
  97.2 13.6 %dynamic-slice-start = ((bf16[4096]{0:T(1024)(128)(2,1)}, s32[]{:T(128)}), bf16[2048]{0:T(1024)(128)(2,1)S(1)}, s32[]{:S(2)}) async-start(bf16[4096]{0:T(1024)(128)(2,1)} %param.21, s32[]{:T(128)} %select_n.79), calls=%async_computation.4 | async-start | bytes 8704 | tf_op jit(solution)/shard_map/dynamic_slice | solution.py:345
  100.7 23.1 %all-to-all-start.1 = ((bf16[16,64,256]{2,1,0:T(8,128)(2,1)}), bf16[16,64,256]{2,1,0:T(8,128)(2,1)S(1)}, u32[]{:S(2)}, u32[]{:S(2)}) async-start(bf16[16,64,256]{2,1,0:T(8,128)(2,1)} %bitcast.27), calls=%async_computation.1 | async-start | bytes 1048576 | tf_op jit(solution)/shard_map/all_to_all | solution.py:342
  126.1 9.1 %collective-permute-start.13 = (bf16[128,896]{1,0:T(8,128)(2,1)S(1)}, bf16[128,896]{1,0:T(8,128)(2,1)S(1)}, u32[]{:S(2)}, u32[]{:S(2)}) collective-permute-start(bf16[128,896]{1,0:T(8,128)(2,1)S(1)} %get-tuple-element.54), channel_id=1, source_target_pairs={{0,256},{256,0},{1,257},{257,1},{2,258},{258,2},{3,259},{259,3},{4... | collective-permute-start | bytes 688136 | tf_op jit(solution)/shard_map/ppermute | solution.py:63
  137.9 17.1 %all-to-all-start.2 = ((bf16[16,8,2304]{2,1,0:T(8,128)(2,1)}), bf16[16,8,2304]{2,1,0:T(8,128)(2,1)S(1)}, u32[]{:S(2)}, u32[]{:S(2)}) async-start(bf16[16,8,2304]{2,1,0:T(8,128)(2,1)} %bitcast.29), calls=%async_computation.2 | async-start | bytes 1179648 | tf_op jit(solution)/shard_map/all_to_all | solution.py:366
  155.8 5.8 %collective-permute-start.14 = (bf16[8,2048]{1,0:T(8,128)(2,1)S(1)}, bf16[8,2048]{1,0:T(8,128)(2,1)S(1)}, u32[]{:S(2)}, u32[]{:S(2)}) collective-permute-start(bf16[8,2048]{1,0:T(8,128)(2,1)S(1)} %get-tuple-element.57), channel_id=1, source_target_pairs={{0,256},{256,0},{1,257},{257,1},{2,258},{258,2},{3,259},{259,3},{4... | collective-permute-start | bytes 98312 | tf_op jit(solution)/shard_map/ppermute | solution.py:63
Sparse Core Ops, SparseCore 0:
  21.5 57.7 all-gather.1

commit v3 on v2

--- a/solution.py
+++ b/solution.py
@@ -8,10 +8,12 @@
 
 DP = ("xl", "y", "core")
 TENSOR = ("xh", "z")
+PAIR_TENSOR = ("xl",) + TENSOR
 RING = 8
 STEPS = (0, -1, 1, -2, 2, -3, 3)
 SLAB = 128
 HALF = 2048
+QUARTER = 1024
 COLS = 256
 HIDDEN = 384
 HEADS_WIDE = 512
@@ -20,6 +22,7 @@
 GROUP = 4
 BLOCKS = 16
 ROWS = 8
+TABLE = 16
 VMEM_BYTES = 48 * 1024 * 1024
 F32, BF16 = jnp.float32, jnp.bfloat16
 
@@ -181,9 +184,10 @@
     send_ref[:, 2 * HIDDEN :] = tail.astype(BF16)
 
 
-def down_kernel(own_ref, recv_ref, residual_ref, weights_hbm, out_ref, weights, sem):
+def down_kernel(place_ref, own_ref, recv_ref, residual_ref, weights_hbm, out_ref, weights, sem):
     copy = pltpu.make_async_copy(weights_hbm.at[:, pl.ds(2 * HIDDEN, HIDDEN)], weights, sem)
     copy.start()
+    xh = place_ref[3]
     slots = 2 * BLOCKS * CAP
     other = recv_ref[:, 2 * HIDDEN :].astype(F32)
     squares = own_ref[:, 2 * HIDDEN : 2 * HIDDEN + 1] + jnp.sum(other, axis=1, keepdims=True)
@@ -191,13 +195,13 @@
     total = (own_ref[:, : 2 * HIDDEN] + recv_ref[:, : 2 * HIDDEN].astype(F32)) * inverse
     gate, up = total[:, :HIDDEN], total[:, HIDDEN:]
     activated = (gate / (1.0 + jnp.exp(-gate)) * up).astype(BF16)
-    to = lax.broadcasted_iota(jnp.int32, (slots, slots), 0)
-    source = lax.broadcasted_iota(jnp.int32, (slots, slots), 1)
-    wanted = ((to >> 2) & 1) * (BLOCKS * CAP) + (to >> 3) * CAP + (to & 3)
-    order = jnp.where(source == wanted, 1.0, 0.0).astype(BF16)
-    activated = jnp.dot(order, activated, preferred_element_type=F32).astype(BF16)
-    copy.wait()
-    for d in range(HALF // 256):
+    to = lax.broadcasted_iota(jnp.int32, (2 * slots, slots), 0)
+    source = lax.broadcasted_iota(jnp.int32, (2 * slots, slots), 1)
+    twice = jnp.where(source == (to >> 3) * CAP + (to & 3), 1.0, 0.0).astype(BF16)
+    activated = jnp.dot(twice, activated, preferred_element_type=F32).astype(BF16)
+    first = (lax.broadcasted_iota(jnp.int32, (2 * slots, COLS), 0) & 4) == 0
+
+    def columns(d):
         rhs = jnp.concatenate(
             [
                 jnp.concatenate(
@@ -210,38 +214,45 @@
             ],
             axis=1,
         )
-        out_ref[:, d * 256 : (d + 1) * 256] = jnp.dot(
-            activated, rhs, preferred_element_type=F32
-        ).astype(BF16)
-    out_ref[:, HALF:] = residual_ref[...]
-
-
-def combine_kernel(place_ref, coefs_ref, returned_ref, keep_ref, send_ref):
+        return jnp.dot(activated, rhs, preferred_element_type=F32)
+
+    copy.wait()
+    chunks = QUARTER // COLS
+    for d in range(chunks):
+        out_ref[:, d * COLS : (d + 1) * COLS] = jnp.where(first, columns(d), columns(d + chunks)).astype(BF16)
+    residual = residual_ref[...].astype(F32)
+    out_ref[:SLAB, QUARTER:] = jnp.where(xh == 0, residual, 0.0).astype(BF16)
+    out_ref[SLAB:, QUARTER:] = jnp.where(xh == 1, residual, 0.0).astype(BF16)
+
+
+def combine_kernel(place_ref, coefs_ref, returned_ref, out_ref):
     xl = place_ref[0]
     coefs = coefs_ref[...]
     high = coefs.astype(BF16)
     rest = coefs - high.astype(F32)
     middle = rest.astype(BF16)
     low = (rest - middle.astype(F32)).astype(BF16)
-    slots = BLOCKS * ROWS
-    to = lax.broadcasted_iota(jnp.int32, (slots, slots), 0)
-    source = lax.broadcasted_iota(jnp.int32, (slots, slots), 1)
-    wanted = ((to >> 3) & 1) * (RING * ROWS) + (to >> 4) * ROWS + (to & 7)
-    order = jnp.where(source == wanted, 1.0, 0.0).astype(BF16)
-    residual = jnp.dot(order, returned_ref[:, HALF:], preferred_element_type=F32)
-    for k in range(RING):
+    rows, slots = 4 * ROWS, 2 * BLOCKS * ROWS
+    to = lax.broadcasted_iota(jnp.int32, (rows, slots), 0)
+    source = lax.broadcasted_iota(jnp.int32, (rows, slots), 1)
+    half, quarter, row = to >> 4, (to >> 3) & 1, to & 7
+    for k in range(QUARTER // COLS):
         at = slice(k * COLS, (k + 1) * COLS)
+        wanted = (half * BLOCKS + xl * RING + quarter * (RING // 2) + k) * ROWS + row
+        picker = jnp.where(source == wanted, 1.0, 0.0).astype(BF16)
         parts = returned_ref[:, at]
         mixed = (
-            residual[k * 16 : (k + 1) * 16]
+            jnp.dot(picker, returned_ref[:, QUARTER:], preferred_element_type=F32)
             + jnp.dot(high, parts, preferred_element_type=F32)
             + (
                 jnp.dot(middle, parts, preferred_element_type=F32)
                 + jnp.dot(low, parts, preferred_element_type=F32)
             )
         )
-        keep_ref[:, at] = jnp.where(xl == 0, mixed[:ROWS], mixed[ROWS:]).astype(BF16)
-        send_ref[:, at] = jnp.where(xl == 0, mixed[ROWS:], mixed[:ROWS]).astype(BF16)
+        for q in range(4):
+            out_ref[:, q * QUARTER + k * COLS : q * QUARTER + (k + 1) * COLS] = mixed[
+                q * ROWS : (q + 1) * ROWS
+            ].astype(BF16)
 
 
 def per_device(
@@ -267,7 +278,14 @@
         out_weight, ("y", "z"), [(a * RING + b, b * RING + a) for a in range(RING) for b in range(RING)]
     )
     context = attend(queries, keys, values, slab_start[0])
-    swapped, context = lax.optimization_barrier((swapped, context))
+    matches = route_ids[:, None, :] == flight_experts[None, :, None]
+    hits = jnp.sum(matches.astype(jnp.int32), axis=2, dtype=jnp.int32)
+    units = jnp.sum(jnp.where(matches, route_weights[:, None, :], 0), axis=2, dtype=jnp.int32)
+
+    hit_rows = jnp.pad(hits.T.astype(BF16), ((0, TABLE - FLIGHT), (0, HEADS_WIDE - SLAB)))
+    extended = jnp.concatenate([context, hit_rows])
+    other = swap(extended, "xl")
+    swapped, _ = lax.optimization_barrier((swapped, context))
     (packed,) = kernel_call(
         pack_weights_kernel,
         [((128, 3 * HIDDEN + HEADS_WIDE), BF16)],
@@ -279,46 +297,55 @@
     )
     weights = lax.all_gather(packed, ("y", "core"), axis=0, tiled=True)
 
-    hidden_own = lax.dynamic_slice(hidden_rows, (0, xl * HALF), (ROWS, HALF))
-    hidden_other = swap(lax.dynamic_slice(hidden_rows, (0, (1 - xl) * HALF), (ROWS, HALF)), "xl")
-    hidden_both = by_slab(hidden_own, hidden_other, xl)
-    hidden_cols = lax.all_to_all(
-        hidden_both.reshape(2, ROWS, RING, COLS).transpose(0, 2, 1, 3).reshape(BLOCKS, ROWS, COLS),
-        TENSOR,
-        split_axis=0,
-        concat_axis=0,
-        tiled=True,
-    ).reshape(SLAB, COLS)
-
-    matches = route_ids[:, None, :] == flight_experts[None, :, None]
-    hits = jnp.sum(matches.astype(jnp.int32), axis=2, dtype=jnp.int32)
-    units = jnp.sum(jnp.where(matches, route_weights[:, None, :], 0), axis=2, dtype=jnp.int32)
-    table = jnp.concatenate([hits, units], axis=1).T
-    tables = by_slab(table, swap(table, "xl"), xl)
-    tables = tables.transpose(0, 2, 1).reshape(2, BLOCKS, ROWS, 2 * FLIGHT)
-    hits, units = tables[..., :FLIGHT], tables[..., FLIGHT:]
-    slot = jnp.cumsum(hits, axis=2) - 1
-    placing = jnp.logical_and(
-        hits[..., None] == 1, slot[..., None] == jnp.arange(CAP, dtype=jnp.int32)
-    )
-    coef = units.astype(F32) / 65536.0
-    here = lax.dynamic_index_in_dim(placing, xh, 0, keepdims=False).astype(BF16)
-    same = jnp.eye(BLOCKS, dtype=BF16)
-    picker = (
-        here.transpose(2, 0, 3, 1)[:, :, :, None, :] * same[None, :, None, :, None]
-    ).reshape(FLIGHT * BLOCKS * CAP, SLAB)
-    mine = lax.dynamic_index_in_dim(placing, tensor_idx, 1, keepdims=False).astype(F32)
-    mine = mine * lax.dynamic_index_in_dim(coef, tensor_idx, 1, keepdims=False)[..., None]
-    coefs = mine[:, :, :, None, None, :] * jnp.eye(2, dtype=F32)[:, None, None, None, :, None]
-    coefs = jnp.broadcast_to(coefs, (2, ROWS, FLIGHT, GROUP, 2, CAP)).reshape(
-        2 * ROWS, BLOCKS * 2 * CAP
-    )
-
-    both = by_slab(context, swap(context, "xl"), xl).reshape(2 * SLAB, HEADS_WIDE)
+    slabs = by_slab(extended, other, xl)
+    both = slabs[:, :SLAB].reshape(2 * SLAB, HEADS_WIDE)
     up1, down1 = along_z(both, 1), along_z(both, -1)
     up2, down2 = along_z(up1, 1), along_z(down1, -1)
     up3, down3 = along_z(up2, 1), along_z(down2, -1)
     up4, down4 = along_z(up3[:SLAB], 1), along_z(down3[SLAB:], -1)
+
+    hidden_later, _ = lax.optimization_barrier((hidden_rows, up1))
+    wanted = jnp.arange(2, dtype=jnp.int32)[None, :, None, None, None] == xl
+    hidden_out = jnp.where(
+        wanted, hidden_later.reshape(ROWS, 2, 1, RING, COLS).transpose(1, 2, 3, 0, 4), 0
+    ).astype(BF16)
+    hidden_in = lax.all_to_all(
+        hidden_out.reshape(2 * BLOCKS, ROWS, COLS), PAIR_TENSOR, split_axis=0, concat_axis=0, tiled=True
+    )
+    hidden_cols = lax.dynamic_slice_in_dim(hidden_in, xh * BLOCKS, BLOCKS, 0).reshape(SLAB, COLS)
+
+    hits_here = lax.dynamic_index_in_dim(slabs, xh, 0, keepdims=False)[SLAB : SLAB + FLIGHT, :SLAB]
+    hits_here = hits_here.astype(jnp.int32).reshape(FLIGHT, BLOCKS, ROWS)
+    slot_here = jnp.cumsum(hits_here, axis=2) - 1
+    here = jnp.logical_and(
+        hits_here[:, :, None, :] == 1,
+        slot_here[:, :, None, :] == jnp.arange(CAP, dtype=jnp.int32)[:, None],
+    ).astype(BF16)
+    same = jnp.eye(BLOCKS, dtype=BF16)
+    picker = (here[:, :, :, None, :] * same[None, :, None, :, None]).reshape(
+        FLIGHT * BLOCKS * CAP, SLAB
+    )
+    hits_mine = lax.dynamic_slice_in_dim(hits, tensor_idx * ROWS, ROWS, 0)
+    coef = lax.dynamic_slice_in_dim(units, tensor_idx * ROWS, ROWS, 0).astype(F32) / 65536.0
+    slot_mine = jnp.cumsum(hits_mine, axis=0) - 1
+    mine = jnp.where(
+        jnp.logical_and(
+            hits_mine[..., None] == 1, slot_mine[..., None] == jnp.arange(CAP, dtype=jnp.int32)
+        ),
+        coef[..., None],
+        0.0,
+    )
+    two = jnp.eye(2, dtype=F32)
+    coefs = (
+        mine[None, None, :, None, :, None, None, :]
+        * two[:, None, None, :, None, None, None, None]
+        * two[None, :, None, None, None, None, :, None]
+    )
+    coefs = jnp.broadcast_to(coefs, (2, 2, ROWS, 2, FLIGHT, GROUP, 2, CAP)).reshape(
+        4 * ROWS, 2 * BLOCKS * 2 * CAP
+    )
+    gain = lax.dynamic_slice(norm_gain, (xl * HALF,), (HALF,)).reshape(1, HALF)
+    weights, picker, coefs, gain = lax.optimization_barrier((weights, picker, coefs, gain))
 
     keep, send = kernel_call(
         project_kernel,
@@ -342,7 +369,6 @@
     rows_in = lax.all_to_all(
         rows_out.reshape(BLOCKS, BLOCKS * CAP, COLS), TENSOR, split_axis=0, concat_axis=0, tiled=True
     ).reshape(BLOCKS * BLOCKS * CAP, COLS)
-    gain = lax.dynamic_slice(norm_gain, (xl * HALF,), (HALF,)).reshape(1, HALF)
     own, part = kernel_call(
         gate_up_kernel,
         [((2 * BLOCKS * CAP, 2 * HIDDEN + 128), F32), ((2 * BLOCKS * CAP, 2 * HIDDEN + 128), BF16)],
@@ -355,30 +381,31 @@
     )
     (outward,) = kernel_call(
         down_kernel,
-        [((2 * BLOCKS * CAP, HALF + COLS), BF16)],
-        (own, swap(part, "xl"), residual, weights),
-        "vvvh",
-        2 * 128 * 384 * 2048,
+        [((4 * BLOCKS * CAP, QUARTER + COLS), BF16)],
+        (place, own, swap(part, "xl"), residual, weights),
+        "svvvh",
+        2 * 256 * 384 * 2048,
         2 << 20,
         "down",
         [pltpu.VMEM((HALF, HIDDEN), BF16), pltpu.SemaphoreType.DMA],
     )
     returned = lax.all_to_all(
-        outward.reshape(BLOCKS, 2 * CAP, HALF + COLS), TENSOR, split_axis=0, concat_axis=0, tiled=True
-    ).reshape(BLOCKS * 2 * CAP, HALF + COLS)
-    kept, sent = kernel_call(
+        outward.reshape(2 * BLOCKS, 2 * CAP, QUARTER + COLS),
+        PAIR_TENSOR,
+        split_axis=0,
+        concat_axis=0,
+        tiled=True,
+    ).reshape(4 * BLOCKS * CAP, QUARTER + COLS)
+    (mixed,) = kernel_call(
         combine_kernel,
-        [((ROWS, HALF), BF16), ((ROWS, HALF), BF16)],
+        [((ROWS, 2 * HALF), BF16)],
         (place, coefs, returned),
         "svv",
-        2 * 48 * 128 * 2304,
+        2 * 128 * 256 * 1024,
         1 << 20,
         "combine",
     )
-    arrived = swap(sent, "xl")
-    return jnp.where(
-        xl == 0, jnp.concatenate([kept, arrived], axis=1), jnp.concatenate([arrived, kept], axis=1)
-    )
+    return mixed
 
 
 def solution(mesh):

time: 170 us -> 164 us (0.965)
  the two profiles are of different devices: /device:TPU:24 before, /device:TPU:88 now
where the time goes in v3:
time: 164 us; the launch traced here: 163 us
  starting transfers between devices  68.1 us (42%)
  waiting for transfers between devices  34.9 us (21%)
  blocking collectives  22.5 us (14%)
  between operations  14.5 us (9%)
  Pallas kernels  11.3 us (7%)
  local copies, waits for them, and re-layouts  4.76 us (3%)
  matrix products  3.74 us (2%)
  other arithmetic  3.02 us (2%)
    ppermute x8, starting transfers between devices, along_z(): lax.ppermute(block, 'z', [(i, (i + step) % RING) for i in range(RING)])  31.2 us
    all_to_all x1, blocking collectives, per_device(): lax.all_to_all(rows_out.reshape(BLOCKS, BLOCKS * CAP, COLS), TENSOR, spli...  22.5 us
    all_to_all x1, waiting for transfers between devices, per_device(): lax.all_to_all(outward.reshape(2 * BLOCKS, 2 * CAP, QUARTER + COLS), PAIR...  15 us
    all_to_all x1, starting transfers between devices, per_device(): lax.all_to_all(hidden_out.reshape(2 * BLOCKS, ROWS, COLS), PAIR_TENSOR, s...  14.8 us
    ppermute x3, waiting for transfers between devices, swap(): return lax.ppermute(block, axis, [(0, 1), (1, 0)])  11.8 us
    pallas_call x6, Pallas kernels, kernel_call(): pl.pallas_call(body, out_shape=[jax.ShapeDtypeStruct(shape, dtype) for sh...  11.3 us
    ppermute x3, starting transfers between devices, swap(): return lax.ppermute(block, axis, [(0, 1), (1, 0)])  10.8 us
    ppermute x8, waiting for transfers between devices, along_z(): lax.ppermute(block, 'z', [(i, (i + step) % RING) for i in range(RING)])  6.21 us
  transfers between devices with their start and end apart: 15, of which 10 were waited for; matrix products, arithmetic and copies ran while one was open for 7% of the time, Pallas kernels for 0%

profile of v3, /device:TPU:88, one launch (start us, length us, event | category | flops | bytes accessed | tf_op | source)
XLA Modules:
  0.0 162.8 jit_solution(10287603903407436329)
XLA Ops:
  6.5 5.8 %collective-permute-start = (bf16[512,128]{1,0:T(8,128)(2,1)}, bf16[512,128]{1,0:T(8,128)(2,1)S(1)}, u32[]{:S(2)}, u32[]{:S(2)}) collective-permute-start(bf16[512,128]{1,0:T(8,128)(2,1)} %param.20), channel_id=1, source_target_pairs={{0,0},{1,32},{2,64},{3,96},{4,128},{5,160},{6,192},{7,224},{32,1},... | collective-permute-start | bytes 393224 | tf_op jit(solution)/shard_map/ppermute | solution.py:277
  12.4 0.9 reshape.139
  14.1 4.5 %while.11 = (s32[]{:T(128)}, bf16[2,256,128]{2,1,0:T(8,128)(2,1)S(1)}, bf16[2,256,128]{2,1,0:T(8,128)(2,1)S(1)}, bf16[1152,128]{1,0:T(8,128)(2,1)}, bf16[1152,128]{1,0:T(8,128)(2,1)}, /*index=5*/s32[256]{0:T(256)S(1)}, s32[]{:T(128)}) while((s32[]{:T(128)}, bf16[2,256,128]{2,1,0:T(8,128)(2,1)S(1)}, ...), condition=%wide.region_3.4_spmd.clone, body=%wide.region_0.3_spmd.clone.sunk | while | flops 153419264 | bytes 5445753 | solution.py:57
  14.1 1.5 fusion.36
  16.4 1.4 fusion.36
  20.5 3.4 %collective-permute-start.1 = (bf16[144,512]{1,0:T(8,128)(2,1)S(1)}, bf16[144,512]{1,0:T(8,128)(2,1)S(1)}, u32[]{:S(2)}, u32[]{:S(2)}) collective-permute-start(bf16[144,512]{1,0:T(8,128)(2,1)S(1)} %get-tuple-element.96), channel_id=1, source_target_pairs={{0,256},{256,0},{1,257},{257,1},{2,258},{258,2},{3,259},{259,3},{4... | collective-permute-start | bytes 442376 | tf_op jit(solution)/shard_map/ppermute | solution.py:66
  24.4 3.6 %collective-permute-done.1 = bf16[144,512]{1,0:T(8,128)(2,1)S(1)} collective-permute-done((bf16[144,512]{1,0:T(8,128)(2,1)S(1)}, bf16[144,512]{1,0:T(8,128)(2,1)S(1)}, u32[]{:S(2)}, u32[]{:S(2)}) %collective-permute-start.1) | collective-permute-done | bytes 147488 | tf_op jit(solution)/shard_map/ppermute | solution.py:66
  28.2 5.2 %collective-permute-start.2 = (bf16[256,512]{1,0:T(8,128)(2,1)S(1)}, bf16[256,512]{1,0:T(8,128)(2,1)S(1)}, u32[]{:S(2)}, u32[]{:S(2)}) collective-permute-start(bf16[256,512]{1,0:T(8,128)(2,1)S(1)} %bitcast.59), channel_id=1, source_target_pairs={{0,1},{1,2},{2,3},{3,4},{4,5},{5,6},{6,7},{7,0},{8,9},{9,10},{10,1... | collective-permute-start | bytes 786440 | tf_op jit(solution)/shard_map/ppermute | solution.py:70
  33.4 1.9 %collective-permute-start.3 = (bf16[256,512]{1,0:T(8,128)(2,1)S(1)}, bf16[256,512]{1,0:T(8,128)(2,1)S(1)}, u32[]{:S(2)}, u32[]{:S(2)}) collective-permute-start(bf16[256,512]{1,0:T(8,128)(2,1)S(1)} %bitcast.60), channel_id=1, source_target_pairs={{0,7},{1,0},{2,1},{3,2},{4,3},{5,4},{6,5},{7,6},{8,15},{9,8},{10,9... | collective-permute-start | bytes 786440 | tf_op jit(solution)/shard_map/ppermute | solution.py:70
  36.3 2.0 %collective-permute-done.2.refs_1_ = bf16[256,512]{1,0:T(8,128)(2,1)S(1)} collective-permute-done((bf16[256,512]{1,0:T(8,128)(2,1)S(1)}, bf16[256,512]{1,0:T(8,128)(2,1)S(1)}, u32[]{:S(2)}, u32[]{:S(2)}) %collective-permute-start.2) | collective-permute-done | bytes 262176 | tf_op jit(solution)/shard_map/ppermute | solution.py:70
  38.3 4.4 %collective-permute-start.4 = (bf16[256,512]{1,0:T(8,128)(2,1)S(1)}, bf16[256,512]{1,0:T(8,128)(2,1)S(1)}, u32[]{:S(2)}, u32[]{:S(2)}) collective-permute-start(bf16[256,512]{1,0:T(8,128)(2,1)S(1)} %collective-permute-done.2.refs_1_), channel_id=1, source_target_pairs={{0,1},{1,2},{2,3},{3,4},{4,5},{5,6},{6,7},{7,0},{8,9},{9,10},{10,1... | collective-permute-start | bytes 786440 | tf_op jit(solution)/shard_map/ppermute | solution.py:70
  42.7 7.0 %collective-permute-start.5 = (bf16[256,512]{1,0:T(8,128)(2,1)S(1)}, bf16[256,512]{1,0:T(8,128)(2,1)S(1)}, u32[]{:S(2)}, u32[]{:S(2)}) collective-permute-start(bf16[256,512]{1,0:T(8,128)(2,1)S(1)} %collective-permute-done.3.refs_2_), channel_id=1, source_target_pairs={{0,7},{1,0},{2,1},{3,2},{4,3},{5,4},{6,5},{7,6},{8,15},{9,8},{10,9... | collective-permute-start | bytes 786440 | tf_op jit(solution)/shard_map/ppermute | solution.py:70
  50.5 1.6 collective-permute-done.4.refs_3_
  52.1 5.0 %collective-permute-start.6 = (bf16[256,512]{1,0:T(8,128)(2,1)S(1)}, bf16[256,512]{1,0:T(8,128)(2,1)S(1)}, u32[]{:S(2)}, u32[]{:S(2)}) collective-permute-start(bf16[256,512]{1,0:T(8,128)(2,1)S(1)} %collective-permute-done.4.refs_3_), channel_id=1, source_target_pairs={{0,1},{1,2},{2,3},{3,4},{4,5},{5,6},{6,7},{7,0},{8,9},{9,10},{10,1... | collective-permute-start | bytes 786440 | tf_op jit(solution)/shard_map/ppermute | solution.py:70
  57.6 1.9 %collective-permute-start.7 = (bf16[256,512]{1,0:T(8,128)(2,1)S(1)}, bf16[256,512]{1,0:T(8,128)(2,1)S(1)}, u32[]{:S(2)}, u32[]{:S(2)}) collective-permute-start(bf16[256,512]{1,0:T(8,128)(2,1)S(1)} %collective-permute-done.5.refs_4_), channel_id=1, source_target_pairs={{0,7},{1,0},{2,1},{3,2},{4,3},{5,4},{6,5},{7,6},{8,15},{9,8},{10,9... | collective-permute-start | bytes 786440 | tf_op jit(solution)/shard_map/ppermute | solution.py:70
  60.3 14.8 %all-to-all-start = ((bf16[32,8,256]{2,1,0:T(8,128)(2,1)}), bf16[32,8,256]{2,1,0:T(8,128)(2,1)S(1)}, u32[]{:S(2)}, u32[]{:S(2)}) async-start(bf16[32,8,256]{2,1,0:T(8,128)(2,1)} %bitcast_select_fusion), calls=%async_computation | async-start | bytes 262144 | tf_op jit(solution)/shard_map/all_to_all | solution.py:312
  75.8 3.4 %collective-permute-start.8 = (bf16[128,512]{1,0:T(8,128)(2,1)}, bf16[128,512]{1,0:T(8,128)(2,1)S(1)}, u32[]{:S(2)}, u32[]{:S(2)}) collective-permute-start(bf16[128,512]{1,0:T(8,128)(2,1)} %slice.18), channel_id=1, source_target_pairs={{0,1},{1,2},{2,3},{3,4},{4,5},{5,6},{6,7},{7,0},{8,9},{9,10},{10,1... | collective-permute-start | bytes 393224 | tf_op jit(solution)/shard_map/ppermute | solution.py:70
  79.8 2.5 %collective-permute-start.9 = (bf16[128,512]{1,0:T(8,128)(2,1)}, bf16[128,512]{1,0:T(8,128)(2,1)S(1)}, u32[]{:S(2)}, u32[]{:S(2)}) collective-permute-start(bf16[128,512]{1,0:T(8,128)(2,1)} %slice.19), channel_id=1, source_target_pairs={{0,7},{1,0},{2,1},{3,2},{4,3},{5,4},{6,5},{7,6},{8,15},{9,8},{10,9... | collective-permute-start | bytes 393224 | tf_op jit(solution)/shard_map/ppermute | solution.py:70
  82.5 1.1 mul.72.place_ref
  83.6 1.2 all-to-all-done
  84.8 2.1 %collective-permute-done.9.refs_8_ = bf16[128,512]{1,0:T(8,128)(2,1)S(1)} collective-permute-done((bf16[128,512]{1,0:T(8,128)(2,1)}, bf16[128,512]{1,0:T(8,128)(2,1)S(1)}, u32[]{:S(2)}, u32[]{:S(2)}) %collective-permute-start.9) | collective-permute-done | bytes 131104 | tf_op jit(solution)/shard_map/ppermute | solution.py:70
  86.9 2.8 %project.1 = (f32[128,256]{1,0:T(8,128)S(1)}, bf16[128,256]{1,0:T(8,128)(2,1)S(1)}) custom-call(s32[5]{0:T(128)S(1)} %stack.37.place_ref, bf16[128,256]{1,0:T(8,128)(2,1)S(1)} %dynamic-slice_bitcast_fusion.1.hidden_ref, bf16[256,512]{1,0:T(8,128)(2,1)S(1)} %bitcast.61, bf16[256,512]{1,0:T(8,128)(2,1)S(1)} %collective-permute-done.2.refs_1_, ...), custom_call_target="tpu_custom_call" | custom-call | flops 536870912 | bytes 4194304 | tf_op jit(solution)/shard_map/project/pallas_call | solution.py:83
  89.8 4.9 %collective-permute-start.10 = (bf16[128,256]{1,0:T(8,128)(2,1)S(1)}, bf16[128,256]{1,0:T(8,128)(2,1)S(1)}, u32[]{:S(2)}, u32[]{:S(2)}) collective-permute-start(bf16[128,256]{1,0:T(8,128)(2,1)S(1)} %get-tuple-element.55), channel_id=1, source_target_pairs={{0,8},{8,0},{1,9},{9,1},{2,10},{10,2},{3,11},{11,3},{4,12},{12,4},... | collective-permute-start | bytes 196616 | tf_op jit(solution)/shard_map/ppermute | solution.py:66
  94.6 2.8 %collective-permute-done.10.recv_ref = bf16[128,256]{1,0:T(8,128)(2,1)S(1)} collective-permute-done((bf16[128,256]{1,0:T(8,128)(2,1)S(1)}, bf16[128,256]{1,0:T(8,128)(2,1)S(1)}, u32[]{:S(2)}, u32[]{:S(2)}) %collective-permute-start.10) | collective-permute-done | bytes 65568 | tf_op jit(solution)/shard_map/ppermute | solution.py:66
  97.6 22.5 %all_to_all.15 = bf16[16,64,256]{2,1,0:T(8,128)(2,1)S(1)} all-to-all(bf16[16,64,256]{2,1,0:T(8,128)(2,1)S(1)} %bitcast.62), channel_id=1, replica_groups=mesh['xl'=2,'y'=8,'core'=2,'xh'=2,'z'=8] {'xh','z'}, dimensions={0} | all-to-all | bytes 1048576 | tf_op jit(solution)/shard_map/all_to_all | solution.py:369
  120.1 2.3 %gate_up.1 = (f32[128,896]{1,0:T(8,128)S(1)}, bf16[128,896]{1,0:T(8,128)(2,1)S(1)}) custom-call(bf16[1024,256]{1,0:T(8,128)(2,1)S(1)} %bitcast.58, bf16[1,2048]{1,0:T(2,128)(2,1)S(1)} %reshape.144.gain_ref, bf16[2048,1664]{1,0:T(8,128)(2,1)} %all-gather.2.cloned.1.call-done.refs_9_.weights_hbm), custom_call_target="tpu_custom_call" | custom-call | flops 402653184 | bytes 3145728 | tf_op jit(solution)/shard_map/gate_up/pallas_call | solution.py:83
  122.4 2.6 %collective-permute-start.11 = (bf16[128,896]{1,0:T(8,128)(2,1)S(1)}, bf16[128,896]{1,0:T(8,128)(2,1)S(1)}, u32[]{:S(2)}, u32[]{:S(2)}) collective-permute-start(bf16[128,896]{1,0:T(8,128)(2,1)S(1)} %get-tuple-element.60), channel_id=1, source_target_pairs={{0,256},{256,0},{1,257},{257,1},{2,258},{258,2},{3,259},{259,3},{4... | collective-permute-start | bytes 688136 | tf_op jit(solution)/shard_map/ppermute | solution.py:66
  124.9 5.4 %collective-permute-done.11.recv_ref = bf16[128,896]{1,0:T(8,128)(2,1)S(1)} collective-permute-done((bf16[128,896]{1,0:T(8,128)(2,1)S(1)}, bf16[128,896]{1,0:T(8,128)(2,1)S(1)}, u32[]{:S(2)}, u32[]{:S(2)}) %collective-permute-start.11) | collective-permute-done | bytes 229408 | tf_op jit(solution)/shard_map/ppermute | solution.py:66
  130.3 3.5 %down.1 = bf16[256,1280]{1,0:T(8,128)(2,1)} custom-call(s32[5]{0:T(128)S(1)} %stack.37.place_ref, f32[128,896]{1,0:T(8,128)S(1)} %get-tuple-element.59.own_ref, bf16[128,896]{1,0:T(8,128)(2,1)S(1)} %collective-permute-done.11.recv_ref, bf16[128,256]{1,0:T(8,128)(2,1)S(1)} %get-tuple-element.61.residual_ref, ...), custom_call_target="tpu_custom_call" | custom-call | flops 402653184 | bytes 2097152 | tf_op jit(solution)/shard_map/down/pallas_call | solution.py:83
  133.8 5.4 %all-to-all-start.2 = ((bf16[32,8,1280]{2,1,0:T(8,128)(2,1)}), bf16[32,8,1280]{2,1,0:T(8,128)(2,1)S(1)}, u32[]{:S(2)}, u32[]{:S(2)}) async-start(bf16[32,8,1280]{2,1,0:T(8,128)(2,1)} %bitcast.22), calls=%async_computation.2 | async-start | bytes 1310720 | tf_op jit(solution)/shard_map/all_to_all | solution.py:392
  139.3 15.0 %all-to-all-done.2 = bf16[32,8,1280]{2,1,0:T(8,128)(2,1)S(1)} async-done(((bf16[32,8,1280]{2,1,0:T(8,128)(2,1)}), bf16[32,8,1280]{2,1,0:T(8,128)(2,1)S(1)}, u32[]{:S(2)}, u32[]{:S(2)}) %all-to-all-start.2) | async-done | bytes 655392 | tf_op jit(solution)/shard_map/all_to_all | solution.py:392
  154.4 1.6 %combine.1 = bf16[8,4096]{1,0:T(8,128)(2,1)} custom-call(s32[5]{0:T(128)S(1)} %stack.37.place_ref, f32[32,256]{1,0:T(8,128)S(1)} %copy.27.coefs_ref, bf16[256,1280]{1,0:T(8,128)(2,1)S(1)} %bitcast.57), custom_call_target="tpu_custom_call" | custom-call | flops 67108864 | bytes 1048576 | tf_op jit(solution)/shard_map/combine/pallas_call | solution.py:83
  (75 shorter events, 8.7 us)
Async XLA Ops:
  6.5 78.3 %all-gather.2.cloned.1.call-start = ((), (), s32[]{:S(2)}) async-start(), calls=%async_computation.3 | async-start | bytes 7241728 | tf_op jit(solution)/shard_map/all_gather | solution.py:298
  6.5 12.9 %collective-permute-start = (bf16[512,128]{1,0:T(8,128)(2,1)}, bf16[512,128]{1,0:T(8,128)(2,1)S(1)}, u32[]{:S(2)}, u32[]{:S(2)}) collective-permute-start(bf16[512,128]{1,0:T(8,128)(2,1)} %param.20), channel_id=1, source_target_pairs={{0,0},{1,32},{2,64},{3,96},{4,128},{5,160},{6,192},{7,224},{32,1},... | collective-permute-start | bytes 393224 | tf_op jit(solution)/shard_map/ppermute | solution.py:277
  14.0 5.4 %copy-start = (bf16[128,384]{1,0:T(8,128)(2,1)S(1)}, bf16[128,384]{1,0:T(8,128)(2,1)}, u32[]{:S(2)}) copy-start(bf16[128,384]{1,0:T(8,128)(2,1)} %gate_ref.1) | copy-start | bytes 294916
  14.0 5.4 %copy-start.1 = (bf16[128,384]{1,0:T(8,128)(2,1)S(1)}, bf16[128,384]{1,0:T(8,128)(2,1)}, u32[]{:S(2)}) copy-start(bf16[128,384]{1,0:T(8,128)(2,1)} %up_ref.1) | copy-start | bytes 294916
  14.1 5.4 %copy-start.2 = (bf16[384,128]{1,0:T(8,128)(2,1)S(1)}, bf16[384,128]{1,0:T(8,128)(2,1)}, u32[]{:S(2)}) copy-start(bf16[384,128]{1,0:T(8,128)(2,1)} %down_ref.1) | copy-start | bytes 294916
  14.1 1.8 %copy-start.8 = (bf16[1152,128]{1,0:T(8,128)(2,1)S(1)}, bf16[1152,128]{1,0:T(8,128)(2,1)}, u32[]{:S(2)}) copy-start(bf16[1152,128]{1,0:T(8,128)(2,1)} %get-tuple-element.156) | copy-start | bytes 884740 | tf_op jit(solution)/shard_map/while
  16.4 1.8 %copy-start.8 = (bf16[1152,128]{1,0:T(8,128)(2,1)S(1)}, bf16[1152,128]{1,0:T(8,128)(2,1)}, u32[]{:S(2)}) copy-start(bf16[1152,128]{1,0:T(8,128)(2,1)} %get-tuple-element.156) | copy-start | bytes 884740 | tf_op jit(solution)/shard_map/while
  18.6 1.7 %copy-start.4 = (s32[128,8]{0,1:T(8,128)S(1)}, s32[128,8]{0,1:T(8,128)}, u32[]{:S(2)}) copy-start(s32[128,8]{0,1:T(8,128)} %param.23) | copy-start | bytes 12292
  18.6 1.7 %copy-start.5 = (s32[128,8]{0,1:T(8,128)S(1)}, s32[128,8]{0,1:T(8,128)}, u32[]{:S(2)}) copy-start(s32[128,8]{0,1:T(8,128)} %param.22) | copy-start | bytes 12292
  18.6 1.7 %copy-start.7 = (s32[4]{0:T(128)S(1)}, s32[4]{0:T(128)}, u32[]{:S(2)}) copy-start(s32[4]{0:T(128)} %param.24) | copy-start | bytes 52
  20.5 7.6 %collective-permute-start.1 = (bf16[144,512]{1,0:T(8,128)(2,1)S(1)}, bf16[144,512]{1,0:T(8,128)(2,1)S(1)}, u32[]{:S(2)}, u32[]{:S(2)}) collective-permute-start(bf16[144,512]{1,0:T(8,128)(2,1)S(1)} %get-tuple-element.96), channel_id=1, source_target_pairs={{0,256},{256,0},{1,257},{257,1},{2,258},{258,2},{3,259},{259,3},{4... | collective-permute-start | bytes 442376 | tf_op jit(solution)/shard_map/ppermute | solution.py:66
  28.1 7.9 %copy-start.6 = (bf16[4096]{0:T(1024)(128)(2,1)S(1)}, bf16[4096]{0:T(1024)(128)(2,1)}, u32[]{:S(2)}) copy-start(bf16[4096]{0:T(1024)(128)(2,1)} %param.21) | copy-start | bytes 24580
  28.1 31.4 %copy-start.3 = (bf16[8,4096]{1,0:T(8,128)(2,1)S(1)}, bf16[8,4096]{1,0:T(8,128)(2,1)}, u32[]{:S(2)}) copy-start(bf16[8,4096]{1,0:T(8,128)(2,1)} %param.15) | copy-start | bytes 196612
  28.2 10.1 %collective-permute-start.2 = (bf16[256,512]{1,0:T(8,128)(2,1)S(1)}, bf16[256,512]{1,0:T(8,128)(2,1)S(1)}, u32[]{:S(2)}, u32[]{:S(2)}) collective-permute-start(bf16[256,512]{1,0:T(8,128)(2,1)S(1)} %bitcast.59), channel_id=1, source_target_pairs={{0,1},{1,2},{2,3},{3,4},{4,5},{5,6},{6,7},{7,0},{8,9},{9,10},{10,1... | collective-permute-start | bytes 786440 | tf_op jit(solution)/shard_map/ppermute | solution.py:70
  33.4 9.3 %collective-permute-start.3 = (bf16[256,512]{1,0:T(8,128)(2,1)S(1)}, bf16[256,512]{1,0:T(8,128)(2,1)S(1)}, u32[]{:S(2)}, u32[]{:S(2)}) collective-permute-start(bf16[256,512]{1,0:T(8,128)(2,1)S(1)} %bitcast.60), channel_id=1, source_target_pairs={{0,7},{1,0},{2,1},{3,2},{4,3},{5,4},{6,5},{7,6},{8,15},{9,8},{10,9... | collective-permute-start | bytes 786440 | tf_op jit(solution)/shard_map/ppermute | solution.py:70
  38.3 13.8 %collective-permute-start.4 = (bf16[256,512]{1,0:T(8,128)(2,1)S(1)}, bf16[256,512]{1,0:T(8,128)(2,1)S(1)}, u32[]{:S(2)}, u32[]{:S(2)}) collective-permute-start(bf16[256,512]{1,0:T(8,128)(2,1)S(1)} %collective-permute-done.2.refs_1_), channel_id=1, source_target_pairs={{0,1},{1,2},{2,3},{3,4},{4,5},{5,6},{6,7},{7,0},{8,9},{9,10},{10,1... | collective-permute-start | bytes 786440 | tf_op jit(solution)/shard_map/ppermute | solution.py:70
  42.7 14.9 %collective-permute-start.5 = (bf16[256,512]{1,0:T(8,128)(2,1)S(1)}, bf16[256,512]{1,0:T(8,128)(2,1)S(1)}, u32[]{:S(2)}, u32[]{:S(2)}) collective-permute-start(bf16[256,512]{1,0:T(8,128)(2,1)S(1)} %collective-permute-done.3.refs_2_), channel_id=1, source_target_pairs={{0,7},{1,0},{2,1},{3,2},{4,3},{5,4},{6,5},{7,6},{8,15},{9,8},{10,9... | collective-permute-start | bytes 786440 | tf_op jit(solution)/shard_map/ppermute | solution.py:70
  52.1 23.0 %collective-permute-start.6 = (bf16[256,512]{1,0:T(8,128)(2,1)S(1)}, bf16[256,512]{1,0:T(8,128)(2,1)S(1)}, u32[]{:S(2)}, u32[]{:S(2)}) collective-permute-start(bf16[256,512]{1,0:T(8,128)(2,1)S(1)} %collective-permute-done.4.refs_3_), channel_id=1, source_target_pairs={{0,1},{1,2},{2,3},{3,4},{4,5},{5,6},{6,7},{7,0},{8,9},{9,10},{10,1... | collective-permute-start | bytes 786440 | tf_op jit(solution)/shard_map/ppermute | solution.py:70
  57.6 21.6 %collective-permute-start.7 = (bf16[256,512]{1,0:T(8,128)(2,1)S(1)}, bf16[256,512]{1,0:T(8,128)(2,1)S(1)}, u32[]{:S(2)}, u32[]{:S(2)}) collective-permute-start(bf16[256,512]{1,0:T(8,128)(2,1)S(1)} %collective-permute-done.5.refs_4_), channel_id=1, source_target_pairs={{0,7},{1,0},{2,1},{3,2},{4,3},{5,4},{6,5},{7,6},{8,15},{9,8},{10,9... | collective-permute-start | bytes 786440 | tf_op jit(solution)/shard_map/ppermute | solution.py:70
  60.3 24.5 %all-to-all-start = ((bf16[32,8,256]{2,1,0:T(8,128)(2,1)}), bf16[32,8,256]{2,1,0:T(8,128)(2,1)S(1)}, u32[]{:S(2)}, u32[]{:S(2)}) async-start(bf16[32,8,256]{2,1,0:T(8,128)(2,1)} %bitcast_select_fusion), calls=%async_computation | async-start | bytes 262144 | tf_op jit(solution)/shard_map/all_to_all | solution.py:312
  75.8 9.0 %collective-permute-start.8 = (bf16[128,512]{1,0:T(8,128)(2,1)}, bf16[128,512]{1,0:T(8,128)(2,1)S(1)}, u32[]{:S(2)}, u32[]{:S(2)}) collective-permute-start(bf16[128,512]{1,0:T(8,128)(2,1)} %slice.18), channel_id=1, source_target_pairs={{0,1},{1,2},{2,3},{3,4},{4,5},{5,6},{6,7},{7,0},{8,9},{9,10},{10,1... | collective-permute-start | bytes 393224 | tf_op jit(solution)/shard_map/ppermute | solution.py:70
  79.8 7.1 %collective-permute-start.9 = (bf16[128,512]{1,0:T(8,128)(2,1)}, bf16[128,512]{1,0:T(8,128)(2,1)S(1)}, u32[]{:S(2)}, u32[]{:S(2)}) collective-permute-start(bf16[128,512]{1,0:T(8,128)(2,1)} %slice.19), channel_id=1, source_target_pairs={{0,7},{1,0},{2,1},{3,2},{4,3},{5,4},{6,5},{7,6},{8,15},{9,8},{10,9... | collective-permute-start | bytes 393224 | tf_op jit(solution)/shard_map/ppermute | solution.py:70
  89.8 7.7 %collective-permute-start.10 = (bf16[128,256]{1,0:T(8,128)(2,1)S(1)}, bf16[128,256]{1,0:T(8,128)(2,1)S(1)}, u32[]{:S(2)}, u32[]{:S(2)}) collective-permute-start(bf16[128,256]{1,0:T(8,128)(2,1)S(1)} %get-tuple-element.55), channel_id=1, source_target_pairs={{0,8},{8,0},{1,9},{9,1},{2,10},{10,2},{3,11},{11,3},{4,12},{12,4},... | collective-permute-start | bytes 196616 | tf_op jit(solution)/shard_map/ppermute | solution.py:66
  122.4 7.9 %collective-permute-start.11 = (bf16[128,896]{1,0:T(8,128)(2,1)S(1)}, bf16[128,896]{1,0:T(8,128)(2,1)S(1)}, u32[]{:S(2)}, u32[]{:S(2)}) collective-permute-start(bf16[128,896]{1,0:T(8,128)(2,1)S(1)} %get-tuple-element.60), channel_id=1, source_target_pairs={{0,256},{256,0},{1,257},{257,1},{2,258},{258,2},{3,259},{259,3},{4... | collective-permute-start | bytes 688136 | tf_op jit(solution)/shard_map/ppermute | solution.py:66
  133.8 20.5 %all-to-all-start.2 = ((bf16[32,8,1280]{2,1,0:T(8,128)(2,1)}), bf16[32,8,1280]{2,1,0:T(8,128)(2,1)S(1)}, u32[]{:S(2)}, u32[]{:S(2)}) async-start(bf16[32,8,1280]{2,1,0:T(8,128)(2,1)} %bitcast.22), calls=%async_computation.2 | async-start | bytes 1310720 | tf_op jit(solution)/shard_map/all_to_all | solution.py:392
Sparse Core Ops, SparseCore 0:
  20.4 58.1 all-gather.1

commit v4 on v3

--- a/solution.py
+++ b/solution.py
@@ -27,39 +27,25 @@
 F32, BF16 = jnp.float32, jnp.bfloat16
 
 
-def attend(q_dev, keys_dev, values_dev, first_pos):
-    slab_rows = q_dev.shape[0]
-    head_size = keys_dev.shape[1]
-    head_count = q_dev.shape[1] // head_size
-    pair_count = head_count // 2
-    grouped = (
-        q_dev.reshape(slab_rows, pair_count, 2, head_size)
-        .transpose(1, 2, 0, 3)
-        .reshape(pair_count, 2 * slab_rows, head_size)
-    )
-    position = first_pos + jnp.arange(2 * slab_rows, dtype=jnp.int32) % slab_rows
-    visible = jnp.arange(keys_dev.shape[0], dtype=jnp.int32)[None, :] <= position[:, None]
-
-    def one_pair(q_block):
+def attend_kernel(start_ref, queries_ref, keys_ref, values_ref, hits_ref, out_ref):
+    keys, values = keys_ref[...], values_ref[...]
+    size = keys.shape[1]
+    shape = (2 * SLAB, keys.shape[0])
+    position = start_ref[0] + (lax.broadcasted_iota(jnp.int32, shape, 0) & (SLAB - 1))
+    visible = lax.broadcasted_iota(jnp.int32, shape, 1) <= position
+    for pair in range(HEADS_WIDE // size // 2):
+        first, second = (slice((2 * pair + i) * size, (2 * pair + i + 1) * size) for i in range(2))
+        block = jnp.concatenate([queries_ref[:, first], queries_ref[:, second]])
         scores = lax.dot_general(
-            q_block, keys_dev, (((1,), (1,)), ((), ())), preferred_element_type=jnp.float32
-        ) * head_size ** (-0.5)
+            block, keys, (((1,), (1,)), ((), ())), preferred_element_type=F32
+        ) * size ** (-0.5)
         scores = jnp.where(visible, scores, -1e30)
-        maxima = jnp.max(scores, axis=1, keepdims=True)
-        exp_scores = jnp.exp(scores - maxima)
+        exp_scores = jnp.exp(scores - jnp.max(scores, axis=1, keepdims=True))
         totals = jnp.sum(exp_scores, axis=1, keepdims=True)
-        context = (
-            jnp.dot(exp_scores.astype(jnp.bfloat16), values_dev, preferred_element_type=jnp.float32)
-            / totals
-        )
-        return context.astype(jnp.bfloat16)
-
-    result = lax.map(one_pair, grouped)
-    return (
-        result.reshape(pair_count, 2, slab_rows, head_size)
-        .transpose(2, 0, 1, 3)
-        .reshape(slab_rows, head_count * head_size)
-    )
+        context = (jnp.dot(exp_scores.astype(BF16), values, preferred_element_type=F32) / totals).astype(BF16)
+        out_ref[:SLAB, first] = context[:SLAB]
+        out_ref[:SLAB, second] = context[SLAB:]
+    out_ref[SLAB:, :] = hits_ref[...]
 
 
 def swap(block, axis):
@@ -68,10 +54,6 @@
 
 def along_z(block, step):
     return lax.ppermute(block, "z", [(i, (i + step) % RING) for i in range(RING)])
-
-
-def by_slab(own, other, xl):
-    return jnp.where(xl == 0, jnp.stack([own, other]), jnp.stack([other, own]))
 
 
 def kernel_call(body, out_shapes, operands, spaces, flops, moved, name, scratch=()):
@@ -92,24 +74,30 @@
     )(*operands)
 
 
-def pack_weights_kernel(gate_ref, up_ref, down_ref, out_weight_ref, packed_ref):
+def pack_weights_kernel(gate_ref, up_ref, *refs):
+    wide, packed_ref = refs[:-1], refs[-1]
     packed_ref[:, :HIDDEN] = gate_ref[...]
     packed_ref[:, HIDDEN : 2 * HIDDEN] = up_ref[...]
     at = 2 * HIDDEN
-    for ref in (down_ref, out_weight_ref):
+    for ref in wide:
         for j in range(ref.shape[0] // 128):
             packed_ref[:, at : at + 128] = ref[j * 128 : (j + 1) * 128, :]
             at += 128
 
 
-def project_kernel(place_ref, hidden_ref, *refs):
+def pack_down_kernel(down_ref, packed_ref):
+    for j in range(HIDDEN // 128):
+        packed_ref[:, j * 128 : (j + 1) * 128] = down_ref[j * 128 : (j + 1) * 128, :]
+
+
+def project_kernel(place_ref, *refs):
     contexts, (weights_hbm, keep_ref, send_ref, weights, sems) = refs[:9], refs[9:]
-    xh, z = place_ref[3], place_ref[4]
+    z = place_ref[4]
 
     def copy(k):
         at = pl.ds(k * 2 * 128, 2 * 128)
         return pltpu.make_async_copy(
-            weights_hbm.at[at, pl.ds(3 * HIDDEN, HEADS_WIDE)], weights.at[at], sems.at[k]
+            weights_hbm.at[at, pl.ds(2 * HIDDEN, HEADS_WIDE)], weights.at[at], sems.at[k]
         )
 
     for k in range(RING):
@@ -122,30 +110,37 @@
             step, context = STEPS[k], contexts[k][...]
         else:
             step, context = 4, jnp.concatenate([contexts[k][...], contexts[k + 1][...]])
-        first = pl.multiple_of(((z + (step + RING)) & (RING - 1)) * 256, 256)
-        block = weights[pl.ds(first, 256), :]
         for half in range(2):
+            first = pl.multiple_of(((z + (step + RING + half * 4)) & (RING - 1)) * 256, 256)
+            lanes = slice(half * 256, half * 256 + 256)
+            block = weights[pl.ds(first, 256), lanes]
             rhs = jnp.concatenate(
                 [
                     jnp.concatenate([block[:128, q * 128 : (q + 1) * 128], block[128:, q * 128 : (q + 1) * 128]], axis=1)
-                    for q in (2 * half, 2 * half + 1)
+                    for q in range(2)
                 ]
             )
-            total += jnp.dot(context[:, half * 256 : (half + 1) * 256], rhs, preferred_element_type=F32)
-    low, high = total[:SLAB], total[SLAB:]
-    keep_ref[...] = jnp.where(xh == 0, low, high) + hidden_ref[...].astype(F32)
-    send_ref[...] = jnp.where(xh == 0, high, low).astype(BF16)
-
-
-def residual_kernel(keep_ref, recv_ref, place_ref, residual_ref, rows_ref):
-    residual = (keep_ref[...] + recv_ref[...].astype(F32)).astype(BF16)
-    residual_ref[...] = residual
-    picked = jnp.dot(place_ref[...], residual, preferred_element_type=F32).astype(BF16)
+            total += jnp.dot(context[:, lanes], rhs, preferred_element_type=F32)
+    keep_ref[...] = total
+    send_ref[...] = total.astype(BF16)
+
+
+def residual_kernel(place_ref, keep_ref, recv_ref, hidden_ref, pickers_ref, residual_ref, rows_ref):
+    xl, xh = place_ref[0], place_ref[3]
+    attention = keep_ref[...] + recv_ref[...].astype(F32)
+    own, other = attention[:SLAB], attention[SLAB:]
     per_expert = BLOCKS * CAP
-    for f in range(FLIGHT):
-        for j in range(GROUP):
-            at = (f * GROUP + j) * per_expert
-            rows_ref[at : at + per_expert, :] = picked[f * per_expert : (f + 1) * per_expert]
+    held = jnp.zeros((SLAB, COLS), F32)
+    for slab in range(2):
+        at = slice(slab * SLAB, (slab + 1) * SLAB)
+        residual = (jnp.where(xl == slab, own, other) + hidden_ref[at, :].astype(F32)).astype(BF16)
+        held = jnp.where(xh == slab, residual.astype(F32), held)
+        picked = jnp.dot(pickers_ref[at, :], residual, preferred_element_type=F32).astype(BF16)
+        for f in range(FLIGHT // 2):
+            for j in range(GROUP):
+                to = ((f * GROUP + j) * 2 + slab) * per_expert
+                rows_ref[to : to + per_expert, :] = picked[f * per_expert : (f + 1) * per_expert]
+    residual_ref[...] = held.astype(BF16)
 
 
 def gate_up_kernel(rows_ref, gain_ref, weights_hbm, own_ref, send_ref, weights, sems):
@@ -163,9 +158,7 @@
     total = jnp.zeros((2 * slots, 2 * HIDDEN), F32)
     squares = jnp.zeros((2 * slots, 1), F32)
     for k in range(RING):
-        rows = jnp.concatenate(
-            [rows_ref[k * slots : (k + 1) * slots, :], rows_ref[(RING + k) * slots : (RING + k + 1) * slots, :]]
-        ).astype(F32)
+        rows = rows_ref[2 * k * slots : 2 * (k + 1) * slots, :].astype(F32)
         squares += jnp.sum(rows * rows, axis=1, keepdims=True)
         scaled = (rows * gain_ref[:, k * part : (k + 1) * part].astype(F32)).astype(BF16)
         copy(k).wait()
@@ -185,7 +178,7 @@
 
 
 def down_kernel(place_ref, own_ref, recv_ref, residual_ref, weights_hbm, out_ref, weights, sem):
-    copy = pltpu.make_async_copy(weights_hbm.at[:, pl.ds(2 * HIDDEN, HIDDEN)], weights, sem)
+    copy = pltpu.make_async_copy(weights_hbm, weights, sem)
     copy.start()
     xh = place_ref[3]
     slots = 2 * BLOCKS * CAP
@@ -274,56 +267,75 @@
     tensor_idx = lax.axis_index(TENSOR)
     place = jnp.stack([lax.axis_index(a) for a in DP + TENSOR]).astype(jnp.int32)
 
-    swapped = lax.ppermute(
-        out_weight, ("y", "z"), [(a * RING + b, b * RING + a) for a in range(RING) for b in range(RING)]
-    )
-    context = attend(queries, keys, values, slab_start[0])
+    def transposed(block, shift):
+        return lax.ppermute(
+            block,
+            ("y", "z"),
+            [(a * RING + b, (b + shift) % RING * RING + a) for a in range(RING) for b in range(RING)],
+        )
+
+    top = transposed(out_weight[: HEADS_WIDE // 2], 0)
+    bottom = transposed(out_weight[HEADS_WIDE // 2 :], RING // 2)
+
+    columns = hidden_rows.reshape(ROWS, 2, 1, RING, COLS).transpose(1, 2, 3, 0, 4)
+    hidden_out = jnp.broadcast_to(columns, (2, 2, RING, ROWS, COLS)).reshape(2 * BLOCKS, ROWS, COLS)
+    hidden_in = lax.all_to_all(
+        hidden_out, PAIR_TENSOR, split_axis=0, concat_axis=0, tiled=True
+    ).reshape(2 * SLAB, COLS)
+
     matches = route_ids[:, None, :] == flight_experts[None, :, None]
     hits = jnp.sum(matches.astype(jnp.int32), axis=2, dtype=jnp.int32)
     units = jnp.sum(jnp.where(matches, route_weights[:, None, :], 0), axis=2, dtype=jnp.int32)
 
     hit_rows = jnp.pad(hits.T.astype(BF16), ((0, TABLE - FLIGHT), (0, HEADS_WIDE - SLAB)))
-    extended = jnp.concatenate([context, hit_rows])
-    other = swap(extended, "xl")
-    swapped, _ = lax.optimization_barrier((swapped, context))
+    (extended,) = kernel_call(
+        attend_kernel,
+        [((SLAB + TABLE, HEADS_WIDE), BF16)],
+        (slab_start, queries, keys, values, hit_rows),
+        "svvvv",
+        4 * 512 * 1152 * 128,
+        1 << 20,
+        "attend",
+    )
+    top, bottom, hidden_in, _ = lax.optimization_barrier((top, bottom, hidden_in, extended))
     (packed,) = kernel_call(
         pack_weights_kernel,
-        [((128, 3 * HIDDEN + HEADS_WIDE), BF16)],
-        (gate_weight, up_weight, down_weight, swapped),
+        [((128, 2 * HIDDEN + HEADS_WIDE), BF16)],
+        (gate_weight, up_weight, top, bottom),
         "vvvv",
         0,
-        4 * 128 * 1664,
+        4 * 128 * 1280,
         "pack_weights",
     )
     weights = lax.all_gather(packed, ("y", "core"), axis=0, tiled=True)
-
-    slabs = by_slab(extended, other, xl)
-    both = slabs[:, :SLAB].reshape(2 * SLAB, HEADS_WIDE)
+    (packed_down,) = kernel_call(
+        pack_down_kernel, [((128, HIDDEN), BF16)], (down_weight,), "v", 0, 4 * 128 * 384, "pack_down"
+    )
+    packed_down, _ = lax.optimization_barrier((packed_down, packed))
+    down_weights = lax.all_gather(packed_down, ("y", "core"), axis=0, tiled=True)
+
+    other = swap(extended, "xl")
+    both = jnp.concatenate([extended[:SLAB], other[:SLAB]])
     up1, down1 = along_z(both, 1), along_z(both, -1)
     up2, down2 = along_z(up1, 1), along_z(down1, -1)
     up3, down3 = along_z(up2, 1), along_z(down2, -1)
     up4, down4 = along_z(up3[:SLAB], 1), along_z(down3[SLAB:], -1)
 
-    hidden_later, _ = lax.optimization_barrier((hidden_rows, up1))
-    wanted = jnp.arange(2, dtype=jnp.int32)[None, :, None, None, None] == xl
-    hidden_out = jnp.where(
-        wanted, hidden_later.reshape(ROWS, 2, 1, RING, COLS).transpose(1, 2, 3, 0, 4), 0
-    ).astype(BF16)
-    hidden_in = lax.all_to_all(
-        hidden_out.reshape(2 * BLOCKS, ROWS, COLS), PAIR_TENSOR, split_axis=0, concat_axis=0, tiled=True
-    )
-    hidden_cols = lax.dynamic_slice_in_dim(hidden_in, xh * BLOCKS, BLOCKS, 0).reshape(SLAB, COLS)
-
-    hits_here = lax.dynamic_index_in_dim(slabs, xh, 0, keepdims=False)[SLAB : SLAB + FLIGHT, :SLAB]
-    hits_here = hits_here.astype(jnp.int32).reshape(FLIGHT, BLOCKS, ROWS)
-    slot_here = jnp.cumsum(hits_here, axis=2) - 1
+    hits_both = jnp.where(
+        xl == 0, jnp.stack([extended[SLAB:], other[SLAB:]]), jnp.stack([other[SLAB:], extended[SLAB:]])
+    )
+    hits_here = lax.dynamic_slice(
+        hits_both, (0, xh * (FLIGHT // 2), 0), (2, FLIGHT // 2, SLAB)
+    )
+    hits_here = hits_here.astype(jnp.int32).reshape(2, FLIGHT // 2, BLOCKS, ROWS)
+    slot_here = jnp.cumsum(hits_here, axis=3) - 1
     here = jnp.logical_and(
-        hits_here[:, :, None, :] == 1,
-        slot_here[:, :, None, :] == jnp.arange(CAP, dtype=jnp.int32)[:, None],
+        hits_here[:, :, :, None, :] == 1,
+        slot_here[:, :, :, None, :] == jnp.arange(CAP, dtype=jnp.int32)[:, None],
     ).astype(BF16)
     same = jnp.eye(BLOCKS, dtype=BF16)
-    picker = (here[:, :, :, None, :] * same[None, :, None, :, None]).reshape(
-        FLIGHT * BLOCKS * CAP, SLAB
+    pickers = (here[:, :, :, :, None, :] * same[None, None, :, None, :, None]).reshape(
+        2 * (FLIGHT // 2) * BLOCKS * CAP, SLAB
     )
     hits_mine = lax.dynamic_slice_in_dim(hits, tensor_idx * ROWS, ROWS, 0)
     coef = lax.dynamic_slice_in_dim(units, tensor_idx * ROWS, ROWS, 0).astype(F32) / 65536.0
@@ -345,13 +357,13 @@
         4 * ROWS, 2 * BLOCKS * 2 * CAP
     )
     gain = lax.dynamic_slice(norm_gain, (xl * HALF,), (HALF,)).reshape(1, HALF)
-    weights, picker, coefs, gain = lax.optimization_barrier((weights, picker, coefs, gain))
+    weights, pickers, coefs, gain = lax.optimization_barrier((weights, pickers, coefs, gain))
 
     keep, send = kernel_call(
         project_kernel,
-        [((SLAB, COLS), F32), ((SLAB, COLS), BF16)],
-        (place, hidden_cols, both, up1, down1, up2, down2, up3, down3, up4, down4, weights),
-        "sv" + "v" * 9 + "h",
+        [((2 * SLAB, COLS), F32), ((2 * SLAB, COLS), BF16)],
+        (place, both, up1, down1, up2, down2, up3, down3, up4, down4, weights),
+        "s" + "v" * 9 + "h",
         2 * 256 * 4096 * 256,
         2 * 2048 * 1024,
         "project",
@@ -359,16 +371,16 @@
     )
     residual, rows_out = kernel_call(
         residual_kernel,
-        [((SLAB, COLS), BF16), ((FLIGHT * GROUP * BLOCKS * CAP, COLS), BF16)],
-        (keep, swap(send, "xh"), picker),
-        "vvv",
+        [((SLAB, COLS), BF16), ((RING * 2 * BLOCKS * CAP, COLS), BF16)],
+        (place, keep, swap(send, "xh"), hidden_in, pickers),
+        "svvvv",
         2 * 256 * 128 * 256,
         1 << 20,
         "residual",
     )
     rows_in = lax.all_to_all(
-        rows_out.reshape(BLOCKS, BLOCKS * CAP, COLS), TENSOR, split_axis=0, concat_axis=0, tiled=True
-    ).reshape(BLOCKS * BLOCKS * CAP, COLS)
+        rows_out.reshape(RING, 2 * BLOCKS * CAP, COLS), "z", split_axis=0, concat_axis=0, tiled=True
+    ).reshape(RING * 2 * BLOCKS * CAP, COLS)
     own, part = kernel_call(
         gate_up_kernel,
         [((2 * BLOCKS * CAP, 2 * HIDDEN + 128), F32), ((2 * BLOCKS * CAP, 2 * HIDDEN + 128), BF16)],
@@ -382,7 +394,7 @@
     (outward,) = kernel_call(
         down_kernel,
         [((4 * BLOCKS * CAP, QUARTER + COLS), BF16)],
-        (place, own, swap(part, "xl"), residual, weights),
+        (place, own, swap(part, "xl"), residual, down_weights),
         "svvvh",
         2 * 256 * 384 * 2048,
         2 << 20,

time: 164 us -> 175 us (1.067)
  the two profiles are of different devices: /device:TPU:88 before, /device:TPU:64 now
where the time goes in v4:
time: 175 us; the launch traced here: 174 us
  starting transfers between devices  65.4 us (37%)
  waiting for transfers between devices  43.2 us (25%)
  blocking collectives  23.2 us (13%)
  between operations  14.4 us (8%)
  Pallas kernels  13.1 us (7%)
  local copies, waits for them, and re-layouts  12.7 us (7%)
  other arithmetic  2.27 us (1%)
    ppermute x8, starting transfers between devices, along_z(): lax.ppermute(block, 'z', [(i, (i + step) % RING) for i in range(RING)])  25.9 us
    all_to_all x1, blocking collectives, per_device(): lax.all_to_all(rows_out.reshape(RING, 2 * BLOCKS * CAP, COLS), 'z', split...  23.2 us
    all_to_all x1, waiting for transfers between devices, per_device(): lax.all_to_all(outward.reshape(2 * BLOCKS, 2 * CAP, QUARTER + COLS), PAIR...  21.1 us
    ppermute x2, starting transfers between devices, transposed(): lax.ppermute(block, ('y', 'z'), [(a * RING + b, (b + shift) % RING * RING...  16.4 us
    pallas_call x8, Pallas kernels, kernel_call(): pl.pallas_call(body, out_shape=[jax.ShapeDtypeStruct(shape, dtype) for sh...  13.1 us
    ppermute x3, starting transfers between devices, swap(): return lax.ppermute(block, axis, [(0, 1), (1, 0)])  10.4 us
    ppermute x3, waiting for transfers between devices, swap(): return lax.ppermute(block, axis, [(0, 1), (1, 0)])  10.4 us
    unnamed x16, local copies, waits for them, and re-layouts  6.91 us
  transfers between devices with their start and end apart: 17, of which 11 were waited for; matrix products, arithmetic and copies ran while one was open for 4% of the time, Pallas kernels for 5%

profile of v4, /device:TPU:64, one launch (start us, length us, event | category | flops | bytes accessed | tf_op | source)
XLA Modules:
  0.0 174.3 jit_solution(14755773121171572020)
XLA Ops:
  7.4 2.6 %collective-permute-start = (bf16[256,128]{1,0:T(8,128)(2,1)S(1)}, bf16[256,128]{1,0:T(8,128)(2,1)S(1)}, u32[]{:S(2)}, u32[]{:S(2)}) collective-permute-start(bf16[256,128]{1,0:T(8,128)(2,1)S(1)} %get-tuple-element.38), channel_id=1, source_target_pairs={{0,0},{1,32},{2,64},{3,96},{4,128},{5,160},{6,192},{7,224},{32,1},... | collective-permute-start | bytes 196616 | tf_op jit(solution)/shard_map/ppermute | solution.py:271
  10.0 13.8 %collective-permute-start.1 = (bf16[256,128]{1,0:T(8,128)(2,1)S(1)}, bf16[256,128]{1,0:T(8,128)(2,1)S(1)}, u32[]{:S(2)}, u32[]{:S(2)}) collective-permute-start(bf16[256,128]{1,0:T(8,128)(2,1)S(1)} %get-tuple-element.37), channel_id=1, source_target_pairs={{0,128},{1,160},{2,192},{3,224},{4,0},{5,32},{6,64},{7,96},{32,129... | collective-permute-start | bytes 196616 | tf_op jit(solution)/shard_map/ppermute | solution.py:271
  23.8 1.5 broadcast_in_dim.31
  25.3 5.9 %all-to-all-start = ((bf16[32,8,256]{2,1,0:T(8,128)(2,1)}), bf16[32,8,256]{2,1,0:T(8,128)(2,1)S(1)}, u32[]{:S(2)}, u32[]{:S(2)}) async-start(bf16[32,8,256]{2,1,0:T(8,128)(2,1)} %bitcast.8), calls=%async_computation | async-start | bytes 262144 | tf_op jit(solution)/shard_map/all_to_all | solution.py:282
  35.6 1.5 attend.1
  37.1 4.0 %all-to-all-done = bf16[32,8,256]{2,1,0:T(8,128)(2,1)S(1)} async-done(((bf16[32,8,256]{2,1,0:T(8,128)(2,1)}), bf16[32,8,256]{2,1,0:T(8,128)(2,1)S(1)}, u32[]{:S(2)}, u32[]{:S(2)}) %all-to-all-start) | async-done | bytes 131104 | tf_op jit(solution)/shard_map/all_to_all | solution.py:282
  43.7 2.5 %collective-permute-start.2 = (bf16[144,512]{1,0:T(8,128)(2,1)S(1)}, bf16[144,512]{1,0:T(8,128)(2,1)S(1)}, u32[]{:S(2)}, u32[]{:S(2)}) collective-permute-start(bf16[144,512]{1,0:T(8,128)(2,1)S(1)} %attend.1), channel_id=1, source_target_pairs={{0,256},{256,0},{1,257},{257,1},{2,258},{258,2},{3,259},{259,3},{4... | collective-permute-start | bytes 442376 | tf_op jit(solution)/shard_map/ppermute | solution.py:52
  48.4 2.3 %collective-permute-done.2 = bf16[144,512]{1,0:T(8,128)(2,1)S(1)} collective-permute-done((bf16[144,512]{1,0:T(8,128)(2,1)S(1)}, bf16[144,512]{1,0:T(8,128)(2,1)S(1)}, u32[]{:S(2)}, u32[]{:S(2)}) %collective-permute-start.2) | collective-permute-done | bytes 147488 | tf_op jit(solution)/shard_map/ppermute | solution.py:52
  50.8 2.6 %collective-permute-start.3 = (bf16[256,512]{1,0:T(8,128)(2,1)S(1)}, bf16[256,512]{1,0:T(8,128)(2,1)S(1)}, u32[]{:S(2)}, u32[]{:S(2)}) collective-permute-start(bf16[256,512]{1,0:T(8,128)(2,1)S(1)} %pad_maximum_fusion.refs_0_), channel_id=1, source_target_pairs={{0,1},{1,2},{2,3},{3,4},{4,5},{5,6},{6,7},{7,0},{8,9},{9,10},{10,1... | collective-permute-start | bytes 786440 | tf_op jit(solution)/shard_map/ppermute | solution.py:56
  53.4 3.3 %collective-permute-start.4 = (bf16[256,512]{1,0:T(8,128)(2,1)S(1)}, bf16[256,512]{1,0:T(8,128)(2,1)S(1)}, u32[]{:S(2)}, u32[]{:S(2)}) collective-permute-start(bf16[256,512]{1,0:T(8,128)(2,1)S(1)} %pad_maximum_fusion.refs_0_), channel_id=1, source_target_pairs={{0,7},{1,0},{2,1},{3,2},{4,3},{5,4},{6,5},{7,6},{8,15},{9,8},{10,9... | collective-permute-start | bytes 786440 | tf_op jit(solution)/shard_map/ppermute | solution.py:56
  57.5 1.6 collective-permute-done.3.refs_1_
  59.1 2.5 %collective-permute-start.5 = (bf16[256,512]{1,0:T(8,128)(2,1)S(1)}, bf16[256,512]{1,0:T(8,128)(2,1)S(1)}, u32[]{:S(2)}, u32[]{:S(2)}) collective-permute-start(bf16[256,512]{1,0:T(8,128)(2,1)S(1)} %collective-permute-done.3.refs_1_), channel_id=1, source_target_pairs={{0,1},{1,2},{2,3},{3,4},{4,5},{5,6},{6,7},{7,0},{8,9},{9,10},{10,1... | collective-permute-start | bytes 786440 | tf_op jit(solution)/shard_map/ppermute | solution.py:56
  61.6 3.4 %collective-permute-start.6 = (bf16[256,512]{1,0:T(8,128)(2,1)S(1)}, bf16[256,512]{1,0:T(8,128)(2,1)S(1)}, u32[]{:S(2)}, u32[]{:S(2)}) collective-permute-start(bf16[256,512]{1,0:T(8,128)(2,1)S(1)} %collective-permute-done.4.refs_2_), channel_id=1, source_target_pairs={{0,7},{1,0},{2,1},{3,2},{4,3},{5,4},{6,5},{7,6},{8,15},{9,8},{10,9... | collective-permute-start | bytes 786440 | tf_op jit(solution)/shard_map/ppermute | solution.py:56
  65.9 1.6 collective-permute-done.5.refs_3_
  67.5 3.0 %collective-permute-start.7 = (bf16[256,512]{1,0:T(8,128)(2,1)S(1)}, bf16[256,512]{1,0:T(8,128)(2,1)S(1)}, u32[]{:S(2)}, u32[]{:S(2)}) collective-permute-start(bf16[256,512]{1,0:T(8,128)(2,1)S(1)} %collective-permute-done.5.refs_3_), channel_id=1, source_target_pairs={{0,1},{1,2},{2,3},{3,4},{4,5},{5,6},{6,7},{7,0},{8,9},{9,10},{10,1... | collective-permute-start | bytes 786440 | tf_op jit(solution)/shard_map/ppermute | solution.py:56
  70.5 4.0 %collective-permute-start.8 = (bf16[256,512]{1,0:T(8,128)(2,1)S(1)}, bf16[256,512]{1,0:T(8,128)(2,1)S(1)}, u32[]{:S(2)}, u32[]{:S(2)}) collective-permute-start(bf16[256,512]{1,0:T(8,128)(2,1)S(1)} %collective-permute-done.6.refs_4_), channel_id=1, source_target_pairs={{0,7},{1,0},{2,1},{3,2},{4,3},{5,4},{6,5},{7,6},{8,15},{9,8},{10,9... | collective-permute-start | bytes 786440 | tf_op jit(solution)/shard_map/ppermute | solution.py:56
  74.6 2.3 %collective-permute-done.7.refs_5_ = bf16[256,512]{1,0:T(8,128)(2,1)S(1)} collective-permute-done((bf16[256,512]{1,0:T(8,128)(2,1)S(1)}, bf16[256,512]{1,0:T(8,128)(2,1)S(1)}, u32[]{:S(2)}, u32[]{:S(2)}) %collective-permute-start.7) | collective-permute-done | bytes 262176 | tf_op jit(solution)/shard_map/ppermute | solution.py:56
  77.6 2.0 %collective-permute-start.9 = (bf16[128,512]{1,0:T(8,128)(2,1)}, bf16[128,512]{1,0:T(8,128)(2,1)S(1)}, u32[]{:S(2)}, u32[]{:S(2)}) collective-permute-start(bf16[128,512]{1,0:T(8,128)(2,1)} %slice.38), channel_id=1, source_target_pairs={{0,1},{1,2},{2,3},{3,4},{4,5},{5,6},{6,7},{7,0},{8,9},{9,10},{10,1... | collective-permute-start | bytes 393224 | tf_op jit(solution)/shard_map/ppermute | solution.py:56
  80.2 5.0 %collective-permute-start.10 = (bf16[128,512]{1,0:T(8,128)(2,1)}, bf16[128,512]{1,0:T(8,128)(2,1)S(1)}, u32[]{:S(2)}, u32[]{:S(2)}) collective-permute-start(bf16[128,512]{1,0:T(8,128)(2,1)} %slice.39), channel_id=1, source_target_pairs={{0,7},{1,0},{2,1},{3,2},{4,3},{5,4},{6,5},{7,6},{8,15},{9,8},{10,9... | collective-permute-start | bytes 393224 | tf_op jit(solution)/shard_map/ppermute | solution.py:56
  86.6 1.2 all-gather.3.cloned.1.call-done.refs_9_.weights_hbm
  88.1 2.8 %project.1 = (f32[256,256]{1,0:T(8,128)S(1)}, bf16[256,256]{1,0:T(8,128)(2,1)S(1)}) custom-call(s32[5]{0:T(128)S(1)} %stack.37.place_ref, bf16[256,512]{1,0:T(8,128)(2,1)S(1)} %pad_maximum_fusion.refs_0_, bf16[256,512]{1,0:T(8,128)(2,1)S(1)} %collective-permute-done.3.refs_1_, bf16[256,512]{1,0:T(8,128)(2,1)S(1)} %collective-permute-done.4.refs_2_, ...), custom_call_target="tpu_custom_call" | custom-call | flops 536870912 | bytes 4194304 | tf_op jit(solution)/shard_map/project/pallas_call | solution.py:65
  91.0 4.5 %collective-permute-start.11 = (bf16[256,256]{1,0:T(8,128)(2,1)S(1)}, bf16[256,256]{1,0:T(8,128)(2,1)S(1)}, u32[]{:S(2)}, u32[]{:S(2)}) collective-permute-start(bf16[256,256]{1,0:T(8,128)(2,1)S(1)} %get-tuple-element.24), channel_id=1, source_target_pairs={{0,8},{8,0},{1,9},{9,1},{2,10},{10,2},{3,11},{11,3},{4,12},{12,4},... | collective-permute-start | bytes 393224 | tf_op jit(solution)/shard_map/ppermute | solution.py:52
  95.5 4.2 %collective-permute-done.11.recv_ref = bf16[256,256]{1,0:T(8,128)(2,1)S(1)} collective-permute-done((bf16[256,256]{1,0:T(8,128)(2,1)S(1)}, bf16[256,256]{1,0:T(8,128)(2,1)S(1)}, u32[]{:S(2)}, u32[]{:S(2)}) %collective-permute-start.11) | collective-permute-done | bytes 131104 | tf_op jit(solution)/shard_map/ppermute | solution.py:52
  100.5 23.2 %all_to_all.15 = bf16[8,128,256]{2,1,0:T(8,128)(2,1)S(1)} all-to-all(bf16[8,128,256]{2,1,0:T(8,128)(2,1)S(1)} %bitcast.28), channel_id=1, replica_groups=mesh['xl'=2,'y'=8,'core'=2,'xh'=2,'z'=8] {'z'}, dimensions={0} | all-to-all | bytes 1048576 | tf_op jit(solution)/shard_map/all_to_all | solution.py:381
  123.7 2.3 %gate_up.1 = (f32[128,896]{1,0:T(8,128)S(1)}, bf16[128,896]{1,0:T(8,128)(2,1)S(1)}) custom-call(bf16[1024,256]{1,0:T(8,128)(2,1)S(1)} %bitcast.27, bf16[1,2048]{1,0:T(2,128)(2,1)S(1)} %reshape.111.gain_ref, bf16[2048,1280]{1,0:T(8,128)(2,1)} %all-gather.3.cloned.1.call-done.refs_9_.weights_hbm), custom_call_target="tpu_custom_call" | custom-call | flops 402653184 | bytes 3145728 | tf_op jit(solution)/shard_map/gate_up/pallas_call | solution.py:65
  126.0 3.4 %collective-permute-start.12 = (bf16[128,896]{1,0:T(8,128)(2,1)S(1)}, bf16[128,896]{1,0:T(8,128)(2,1)S(1)}, u32[]{:S(2)}, u32[]{:S(2)}) collective-permute-start(bf16[128,896]{1,0:T(8,128)(2,1)S(1)} %get-tuple-element.30), channel_id=1, source_target_pairs={{0,256},{256,0},{1,257},{257,1},{2,258},{258,2},{3,259},{259,3},{4... | collective-permute-start | bytes 688136 | tf_op jit(solution)/shard_map/ppermute | solution.py:52
  130.1 3.9 %collective-permute-done.12.recv_ref = bf16[128,896]{1,0:T(8,128)(2,1)S(1)} collective-permute-done((bf16[128,896]{1,0:T(8,128)(2,1)S(1)}, bf16[128,896]{1,0:T(8,128)(2,1)S(1)}, u32[]{:S(2)}, u32[]{:S(2)}) %collective-permute-start.12) | collective-permute-done | bytes 229408 | tf_op jit(solution)/shard_map/ppermute | solution.py:52
  134.0 1.4 copy-done
  135.4 2.6 %down.1 = bf16[256,1280]{1,0:T(8,128)(2,1)} custom-call(s32[5]{0:T(128)S(1)} %stack.37.place_ref, f32[128,896]{1,0:T(8,128)S(1)} %get-tuple-element.29.own_ref, bf16[128,896]{1,0:T(8,128)(2,1)S(1)} %collective-permute-done.12.recv_ref, bf16[128,256]{1,0:T(8,128)(2,1)S(1)} %get-tuple-element.31.residual_ref, bf16[2048,384]{1,0:T(8,128)(2,1)S(1)} %copy-done), custom_call_target="tpu_custom_call" | custom-call | flops 402653184 | bytes 2097152 | tf_op jit(solution)/shard_map/down/pallas_call | solution.py:65
  138.0 6.6 %all-to-all-start.2 = ((bf16[32,8,1280]{2,1,0:T(8,128)(2,1)}), bf16[32,8,1280]{2,1,0:T(8,128)(2,1)S(1)}, u32[]{:S(2)}, u32[]{:S(2)}) async-start(bf16[32,8,1280]{2,1,0:T(8,128)(2,1)} %bitcast.15), calls=%async_computation.2 | async-start | bytes 1310720 | tf_op jit(solution)/shard_map/all_to_all | solution.py:404
  144.7 21.1 %all-to-all-done.2 = bf16[32,8,1280]{2,1,0:T(8,128)(2,1)S(1)} async-done(((bf16[32,8,1280]{2,1,0:T(8,128)(2,1)}), bf16[32,8,1280]{2,1,0:T(8,128)(2,1)S(1)}, u32[]{:S(2)}, u32[]{:S(2)}) %all-to-all-start.2) | async-done | bytes 655392 | tf_op jit(solution)/shard_map/all_to_all | solution.py:404
  165.8 1.6 combine.1
  (64 shorter events, 15.4 us)
Async XLA Ops:
  6.5 50.8 %copy-start.7 = (bf16[4096]{0:T(1024)(128)(2,1)S(1)}, bf16[4096]{0:T(1024)(128)(2,1)}, u32[]{:S(2)}) copy-start(bf16[4096]{0:T(1024)(128)(2,1)} %param.19) | copy-start | bytes 24580
  7.4 29.7 %collective-permute-start = (bf16[256,128]{1,0:T(8,128)(2,1)S(1)}, bf16[256,128]{1,0:T(8,128)(2,1)S(1)}, u32[]{:S(2)}, u32[]{:S(2)}) collective-permute-start(bf16[256,128]{1,0:T(8,128)(2,1)S(1)} %get-tuple-element.38), channel_id=1, source_target_pairs={{0,0},{1,32},{2,64},{3,96},{4,128},{5,160},{6,192},{7,224},{32,1},... | collective-permute-start | bytes 196616 | tf_op jit(solution)/shard_map/ppermute | solution.py:271
  10.0 27.1 %collective-permute-start.1 = (bf16[256,128]{1,0:T(8,128)(2,1)S(1)}, bf16[256,128]{1,0:T(8,128)(2,1)S(1)}, u32[]{:S(2)}, u32[]{:S(2)}) collective-permute-start(bf16[256,128]{1,0:T(8,128)(2,1)S(1)} %get-tuple-element.37), channel_id=1, source_target_pairs={{0,128},{1,160},{2,192},{3,224},{4,0},{5,32},{6,64},{7,96},{32,129... | collective-permute-start | bytes 196616 | tf_op jit(solution)/shard_map/ppermute | solution.py:271
  25.3 15.8 %all-to-all-start = ((bf16[32,8,256]{2,1,0:T(8,128)(2,1)}), bf16[32,8,256]{2,1,0:T(8,128)(2,1)S(1)}, u32[]{:S(2)}, u32[]{:S(2)}) async-start(bf16[32,8,256]{2,1,0:T(8,128)(2,1)} %bitcast.8), calls=%async_computation | async-start | bytes 262144 | tf_op jit(solution)/shard_map/all_to_all | solution.py:282
  31.3 56.5 %all-gather.3.cloned.1.call-start = ((), (), s32[]{:S(2)}) async-start(), calls=%async_computation.3 | async-start | bytes 5570560 | tf_op jit(solution)/shard_map/all_gather | solution.py:310
  32.8 1.0 copy-start.4
  33.8 1.0 copy-start.5
  34.7 0.9 copy-start.6
  41.1 0.9 copy-start.1
  42.0 0.9 copy-start.2
  43.7 86.4 %all-gather.5.cloned.1.call-start = ((), (), s32[]{:S(2)}) async-start(), calls=%async_computation.4 | async-start | bytes 1671168 | tf_op jit(solution)/shard_map/all_gather | solution.py:315
  43.7 7.0 %collective-permute-start.2 = (bf16[144,512]{1,0:T(8,128)(2,1)S(1)}, bf16[144,512]{1,0:T(8,128)(2,1)S(1)}, u32[]{:S(2)}, u32[]{:S(2)}) collective-permute-start(bf16[144,512]{1,0:T(8,128)(2,1)S(1)} %attend.1), channel_id=1, source_target_pairs={{0,256},{256,0},{1,257},{257,1},{2,258},{258,2},{3,259},{259,3},{4... | collective-permute-start | bytes 442376 | tf_op jit(solution)/shard_map/ppermute | solution.py:52
  46.5 0.9 copy-start.3
  50.8 8.3 %collective-permute-start.3 = (bf16[256,512]{1,0:T(8,128)(2,1)S(1)}, bf16[256,512]{1,0:T(8,128)(2,1)S(1)}, u32[]{:S(2)}, u32[]{:S(2)}) collective-permute-start(bf16[256,512]{1,0:T(8,128)(2,1)S(1)} %pad_maximum_fusion.refs_0_), channel_id=1, source_target_pairs={{0,1},{1,2},{2,3},{3,4},{4,5},{5,6},{6,7},{7,0},{8,9},{9,10},{10,1... | collective-permute-start | bytes 786440 | tf_op jit(solution)/shard_map/ppermute | solution.py:56
  53.4 8.3 %collective-permute-start.4 = (bf16[256,512]{1,0:T(8,128)(2,1)S(1)}, bf16[256,512]{1,0:T(8,128)(2,1)S(1)}, u32[]{:S(2)}, u32[]{:S(2)}) collective-permute-start(bf16[256,512]{1,0:T(8,128)(2,1)S(1)} %pad_maximum_fusion.refs_0_), channel_id=1, source_target_pairs={{0,7},{1,0},{2,1},{3,2},{4,3},{5,4},{6,5},{7,6},{8,15},{9,8},{10,9... | collective-permute-start | bytes 786440 | tf_op jit(solution)/shard_map/ppermute | solution.py:56
  59.1 8.4 %collective-permute-start.5 = (bf16[256,512]{1,0:T(8,128)(2,1)S(1)}, bf16[256,512]{1,0:T(8,128)(2,1)S(1)}, u32[]{:S(2)}, u32[]{:S(2)}) collective-permute-start(bf16[256,512]{1,0:T(8,128)(2,1)S(1)} %collective-permute-done.3.refs_1_), channel_id=1, source_target_pairs={{0,1},{1,2},{2,3},{3,4},{4,5},{5,6},{6,7},{7,0},{8,9},{9,10},{10,1... | collective-permute-start | bytes 786440 | tf_op jit(solution)/shard_map/ppermute | solution.py:56
  61.6 8.9 %collective-permute-start.6 = (bf16[256,512]{1,0:T(8,128)(2,1)S(1)}, bf16[256,512]{1,0:T(8,128)(2,1)S(1)}, u32[]{:S(2)}, u32[]{:S(2)}) collective-permute-start(bf16[256,512]{1,0:T(8,128)(2,1)S(1)} %collective-permute-done.4.refs_2_), channel_id=1, source_target_pairs={{0,7},{1,0},{2,1},{3,2},{4,3},{5,4},{6,5},{7,6},{8,15},{9,8},{10,9... | collective-permute-start | bytes 786440 | tf_op jit(solution)/shard_map/ppermute | solution.py:56
  67.5 9.5 %collective-permute-start.7 = (bf16[256,512]{1,0:T(8,128)(2,1)S(1)}, bf16[256,512]{1,0:T(8,128)(2,1)S(1)}, u32[]{:S(2)}, u32[]{:S(2)}) collective-permute-start(bf16[256,512]{1,0:T(8,128)(2,1)S(1)} %collective-permute-done.5.refs_3_), channel_id=1, source_target_pairs={{0,1},{1,2},{2,3},{3,4},{4,5},{5,6},{6,7},{7,0},{8,9},{9,10},{10,1... | collective-permute-start | bytes 786440 | tf_op jit(solution)/shard_map/ppermute | solution.py:56
  70.5 9.1 %collective-permute-start.8 = (bf16[256,512]{1,0:T(8,128)(2,1)S(1)}, bf16[256,512]{1,0:T(8,128)(2,1)S(1)}, u32[]{:S(2)}, u32[]{:S(2)}) collective-permute-start(bf16[256,512]{1,0:T(8,128)(2,1)S(1)} %collective-permute-done.6.refs_4_), channel_id=1, source_target_pairs={{0,7},{1,0},{2,1},{3,2},{4,3},{5,4},{6,5},{7,6},{8,15},{9,8},{10,9... | collective-permute-start | bytes 786440 | tf_op jit(solution)/shard_map/ppermute | solution.py:56
  77.6 10.2 %collective-permute-start.9 = (bf16[128,512]{1,0:T(8,128)(2,1)}, bf16[128,512]{1,0:T(8,128)(2,1)S(1)}, u32[]{:S(2)}, u32[]{:S(2)}) collective-permute-start(bf16[128,512]{1,0:T(8,128)(2,1)} %slice.38), channel_id=1, source_target_pairs={{0,1},{1,2},{2,3},{3,4},{4,5},{5,6},{6,7},{7,0},{8,9},{9,10},{10,1... | collective-permute-start | bytes 393224 | tf_op jit(solution)/shard_map/ppermute | solution.py:56
  80.2 7.9 %collective-permute-start.10 = (bf16[128,512]{1,0:T(8,128)(2,1)}, bf16[128,512]{1,0:T(8,128)(2,1)S(1)}, u32[]{:S(2)}, u32[]{:S(2)}) collective-permute-start(bf16[128,512]{1,0:T(8,128)(2,1)} %slice.39), channel_id=1, source_target_pairs={{0,7},{1,0},{2,1},{3,2},{4,3},{5,4},{6,5},{7,6},{8,15},{9,8},{10,9... | collective-permute-start | bytes 393224 | tf_op jit(solution)/shard_map/ppermute | solution.py:56
  91.0 8.7 %collective-permute-start.11 = (bf16[256,256]{1,0:T(8,128)(2,1)S(1)}, bf16[256,256]{1,0:T(8,128)(2,1)S(1)}, u32[]{:S(2)}, u32[]{:S(2)}) collective-permute-start(bf16[256,256]{1,0:T(8,128)(2,1)S(1)} %get-tuple-element.24), channel_id=1, source_target_pairs={{0,8},{8,0},{1,9},{9,1},{2,10},{10,2},{3,11},{11,3},{4,12},{12,4},... | collective-permute-start | bytes 393224 | tf_op jit(solution)/shard_map/ppermute | solution.py:52
  126.0 7.9 %collective-permute-start.12 = (bf16[128,896]{1,0:T(8,128)(2,1)S(1)}, bf16[128,896]{1,0:T(8,128)(2,1)S(1)}, u32[]{:S(2)}, u32[]{:S(2)}) collective-permute-start(bf16[128,896]{1,0:T(8,128)(2,1)S(1)} %get-tuple-element.30), channel_id=1, source_target_pairs={{0,256},{256,0},{1,257},{257,1},{2,258},{258,2},{3,259},{259,3},{4... | collective-permute-start | bytes 688136 | tf_op jit(solution)/shard_map/ppermute | solution.py:52
  133.9 1.4 copy-start
  138.0 27.8 %all-to-all-start.2 = ((bf16[32,8,1280]{2,1,0:T(8,128)(2,1)}), bf16[32,8,1280]{2,1,0:T(8,128)(2,1)S(1)}, u32[]{:S(2)}, u32[]{:S(2)}) async-start(bf16[32,8,1280]{2,1,0:T(8,128)(2,1)} %bitcast.15), calls=%async_computation.2 | async-start | bytes 1310720 | tf_op jit(solution)/shard_map/all_to_all | solution.py:404
Sparse Core Ops, SparseCore 0:
  43.8 43.9 all-gather.2
  89.9 40.1 all-gather.4

commit v5 on v4

--- a/solution.py
+++ b/solution.py
@@ -24,10 +24,23 @@
 ROWS = 8
 TABLE = 16
 VMEM_BYTES = 48 * 1024 * 1024
+ALL_VMEM_BYTES = 63400000
 F32, BF16 = jnp.float32, jnp.bfloat16
 
 
-def attend_kernel(start_ref, queries_ref, keys_ref, values_ref, hits_ref, out_ref):
+def attend_kernel(
+    start_ref, flight_ref, ids_hbm, queries_hbm, keys_hbm, values_hbm, out_ref, ids_ref, queries_ref, keys_ref, values_ref, sems
+):
+    copies = [
+        pltpu.make_async_copy(source, target, sems.at[i])
+        for i, (source, target) in enumerate(
+            ((keys_hbm, keys_ref), (queries_hbm, queries_ref), (values_hbm, values_ref), (ids_hbm, ids_ref))
+        )
+    ]
+    for copy in copies:
+        copy.start()
+    for copy in copies:
+        copy.wait()
     keys, values = keys_ref[...], values_ref[...]
     size = keys.shape[1]
     shape = (2 * SLAB, keys.shape[0])
@@ -45,7 +58,13 @@
         context = (jnp.dot(exp_scores.astype(BF16), values, preferred_element_type=F32) / totals).astype(BF16)
         out_ref[:SLAB, first] = context[:SLAB]
         out_ref[:SLAB, second] = context[SLAB:]
-    out_ref[SLAB:, :] = hits_ref[...]
+    line = lax.broadcasted_iota(jnp.int32, (TABLE, SLAB), 0)
+    table = jnp.zeros((TABLE, SLAB), F32)
+    for f in range(FLIGHT):
+        named = jnp.max(jnp.where(ids_ref[...] == flight_ref[f], 1.0, 0.0), axis=0, keepdims=True)
+        table = jnp.where(line == f, named, table)
+    out_ref[SLAB:, :SLAB] = table.astype(BF16)
+    out_ref[SLAB:, SLAB:] = jnp.zeros((TABLE, HEADS_WIDE - SLAB), BF16)
 
 
 def swap(block, axis):
@@ -56,7 +75,7 @@
     return lax.ppermute(block, "z", [(i, (i + step) % RING) for i in range(RING)])
 
 
-def kernel_call(body, out_shapes, operands, spaces, flops, moved, name, scratch=()):
+def kernel_call(body, out_shapes, operands, spaces, flops, moved, name, scratch=(), out_space="v", vmem=VMEM_BYTES):
     kinds = {
         "v": pl.BlockSpec(memory_space=pltpu.VMEM),
         "s": pl.BlockSpec(memory_space=pltpu.SMEM),
@@ -66,38 +85,38 @@
         body,
         out_shape=[jax.ShapeDtypeStruct(shape, dtype) for shape, dtype in out_shapes],
         in_specs=[kinds[s] for s in spaces],
-        out_specs=[kinds["v"]] * len(out_shapes),
+        out_specs=[kinds[out_space]] * len(out_shapes),
         scratch_shapes=list(scratch),
-        compiler_params=pltpu.CompilerParams(vmem_limit_bytes=VMEM_BYTES),
+        compiler_params=pltpu.CompilerParams(vmem_limit_bytes=vmem),
         cost_estimate=pl.CostEstimate(flops=flops, bytes_accessed=moved, transcendentals=0),
         name=name,
     )(*operands)
 
 
-def pack_weights_kernel(gate_ref, up_ref, *refs):
-    wide, packed_ref = refs[:-1], refs[-1]
-    packed_ref[:, :HIDDEN] = gate_ref[...]
-    packed_ref[:, HIDDEN : 2 * HIDDEN] = up_ref[...]
-    at = 2 * HIDDEN
-    for ref in wide:
-        for j in range(ref.shape[0] // 128):
-            packed_ref[:, at : at + 128] = ref[j * 128 : (j + 1) * 128, :]
-            at += 128
-
-
-def pack_down_kernel(down_ref, packed_ref):
-    for j in range(HIDDEN // 128):
-        packed_ref[:, j * 128 : (j + 1) * 128] = down_ref[j * 128 : (j + 1) * 128, :]
-
-
-def project_kernel(place_ref, *refs):
+def pack_weights_kernel(gate_ref, up_ref, down_ref, swapped_ref, packed_ref, sems):
+    pieces = [(gate_ref, HIDDEN), (up_ref, HIDDEN)] + [
+        (ref.at[pl.ds(j * 128, 128)], 128)
+        for ref in (down_ref, swapped_ref)
+        for j in range(ref.shape[0] // 128)
+    ]
+    copies, at = [], 0
+    for i, (piece, lanes) in enumerate(pieces):
+        copies.append(pltpu.make_async_copy(piece, packed_ref.at[:, pl.ds(at, lanes)], sems.at[i]))
+        at += lanes
+    for copy in copies:
+        copy.start()
+    for copy in copies:
+        copy.wait()
+
+
+def project_kernel(place_ref, hidden_ref, *refs):
     contexts, (weights_hbm, keep_ref, send_ref, weights, sems) = refs[:9], refs[9:]
-    z = place_ref[4]
+    xl, xh, z = place_ref[0], place_ref[3], place_ref[4]
 
     def copy(k):
         at = pl.ds(k * 2 * 128, 2 * 128)
         return pltpu.make_async_copy(
-            weights_hbm.at[at, pl.ds(2 * HIDDEN, HEADS_WIDE)], weights.at[at], sems.at[k]
+            weights_hbm.at[at, pl.ds(3 * HIDDEN, HEADS_WIDE)], weights.at[at], sems.at[k]
         )
 
     for k in range(RING):
@@ -110,8 +129,8 @@
             step, context = STEPS[k], contexts[k][...]
         else:
             step, context = 4, jnp.concatenate([contexts[k][...], contexts[k + 1][...]])
+        first = pl.multiple_of(((z + (step + RING)) & (RING - 1)) * 256, 256)
         for half in range(2):
-            first = pl.multiple_of(((z + (step + RING + half * 4)) & (RING - 1)) * 256, 256)
             lanes = slice(half * 256, half * 256 + 256)
             block = weights[pl.ds(first, 256), lanes]
             rhs = jnp.concatenate(
@@ -121,19 +140,26 @@
                 ]
             )
             total += jnp.dot(context[:, lanes], rhs, preferred_element_type=F32)
+    hidden = hidden_ref[...].astype(F32)
+    rows = SLAB // 2
+    own = jnp.where(xl == 0, hidden[:rows], hidden[rows:])
+    other = jnp.where(xl == 0, hidden[rows:], hidden[:rows])
+    total += jnp.concatenate(
+        [jnp.where(xh == at, block, 0.0) for block in (own, other) for at in range(2)]
+    )
     keep_ref[...] = total
     send_ref[...] = total.astype(BF16)
 
 
-def residual_kernel(place_ref, keep_ref, recv_ref, hidden_ref, pickers_ref, residual_ref, rows_ref):
+def residual_kernel(place_ref, keep_ref, recv_ref, pickers_ref, residual_ref, rows_ref):
     xl, xh = place_ref[0], place_ref[3]
-    attention = keep_ref[...] + recv_ref[...].astype(F32)
-    own, other = attention[:SLAB], attention[SLAB:]
+    summed = keep_ref[...] + recv_ref[...].astype(F32)
+    own, other = summed[:SLAB], summed[SLAB:]
     per_expert = BLOCKS * CAP
     held = jnp.zeros((SLAB, COLS), F32)
     for slab in range(2):
         at = slice(slab * SLAB, (slab + 1) * SLAB)
-        residual = (jnp.where(xl == slab, own, other) + hidden_ref[at, :].astype(F32)).astype(BF16)
+        residual = jnp.where(xl == slab, own, other).astype(BF16)
         held = jnp.where(xh == slab, residual.astype(F32), held)
         picked = jnp.dot(pickers_ref[at, :], residual, preferred_element_type=F32).astype(BF16)
         for f in range(FLIGHT // 2):
@@ -178,7 +204,7 @@
 
 
 def down_kernel(place_ref, own_ref, recv_ref, residual_ref, weights_hbm, out_ref, weights, sem):
-    copy = pltpu.make_async_copy(weights_hbm, weights, sem)
+    copy = pltpu.make_async_copy(weights_hbm.at[:, pl.ds(2 * HIDDEN, HIDDEN)], weights, sem)
     copy.start()
     xh = place_ref[3]
     slots = 2 * BLOCKS * CAP
@@ -267,53 +293,47 @@
     tensor_idx = lax.axis_index(TENSOR)
     place = jnp.stack([lax.axis_index(a) for a in DP + TENSOR]).astype(jnp.int32)
 
-    def transposed(block, shift):
-        return lax.ppermute(
-            block,
-            ("y", "z"),
-            [(a * RING + b, (b + shift) % RING * RING + a) for a in range(RING) for b in range(RING)],
-        )
-
-    top = transposed(out_weight[: HEADS_WIDE // 2], 0)
-    bottom = transposed(out_weight[HEADS_WIDE // 2 :], RING // 2)
-
-    columns = hidden_rows.reshape(ROWS, 2, 1, RING, COLS).transpose(1, 2, 3, 0, 4)
-    hidden_out = jnp.broadcast_to(columns, (2, 2, RING, ROWS, COLS)).reshape(2 * BLOCKS, ROWS, COLS)
+    swapped = lax.ppermute(
+        out_weight, ("y", "z"), [(a * RING + b, b * RING + a) for a in range(RING) for b in range(RING)]
+    )
     hidden_in = lax.all_to_all(
-        hidden_out, PAIR_TENSOR, split_axis=0, concat_axis=0, tiled=True
-    ).reshape(2 * SLAB, COLS)
-
-    matches = route_ids[:, None, :] == flight_experts[None, :, None]
-    hits = jnp.sum(matches.astype(jnp.int32), axis=2, dtype=jnp.int32)
-    units = jnp.sum(jnp.where(matches, route_weights[:, None, :], 0), axis=2, dtype=jnp.int32)
-
-    hit_rows = jnp.pad(hits.T.astype(BF16), ((0, TABLE - FLIGHT), (0, HEADS_WIDE - SLAB)))
+        hidden_rows.reshape(ROWS, BLOCKS, COLS).transpose(1, 0, 2),
+        ("xl", "z"),
+        split_axis=0,
+        concat_axis=0,
+        tiled=True,
+    ).reshape(SLAB, COLS)
     (extended,) = kernel_call(
         attend_kernel,
         [((SLAB + TABLE, HEADS_WIDE), BF16)],
-        (slab_start, queries, keys, values, hit_rows),
-        "svvvv",
+        (slab_start, flight_experts, route_ids.T, queries, keys, values),
+        "sshhhh",
         4 * 512 * 1152 * 128,
         1 << 20,
         "attend",
-    )
-    top, bottom, hidden_in, _ = lax.optimization_barrier((top, bottom, hidden_in, extended))
+        [
+            pltpu.VMEM((8, SLAB), jnp.int32),
+            pltpu.VMEM(queries.shape, BF16),
+            pltpu.VMEM(keys.shape, BF16),
+            pltpu.VMEM(values.shape, BF16),
+            pltpu.SemaphoreType.DMA((4,)),
+        ],
+        vmem=ALL_VMEM_BYTES,
+    )
+    swapped, hidden_in, _ = lax.optimization_barrier((swapped, hidden_in, extended))
     (packed,) = kernel_call(
         pack_weights_kernel,
-        [((128, 2 * HIDDEN + HEADS_WIDE), BF16)],
-        (gate_weight, up_weight, top, bottom),
-        "vvvv",
+        [((128, 3 * HIDDEN + HEADS_WIDE), BF16)],
+        (gate_weight, up_weight, down_weight, swapped),
+        "hhhh",
         0,
-        4 * 128 * 1280,
+        4 * 128 * 1664,
         "pack_weights",
+        [pltpu.SemaphoreType.DMA((2 + HIDDEN // 128 + HEADS_WIDE // 128,))],
+        "h",
+        ALL_VMEM_BYTES,
     )
     weights = lax.all_gather(packed, ("y", "core"), axis=0, tiled=True)
-    (packed_down,) = kernel_call(
-        pack_down_kernel, [((128, HIDDEN), BF16)], (down_weight,), "v", 0, 4 * 128 * 384, "pack_down"
-    )
-    packed_down, _ = lax.optimization_barrier((packed_down, packed))
-    down_weights = lax.all_gather(packed_down, ("y", "core"), axis=0, tiled=True)
-
     other = swap(extended, "xl")
     both = jnp.concatenate([extended[:SLAB], other[:SLAB]])
     up1, down1 = along_z(both, 1), along_z(both, -1)
@@ -321,6 +341,9 @@
     up3, down3 = along_z(up2, 1), along_z(down2, -1)
     up4, down4 = along_z(up3[:SLAB], 1), along_z(down3[SLAB:], -1)
 
+    matches = route_ids[:, None, :] == flight_experts[None, :, None]
+    hits = jnp.sum(matches.astype(jnp.int32), axis=2, dtype=jnp.int32)
+    units = jnp.sum(jnp.where(matches, route_weights[:, None, :], 0), axis=2, dtype=jnp.int32)
     hits_both = jnp.where(
         xl == 0, jnp.stack([extended[SLAB:], other[SLAB:]]), jnp.stack([other[SLAB:], extended[SLAB:]])
     )
@@ -362,8 +385,8 @@
     keep, send = kernel_call(
         project_kernel,
         [((2 * SLAB, COLS), F32), ((2 * SLAB, COLS), BF16)],
-        (place, both, up1, down1, up2, down2, up3, down3, up4, down4, weights),
-        "s" + "v" * 9 + "h",
+        (place, hidden_in, both, up1, down1, up2, down2, up3, down3, up4, down4, weights),
+        "s" + "v" * 10 + "h",
         2 * 256 * 4096 * 256,
         2 * 2048 * 1024,
         "project",
@@ -372,8 +395,8 @@
     residual, rows_out = kernel_call(
         residual_kernel,
         [((SLAB, COLS), BF16), ((RING * 2 * BLOCKS * CAP, COLS), BF16)],
-        (place, keep, swap(send, "xh"), hidden_in, pickers),
-        "svvvv",
+        (place, keep, swap(send, "xh"), pickers),
+        "svvv",
         2 * 256 * 128 * 256,
         1 << 20,
         "residual",
@@ -394,7 +417,7 @@
     (outward,) = kernel_call(
         down_kernel,
         [((4 * BLOCKS * CAP, QUARTER + COLS), BF16)],
-        (place, own, swap(part, "xl"), residual, down_weights),
+        (place, own, swap(part, "xl"), residual, weights),
         "svvvh",
         2 * 256 * 384 * 2048,
         2 << 20,

time: 175 us -> 179 us (1.023)
  Pallas kernels: 13.1 us -> 29.1 us
  local copies, waits for them, and re-layouts: 12.7 us -> 5.69 us
  starting transfers between devices: 65.4 us -> 59.7 us
    pallas_call x8 -> x7, Pallas kernels: 13.1 us -> 29.1 us  [kernel_call(): pl.pallas_call(body, out_shape=[jax.ShapeDtypeStruct(shape, dtype) for sh...]
    ppermute x2 -> x1, starting transfers between devices: 16.4 us -> 2.56 us  [per_device(): lax.ppermute(out_weight, ('y', 'z'), [(a * RING + b, b * RING + a) for a...]
    all_to_all x1, starting transfers between devices: 5.94 us -> 12.4 us  [per_device(): lax.all_to_all(hidden_rows.reshape(ROWS, BLOCKS, COLS).transpose(1, 0, 2)...]
    unnamed x16 -> x2, local copies, waits for them, and re-layouts: 6.91 us -> 0.65 us
    all_gather x1, waiting for transfers between devices: 1.22 us -> 6.79 us  [per_device(): weights = lax.all_gather(packed, ('y', 'core'), axis=0, tiled=True)]
    all_to_all x1, waiting for transfers between devices: 21.1 us -> 19.2 us  [per_device(): lax.all_to_all(outward.reshape(2 * BLOCKS, 2 * CAP, QUARTER + COLS), PAIR...]
  transfers between devices with their start and end apart: 17 -> 15, of which waited for: 11 -> 9; matrix products, arithmetic and copies ran while one was open for 4% -> 4% of each run, Pallas kernels for 5% -> 2%
where the time goes in v5:
time: 179 us; the launch traced here: 178 us
  starting transfers between devices  59.7 us (33%)
  waiting for transfers between devices  43.9 us (25%)
  Pallas kernels  29.1 us (16%)
  blocking collectives  23.2 us (13%)
  between operations  14.3 us (8%)
  local copies, waits for them, and re-layouts  5.69 us (3%)
  other arithmetic  2.28 us (1%)
    pallas_call x7, Pallas kernels, kernel_call(): pl.pallas_call(body, out_shape=[jax.ShapeDtypeStruct(shape, dtype) for sh...  29.1 us
    ppermute x8, starting transfers between devices, along_z(): lax.ppermute(block, 'z', [(i, (i + step) % RING) for i in range(RING)])  27.2 us
    all_to_all x1, blocking collectives, per_device(): lax.all_to_all(rows_out.reshape(RING, 2 * BLOCKS * CAP, COLS), 'z', split...  23.2 us
    all_to_all x1, waiting for transfers between devices, per_device(): lax.all_to_all(outward.reshape(2 * BLOCKS, 2 * CAP, QUARTER + COLS), PAIR...  19.2 us
    all_to_all x1, starting transfers between devices, per_device(): lax.all_to_all(hidden_rows.reshape(ROWS, BLOCKS, COLS).transpose(1, 0, 2)...  12.4 us
    ppermute x3, starting transfers between devices, swap(): return lax.ppermute(block, axis, [(0, 1), (1, 0)])  11 us
    ppermute x3, waiting for transfers between devices, swap(): return lax.ppermute(block, axis, [(0, 1), (1, 0)])  10.2 us
    all_gather x1, waiting for transfers between devices, per_device(): weights = lax.all_gather(packed, ('y', 'core'), axis=0, tiled=True)  6.79 us
  transfers between devices with their start and end apart: 15, of which 9 were waited for; matrix products, arithmetic and copies ran while one was open for 4% of the time, Pallas kernels for 2%

profile of v5, /device:TPU:64, one launch (start us, length us, event | category | flops | bytes accessed | tf_op | source)
XLA Modules:
  0.0 178.2 jit_solution(6177283736868497432)
XLA Ops:
  6.5 2.6 %collective-permute-start = (bf16[512,128]{1,0:T(8,128)(2,1)}, bf16[512,128]{1,0:T(8,128)(2,1)S(1)}, u32[]{:S(2)}, u32[]{:S(2)}) collective-permute-start(bf16[512,128]{1,0:T(8,128)(2,1)} %param.18), channel_id=1, source_target_pairs={{0,0},{1,32},{2,64},{3,96},{4,128},{5,160},{6,192},{7,224},{32,1},... | collective-permute-start | bytes 393224 | tf_op jit(solution)/shard_map/ppermute | solution.py:296
  9.1 12.4 %all-to-all-start = ((bf16[16,8,256]{2,1,0:T(8,128)(2,1)}), bf16[16,8,256]{2,1,0:T(8,128)(2,1)S(1)}, u32[]{:S(2)}, u32[]{:S(2)}) async-start(bf16[16,8,256]{2,1,0:T(8,128)(2,1)} %bitcast.26), calls=%async_computation | async-start | bytes 131072 | tf_op jit(solution)/shard_map/all_to_all | solution.py:299
  22.2 4.0 %attend.1 = bf16[144,512]{1,0:T(8,128)(2,1)} custom-call(s32[1]{0:T(128)S(6)} %copy.20.start_ref, s32[4]{0:T(128)} %flight_ref.1, s32[8,128]{1,0:T(8,128)} %bitcast.27, bf16[128,512]{1,0:T(8,128)(2,1)} %queries_hbm.1, bf16[1152,128]{1,0:T(8,128)(2,1)} %keys_hbm.1, bf16[1152,128]{1,0:T(8,128)(2,1)} %values_hbm.1), custom_call_target="tpu_custom_call" | custom-call | flops 301989888 | bytes 1048576 | tf_op jit(solution)/shard_map/attend/pallas_call | solution.py:84
  26.2 2.8 %all-to-all-done = bf16[16,8,256]{2,1,0:T(8,128)(2,1)S(1)} async-done(((bf16[16,8,256]{2,1,0:T(8,128)(2,1)}), bf16[16,8,256]{2,1,0:T(8,128)(2,1)S(1)}, u32[]{:S(2)}, u32[]{:S(2)}) %all-to-all-start) | async-done | bytes 65568 | tf_op jit(solution)/shard_map/all_to_all | solution.py:299
  29.7 14.1 %pack_weights.1 = bf16[128,1664]{1,0:T(8,128)(2,1)} custom-call(bf16[128,384]{1,0:T(8,128)(2,1)} %gate_ref.1, bf16[128,384]{1,0:T(8,128)(2,1)} %up_ref.1, bf16[384,128]{1,0:T(8,128)(2,1)} %down_ref.1, bf16[512,128]{1,0:T(8,128)(2,1)} %copy-done), custom_call_target="tpu_custom_call" | custom-call | bytes 851968 | tf_op jit(solution)/shard_map/pack_weights/pallas_call | solution.py:84
  43.8 2.7 %collective-permute-start.1 = (bf16[144,512]{1,0:T(8,128)(2,1)}, bf16[144,512]{1,0:T(8,128)(2,1)S(1)}, u32[]{:S(2)}, u32[]{:S(2)}) collective-permute-start(bf16[144,512]{1,0:T(8,128)(2,1)} %attend.1), channel_id=1, source_target_pairs={{0,256},{256,0},{1,257},{257,1},{2,258},{258,2},{3,259},{259,3},{4... | collective-permute-start | bytes 442376 | tf_op jit(solution)/shard_map/ppermute | solution.py:71
  46.5 0.9 slice.28
  49.5 1.5 collective-permute-done.1
  51.1 2.6 %collective-permute-start.2 = (bf16[256,512]{1,0:T(8,128)(2,1)S(1)}, bf16[256,512]{1,0:T(8,128)(2,1)S(1)}, u32[]{:S(2)}, u32[]{:S(2)}) collective-permute-start(bf16[256,512]{1,0:T(8,128)(2,1)S(1)} %pad_maximum_fusion.refs_0_), channel_id=1, source_target_pairs={{0,1},{1,2},{2,3},{3,4},{4,5},{5,6},{6,7},{7,0},{8,9},{9,10},{10,1... | collective-permute-start | bytes 786440 | tf_op jit(solution)/shard_map/ppermute | solution.py:75
  53.7 3.2 %collective-permute-start.3 = (bf16[256,512]{1,0:T(8,128)(2,1)S(1)}, bf16[256,512]{1,0:T(8,128)(2,1)S(1)}, u32[]{:S(2)}, u32[]{:S(2)}) collective-permute-start(bf16[256,512]{1,0:T(8,128)(2,1)S(1)} %pad_maximum_fusion.refs_0_), channel_id=1, source_target_pairs={{0,7},{1,0},{2,1},{3,2},{4,3},{5,4},{6,5},{7,6},{8,15},{9,8},{10,9... | collective-permute-start | bytes 786440 | tf_op jit(solution)/shard_map/ppermute | solution.py:75
  58.4 0.9 collective-permute-done.2.refs_1_
  59.4 2.6 %collective-permute-start.4 = (bf16[256,512]{1,0:T(8,128)(2,1)S(1)}, bf16[256,512]{1,0:T(8,128)(2,1)S(1)}, u32[]{:S(2)}, u32[]{:S(2)}) collective-permute-start(bf16[256,512]{1,0:T(8,128)(2,1)S(1)} %collective-permute-done.2.refs_1_), channel_id=1, source_target_pairs={{0,1},{1,2},{2,3},{3,4},{4,5},{5,6},{6,7},{7,0},{8,9},{9,10},{10,1... | collective-permute-start | bytes 786440 | tf_op jit(solution)/shard_map/ppermute | solution.py:75
  62.0 4.7 %collective-permute-start.5 = (bf16[256,512]{1,0:T(8,128)(2,1)S(1)}, bf16[256,512]{1,0:T(8,128)(2,1)S(1)}, u32[]{:S(2)}, u32[]{:S(2)}) collective-permute-start(bf16[256,512]{1,0:T(8,128)(2,1)S(1)} %collective-permute-done.3.refs_2_), channel_id=1, source_target_pairs={{0,7},{1,0},{2,1},{3,2},{4,3},{5,4},{6,5},{7,6},{8,15},{9,8},{10,9... | collective-permute-start | bytes 786440 | tf_op jit(solution)/shard_map/ppermute | solution.py:75
  67.5 1.6 collective-permute-done.4.refs_3_
  69.1 1.9 %collective-permute-start.6 = (bf16[256,512]{1,0:T(8,128)(2,1)S(1)}, bf16[256,512]{1,0:T(8,128)(2,1)S(1)}, u32[]{:S(2)}, u32[]{:S(2)}) collective-permute-start(bf16[256,512]{1,0:T(8,128)(2,1)S(1)} %collective-permute-done.4.refs_3_), channel_id=1, source_target_pairs={{0,1},{1,2},{2,3},{3,4},{4,5},{5,6},{6,7},{7,0},{8,9},{9,10},{10,1... | collective-permute-start | bytes 786440 | tf_op jit(solution)/shard_map/ppermute | solution.py:75
  71.0 5.1 %collective-permute-start.7 = (bf16[256,512]{1,0:T(8,128)(2,1)S(1)}, bf16[256,512]{1,0:T(8,128)(2,1)S(1)}, u32[]{:S(2)}, u32[]{:S(2)}) collective-permute-start(bf16[256,512]{1,0:T(8,128)(2,1)S(1)} %collective-permute-done.5.refs_4_), channel_id=1, source_target_pairs={{0,7},{1,0},{2,1},{3,2},{4,3},{5,4},{6,5},{7,6},{8,15},{9,8},{10,9... | collective-permute-start | bytes 786440 | tf_op jit(solution)/shard_map/ppermute | solution.py:75
  76.2 2.3 %collective-permute-done.6.refs_5_ = bf16[256,512]{1,0:T(8,128)(2,1)S(1)} collective-permute-done((bf16[256,512]{1,0:T(8,128)(2,1)S(1)}, bf16[256,512]{1,0:T(8,128)(2,1)S(1)}, u32[]{:S(2)}, u32[]{:S(2)}) %collective-permute-start.6) | collective-permute-done | bytes 262176 | tf_op jit(solution)/shard_map/ppermute | solution.py:75
  78.6 1.9 %collective-permute-start.8 = (bf16[128,512]{1,0:T(8,128)(2,1)S(1)}, bf16[128,512]{1,0:T(8,128)(2,1)S(1)}, u32[]{:S(2)}, u32[]{:S(2)}) collective-permute-start(bf16[128,512]{1,0:T(8,128)(2,1)S(1)} %slice.30), channel_id=1, source_target_pairs={{0,1},{1,2},{2,3},{3,4},{4,5},{5,6},{6,7},{7,0},{8,9},{9,10},{10,1... | collective-permute-start | bytes 393224 | tf_op jit(solution)/shard_map/ppermute | solution.py:75
  81.2 5.1 %collective-permute-start.9 = (bf16[128,512]{1,0:T(8,128)(2,1)}, bf16[128,512]{1,0:T(8,128)(2,1)S(1)}, u32[]{:S(2)}, u32[]{:S(2)}) collective-permute-start(bf16[128,512]{1,0:T(8,128)(2,1)} %slice.31), channel_id=1, source_target_pairs={{0,7},{1,0},{2,1},{3,2},{4,3},{5,4},{6,5},{7,6},{8,15},{9,8},{10,9... | collective-permute-start | bytes 393224 | tf_op jit(solution)/shard_map/ppermute | solution.py:75
  86.4 1.1 mul.70.pickers_ref
  87.6 6.8 %all-gather.2.cloned.1.call-done.refs_9_.weights_hbm = bf16[2048,1664]{1,0:T(8,128)(2,1)} async-done(((bf16[128,1664]{1,0:T(8,128)(2,1)}), bf16[2048,1664]{1,0:T(8,128)(2,1)}) %all-gather.2.cloned.1.call-update) | async-done | bytes 6815760 | tf_op jit(solution)/shard_map/all_gather | solution.py:336
  94.4 2.8 %project.1 = (f32[256,256]{1,0:T(8,128)S(1)}, bf16[256,256]{1,0:T(8,128)(2,1)S(1)}) custom-call(s32[5]{0:T(128)S(1)} %stack.37.place_ref, bf16[128,256]{1,0:T(8,128)(2,1)S(1)} %bitcast.25, bf16[256,512]{1,0:T(8,128)(2,1)S(1)} %pad_maximum_fusion.refs_0_, bf16[256,512]{1,0:T(8,128)(2,1)S(1)} %collective-permute-done.2.refs_1_, ...), custom_call_target="tpu_custom_call" | custom-call | flops 536870912 | bytes 4194304 | tf_op jit(solution)/shard_map/project/pallas_call | solution.py:84
  97.2 4.9 %collective-permute-start.10 = (bf16[256,256]{1,0:T(8,128)(2,1)S(1)}, bf16[256,256]{1,0:T(8,128)(2,1)S(1)}, u32[]{:S(2)}, u32[]{:S(2)}) collective-permute-start(bf16[256,256]{1,0:T(8,128)(2,1)S(1)} %get-tuple-element.22), channel_id=1, source_target_pairs={{0,8},{8,0},{1,9},{9,1},{2,10},{10,2},{3,11},{11,3},{4,12},{12,4},... | collective-permute-start | bytes 393224 | tf_op jit(solution)/shard_map/ppermute | solution.py:71
  102.1 4.2 %collective-permute-done.10.recv_ref = bf16[256,256]{1,0:T(8,128)(2,1)S(1)} collective-permute-done((bf16[256,256]{1,0:T(8,128)(2,1)S(1)}, bf16[256,256]{1,0:T(8,128)(2,1)S(1)}, u32[]{:S(2)}, u32[]{:S(2)}) %collective-permute-start.10) | collective-permute-done | bytes 131104 | tf_op jit(solution)/shard_map/ppermute | solution.py:71
  107.0 23.2 %all_to_all.15 = bf16[8,128,256]{2,1,0:T(8,128)(2,1)S(1)} all-to-all(bf16[8,128,256]{2,1,0:T(8,128)(2,1)S(1)} %bitcast.24), channel_id=1, replica_groups=mesh['xl'=2,'y'=8,'core'=2,'xh'=2,'z'=8] {'z'}, dimensions={0} | all-to-all | bytes 1048576 | tf_op jit(solution)/shard_map/all_to_all | solution.py:404
  130.2 2.3 %gate_up.1 = (f32[128,896]{1,0:T(8,128)S(1)}, bf16[128,896]{1,0:T(8,128)(2,1)S(1)}) custom-call(bf16[1024,256]{1,0:T(8,128)(2,1)S(1)} %bitcast.23, bf16[1,2048]{1,0:T(2,128)(2,1)S(1)} %reshape.107.gain_ref, bf16[2048,1664]{1,0:T(8,128)(2,1)} %all-gather.2.cloned.1.call-done.refs_9_.weights_hbm), custom_call_target="tpu_custom_call" | custom-call | flops 402653184 | bytes 3145728 | tf_op jit(solution)/shard_map/gate_up/pallas_call | solution.py:84
  132.5 3.4 %collective-permute-start.11 = (bf16[128,896]{1,0:T(8,128)(2,1)S(1)}, bf16[128,896]{1,0:T(8,128)(2,1)S(1)}, u32[]{:S(2)}, u32[]{:S(2)}) collective-permute-start(bf16[128,896]{1,0:T(8,128)(2,1)S(1)} %get-tuple-element.27), channel_id=1, source_target_pairs={{0,256},{256,0},{1,257},{257,1},{2,258},{258,2},{3,259},{259,3},{4... | collective-permute-start | bytes 688136 | tf_op jit(solution)/shard_map/ppermute | solution.py:71
  135.9 4.5 %collective-permute-done.11.recv_ref = bf16[128,896]{1,0:T(8,128)(2,1)S(1)} collective-permute-done((bf16[128,896]{1,0:T(8,128)(2,1)S(1)}, bf16[128,896]{1,0:T(8,128)(2,1)S(1)}, u32[]{:S(2)}, u32[]{:S(2)}) %collective-permute-start.11) | collective-permute-done | bytes 229408 | tf_op jit(solution)/shard_map/ppermute | solution.py:71
  140.4 3.5 %down.1 = bf16[256,1280]{1,0:T(8,128)(2,1)} custom-call(s32[5]{0:T(128)S(1)} %stack.37.place_ref, f32[128,896]{1,0:T(8,128)S(1)} %get-tuple-element.26.own_ref, bf16[128,896]{1,0:T(8,128)(2,1)S(1)} %collective-permute-done.11.recv_ref, bf16[128,256]{1,0:T(8,128)(2,1)S(1)} %get-tuple-element.28.residual_ref, ...), custom_call_target="tpu_custom_call" | custom-call | flops 402653184 | bytes 2097152 | tf_op jit(solution)/shard_map/down/pallas_call | solution.py:84
  144.0 6.5 %all-to-all-start.2 = ((bf16[32,8,1280]{2,1,0:T(8,128)(2,1)}), bf16[32,8,1280]{2,1,0:T(8,128)(2,1)S(1)}, u32[]{:S(2)}, u32[]{:S(2)}) async-start(bf16[32,8,1280]{2,1,0:T(8,128)(2,1)} %bitcast.13), calls=%async_computation.2 | async-start | bytes 1310720 | tf_op jit(solution)/shard_map/all_to_all | solution.py:427
  150.5 19.2 %all-to-all-done.2 = bf16[32,8,1280]{2,1,0:T(8,128)(2,1)S(1)} async-done(((bf16[32,8,1280]{2,1,0:T(8,128)(2,1)}), bf16[32,8,1280]{2,1,0:T(8,128)(2,1)S(1)}, u32[]{:S(2)}, u32[]{:S(2)}) %all-to-all-start.2) | async-done | bytes 655392 | tf_op jit(solution)/shard_map/all_to_all | solution.py:427
  169.7 1.6 combine.1
  (40 shorter events, 6.7 us)
Async XLA Ops:
  6.5 22.5 %collective-permute-start = (bf16[512,128]{1,0:T(8,128)(2,1)}, bf16[512,128]{1,0:T(8,128)(2,1)S(1)}, u32[]{:S(2)}, u32[]{:S(2)}) collective-permute-start(bf16[512,128]{1,0:T(8,128)(2,1)} %param.18), channel_id=1, source_target_pairs={{0,0},{1,32},{2,64},{3,96},{4,128},{5,160},{6,192},{7,224},{32,1},... | collective-permute-start | bytes 393224 | tf_op jit(solution)/shard_map/ppermute | solution.py:296
  9.1 19.9 %all-to-all-start = ((bf16[16,8,256]{2,1,0:T(8,128)(2,1)}), bf16[16,8,256]{2,1,0:T(8,128)(2,1)S(1)}, u32[]{:S(2)}, u32[]{:S(2)}) async-start(bf16[16,8,256]{2,1,0:T(8,128)(2,1)} %bitcast.26), calls=%async_computation | async-start | bytes 131072 | tf_op jit(solution)/shard_map/all_to_all | solution.py:299
  21.5 72.9 %all-gather.2.cloned.1.call-start = ((), (), s32[]{:S(2)}) async-start(), calls=%async_computation.3 | async-start | bytes 7241728 | tf_op jit(solution)/shard_map/all_gather | solution.py:336
  29.0 0.7 copy-start
  43.8 7.2 %collective-permute-start.1 = (bf16[144,512]{1,0:T(8,128)(2,1)}, bf16[144,512]{1,0:T(8,128)(2,1)S(1)}, u32[]{:S(2)}, u32[]{:S(2)}) collective-permute-start(bf16[144,512]{1,0:T(8,128)(2,1)} %attend.1), channel_id=1, source_target_pairs={{0,256},{256,0},{1,257},{257,1},{2,258},{258,2},{3,259},{259,3},{4... | collective-permute-start | bytes 442376 | tf_op jit(solution)/shard_map/ppermute | solution.py:71
  51.1 8.3 %collective-permute-start.2 = (bf16[256,512]{1,0:T(8,128)(2,1)S(1)}, bf16[256,512]{1,0:T(8,128)(2,1)S(1)}, u32[]{:S(2)}, u32[]{:S(2)}) collective-permute-start(bf16[256,512]{1,0:T(8,128)(2,1)S(1)} %pad_maximum_fusion.refs_0_), channel_id=1, source_target_pairs={{0,1},{1,2},{2,3},{3,4},{4,5},{5,6},{6,7},{7,0},{8,9},{9,10},{10,1... | collective-permute-start | bytes 786440 | tf_op jit(solution)/shard_map/ppermute | solution.py:75
  53.7 8.3 %collective-permute-start.3 = (bf16[256,512]{1,0:T(8,128)(2,1)S(1)}, bf16[256,512]{1,0:T(8,128)(2,1)S(1)}, u32[]{:S(2)}, u32[]{:S(2)}) collective-permute-start(bf16[256,512]{1,0:T(8,128)(2,1)S(1)} %pad_maximum_fusion.refs_0_), channel_id=1, source_target_pairs={{0,7},{1,0},{2,1},{3,2},{4,3},{5,4},{6,5},{7,6},{8,15},{9,8},{10,9... | collective-permute-start | bytes 786440 | tf_op jit(solution)/shard_map/ppermute | solution.py:75
  59.4 9.7 %collective-permute-start.4 = (bf16[256,512]{1,0:T(8,128)(2,1)S(1)}, bf16[256,512]{1,0:T(8,128)(2,1)S(1)}, u32[]{:S(2)}, u32[]{:S(2)}) collective-permute-start(bf16[256,512]{1,0:T(8,128)(2,1)S(1)} %collective-permute-done.2.refs_1_), channel_id=1, source_target_pairs={{0,1},{1,2},{2,3},{3,4},{4,5},{5,6},{6,7},{7,0},{8,9},{9,10},{10,1... | collective-permute-start | bytes 786440 | tf_op jit(solution)/shard_map/ppermute | solution.py:75
  62.0 9.1 %collective-permute-start.5 = (bf16[256,512]{1,0:T(8,128)(2,1)S(1)}, bf16[256,512]{1,0:T(8,128)(2,1)S(1)}, u32[]{:S(2)}, u32[]{:S(2)}) collective-permute-start(bf16[256,512]{1,0:T(8,128)(2,1)S(1)} %collective-permute-done.3.refs_2_), channel_id=1, source_target_pairs={{0,7},{1,0},{2,1},{3,2},{4,3},{5,4},{6,5},{7,6},{8,15},{9,8},{10,9... | collective-permute-start | bytes 786440 | tf_op jit(solution)/shard_map/ppermute | solution.py:75
  69.1 9.5 %collective-permute-start.6 = (bf16[256,512]{1,0:T(8,128)(2,1)S(1)}, bf16[256,512]{1,0:T(8,128)(2,1)S(1)}, u32[]{:S(2)}, u32[]{:S(2)}) collective-permute-start(bf16[256,512]{1,0:T(8,128)(2,1)S(1)} %collective-permute-done.4.refs_3_), channel_id=1, source_target_pairs={{0,1},{1,2},{2,3},{3,4},{4,5},{5,6},{6,7},{7,0},{8,9},{9,10},{10,1... | collective-permute-start | bytes 786440 | tf_op jit(solution)/shard_map/ppermute | solution.py:75
  71.0 9.5 %collective-permute-start.7 = (bf16[256,512]{1,0:T(8,128)(2,1)S(1)}, bf16[256,512]{1,0:T(8,128)(2,1)S(1)}, u32[]{:S(2)}, u32[]{:S(2)}) collective-permute-start(bf16[256,512]{1,0:T(8,128)(2,1)S(1)} %collective-permute-done.5.refs_4_), channel_id=1, source_target_pairs={{0,7},{1,0},{2,1},{3,2},{4,3},{5,4},{6,5},{7,6},{8,15},{9,8},{10,9... | collective-permute-start | bytes 786440 | tf_op jit(solution)/shard_map/ppermute | solution.py:75
  78.6 15.8 %collective-permute-start.8 = (bf16[128,512]{1,0:T(8,128)(2,1)S(1)}, bf16[128,512]{1,0:T(8,128)(2,1)S(1)}, u32[]{:S(2)}, u32[]{:S(2)}) collective-permute-start(bf16[128,512]{1,0:T(8,128)(2,1)S(1)} %slice.30), channel_id=1, source_target_pairs={{0,1},{1,2},{2,3},{3,4},{4,5},{5,6},{6,7},{7,0},{8,9},{9,10},{10,1... | collective-permute-start | bytes 393224 | tf_op jit(solution)/shard_map/ppermute | solution.py:75
  81.2 13.2 %collective-permute-start.9 = (bf16[128,512]{1,0:T(8,128)(2,1)}, bf16[128,512]{1,0:T(8,128)(2,1)S(1)}, u32[]{:S(2)}, u32[]{:S(2)}) collective-permute-start(bf16[128,512]{1,0:T(8,128)(2,1)} %slice.31), channel_id=1, source_target_pairs={{0,7},{1,0},{2,1},{3,2},{4,3},{5,4},{6,5},{7,6},{8,15},{9,8},{10,9... | collective-permute-start | bytes 393224 | tf_op jit(solution)/shard_map/ppermute | solution.py:75
  97.2 9.1 %collective-permute-start.10 = (bf16[256,256]{1,0:T(8,128)(2,1)S(1)}, bf16[256,256]{1,0:T(8,128)(2,1)S(1)}, u32[]{:S(2)}, u32[]{:S(2)}) collective-permute-start(bf16[256,256]{1,0:T(8,128)(2,1)S(1)} %get-tuple-element.22), channel_id=1, source_target_pairs={{0,8},{8,0},{1,9},{9,1},{2,10},{10,2},{3,11},{11,3},{4,12},{12,4},... | collective-permute-start | bytes 393224 | tf_op jit(solution)/shard_map/ppermute | solution.py:71
  132.5 7.9 %collective-permute-start.11 = (bf16[128,896]{1,0:T(8,128)(2,1)S(1)}, bf16[128,896]{1,0:T(8,128)(2,1)S(1)}, u32[]{:S(2)}, u32[]{:S(2)}) collective-permute-start(bf16[128,896]{1,0:T(8,128)(2,1)S(1)} %get-tuple-element.27), channel_id=1, source_target_pairs={{0,256},{256,0},{1,257},{257,1},{2,258},{258,2},{3,259},{259,3},{4... | collective-permute-start | bytes 688136 | tf_op jit(solution)/shard_map/ppermute | solution.py:71
  144.0 25.7 %all-to-all-start.2 = ((bf16[32,8,1280]{2,1,0:T(8,128)(2,1)}), bf16[32,8,1280]{2,1,0:T(8,128)(2,1)S(1)}, u32[]{:S(2)}, u32[]{:S(2)}) async-start(bf16[32,8,1280]{2,1,0:T(8,128)(2,1)} %bitcast.13), calls=%async_computation.2 | async-start | bytes 1310720 | tf_op jit(solution)/shard_map/all_to_all | solution.py:427
Sparse Core Ops, SparseCore 0:
  43.9 50.3 all-gather.1

commit v6 on v5

--- a/solution.py
+++ b/solution.py
@@ -10,7 +10,7 @@
 TENSOR = ("xh", "z")
 PAIR_TENSOR = ("xl",) + TENSOR
 RING = 8
-STEPS = (0, -1, 1, -2, 2, -3, 3)
+STEPS = (0, -1, 1, -2, 2, -3, 3, 4)
 SLAB = 128
 HALF = 2048
 QUARTER = 1024
@@ -23,6 +23,7 @@
 BLOCKS = 16
 ROWS = 8
 TABLE = 16
+SPARE = 80
 VMEM_BYTES = 48 * 1024 * 1024
 ALL_VMEM_BYTES = 63400000
 F32, BF16 = jnp.float32, jnp.bfloat16
@@ -93,30 +94,27 @@
     )(*operands)
 
 
-def pack_weights_kernel(gate_ref, up_ref, down_ref, swapped_ref, packed_ref, sems):
-    pieces = [(gate_ref, HIDDEN), (up_ref, HIDDEN)] + [
-        (ref.at[pl.ds(j * 128, 128)], 128)
-        for ref in (down_ref, swapped_ref)
-        for j in range(ref.shape[0] // 128)
-    ]
-    copies, at = [], 0
-    for i, (piece, lanes) in enumerate(pieces):
-        copies.append(pltpu.make_async_copy(piece, packed_ref.at[:, pl.ds(at, lanes)], sems.at[i]))
-        at += lanes
-    for copy in copies:
-        copy.start()
-    for copy in copies:
-        copy.wait()
-
-
-def project_kernel(place_ref, hidden_ref, *refs):
-    contexts, (weights_hbm, keep_ref, send_ref, weights, sems) = refs[:9], refs[9:]
-    xl, xh, z = place_ref[0], place_ref[3], place_ref[4]
+def pack_weights_kernel(gate_ref, up_ref, swapped_ref, packed_ref):
+    packed_ref[:, :HIDDEN] = gate_ref[...]
+    packed_ref[:, HIDDEN : 2 * HIDDEN] = up_ref[...]
+    for j in range(HEADS_WIDE // 128):
+        at = 2 * HIDDEN + j * 128
+        packed_ref[:, at : at + 128] = swapped_ref[j * 128 : (j + 1) * 128, :]
+
+
+def pack_down_kernel(down_ref, packed_ref):
+    for j in range(HIDDEN // 128):
+        packed_ref[:, j * 128 : (j + 1) * 128] = down_ref[j * 128 : (j + 1) * 128, :]
+
+
+def project_kernel(place_ref, *refs):
+    contexts, (weights_hbm, keep_ref, send_ref, weights, sems) = refs[:RING], refs[RING:]
+    z = place_ref[4]
 
     def copy(k):
         at = pl.ds(k * 2 * 128, 2 * 128)
         return pltpu.make_async_copy(
-            weights_hbm.at[at, pl.ds(3 * HIDDEN, HEADS_WIDE)], weights.at[at], sems.at[k]
+            weights_hbm.at[at, pl.ds(2 * HIDDEN, HEADS_WIDE)], weights.at[at], sems.at[k]
         )
 
     for k in range(RING):
@@ -125,11 +123,8 @@
         copy(k).wait()
     total = jnp.zeros((2 * SLAB, COLS), F32)
     for k in range(RING):
-        if k < len(STEPS):
-            step, context = STEPS[k], contexts[k][...]
-        else:
-            step, context = 4, jnp.concatenate([contexts[k][...], contexts[k + 1][...]])
-        first = pl.multiple_of(((z + (step + RING)) & (RING - 1)) * 256, 256)
+        context = contexts[k][...]
+        first = pl.multiple_of(((z + (STEPS[k] + RING + RING // 2)) & (RING - 1)) * 256, 256)
         for half in range(2):
             lanes = slice(half * 256, half * 256 + 256)
             block = weights[pl.ds(first, 256), lanes]
@@ -140,18 +135,11 @@
                 ]
             )
             total += jnp.dot(context[:, lanes], rhs, preferred_element_type=F32)
-    hidden = hidden_ref[...].astype(F32)
-    rows = SLAB // 2
-    own = jnp.where(xl == 0, hidden[:rows], hidden[rows:])
-    other = jnp.where(xl == 0, hidden[rows:], hidden[:rows])
-    total += jnp.concatenate(
-        [jnp.where(xh == at, block, 0.0) for block in (own, other) for at in range(2)]
-    )
     keep_ref[...] = total
     send_ref[...] = total.astype(BF16)
 
 
-def residual_kernel(place_ref, keep_ref, recv_ref, pickers_ref, residual_ref, rows_ref):
+def residual_kernel(place_ref, keep_ref, recv_ref, hidden_ref, pickers_ref, residual_ref, rows_ref):
     xl, xh = place_ref[0], place_ref[3]
     summed = keep_ref[...] + recv_ref[...].astype(F32)
     own, other = summed[:SLAB], summed[SLAB:]
@@ -159,7 +147,7 @@
     held = jnp.zeros((SLAB, COLS), F32)
     for slab in range(2):
         at = slice(slab * SLAB, (slab + 1) * SLAB)
-        residual = jnp.where(xl == slab, own, other).astype(BF16)
+        residual = (jnp.where(xl == slab, own, other) + hidden_ref[at, :].astype(F32)).astype(BF16)
         held = jnp.where(xh == slab, residual.astype(F32), held)
         picked = jnp.dot(pickers_ref[at, :], residual, preferred_element_type=F32).astype(BF16)
         for f in range(FLIGHT // 2):
@@ -204,7 +192,7 @@
 
 
 def down_kernel(place_ref, own_ref, recv_ref, residual_ref, weights_hbm, out_ref, weights, sem):
-    copy = pltpu.make_async_copy(weights_hbm.at[:, pl.ds(2 * HIDDEN, HIDDEN)], weights, sem)
+    copy = pltpu.make_async_copy(weights_hbm, weights, sem)
     copy.start()
     xh = place_ref[3]
     slots = 2 * BLOCKS * CAP
@@ -294,15 +282,10 @@
     place = jnp.stack([lax.axis_index(a) for a in DP + TENSOR]).astype(jnp.int32)
 
     swapped = lax.ppermute(
-        out_weight, ("y", "z"), [(a * RING + b, b * RING + a) for a in range(RING) for b in range(RING)]
-    )
-    hidden_in = lax.all_to_all(
-        hidden_rows.reshape(ROWS, BLOCKS, COLS).transpose(1, 0, 2),
-        ("xl", "z"),
-        split_axis=0,
-        concat_axis=0,
-        tiled=True,
-    ).reshape(SLAB, COLS)
+        jnp.pad(out_weight, ((0, SPARE), (0, 0))),
+        ("y", "z"),
+        [(a * RING + b, (b + RING // 2) % RING * RING + a) for a in range(RING) for b in range(RING)],
+    )
     (extended,) = kernel_call(
         attend_kernel,
         [((SLAB + TABLE, HEADS_WIDE), BF16)],
@@ -320,26 +303,38 @@
         ],
         vmem=ALL_VMEM_BYTES,
     )
-    swapped, hidden_in, _ = lax.optimization_barrier((swapped, hidden_in, extended))
+    other = swap(extended, "xl")
+    swapped, _ = lax.optimization_barrier((swapped, other))
     (packed,) = kernel_call(
         pack_weights_kernel,
-        [((128, 3 * HIDDEN + HEADS_WIDE), BF16)],
-        (gate_weight, up_weight, down_weight, swapped),
-        "hhhh",
+        [((128, 2 * HIDDEN + HEADS_WIDE), BF16)],
+        (gate_weight, up_weight, swapped),
+        "vvv",
         0,
-        4 * 128 * 1664,
+        4 * 128 * 1280,
         "pack_weights",
-        [pltpu.SemaphoreType.DMA((2 + HIDDEN // 128 + HEADS_WIDE // 128,))],
-        "h",
-        ALL_VMEM_BYTES,
     )
     weights = lax.all_gather(packed, ("y", "core"), axis=0, tiled=True)
-    other = swap(extended, "xl")
+    (packed_down,) = kernel_call(
+        pack_down_kernel, [((128, HIDDEN), BF16)], (down_weight,), "v", 0, 4 * 128 * 384, "pack_down"
+    )
+    packed_down, _ = lax.optimization_barrier((packed_down, packed))
+    down_weights = lax.all_gather(packed_down, ("y", "core"), axis=0, tiled=True)
     both = jnp.concatenate([extended[:SLAB], other[:SLAB]])
     up1, down1 = along_z(both, 1), along_z(both, -1)
     up2, down2 = along_z(up1, 1), along_z(down1, -1)
     up3, down3 = along_z(up2, 1), along_z(down2, -1)
-    up4, down4 = along_z(up3[:SLAB], 1), along_z(down3[SLAB:], -1)
+    up4 = along_z(up3, 1)
+
+    hidden_later, _, _ = lax.optimization_barrier((hidden_rows, up4, down3))
+    columns = hidden_later.reshape(ROWS, 2, 1, RING, COLS).transpose(1, 2, 3, 0, 4)
+    hidden_in = lax.all_to_all(
+        jnp.broadcast_to(columns, (2, 2, RING, ROWS, COLS)).reshape(2 * BLOCKS, ROWS, COLS),
+        PAIR_TENSOR,
+        split_axis=0,
+        concat_axis=0,
+        tiled=True,
+    ).reshape(2 * SLAB, COLS)
 
     matches = route_ids[:, None, :] == flight_experts[None, :, None]
     hits = jnp.sum(matches.astype(jnp.int32), axis=2, dtype=jnp.int32)
@@ -385,8 +380,8 @@
     keep, send = kernel_call(
         project_kernel,
         [((2 * SLAB, COLS), F32), ((2 * SLAB, COLS), BF16)],
-        (place, hidden_in, both, up1, down1, up2, down2, up3, down3, up4, down4, weights),
-        "s" + "v" * 10 + "h",
+        (place, both, up1, down1, up2, down2, up3, down3, up4, weights),
+        "s" + "v" * RING + "h",
         2 * 256 * 4096 * 256,
         2 * 2048 * 1024,
         "project",
@@ -395,8 +390,8 @@
     residual, rows_out = kernel_call(
         residual_kernel,
         [((SLAB, COLS), BF16), ((RING * 2 * BLOCKS * CAP, COLS), BF16)],
-        (place, keep, swap(send, "xh"), pickers),
-        "svvv",
+        (place, keep, swap(send, "xh"), hidden_in, pickers),
+        "svvvv",
         2 * 256 * 128 * 256,
         1 << 20,
         "residual",
@@ -417,7 +412,7 @@
     (outward,) = kernel_call(
         down_kernel,
         [((4 * BLOCKS * CAP, QUARTER + COLS), BF16)],
-        (place, own, swap(part, "xl"), residual, weights),
+        (place, own, swap(part, "xl"), residual, down_weights),
         "svvvh",
         2 * 256 * 384 * 2048,
         2 << 20,

time: 179 us -> 168 us (0.939)
  the two profiles are of different devices: /device:TPU:64 before, /device:TPU:24 now
where the time goes in v6:
time: 168 us; the launch traced here: 167 us
  starting transfers between devices  63.3 us (38%)
  waiting for transfers between devices  42.4 us (25%)
  blocking collectives  20.1 us (12%)
  Pallas kernels  15.6 us (9%)
  between operations  14.3 us (9%)
  local copies, waits for them, and re-layouts  9.38 us (6%)
  other arithmetic  2.28 us (1%)
    ppermute x7, starting transfers between devices, along_z(): lax.ppermute(block, 'z', [(i, (i + step) % RING) for i in range(RING)])  23.9 us
    all_to_all x1, waiting for transfers between devices, per_device(): lax.all_to_all(outward.reshape(2 * BLOCKS, 2 * CAP, QUARTER + COLS), PAIR...  20.4 us
    all_to_all x1, blocking collectives, per_device(): lax.all_to_all(rows_out.reshape(RING, 2 * BLOCKS * CAP, COLS), 'z', split...  20.1 us
    pallas_call x8, Pallas kernels, kernel_call(): pl.pallas_call(body, out_shape=[jax.ShapeDtypeStruct(shape, dtype) for sh...  15.6 us
    all_to_all x1, starting transfers between devices, per_device(): lax.all_to_all(jnp.broadcast_to(columns, (2, 2, RING, ROWS, COLS)).reshap...  12.6 us
    ppermute x3, starting transfers between devices, swap(): return lax.ppermute(block, axis, [(0, 1), (1, 0)])  12 us
    ppermute x3, waiting for transfers between devices, swap(): return lax.ppermute(block, axis, [(0, 1), (1, 0)])  10.6 us
    ppermute x7, waiting for transfers between devices, along_z(): lax.ppermute(block, 'z', [(i, (i + step) % RING) for i in range(RING)])  10.3 us
  transfers between devices with their start and end apart: 15, of which 12 were waited for; matrix products, arithmetic and copies ran while one was open for 4% of the time, Pallas kernels for 6%

profile of v6, /device:TPU:24, one launch (start us, length us, event | category | flops | bytes accessed | tf_op | source)
XLA Modules:
  0.0 167.4 jit_solution(12488238772229260867)
XLA Ops:
  6.5 0.9 pad.4
  7.5 10.1 %collective-permute-start = (bf16[592,128]{1,0:T(8,128)(2,1)S(1)}, bf16[592,128]{1,0:T(8,128)(2,1)S(1)}, u32[]{:S(2)}, u32[]{:S(2)}) collective-permute-start(bf16[592,128]{1,0:T(8,128)(2,1)S(1)} %pad.4), channel_id=1, source_target_pairs={{0,128},{1,160},{2,192},{3,224},{4,0},{5,32},{6,64},{7,96},{32,129... | collective-permute-start | bytes 454664 | tf_op jit(solution)/shard_map/ppermute | solution.py:284
  18.3 4.0 %attend.1 = bf16[144,512]{1,0:T(8,128)(2,1)} custom-call(s32[1]{0:T(128)S(6)} %copy.20.start_ref, s32[4]{0:T(128)} %flight_ref.1, s32[8,128]{1,0:T(8,128)} %bitcast.30, bf16[128,512]{1,0:T(8,128)(2,1)} %queries_hbm.1, bf16[1152,128]{1,0:T(8,128)(2,1)} %keys_hbm.1, bf16[1152,128]{1,0:T(8,128)(2,1)} %values_hbm.1), custom_call_target="tpu_custom_call" | custom-call | flops 301989888 | bytes 1048576 | tf_op jit(solution)/shard_map/attend/pallas_call | solution.py:85
  22.2 3.4 %collective-permute-start.1 = (bf16[144,512]{1,0:T(8,128)(2,1)}, bf16[144,512]{1,0:T(8,128)(2,1)S(1)}, u32[]{:S(2)}, u32[]{:S(2)}) collective-permute-start(bf16[144,512]{1,0:T(8,128)(2,1)} %attend.1), channel_id=1, source_target_pairs={{0,256},{256,0},{1,257},{257,1},{2,258},{258,2},{3,259},{259,3},{4... | collective-permute-start | bytes 442376 | tf_op jit(solution)/shard_map/ppermute | solution.py:72
  25.7 4.0 %collective-permute-done.1 = bf16[144,512]{1,0:T(8,128)(2,1)S(1)} collective-permute-done((bf16[144,512]{1,0:T(8,128)(2,1)}, bf16[144,512]{1,0:T(8,128)(2,1)S(1)}, u32[]{:S(2)}, u32[]{:S(2)}) %collective-permute-start.1) | collective-permute-done | bytes 147488 | tf_op jit(solution)/shard_map/ppermute | solution.py:72
  32.3 0.9 slice.20
  34.5 2.6 %collective-permute-start.2 = (bf16[256,512]{1,0:T(8,128)(2,1)S(1)}, bf16[256,512]{1,0:T(8,128)(2,1)S(1)}, u32[]{:S(2)}, u32[]{:S(2)}) collective-permute-start(bf16[256,512]{1,0:T(8,128)(2,1)S(1)} %pad_maximum_fusion.refs_0_), channel_id=1, source_target_pairs={{0,1},{1,2},{2,3},{3,4},{4,5},{5,6},{6,7},{7,0},{8,9},{9,10},{10,1... | collective-permute-start | bytes 786440 | tf_op jit(solution)/shard_map/ppermute | solution.py:76
  39.5 4.5 %collective-permute-start.3 = (bf16[256,512]{1,0:T(8,128)(2,1)S(1)}, bf16[256,512]{1,0:T(8,128)(2,1)S(1)}, u32[]{:S(2)}, u32[]{:S(2)}) collective-permute-start(bf16[256,512]{1,0:T(8,128)(2,1)S(1)} %pad_maximum_fusion.refs_0_), channel_id=1, source_target_pairs={{0,7},{1,0},{2,1},{3,2},{4,3},{5,4},{6,5},{7,6},{8,15},{9,8},{10,9... | collective-permute-start | bytes 786440 | tf_op jit(solution)/shard_map/ppermute | solution.py:76
  44.5 1.9 %collective-permute-start.4 = (bf16[256,512]{1,0:T(8,128)(2,1)S(1)}, bf16[256,512]{1,0:T(8,128)(2,1)S(1)}, u32[]{:S(2)}, u32[]{:S(2)}) collective-permute-start(bf16[256,512]{1,0:T(8,128)(2,1)S(1)} %collective-permute-done.2.refs_1_), channel_id=1, source_target_pairs={{0,1},{1,2},{2,3},{3,4},{4,5},{5,6},{6,7},{7,0},{8,9},{9,10},{10,1... | collective-permute-start | bytes 786440 | tf_op jit(solution)/shard_map/ppermute | solution.py:76
  47.2 1.5 collective-permute-done.3.refs_2_
  48.8 4.9 %collective-permute-start.5 = (bf16[256,512]{1,0:T(8,128)(2,1)S(1)}, bf16[256,512]{1,0:T(8,128)(2,1)S(1)}, u32[]{:S(2)}, u32[]{:S(2)}) collective-permute-start(bf16[256,512]{1,0:T(8,128)(2,1)S(1)} %collective-permute-done.3.refs_2_), channel_id=1, source_target_pairs={{0,7},{1,0},{2,1},{3,2},{4,3},{5,4},{6,5},{7,6},{8,15},{9,8},{10,9... | collective-permute-start | bytes 786440 | tf_op jit(solution)/shard_map/ppermute | solution.py:76
  54.0 1.9 %collective-permute-start.6 = (bf16[256,512]{1,0:T(8,128)(2,1)S(1)}, bf16[256,512]{1,0:T(8,128)(2,1)S(1)}, u32[]{:S(2)}, u32[]{:S(2)}) collective-permute-start(bf16[256,512]{1,0:T(8,128)(2,1)S(1)} %collective-permute-done.4.refs_3_), channel_id=1, source_target_pairs={{0,1},{1,2},{2,3},{3,4},{4,5},{5,6},{6,7},{7,0},{8,9},{9,10},{10,1... | collective-permute-start | bytes 786440 | tf_op jit(solution)/shard_map/ppermute | solution.py:76
  56.7 1.1 collective-permute-done.5.refs_4_
  57.7 5.4 %collective-permute-start.7 = (bf16[256,512]{1,0:T(8,128)(2,1)S(1)}, bf16[256,512]{1,0:T(8,128)(2,1)S(1)}, u32[]{:S(2)}, u32[]{:S(2)}) collective-permute-start(bf16[256,512]{1,0:T(8,128)(2,1)S(1)} %collective-permute-done.5.refs_4_), channel_id=1, source_target_pairs={{0,7},{1,0},{2,1},{3,2},{4,3},{5,4},{6,5},{7,6},{8,15},{9,8},{10,9... | collective-permute-start | bytes 786440 | tf_op jit(solution)/shard_map/ppermute | solution.py:76
  63.4 2.7 %collective-permute-start.8 = (bf16[256,512]{1,0:T(8,128)(2,1)S(1)}, bf16[256,512]{1,0:T(8,128)(2,1)S(1)}, u32[]{:S(2)}, u32[]{:S(2)}) collective-permute-start(bf16[256,512]{1,0:T(8,128)(2,1)S(1)} %collective-permute-done.6.refs_5_), channel_id=1, source_target_pairs={{0,1},{1,2},{2,3},{3,4},{4,5},{5,6},{6,7},{7,0},{8,9},{9,10},{10,1... | collective-permute-start | bytes 786440 | tf_op jit(solution)/shard_map/ppermute | solution.py:76
  66.2 2.3 %collective-permute-done.7.refs_6_ = bf16[256,512]{1,0:T(8,128)(2,1)S(1)} collective-permute-done((bf16[256,512]{1,0:T(8,128)(2,1)S(1)}, bf16[256,512]{1,0:T(8,128)(2,1)S(1)}, u32[]{:S(2)}, u32[]{:S(2)}) %collective-permute-start.7) | collective-permute-done | bytes 262176 | tf_op jit(solution)/shard_map/ppermute | solution.py:76
  68.5 4.3 %collective-permute-done.8.refs_7_ = bf16[256,512]{1,0:T(8,128)(2,1)S(1)} collective-permute-done((bf16[256,512]{1,0:T(8,128)(2,1)S(1)}, bf16[256,512]{1,0:T(8,128)(2,1)S(1)}, u32[]{:S(2)}, u32[]{:S(2)}) %collective-permute-start.8) | collective-permute-done | bytes 262176 | tf_op jit(solution)/shard_map/ppermute | solution.py:76
  73.5 12.6 %all-to-all-start = ((bf16[32,8,256]{2,1,0:T(8,128)(2,1)}), bf16[32,8,256]{2,1,0:T(8,128)(2,1)S(1)}, u32[]{:S(2)}, u32[]{:S(2)}) async-start(bf16[32,8,256]{2,1,0:T(8,128)(2,1)} %bitcast.11), calls=%async_computation | async-start | bytes 262144 | tf_op jit(solution)/shard_map/all_to_all | solution.py:331
  86.3 1.1 mul.70.pickers_ref
  87.5 2.9 %project.1 = (f32[256,256]{1,0:T(8,128)S(1)}, bf16[256,256]{1,0:T(8,128)(2,1)S(1)}) custom-call(s32[5]{0:T(128)S(1)} %stack.37.place_ref, bf16[256,512]{1,0:T(8,128)(2,1)S(1)} %pad_maximum_fusion.refs_0_, bf16[256,512]{1,0:T(8,128)(2,1)S(1)} %collective-permute-done.2.refs_1_, bf16[256,512]{1,0:T(8,128)(2,1)S(1)} %collective-permute-done.3.refs_2_, ...), custom_call_target="tpu_custom_call" | custom-call | flops 536870912 | bytes 4194304 | tf_op jit(solution)/shard_map/project/pallas_call | solution.py:85
  90.4 5.2 %collective-permute-start.9 = (bf16[256,256]{1,0:T(8,128)(2,1)S(1)}, bf16[256,256]{1,0:T(8,128)(2,1)S(1)}, u32[]{:S(2)}, u32[]{:S(2)}) collective-permute-start(bf16[256,256]{1,0:T(8,128)(2,1)S(1)} %get-tuple-element.22), channel_id=1, source_target_pairs={{0,8},{8,0},{1,9},{9,1},{2,10},{10,2},{3,11},{11,3},{4,12},{12,4},... | collective-permute-start | bytes 393224 | tf_op jit(solution)/shard_map/ppermute | solution.py:72
  95.6 1.1 all-to-all-done
  96.6 2.1 %collective-permute-done.9.recv_ref = bf16[256,256]{1,0:T(8,128)(2,1)S(1)} collective-permute-done((bf16[256,256]{1,0:T(8,128)(2,1)S(1)}, bf16[256,256]{1,0:T(8,128)(2,1)S(1)}, u32[]{:S(2)}, u32[]{:S(2)}) %collective-permute-start.9) | collective-permute-done | bytes 131104 | tf_op jit(solution)/shard_map/ppermute | solution.py:72
  99.5 20.1 %all_to_all.15 = bf16[8,128,256]{2,1,0:T(8,128)(2,1)S(1)} all-to-all(bf16[8,128,256]{2,1,0:T(8,128)(2,1)S(1)} %bitcast.27), channel_id=1, replica_groups=mesh['xl'=2,'y'=8,'core'=2,'xh'=2,'z'=8] {'z'}, dimensions={0} | all-to-all | bytes 1048576 | tf_op jit(solution)/shard_map/all_to_all | solution.py:399
  119.6 2.3 %gate_up.1 = (f32[128,896]{1,0:T(8,128)S(1)}, bf16[128,896]{1,0:T(8,128)(2,1)S(1)}) custom-call(bf16[1024,256]{1,0:T(8,128)(2,1)S(1)} %bitcast.26, bf16[1,2048]{1,0:T(2,128)(2,1)S(1)} %reshape.108.gain_ref, bf16[2048,1280]{1,0:T(8,128)(2,1)} %all-gather.3.cloned.1.call-done.refs_8_.weights_hbm), custom_call_target="tpu_custom_call" | custom-call | flops 402653184 | bytes 3145728 | tf_op jit(solution)/shard_map/gate_up/pallas_call | solution.py:85
  121.9 3.4 %collective-permute-start.10 = (bf16[128,896]{1,0:T(8,128)(2,1)S(1)}, bf16[128,896]{1,0:T(8,128)(2,1)S(1)}, u32[]{:S(2)}, u32[]{:S(2)}) collective-permute-start(bf16[128,896]{1,0:T(8,128)(2,1)S(1)} %get-tuple-element.28), channel_id=1, source_target_pairs={{0,256},{256,0},{1,257},{257,1},{2,258},{258,2},{3,259},{259,3},{4... | collective-permute-start | bytes 688136 | tf_op jit(solution)/shard_map/ppermute | solution.py:72
  125.3 4.5 %collective-permute-done.10.recv_ref = bf16[128,896]{1,0:T(8,128)(2,1)S(1)} collective-permute-done((bf16[128,896]{1,0:T(8,128)(2,1)S(1)}, bf16[128,896]{1,0:T(8,128)(2,1)S(1)}, u32[]{:S(2)}, u32[]{:S(2)}) %collective-permute-start.10) | collective-permute-done | bytes 229408 | tf_op jit(solution)/shard_map/ppermute | solution.py:72
  129.8 1.4 copy-done
  131.2 2.6 %down.1 = bf16[256,1280]{1,0:T(8,128)(2,1)} custom-call(s32[5]{0:T(128)S(1)} %stack.37.place_ref, f32[128,896]{1,0:T(8,128)S(1)} %get-tuple-element.27.own_ref, bf16[128,896]{1,0:T(8,128)(2,1)S(1)} %collective-permute-done.10.recv_ref, bf16[128,256]{1,0:T(8,128)(2,1)S(1)} %get-tuple-element.29.residual_ref, bf16[2048,384]{1,0:T(8,128)(2,1)S(1)} %copy-done), custom_call_target="tpu_custom_call" | custom-call | flops 402653184 | bytes 2097152 | tf_op jit(solution)/shard_map/down/pallas_call | solution.py:85
  133.9 4.7 %all-to-all-start.2 = ((bf16[32,8,1280]{2,1,0:T(8,128)(2,1)}), bf16[32,8,1280]{2,1,0:T(8,128)(2,1)S(1)}, u32[]{:S(2)}, u32[]{:S(2)}) async-start(bf16[32,8,1280]{2,1,0:T(8,128)(2,1)} %bitcast.15), calls=%async_computation.2 | async-start | bytes 1310720 | tf_op jit(solution)/shard_map/all_to_all | solution.py:422
  138.6 20.4 %all-to-all-done.2 = bf16[32,8,1280]{2,1,0:T(8,128)(2,1)S(1)} async-done(((bf16[32,8,1280]{2,1,0:T(8,128)(2,1)}), bf16[32,8,1280]{2,1,0:T(8,128)(2,1)S(1)}, u32[]{:S(2)}, u32[]{:S(2)}) %all-to-all-start.2) | async-done | bytes 655392 | tf_op jit(solution)/shard_map/all_to_all | solution.py:422
  159.0 1.6 combine.1
  (52 shorter events, 10.7 us)
Async XLA Ops:
  6.5 40.6 %copy-start.5 = (bf16[4096]{0:T(1024)(128)(2,1)S(1)}, bf16[4096]{0:T(1024)(128)(2,1)}, u32[]{:S(2)}) copy-start(bf16[4096]{0:T(1024)(128)(2,1)} %param.19) | copy-start | bytes 24580
  6.5 66.3 %copy-start.4 = (bf16[8,4096]{1,0:T(8,128)(2,1)S(1)}, bf16[8,4096]{1,0:T(8,128)(2,1)}, u32[]{:S(2)}) copy-start(bf16[8,4096]{1,0:T(8,128)(2,1)} %param.13) | copy-start | bytes 196612
  6.5 81.0 %all-gather.3.cloned.1.call-start = ((), (), s32[]{:S(2)}) async-start(), calls=%async_computation.3 | async-start | bytes 5570560 | tf_op jit(solution)/shard_map/all_gather | solution.py:317
  7.5 22.2 %collective-permute-start = (bf16[592,128]{1,0:T(8,128)(2,1)S(1)}, bf16[592,128]{1,0:T(8,128)(2,1)S(1)}, u32[]{:S(2)}, u32[]{:S(2)}) collective-permute-start(bf16[592,128]{1,0:T(8,128)(2,1)S(1)} %pad.4), channel_id=1, source_target_pairs={{0,128},{1,160},{2,192},{3,224},{4,0},{5,32},{6,64},{7,96},{32,129... | collective-permute-start | bytes 454664 | tf_op jit(solution)/shard_map/ppermute | solution.py:284
  22.2 7.4 %collective-permute-start.1 = (bf16[144,512]{1,0:T(8,128)(2,1)}, bf16[144,512]{1,0:T(8,128)(2,1)S(1)}, u32[]{:S(2)}, u32[]{:S(2)}) collective-permute-start(bf16[144,512]{1,0:T(8,128)(2,1)} %attend.1), channel_id=1, source_target_pairs={{0,256},{256,0},{1,257},{257,1},{2,258},{258,2},{3,259},{259,3},{4... | collective-permute-start | bytes 442376 | tf_op jit(solution)/shard_map/ppermute | solution.py:72
  29.7 0.9 copy-start.2
  30.6 0.9 copy-start.3
  32.3 93.1 %all-gather.5.cloned.1.call-start = ((), (), s32[]{:S(2)}) async-start(), calls=%async_computation.4 | async-start | bytes 1671168 | tf_op jit(solution)/shard_map/all_gather | solution.py:322
  34.5 10.0 %collective-permute-start.2 = (bf16[256,512]{1,0:T(8,128)(2,1)S(1)}, bf16[256,512]{1,0:T(8,128)(2,1)S(1)}, u32[]{:S(2)}, u32[]{:S(2)}) collective-permute-start(bf16[256,512]{1,0:T(8,128)(2,1)S(1)} %pad_maximum_fusion.refs_0_), channel_id=1, source_target_pairs={{0,1},{1,2},{2,3},{3,4},{4,5},{5,6},{6,7},{7,0},{8,9},{9,10},{10,1... | collective-permute-start | bytes 786440 | tf_op jit(solution)/shard_map/ppermute | solution.py:76
  37.2 0.9 copy-start.1
  39.5 9.2 %collective-permute-start.3 = (bf16[256,512]{1,0:T(8,128)(2,1)S(1)}, bf16[256,512]{1,0:T(8,128)(2,1)S(1)}, u32[]{:S(2)}, u32[]{:S(2)}) collective-permute-start(bf16[256,512]{1,0:T(8,128)(2,1)S(1)} %pad_maximum_fusion.refs_0_), channel_id=1, source_target_pairs={{0,7},{1,0},{2,1},{3,2},{4,3},{5,4},{6,5},{7,6},{8,15},{9,8},{10,9... | collective-permute-start | bytes 786440 | tf_op jit(solution)/shard_map/ppermute | solution.py:76
  44.5 9.5 %collective-permute-start.4 = (bf16[256,512]{1,0:T(8,128)(2,1)S(1)}, bf16[256,512]{1,0:T(8,128)(2,1)S(1)}, u32[]{:S(2)}, u32[]{:S(2)}) collective-permute-start(bf16[256,512]{1,0:T(8,128)(2,1)S(1)} %collective-permute-done.2.refs_1_), channel_id=1, source_target_pairs={{0,1},{1,2},{2,3},{3,4},{4,5},{5,6},{6,7},{7,0},{8,9},{9,10},{10,1... | collective-permute-start | bytes 786440 | tf_op jit(solution)/shard_map/ppermute | solution.py:76
  48.8 9.0 %collective-permute-start.5 = (bf16[256,512]{1,0:T(8,128)(2,1)S(1)}, bf16[256,512]{1,0:T(8,128)(2,1)S(1)}, u32[]{:S(2)}, u32[]{:S(2)}) collective-permute-start(bf16[256,512]{1,0:T(8,128)(2,1)S(1)} %collective-permute-done.3.refs_2_), channel_id=1, source_target_pairs={{0,7},{1,0},{2,1},{3,2},{4,3},{5,4},{6,5},{7,6},{8,15},{9,8},{10,9... | collective-permute-start | bytes 786440 | tf_op jit(solution)/shard_map/ppermute | solution.py:76
  54.0 9.5 %collective-permute-start.6 = (bf16[256,512]{1,0:T(8,128)(2,1)S(1)}, bf16[256,512]{1,0:T(8,128)(2,1)S(1)}, u32[]{:S(2)}, u32[]{:S(2)}) collective-permute-start(bf16[256,512]{1,0:T(8,128)(2,1)S(1)} %collective-permute-done.4.refs_3_), channel_id=1, source_target_pairs={{0,1},{1,2},{2,3},{3,4},{4,5},{5,6},{6,7},{7,0},{8,9},{9,10},{10,1... | collective-permute-start | bytes 786440 | tf_op jit(solution)/shard_map/ppermute | solution.py:76
  57.7 10.8 %collective-permute-start.7 = (bf16[256,512]{1,0:T(8,128)(2,1)S(1)}, bf16[256,512]{1,0:T(8,128)(2,1)S(1)}, u32[]{:S(2)}, u32[]{:S(2)}) collective-permute-start(bf16[256,512]{1,0:T(8,128)(2,1)S(1)} %collective-permute-done.5.refs_4_), channel_id=1, source_target_pairs={{0,7},{1,0},{2,1},{3,2},{4,3},{5,4},{6,5},{7,6},{8,15},{9,8},{10,9... | collective-permute-start | bytes 786440 | tf_op jit(solution)/shard_map/ppermute | solution.py:76
  63.4 9.5 %collective-permute-start.8 = (bf16[256,512]{1,0:T(8,128)(2,1)S(1)}, bf16[256,512]{1,0:T(8,128)(2,1)S(1)}, u32[]{:S(2)}, u32[]{:S(2)}) collective-permute-start(bf16[256,512]{1,0:T(8,128)(2,1)S(1)} %collective-permute-done.6.refs_5_), channel_id=1, source_target_pairs={{0,1},{1,2},{2,3},{3,4},{4,5},{5,6},{6,7},{7,0},{8,9},{9,10},{10,1... | collective-permute-start | bytes 786440 | tf_op jit(solution)/shard_map/ppermute | solution.py:76
  73.5 23.1 %all-to-all-start = ((bf16[32,8,256]{2,1,0:T(8,128)(2,1)}), bf16[32,8,256]{2,1,0:T(8,128)(2,1)S(1)}, u32[]{:S(2)}, u32[]{:S(2)}) async-start(bf16[32,8,256]{2,1,0:T(8,128)(2,1)} %bitcast.11), calls=%async_computation | async-start | bytes 262144 | tf_op jit(solution)/shard_map/all_to_all | solution.py:331
  90.4 8.4 %collective-permute-start.9 = (bf16[256,256]{1,0:T(8,128)(2,1)S(1)}, bf16[256,256]{1,0:T(8,128)(2,1)S(1)}, u32[]{:S(2)}, u32[]{:S(2)}) collective-permute-start(bf16[256,256]{1,0:T(8,128)(2,1)S(1)} %get-tuple-element.22), channel_id=1, source_target_pairs={{0,8},{8,0},{1,9},{9,1},{2,10},{10,2},{3,11},{11,3},{4,12},{12,4},... | collective-permute-start | bytes 393224 | tf_op jit(solution)/shard_map/ppermute | solution.py:72
  121.9 7.9 %collective-permute-start.10 = (bf16[128,896]{1,0:T(8,128)(2,1)S(1)}, bf16[128,896]{1,0:T(8,128)(2,1)S(1)}, u32[]{:S(2)}, u32[]{:S(2)}) collective-permute-start(bf16[128,896]{1,0:T(8,128)(2,1)S(1)} %get-tuple-element.28), channel_id=1, source_target_pairs={{0,256},{256,0},{1,257},{257,1},{2,258},{258,2},{3,259},{259,3},{4... | collective-permute-start | bytes 688136 | tf_op jit(solution)/shard_map/ppermute | solution.py:72
  129.8 1.4 copy-start
  133.9 25.1 %all-to-all-start.2 = ((bf16[32,8,1280]{2,1,0:T(8,128)(2,1)}), bf16[32,8,1280]{2,1,0:T(8,128)(2,1)S(1)}, u32[]{:S(2)}, u32[]{:S(2)}) async-start(bf16[32,8,1280]{2,1,0:T(8,128)(2,1)} %bitcast.15), calls=%async_computation.2 | async-start | bytes 1310720 | tf_op jit(solution)/shard_map/all_to_all | solution.py:422
Sparse Core Ops, SparseCore 0:
  32.4 48.2 all-gather.2
  82.8 41.0 all-gather.4

commit v7 on v6

--- a/solution.py
+++ b/solution.py
@@ -22,20 +22,18 @@
 GROUP = 4
 BLOCKS = 16
 ROWS = 8
-TABLE = 16
-SPARE = 80
 VMEM_BYTES = 48 * 1024 * 1024
 ALL_VMEM_BYTES = 63400000
 F32, BF16 = jnp.float32, jnp.bfloat16
 
 
 def attend_kernel(
-    start_ref, flight_ref, ids_hbm, queries_hbm, keys_hbm, values_hbm, out_ref, ids_ref, queries_ref, keys_ref, values_ref, sems
+    start_ref, queries_hbm, keys_hbm, values_hbm, out_ref, queries_ref, keys_ref, values_ref, sems
 ):
     copies = [
         pltpu.make_async_copy(source, target, sems.at[i])
         for i, (source, target) in enumerate(
-            ((keys_hbm, keys_ref), (queries_hbm, queries_ref), (values_hbm, values_ref), (ids_hbm, ids_ref))
+            ((keys_hbm, keys_ref), (queries_hbm, queries_ref), (values_hbm, values_ref))
         )
     ]
     for copy in copies:
@@ -57,15 +55,8 @@
         exp_scores = jnp.exp(scores - jnp.max(scores, axis=1, keepdims=True))
         totals = jnp.sum(exp_scores, axis=1, keepdims=True)
         context = (jnp.dot(exp_scores.astype(BF16), values, preferred_element_type=F32) / totals).astype(BF16)
-        out_ref[:SLAB, first] = context[:SLAB]
-        out_ref[:SLAB, second] = context[SLAB:]
-    line = lax.broadcasted_iota(jnp.int32, (TABLE, SLAB), 0)
-    table = jnp.zeros((TABLE, SLAB), F32)
-    for f in range(FLIGHT):
-        named = jnp.max(jnp.where(ids_ref[...] == flight_ref[f], 1.0, 0.0), axis=0, keepdims=True)
-        table = jnp.where(line == f, named, table)
-    out_ref[SLAB:, :SLAB] = table.astype(BF16)
-    out_ref[SLAB:, SLAB:] = jnp.zeros((TABLE, HEADS_WIDE - SLAB), BF16)
+        out_ref[:, first] = context[:SLAB]
+        out_ref[:, second] = context[SLAB:]
 
 
 def swap(block, axis):
@@ -107,9 +98,36 @@
         packed_ref[:, j * 128 : (j + 1) * 128] = down_ref[j * 128 : (j + 1) * 128, :]
 
 
-def project_kernel(place_ref, *refs):
+def unpack_kernel(place_ref, incoming_ref, hidden_ref, pickers_ref):
+    xh = place_ref[3]
+    shape = (SLAB, 2 * SLAB)
+    to, source = (lax.broadcasted_iota(jnp.int32, shape, d) for d in range(2))
+    taken = jnp.where(source == (to >> 3) * 2 * ROWS + (to & 7), 1.0, 0.0).astype(BF16)
+    hidden_ref[...] = jnp.dot(taken, incoming_ref[...], preferred_element_type=F32).astype(BF16)
+    line = lax.broadcasted_iota(jnp.int32, (2 * ROWS, COLS), 0)
+    hits = []
+    for slab in range(2):
+        rows = incoming_ref[slab * SLAB : slab * SLAB + 2 * ROWS, :].astype(F32)
+        both = jnp.sum(jnp.where(line == ROWS + xh, rows, 0.0), axis=0, keepdims=True)
+        hits += [both[:, :SLAB], both[:, SLAB:]]
+    above, row = (lax.broadcasted_iota(jnp.int32, (SLAB, SLAB), d) for d in range(2))
+    earlier = jnp.where(jnp.logical_and(above >> 3 == row >> 3, above <= row), 1.0, 0.0).astype(BF16)
+    slots = BLOCKS * CAP
+    shape = (slots, SLAB)
+    place, row = (lax.broadcasted_iota(jnp.int32, shape, d) for d in range(2))
+    number = ((place & (CAP - 1)) + 1).astype(F32)
+    for i, hit in enumerate(hits):
+        count = jnp.dot(
+            jnp.broadcast_to(hit, (ROWS, SLAB)).astype(BF16), earlier, preferred_element_type=F32
+        )[:1]
+        count = jnp.where(hit > 0.5, count, 0.0)
+        named = jnp.logical_and(place >> 2 == row >> 3, count == number)
+        pickers_ref[i * slots : (i + 1) * slots, :] = jnp.where(named, 1.0, 0.0).astype(BF16)
+
+
+def project_kernel(place_ref, hidden_ref, *refs):
     contexts, (weights_hbm, keep_ref, send_ref, weights, sems) = refs[:RING], refs[RING:]
-    z = place_ref[4]
+    xl, xh, z = place_ref[0], place_ref[3], place_ref[4]
 
     def copy(k):
         at = pl.ds(k * 2 * 128, 2 * 128)
@@ -124,7 +142,7 @@
     total = jnp.zeros((2 * SLAB, COLS), F32)
     for k in range(RING):
         context = contexts[k][...]
-        first = pl.multiple_of(((z + (STEPS[k] + RING + RING // 2)) & (RING - 1)) * 256, 256)
+        first = pl.multiple_of(((z + (RING + RING // 2 - STEPS[k])) & (RING - 1)) * 256, 256)
         for half in range(2):
             lanes = slice(half * 256, half * 256 + 256)
             block = weights[pl.ds(first, 256), lanes]
@@ -135,11 +153,18 @@
                 ]
             )
             total += jnp.dot(context[:, lanes], rhs, preferred_element_type=F32)
+    hidden = hidden_ref[...].astype(F32)
+    rows = SLAB // 2
+    own = jnp.where(xl == 0, hidden[:rows], hidden[rows:])
+    other = jnp.where(xl == 0, hidden[rows:], hidden[:rows])
+    total += jnp.concatenate(
+        [jnp.where(xh == at, block, 0.0) for block in (own, other) for at in range(2)]
+    )
     keep_ref[...] = total
     send_ref[...] = total.astype(BF16)
 
 
-def residual_kernel(place_ref, keep_ref, recv_ref, hidden_ref, pickers_ref, residual_ref, rows_ref):
+def residual_kernel(place_ref, keep_ref, recv_ref, pickers_ref, residual_ref, rows_ref):
     xl, xh = place_ref[0], place_ref[3]
     summed = keep_ref[...] + recv_ref[...].astype(F32)
     own, other = summed[:SLAB], summed[SLAB:]
@@ -147,7 +172,7 @@
     held = jnp.zeros((SLAB, COLS), F32)
     for slab in range(2):
         at = slice(slab * SLAB, (slab + 1) * SLAB)
-        residual = (jnp.where(xl == slab, own, other) + hidden_ref[at, :].astype(F32)).astype(BF16)
+        residual = jnp.where(xl == slab, own, other).astype(BF16)
         held = jnp.where(xh == slab, residual.astype(F32), held)
         picked = jnp.dot(pickers_ref[at, :], residual, preferred_element_type=F32).astype(BF16)
         for f in range(FLIGHT // 2):
@@ -282,29 +307,48 @@
     place = jnp.stack([lax.axis_index(a) for a in DP + TENSOR]).astype(jnp.int32)
 
     swapped = lax.ppermute(
-        jnp.pad(out_weight, ((0, SPARE), (0, 0))),
+        out_weight,
         ("y", "z"),
-        [(a * RING + b, (b + RING // 2) % RING * RING + a) for a in range(RING) for b in range(RING)],
-    )
-    (extended,) = kernel_call(
+        [
+            (a * RING + b, (2 * a - b + RING // 2) % RING * RING + a)
+            for a in range(RING)
+            for b in range(RING)
+        ],
+    )
+    (context,) = kernel_call(
         attend_kernel,
-        [((SLAB + TABLE, HEADS_WIDE), BF16)],
-        (slab_start, flight_experts, route_ids.T, queries, keys, values),
-        "sshhhh",
+        [((SLAB, HEADS_WIDE), BF16)],
+        (slab_start, queries, keys, values),
+        "shhh",
         4 * 512 * 1152 * 128,
         1 << 20,
         "attend",
         [
-            pltpu.VMEM((8, SLAB), jnp.int32),
             pltpu.VMEM(queries.shape, BF16),
             pltpu.VMEM(keys.shape, BF16),
             pltpu.VMEM(values.shape, BF16),
-            pltpu.SemaphoreType.DMA((4,)),
+            pltpu.SemaphoreType.DMA((3,)),
         ],
         vmem=ALL_VMEM_BYTES,
     )
-    other = swap(extended, "xl")
-    swapped, _ = lax.optimization_barrier((swapped, other))
+    other = swap(context, "xl")
+    both = jnp.concatenate([context, other])
+    matches = route_ids[:, None, :] == flight_experts[None, :, None]
+    hits = jnp.sum(matches.astype(jnp.int32), axis=2, dtype=jnp.int32)
+    units = jnp.sum(jnp.where(matches, route_weights[:, None, :], 0), axis=2, dtype=jnp.int32)
+
+    table = jnp.pad(hits.T.astype(BF16).reshape(2, COLS), ((0, ROWS - 2), (0, 0)))
+    outgoing = jnp.concatenate(
+        [hidden_rows.reshape(ROWS, BLOCKS, COLS).transpose(1, 0, 2), jnp.broadcast_to(table, (BLOCKS, ROWS, COLS))],
+        axis=1,
+    )
+    gain = lax.dynamic_slice(norm_gain, (xl * HALF,), (HALF,)).reshape(1, HALF)
+    (packed_down,) = kernel_call(
+        pack_down_kernel, [((128, HIDDEN), BF16)], (down_weight,), "v", 0, 4 * 128 * 384, "pack_down"
+    )
+    swapped, outgoing, gain, packed_down, _ = lax.optimization_barrier(
+        (swapped, outgoing, gain, packed_down, other)
+    )
     (packed,) = kernel_call(
         pack_weights_kernel,
         [((128, 2 * HIDDEN + HEADS_WIDE), BF16)],
@@ -315,45 +359,23 @@
         "pack_weights",
     )
     weights = lax.all_gather(packed, ("y", "core"), axis=0, tiled=True)
-    (packed_down,) = kernel_call(
-        pack_down_kernel, [((128, HIDDEN), BF16)], (down_weight,), "v", 0, 4 * 128 * 384, "pack_down"
-    )
     packed_down, _ = lax.optimization_barrier((packed_down, packed))
     down_weights = lax.all_gather(packed_down, ("y", "core"), axis=0, tiled=True)
-    both = jnp.concatenate([extended[:SLAB], other[:SLAB]])
     up1, down1 = along_z(both, 1), along_z(both, -1)
     up2, down2 = along_z(up1, 1), along_z(down1, -1)
     up3, down3 = along_z(up2, 1), along_z(down2, -1)
     up4 = along_z(up3, 1)
 
-    hidden_later, _, _ = lax.optimization_barrier((hidden_rows, up4, down3))
-    columns = hidden_later.reshape(ROWS, 2, 1, RING, COLS).transpose(1, 2, 3, 0, 4)
-    hidden_in = lax.all_to_all(
-        jnp.broadcast_to(columns, (2, 2, RING, ROWS, COLS)).reshape(2 * BLOCKS, ROWS, COLS),
-        PAIR_TENSOR,
-        split_axis=0,
-        concat_axis=0,
-        tiled=True,
-    ).reshape(2 * SLAB, COLS)
-
-    matches = route_ids[:, None, :] == flight_experts[None, :, None]
-    hits = jnp.sum(matches.astype(jnp.int32), axis=2, dtype=jnp.int32)
-    units = jnp.sum(jnp.where(matches, route_weights[:, None, :], 0), axis=2, dtype=jnp.int32)
-    hits_both = jnp.where(
-        xl == 0, jnp.stack([extended[SLAB:], other[SLAB:]]), jnp.stack([other[SLAB:], extended[SLAB:]])
-    )
-    hits_here = lax.dynamic_slice(
-        hits_both, (0, xh * (FLIGHT // 2), 0), (2, FLIGHT // 2, SLAB)
-    )
-    hits_here = hits_here.astype(jnp.int32).reshape(2, FLIGHT // 2, BLOCKS, ROWS)
-    slot_here = jnp.cumsum(hits_here, axis=3) - 1
-    here = jnp.logical_and(
-        hits_here[:, :, :, None, :] == 1,
-        slot_here[:, :, :, None, :] == jnp.arange(CAP, dtype=jnp.int32)[:, None],
-    ).astype(BF16)
-    same = jnp.eye(BLOCKS, dtype=BF16)
-    pickers = (here[:, :, :, :, None, :] * same[None, None, :, None, :, None]).reshape(
-        2 * (FLIGHT // 2) * BLOCKS * CAP, SLAB
+    outgoing, _ = lax.optimization_barrier((outgoing, up1))
+    incoming = lax.all_to_all(outgoing, ("xl", "z"), split_axis=0, concat_axis=0, tiled=True)
+    hidden_in, pickers = kernel_call(
+        unpack_kernel,
+        [((SLAB, COLS), BF16), ((2 * (FLIGHT // 2) * BLOCKS * CAP, SLAB), BF16)],
+        (place, incoming.reshape(2 * SLAB, COLS)),
+        "sv",
+        0,
+        1 << 18,
+        "unpack",
     )
     hits_mine = lax.dynamic_slice_in_dim(hits, tensor_idx * ROWS, ROWS, 0)
     coef = lax.dynamic_slice_in_dim(units, tensor_idx * ROWS, ROWS, 0).astype(F32) / 65536.0
@@ -374,14 +396,13 @@
     coefs = jnp.broadcast_to(coefs, (2, 2, ROWS, 2, FLIGHT, GROUP, 2, CAP)).reshape(
         4 * ROWS, 2 * BLOCKS * 2 * CAP
     )
-    gain = lax.dynamic_slice(norm_gain, (xl * HALF,), (HALF,)).reshape(1, HALF)
     weights, pickers, coefs, gain = lax.optimization_barrier((weights, pickers, coefs, gain))
 
     keep, send = kernel_call(
         project_kernel,
         [((2 * SLAB, COLS), F32), ((2 * SLAB, COLS), BF16)],
-        (place, both, up1, down1, up2, down2, up3, down3, up4, weights),
-        "s" + "v" * RING + "h",
+        (place, hidden_in, both, up1, down1, up2, down2, up3, down3, up4, weights),
+        "sv" + "v" * RING + "h",
         2 * 256 * 4096 * 256,
         2 * 2048 * 1024,
         "project",
@@ -390,8 +411,8 @@
     residual, rows_out = kernel_call(
         residual_kernel,
         [((SLAB, COLS), BF16), ((RING * 2 * BLOCKS * CAP, COLS), BF16)],
-        (place, keep, swap(send, "xh"), hidden_in, pickers),
-        "svvvv",
+        (place, keep, swap(send, "xh"), pickers),
+        "svvv",
         2 * 256 * 128 * 256,
         1 << 20,
         "residual",

time: 168 us -> 162 us (0.964)
  the two profiles are of different devices: /device:TPU:24 before, /device:TPU:64 now
where the time goes in v7:
time: 162 us
  starting transfers between devices  52.4 us (32%)
  waiting for transfers between devices  46.3 us (29%)
  blocking collectives  23.5 us (15%)
  Pallas kernels  15.7 us (10%)
  between operations  14.3 us (9%)
  local copies, waits for them, and re-layouts  5.64 us (3%)
  other arithmetic  3.76 us (2%)
    all_to_all x1, blocking collectives, per_device(): lax.all_to_all(rows_out.reshape(RING, 2 * BLOCKS * CAP, COLS), 'z', split...  23.5 us
    ppermute x7, starting transfers between devices, along_z(): lax.ppermute(block, 'z', [(i, (i + step) % RING) for i in range(RING)])  21.7 us
    all_to_all x1, waiting for transfers between devices, per_device(): lax.all_to_all(outward.reshape(2 * BLOCKS, 2 * CAP, QUARTER + COLS), PAIR...  21.1 us
    pallas_call x9, Pallas kernels, kernel_call(): pl.pallas_call(body, out_shape=[jax.ShapeDtypeStruct(shape, dtype) for sh...  15.7 us
    ppermute x3, starting transfers between devices, swap(): return lax.ppermute(block, axis, [(0, 1), (1, 0)])  11.3 us
    all_to_all x1, starting transfers between devices, per_device(): lax.all_to_all(outgoing, ('xl', 'z'), split_axis=0, concat_axis=0, tiled=...  8.31 us
    all_gather x1, waiting for transfers between devices, per_device(): weights = lax.all_gather(packed, ('y', 'core'), axis=0, tiled=True)  8.29 us
    ppermute x3, waiting for transfers between devices, swap(): return lax.ppermute(block, axis, [(0, 1), (1, 0)])  8.09 us
  transfers between devices with their start and end apart: 15, of which 8 were waited for; matrix products, arithmetic and copies ran while one was open for 3% of the time, Pallas kernels for 7%

profile of v7, /device:TPU:64, one launch (start us, length us, event | category | flops | bytes accessed | tf_op | source)
XLA Modules:
  0.0 161.6 jit_solution(10265898801699478377)
XLA Ops:
  6.5 4.6 %collective-permute-start = (bf16[512,128]{1,0:T(8,128)(2,1)}, bf16[512,128]{1,0:T(8,128)(2,1)S(1)}, u32[]{:S(2)}, u32[]{:S(2)}) collective-permute-start(bf16[512,128]{1,0:T(8,128)(2,1)} %param.18), channel_id=1, source_target_pairs={{0,128},{1,96},{2,64},{3,32},{4,0},{5,224},{6,192},{7,160},{32,193... | collective-permute-start | bytes 393224 | tf_op jit(solution)/shard_map/ppermute | solution.py:309
  11.8 3.3 %attend.1 = bf16[128,512]{1,0:T(8,128)(2,1)} custom-call(s32[1]{0:T(128)S(6)} %copy.22.start_ref, bf16[128,512]{1,0:T(8,128)(2,1)} %queries_hbm.1, bf16[1152,128]{1,0:T(8,128)(2,1)} %keys_hbm.1, bf16[1152,128]{1,0:T(8,128)(2,1)} %values_hbm.1), custom_call_target="tpu_custom_call" | custom-call | flops 301989888 | bytes 1048576 | tf_op jit(solution)/shard_map/attend/pallas_call | solution.py:76
  15.1 3.4 %collective-permute-start.1 = (bf16[128,512]{1,0:T(8,128)(2,1)}, bf16[128,512]{1,0:T(8,128)(2,1)S(1)}, u32[]{:S(2)}, u32[]{:S(2)}) collective-permute-start(bf16[128,512]{1,0:T(8,128)(2,1)} %attend.1), channel_id=1, source_target_pairs={{0,256},{256,0},{1,257},{257,1},{2,258},{258,2},{3,259},{259,3},{4... | collective-permute-start | bytes 393224 | tf_op jit(solution)/shard_map/ppermute | solution.py:63
  20.0 0.9 copy-done.3
  21.6 1.5 pad_maximum_fusion.1
  23.1 0.9 copy-done.1
  24.0 0.9 copy-done.2
  26.4 0.9 pad_maximum_fusion.refs_0_
  27.3 2.4 %collective-permute-start.2 = (bf16[256,512]{1,0:T(8,128)(2,1)S(1)}, bf16[256,512]{1,0:T(8,128)(2,1)S(1)}, u32[]{:S(2)}, u32[]{:S(2)}) collective-permute-start(bf16[256,512]{1,0:T(8,128)(2,1)S(1)} %pad_maximum_fusion.refs_0_), channel_id=1, source_target_pairs={{0,1},{1,2},{2,3},{3,4},{4,5},{5,6},{6,7},{7,0},{8,9},{9,10},{10,1... | collective-permute-start | bytes 786440 | tf_op jit(solution)/shard_map/ppermute | solution.py:67
  29.8 4.2 %collective-permute-start.3 = (bf16[256,512]{1,0:T(8,128)(2,1)S(1)}, bf16[256,512]{1,0:T(8,128)(2,1)S(1)}, u32[]{:S(2)}, u32[]{:S(2)}) collective-permute-start(bf16[256,512]{1,0:T(8,128)(2,1)S(1)} %pad_maximum_fusion.refs_0_), channel_id=1, source_target_pairs={{0,7},{1,0},{2,1},{3,2},{4,3},{5,4},{6,5},{7,6},{8,15},{9,8},{10,9... | collective-permute-start | bytes 786440 | tf_op jit(solution)/shard_map/ppermute | solution.py:67
  34.1 3.7 %collective-permute-done.2.refs_1_ = bf16[256,512]{1,0:T(8,128)(2,1)S(1)} collective-permute-done((bf16[256,512]{1,0:T(8,128)(2,1)S(1)}, bf16[256,512]{1,0:T(8,128)(2,1)S(1)}, u32[]{:S(2)}, u32[]{:S(2)}) %collective-permute-start.2) | collective-permute-done | bytes 262176 | tf_op jit(solution)/shard_map/ppermute | solution.py:67
  37.8 1.9 %collective-permute-start.4 = (bf16[256,512]{1,0:T(8,128)(2,1)S(1)}, bf16[256,512]{1,0:T(8,128)(2,1)S(1)}, u32[]{:S(2)}, u32[]{:S(2)}) collective-permute-start(bf16[256,512]{1,0:T(8,128)(2,1)S(1)} %collective-permute-done.2.refs_1_), channel_id=1, source_target_pairs={{0,1},{1,2},{2,3},{3,4},{4,5},{5,6},{6,7},{7,0},{8,9},{9,10},{10,1... | collective-permute-start | bytes 786440 | tf_op jit(solution)/shard_map/ppermute | solution.py:67
  40.0 5.4 %collective-permute-start.5 = (bf16[256,512]{1,0:T(8,128)(2,1)S(1)}, bf16[256,512]{1,0:T(8,128)(2,1)S(1)}, u32[]{:S(2)}, u32[]{:S(2)}) collective-permute-start(bf16[256,512]{1,0:T(8,128)(2,1)S(1)} %collective-permute-done.3.refs_2_), channel_id=1, source_target_pairs={{0,7},{1,0},{2,1},{3,2},{4,3},{5,4},{6,5},{7,6},{8,15},{9,8},{10,9... | collective-permute-start | bytes 786440 | tf_op jit(solution)/shard_map/ppermute | solution.py:67
  45.4 2.7 %collective-permute-done.4.refs_3_ = bf16[256,512]{1,0:T(8,128)(2,1)S(1)} collective-permute-done((bf16[256,512]{1,0:T(8,128)(2,1)S(1)}, bf16[256,512]{1,0:T(8,128)(2,1)S(1)}, u32[]{:S(2)}, u32[]{:S(2)}) %collective-permute-start.4) | collective-permute-done | bytes 262176 | tf_op jit(solution)/shard_map/ppermute | solution.py:67
  48.1 1.9 %collective-permute-start.6 = (bf16[256,512]{1,0:T(8,128)(2,1)S(1)}, bf16[256,512]{1,0:T(8,128)(2,1)S(1)}, u32[]{:S(2)}, u32[]{:S(2)}) collective-permute-start(bf16[256,512]{1,0:T(8,128)(2,1)S(1)} %collective-permute-done.4.refs_3_), channel_id=1, source_target_pairs={{0,1},{1,2},{2,3},{3,4},{4,5},{5,6},{6,7},{7,0},{8,9},{9,10},{10,1... | collective-permute-start | bytes 786440 | tf_op jit(solution)/shard_map/ppermute | solution.py:67
  50.0 8.3 %all-to-all-start = ((bf16[16,16,256]{2,1,0:T(8,128)(2,1)}), bf16[16,16,256]{2,1,0:T(8,128)(2,1)S(1)}, u32[]{:S(2)}, u32[]{:S(2)}) async-start(bf16[16,16,256]{2,1,0:T(8,128)(2,1)} %pad_maximum_fusion.1), calls=%async_computation | async-start | bytes 262144 | tf_op jit(solution)/shard_map/all_to_all | solution.py:370
  58.3 2.0 %collective-permute-start.7 = (bf16[256,512]{1,0:T(8,128)(2,1)S(1)}, bf16[256,512]{1,0:T(8,128)(2,1)S(1)}, u32[]{:S(2)}, u32[]{:S(2)}) collective-permute-start(bf16[256,512]{1,0:T(8,128)(2,1)S(1)} %collective-permute-done.5.refs_4_), channel_id=1, source_target_pairs={{0,7},{1,0},{2,1},{3,2},{4,3},{5,4},{6,5},{7,6},{8,15},{9,8},{10,9... | collective-permute-start | bytes 786440 | tf_op jit(solution)/shard_map/ppermute | solution.py:67
  60.4 3.8 %collective-permute-start.8 = (bf16[256,512]{1,0:T(8,128)(2,1)S(1)}, bf16[256,512]{1,0:T(8,128)(2,1)S(1)}, u32[]{:S(2)}, u32[]{:S(2)}) collective-permute-start(bf16[256,512]{1,0:T(8,128)(2,1)S(1)} %collective-permute-done.6.refs_5_), channel_id=1, source_target_pairs={{0,1},{1,2},{2,3},{3,4},{4,5},{5,6},{6,7},{7,0},{8,9},{9,10},{10,1... | collective-permute-start | bytes 786440 | tf_op jit(solution)/shard_map/ppermute | solution.py:67
  66.7 8.3 %all-gather.3.cloned.1.call-done.refs_8_.weights_hbm = bf16[2048,1280]{1,0:T(8,128)(2,1)} async-done(((bf16[128,1280]{1,0:T(8,128)(2,1)}), bf16[2048,1280]{1,0:T(8,128)(2,1)}) %all-gather.3.cloned.1.call-update) | async-done | bytes 5242896 | tf_op jit(solution)/shard_map/all_gather | solution.py:361
  75.0 2.8 %project.1 = (f32[256,256]{1,0:T(8,128)S(1)}, bf16[256,256]{1,0:T(8,128)(2,1)S(1)}) custom-call(s32[5]{0:T(128)S(1)} %stack.23.place_ref, bf16[128,256]{1,0:T(8,128)(2,1)S(1)} %get-tuple-element.29.hidden_ref, bf16[256,512]{1,0:T(8,128)(2,1)S(1)} %pad_maximum_fusion.refs_0_, bf16[256,512]{1,0:T(8,128)(2,1)S(1)} %collective-permute-done.2.refs_1_, ...), custom_call_target="tpu_custom_call" | custom-call | flops 536870912 | bytes 4194304 | tf_op jit(solution)/shard_map/project/pallas_call | solution.py:76
  77.8 4.9 %collective-permute-start.9 = (bf16[256,256]{1,0:T(8,128)(2,1)S(1)}, bf16[256,256]{1,0:T(8,128)(2,1)S(1)}, u32[]{:S(2)}, u32[]{:S(2)}) collective-permute-start(bf16[256,256]{1,0:T(8,128)(2,1)S(1)} %get-tuple-element.32), channel_id=1, source_target_pairs={{0,8},{8,0},{1,9},{9,1},{2,10},{10,2},{3,11},{11,3},{4,12},{12,4},... | collective-permute-start | bytes 393224 | tf_op jit(solution)/shard_map/ppermute | solution.py:63
  82.8 4.1 %collective-permute-done.9.recv_ref = bf16[256,256]{1,0:T(8,128)(2,1)S(1)} collective-permute-done((bf16[256,256]{1,0:T(8,128)(2,1)S(1)}, bf16[256,256]{1,0:T(8,128)(2,1)S(1)}, u32[]{:S(2)}, u32[]{:S(2)}) %collective-permute-start.9) | collective-permute-done | bytes 131104 | tf_op jit(solution)/shard_map/ppermute | solution.py:63
  87.6 23.5 %all_to_all.15 = bf16[8,128,256]{2,1,0:T(8,128)(2,1)S(1)} all-to-all(bf16[8,128,256]{2,1,0:T(8,128)(2,1)S(1)} %bitcast.19), channel_id=1, replica_groups=mesh['xl'=2,'y'=8,'core'=2,'xh'=2,'z'=8] {'z'}, dimensions={0} | all-to-all | bytes 1048576 | tf_op jit(solution)/shard_map/all_to_all | solution.py:420
  111.1 2.3 %gate_up.1 = (f32[128,896]{1,0:T(8,128)S(1)}, bf16[128,896]{1,0:T(8,128)(2,1)S(1)}) custom-call(bf16[1024,256]{1,0:T(8,128)(2,1)S(1)} %bitcast.18, bf16[1,2048]{1,0:T(2,128)(2,1)S(1)} %reshape.75.gain_ref, bf16[2048,1280]{1,0:T(8,128)(2,1)} %all-gather.3.cloned.1.call-done.refs_8_.weights_hbm), custom_call_target="tpu_custom_call" | custom-call | flops 402653184 | bytes 3145728 | tf_op jit(solution)/shard_map/gate_up/pallas_call | solution.py:76
  113.4 2.9 %collective-permute-start.10 = (bf16[128,896]{1,0:T(8,128)(2,1)S(1)}, bf16[128,896]{1,0:T(8,128)(2,1)S(1)}, u32[]{:S(2)}, u32[]{:S(2)}) collective-permute-start(bf16[128,896]{1,0:T(8,128)(2,1)S(1)} %get-tuple-element.37), channel_id=1, source_target_pairs={{0,256},{256,0},{1,257},{257,1},{2,258},{258,2},{3,259},{259,3},{4... | collective-permute-start | bytes 688136 | tf_op jit(solution)/shard_map/ppermute | solution.py:63
  116.4 1.0 all-gather.5.cloned.1.call-done.weights_hbm
  117.4 4.0 %collective-permute-done.10.recv_ref = bf16[128,896]{1,0:T(8,128)(2,1)S(1)} collective-permute-done((bf16[128,896]{1,0:T(8,128)(2,1)S(1)}, bf16[128,896]{1,0:T(8,128)(2,1)S(1)}, u32[]{:S(2)}, u32[]{:S(2)}) %collective-permute-start.10) | collective-permute-done | bytes 229408 | tf_op jit(solution)/shard_map/ppermute | solution.py:63
  121.4 1.4 copy-done
  122.8 2.7 %down.1 = bf16[256,1280]{1,0:T(8,128)(2,1)} custom-call(s32[5]{0:T(128)S(1)} %stack.23.place_ref, f32[128,896]{1,0:T(8,128)S(1)} %get-tuple-element.36.own_ref, bf16[128,896]{1,0:T(8,128)(2,1)S(1)} %collective-permute-done.10.recv_ref, bf16[128,256]{1,0:T(8,128)(2,1)S(1)} %get-tuple-element.38.residual_ref, bf16[2048,384]{1,0:T(8,128)(2,1)S(1)} %copy-done), custom_call_target="tpu_custom_call" | custom-call | flops 402653184 | bytes 2097152 | tf_op jit(solution)/shard_map/down/pallas_call | solution.py:76
  125.4 6.5 %all-to-all-start.2 = ((bf16[32,8,1280]{2,1,0:T(8,128)(2,1)}), bf16[32,8,1280]{2,1,0:T(8,128)(2,1)S(1)}, u32[]{:S(2)}, u32[]{:S(2)}) async-start(bf16[32,8,1280]{2,1,0:T(8,128)(2,1)} %bitcast.11), calls=%async_computation.2 | async-start | bytes 1310720 | tf_op jit(solution)/shard_map/all_to_all | solution.py:443
  132.0 21.1 %all-to-all-done.2 = bf16[32,8,1280]{2,1,0:T(8,128)(2,1)S(1)} async-done(((bf16[32,8,1280]{2,1,0:T(8,128)(2,1)}), bf16[32,8,1280]{2,1,0:T(8,128)(2,1)S(1)}, u32[]{:S(2)}, u32[]{:S(2)}) %all-to-all-start.2) | async-done | bytes 655392 | tf_op jit(solution)/shard_map/all_to_all | solution.py:443
  153.1 1.6 %combine.1 = bf16[8,4096]{1,0:T(8,128)(2,1)} custom-call(s32[5]{0:T(128)S(1)} %stack.23.place_ref, f32[32,256]{1,0:T(8,128)S(1)} %copy.21.coefs_ref, bf16[256,1280]{1,0:T(8,128)(2,1)S(1)} %bitcast.17), custom_call_target="tpu_custom_call" | custom-call | flops 67108864 | bytes 1048576 | tf_op jit(solution)/shard_map/combine/pallas_call | solution.py:76
  (39 shorter events, 7.3 us)
Async XLA Ops:
  6.5 68.4 %all-gather.3.cloned.1.call-start = ((), (), s32[]{:S(2)}) async-start(), calls=%async_computation.3 | async-start | bytes 5570560 | tf_op jit(solution)/shard_map/all_gather | solution.py:361
  6.5 16.5 %collective-permute-start = (bf16[512,128]{1,0:T(8,128)(2,1)}, bf16[512,128]{1,0:T(8,128)(2,1)S(1)}, u32[]{:S(2)}, u32[]{:S(2)}) collective-permute-start(bf16[512,128]{1,0:T(8,128)(2,1)} %param.18), channel_id=1, source_target_pairs={{0,128},{1,96},{2,64},{3,32},{4,0},{5,224},{6,192},{7,160},{32,193... | collective-permute-start | bytes 393224 | tf_op jit(solution)/shard_map/ppermute | solution.py:309
  15.1 8.0 %collective-permute-start.1 = (bf16[128,512]{1,0:T(8,128)(2,1)}, bf16[128,512]{1,0:T(8,128)(2,1)S(1)}, u32[]{:S(2)}, u32[]{:S(2)}) collective-permute-start(bf16[128,512]{1,0:T(8,128)(2,1)} %attend.1), channel_id=1, source_target_pairs={{0,256},{256,0},{1,257},{257,1},{2,258},{258,2},{3,259},{259,3},{4... | collective-permute-start | bytes 393224 | tf_op jit(solution)/shard_map/ppermute | solution.py:63
  20.0 0.9 copy-start.3
  23.1 0.9 copy-start.1
  24.0 0.9 copy-start.2
  25.7 91.7 %all-gather.5.cloned.1.call-start = ((), (), s32[]{:S(2)}) async-start(), calls=%async_computation.4 | async-start | bytes 1671168 | tf_op jit(solution)/shard_map/all_gather | solution.py:363
  27.3 10.4 %collective-permute-start.2 = (bf16[256,512]{1,0:T(8,128)(2,1)S(1)}, bf16[256,512]{1,0:T(8,128)(2,1)S(1)}, u32[]{:S(2)}, u32[]{:S(2)}) collective-permute-start(bf16[256,512]{1,0:T(8,128)(2,1)S(1)} %pad_maximum_fusion.refs_0_), channel_id=1, source_target_pairs={{0,1},{1,2},{2,3},{3,4},{4,5},{5,6},{6,7},{7,0},{8,9},{9,10},{10,1... | collective-permute-start | bytes 786440 | tf_op jit(solution)/shard_map/ppermute | solution.py:67
  29.8 10.2 %collective-permute-start.3 = (bf16[256,512]{1,0:T(8,128)(2,1)S(1)}, bf16[256,512]{1,0:T(8,128)(2,1)S(1)}, u32[]{:S(2)}, u32[]{:S(2)}) collective-permute-start(bf16[256,512]{1,0:T(8,128)(2,1)S(1)} %pad_maximum_fusion.refs_0_), channel_id=1, source_target_pairs={{0,7},{1,0},{2,1},{3,2},{4,3},{5,4},{6,5},{7,6},{8,15},{9,8},{10,9... | collective-permute-start | bytes 786440 | tf_op jit(solution)/shard_map/ppermute | solution.py:67
  37.8 10.3 %collective-permute-start.4 = (bf16[256,512]{1,0:T(8,128)(2,1)S(1)}, bf16[256,512]{1,0:T(8,128)(2,1)S(1)}, u32[]{:S(2)}, u32[]{:S(2)}) collective-permute-start(bf16[256,512]{1,0:T(8,128)(2,1)S(1)} %collective-permute-done.2.refs_1_), channel_id=1, source_target_pairs={{0,1},{1,2},{2,3},{3,4},{4,5},{5,6},{6,7},{7,0},{8,9},{9,10},{10,1... | collective-permute-start | bytes 786440 | tf_op jit(solution)/shard_map/ppermute | solution.py:67
  40.0 18.4 %collective-permute-start.5 = (bf16[256,512]{1,0:T(8,128)(2,1)S(1)}, bf16[256,512]{1,0:T(8,128)(2,1)S(1)}, u32[]{:S(2)}, u32[]{:S(2)}) collective-permute-start(bf16[256,512]{1,0:T(8,128)(2,1)S(1)} %collective-permute-done.3.refs_2_), channel_id=1, source_target_pairs={{0,7},{1,0},{2,1},{3,2},{4,3},{5,4},{6,5},{7,6},{8,15},{9,8},{10,9... | collective-permute-start | bytes 786440 | tf_op jit(solution)/shard_map/ppermute | solution.py:67
  48.1 12.3 %collective-permute-start.6 = (bf16[256,512]{1,0:T(8,128)(2,1)S(1)}, bf16[256,512]{1,0:T(8,128)(2,1)S(1)}, u32[]{:S(2)}, u32[]{:S(2)}) collective-permute-start(bf16[256,512]{1,0:T(8,128)(2,1)S(1)} %collective-permute-done.4.refs_3_), channel_id=1, source_target_pairs={{0,1},{1,2},{2,3},{3,4},{4,5},{5,6},{6,7},{7,0},{8,9},{9,10},{10,1... | collective-permute-start | bytes 786440 | tf_op jit(solution)/shard_map/ppermute | solution.py:67
  50.0 15.9 %all-to-all-start = ((bf16[16,16,256]{2,1,0:T(8,128)(2,1)}), bf16[16,16,256]{2,1,0:T(8,128)(2,1)S(1)}, u32[]{:S(2)}, u32[]{:S(2)}) async-start(bf16[16,16,256]{2,1,0:T(8,128)(2,1)} %pad_maximum_fusion.1), calls=%async_computation | async-start | bytes 262144 | tf_op jit(solution)/shard_map/all_to_all | solution.py:370
  58.3 16.6 %collective-permute-start.7 = (bf16[256,512]{1,0:T(8,128)(2,1)S(1)}, bf16[256,512]{1,0:T(8,128)(2,1)S(1)}, u32[]{:S(2)}, u32[]{:S(2)}) collective-permute-start(bf16[256,512]{1,0:T(8,128)(2,1)S(1)} %collective-permute-done.5.refs_4_), channel_id=1, source_target_pairs={{0,7},{1,0},{2,1},{3,2},{4,3},{5,4},{6,5},{7,6},{8,15},{9,8},{10,9... | collective-permute-start | bytes 786440 | tf_op jit(solution)/shard_map/ppermute | solution.py:67
  60.4 14.6 %collective-permute-start.8 = (bf16[256,512]{1,0:T(8,128)(2,1)S(1)}, bf16[256,512]{1,0:T(8,128)(2,1)S(1)}, u32[]{:S(2)}, u32[]{:S(2)}) collective-permute-start(bf16[256,512]{1,0:T(8,128)(2,1)S(1)} %collective-permute-done.6.refs_5_), channel_id=1, source_target_pairs={{0,1},{1,2},{2,3},{3,4},{4,5},{5,6},{6,7},{7,0},{8,9},{9,10},{10,1... | collective-permute-start | bytes 786440 | tf_op jit(solution)/shard_map/ppermute | solution.py:67
  77.8 9.1 %collective-permute-start.9 = (bf16[256,256]{1,0:T(8,128)(2,1)S(1)}, bf16[256,256]{1,0:T(8,128)(2,1)S(1)}, u32[]{:S(2)}, u32[]{:S(2)}) collective-permute-start(bf16[256,256]{1,0:T(8,128)(2,1)S(1)} %get-tuple-element.32), channel_id=1, source_target_pairs={{0,8},{8,0},{1,9},{9,1},{2,10},{10,2},{3,11},{11,3},{4,12},{12,4},... | collective-permute-start | bytes 393224 | tf_op jit(solution)/shard_map/ppermute | solution.py:63
  113.4 7.9 %collective-permute-start.10 = (bf16[128,896]{1,0:T(8,128)(2,1)S(1)}, bf16[128,896]{1,0:T(8,128)(2,1)S(1)}, u32[]{:S(2)}, u32[]{:S(2)}) collective-permute-start(bf16[128,896]{1,0:T(8,128)(2,1)S(1)} %get-tuple-element.37), channel_id=1, source_target_pairs={{0,256},{256,0},{1,257},{257,1},{2,258},{258,2},{3,259},{259,3},{4... | collective-permute-start | bytes 688136 | tf_op jit(solution)/shard_map/ppermute | solution.py:63
  121.4 1.4 copy-start
  125.4 27.6 %all-to-all-start.2 = ((bf16[32,8,1280]{2,1,0:T(8,128)(2,1)}), bf16[32,8,1280]{2,1,0:T(8,128)(2,1)S(1)}, u32[]{:S(2)}, u32[]{:S(2)}) async-start(bf16[32,8,1280]{2,1,0:T(8,128)(2,1)} %bitcast.11), calls=%async_computation.2 | async-start | bytes 1310720 | tf_op jit(solution)/shard_map/all_to_all | solution.py:443
Sparse Core Ops, SparseCore 0:
  25.8 49.1 all-gather.2
  77.1 40.2 all-gather.4

commit v8 on v7

--- a/solution.py
+++ b/solution.py
@@ -24,6 +24,8 @@
 ROWS = 8
 VMEM_BYTES = 48 * 1024 * 1024
 ALL_VMEM_BYTES = 63400000
+MOST_VMEM_BYTES = 57000000
+DOWN_VMEM_BYTES = 55000000
 F32, BF16 = jnp.float32, jnp.bfloat16
 
 
@@ -67,7 +69,7 @@
     return lax.ppermute(block, "z", [(i, (i + step) % RING) for i in range(RING)])
 
 
-def kernel_call(body, out_shapes, operands, spaces, flops, moved, name, scratch=(), out_space="v", vmem=VMEM_BYTES):
+def kernel_call(body, out_shapes, operands, spaces, flops, moved, name, scratch=(), out_space="v", vmem=VMEM_BYTES, aliases=None):
     kinds = {
         "v": pl.BlockSpec(memory_space=pltpu.VMEM),
         "s": pl.BlockSpec(memory_space=pltpu.SMEM),
@@ -79,18 +81,40 @@
         in_specs=[kinds[s] for s in spaces],
         out_specs=[kinds[out_space]] * len(out_shapes),
         scratch_shapes=list(scratch),
+        input_output_aliases=aliases or {},
         compiler_params=pltpu.CompilerParams(vmem_limit_bytes=vmem),
         cost_estimate=pl.CostEstimate(flops=flops, bytes_accessed=moved, transcendentals=0),
         name=name,
     )(*operands)
 
 
-def pack_weights_kernel(gate_ref, up_ref, swapped_ref, packed_ref):
-    packed_ref[:, :HIDDEN] = gate_ref[...]
-    packed_ref[:, HIDDEN : 2 * HIDDEN] = up_ref[...]
-    for j in range(HEADS_WIDE // 128):
-        at = 2 * HIDDEN + j * 128
-        packed_ref[:, at : at + 128] = swapped_ref[j * 128 : (j + 1) * 128, :]
+def pack_gate_up_kernel(gate_hbm, up_hbm, packed_hbm, held, sems):
+    copies = [
+        pltpu.make_async_copy(source, held.at[:, pl.ds(i * HIDDEN, HIDDEN)], sems.at[i])
+        for i, source in enumerate((gate_hbm, up_hbm))
+    ]
+    for copy in copies:
+        copy.start()
+    for copy in copies:
+        copy.wait()
+    whole = pltpu.make_async_copy(held, packed_hbm.at[:, pl.ds(0, 2 * HIDDEN)], sems.at[2])
+    whole.start()
+    whole.wait()
+
+
+def pack_out_kernel(swapped_ref, started_hbm, packed_hbm, sems):
+    copies = [
+        pltpu.make_async_copy(
+            swapped_ref.at[pl.ds(j * 128, 128)],
+            packed_hbm.at[:, pl.ds(2 * HIDDEN + j * 128, 128)],
+            sems.at[j],
+        )
+        for j in range(HEADS_WIDE // 128)
+    ]
+    for copy in copies:
+        copy.start()
+    for copy in copies:
+        copy.wait()
 
 
 def pack_down_kernel(down_ref, packed_ref):
@@ -130,19 +154,20 @@
     xl, xh, z = place_ref[0], place_ref[3], place_ref[4]
 
     def copy(k):
-        at = pl.ds(k * 2 * 128, 2 * 128)
+        at = pl.ds(pl.multiple_of(k * 2 * 128, 2 * 128), 2 * 128)
         return pltpu.make_async_copy(
             weights_hbm.at[at, pl.ds(2 * HIDDEN, HEADS_WIDE)], weights.at[at], sems.at[k]
         )
 
-    for k in range(RING):
-        copy(k).start()
-    for k in range(RING):
-        copy(k).wait()
+    blocks = [(z + (RING + RING // 2 - step)) & (RING - 1) for step in STEPS]
+    for block in blocks:
+        copy(block).start()
+    for block in blocks:
+        copy(block).wait()
     total = jnp.zeros((2 * SLAB, COLS), F32)
     for k in range(RING):
         context = contexts[k][...]
-        first = pl.multiple_of(((z + (RING + RING // 2 - STEPS[k])) & (RING - 1)) * 256, 256)
+        first = pl.multiple_of(blocks[k] * 256, 256)
         for half in range(2):
             lanes = slice(half * 256, half * 256 + 256)
             block = weights[pl.ds(first, 256), lanes]
@@ -346,17 +371,31 @@
     (packed_down,) = kernel_call(
         pack_down_kernel, [((128, HIDDEN), BF16)], (down_weight,), "v", 0, 4 * 128 * 384, "pack_down"
     )
-    swapped, outgoing, gain, packed_down, _ = lax.optimization_barrier(
-        (swapped, outgoing, gain, packed_down, other)
-    )
+    (started,) = kernel_call(
+        pack_gate_up_kernel,
+        [((128, 2 * HIDDEN + HEADS_WIDE), BF16)],
+        (gate_weight, up_weight),
+        "hh",
+        0,
+        4 * 128 * 768,
+        "pack_gate_up",
+        [pltpu.VMEM((128, 2 * HIDDEN), BF16), pltpu.SemaphoreType.DMA((3,))],
+        "h",
+        MOST_VMEM_BYTES,
+    )
+    swapped, started, _ = lax.optimization_barrier((swapped, started, other))
     (packed,) = kernel_call(
-        pack_weights_kernel,
+        pack_out_kernel,
         [((128, 2 * HIDDEN + HEADS_WIDE), BF16)],
-        (gate_weight, up_weight, swapped),
-        "vvv",
+        (swapped, started),
+        "vh",
         0,
-        4 * 128 * 1280,
-        "pack_weights",
+        4 * 128 * 512,
+        "pack_out",
+        [pltpu.SemaphoreType.DMA((HEADS_WIDE // 128,))],
+        "h",
+        vmem=MOST_VMEM_BYTES,
+        aliases={1: 0},
     )
     weights = lax.all_gather(packed, ("y", "core"), axis=0, tiled=True)
     packed_down, _ = lax.optimization_barrier((packed_down, packed))
@@ -439,6 +478,7 @@
         2 << 20,
         "down",
         [pltpu.VMEM((HALF, HIDDEN), BF16), pltpu.SemaphoreType.DMA],
+        vmem=DOWN_VMEM_BYTES,
     )
     returned = lax.all_to_all(
         outward.reshape(2 * BLOCKS, 2 * CAP, QUARTER + COLS),

time: 162 us -> 161 us (level)
  Pallas kernels: 15.7 us -> 19.3 us
  waiting for transfers between devices: 46.3 us -> 42.7 us
  local copies, waits for them, and re-layouts: 5.64 us -> 2.41 us
  starting transfers between devices: 52.4 us -> 54.2 us
    pallas_call x9 -> x10, Pallas kernels: 15.7 us -> 19.3 us  [kernel_call(): pl.pallas_call(body, out_shape=[jax.ShapeDtypeStruct(shape, dtype) for sh...]
    all_gather x1, waiting for transfers between devices: 8.29 us -> 5.19 us  [per_device(): weights = lax.all_gather(packed, ('y', 'core'), axis=0, tiled=True)]
    ppermute x7, waiting for transfers between devices: 6.43 us -> 3.67 us  [along_z(): lax.ppermute(block, 'z', [(i, (i + step) % RING) for i in range(RING)])]
    unnamed x8 -> x6, local copies, waits for them, and re-layouts: 4.08 us -> 1.54 us
    ppermute x1, waiting for transfers between devices: 0.01 us -> 2.51 us  [per_device(): lax.ppermute(out_weight, ('y', 'z'), [(a * RING + b, (2 * a - b + RING //...]
  transfers between devices with their start and end apart: 15 -> 15, of which waited for: 8 -> 10; matrix products, arithmetic and copies ran while one was open for 3% -> 3% of each run, Pallas kernels for 7% -> 8%
where the time goes in v8:
time: 161 us; the launch traced here: 160 us
  starting transfers between devices  54.2 us (34%)
  waiting for transfers between devices  42.7 us (27%)
  blocking collectives  23.2 us (14%)
  Pallas kernels  19.3 us (12%)
  between operations  14.3 us (9%)
  other arithmetic  3.75 us (2%)
  local copies, waits for them, and re-layouts  2.41 us (1%)
    all_to_all x1, blocking collectives, per_device(): lax.all_to_all(rows_out.reshape(RING, 2 * BLOCKS * CAP, COLS), 'z', split...  23.2 us
    ppermute x7, starting transfers between devices, along_z(): lax.ppermute(block, 'z', [(i, (i + step) % RING) for i in range(RING)])  22.5 us
    all_to_all x1, waiting for transfers between devices, per_device(): lax.all_to_all(outward.reshape(2 * BLOCKS, 2 * CAP, QUARTER + COLS), PAIR...  21.1 us
    pallas_call x10, Pallas kernels, kernel_call(): pl.pallas_call(body, out_shape=[jax.ShapeDtypeStruct(shape, dtype) for sh...  19.3 us
    ppermute x3, starting transfers between devices, swap(): return lax.ppermute(block, axis, [(0, 1), (1, 0)])  11.6 us
    all_to_all x1, starting transfers between devices, per_device(): lax.all_to_all(outgoing, ('xl', 'z'), split_axis=0, concat_axis=0, tiled=...  8.53 us
    ppermute x3, waiting for transfers between devices, swap(): return lax.ppermute(block, axis, [(0, 1), (1, 0)])  7.76 us
    all_to_all x1, starting transfers between devices, per_device(): lax.all_to_all(outward.reshape(2 * BLOCKS, 2 * CAP, QUARTER + COLS), PAIR...  6.85 us
  transfers between devices with their start and end apart: 15, of which 10 were waited for; matrix products, arithmetic and copies ran while one was open for 3% of the time, Pallas kernels for 8%

profile of v8, /device:TPU:64, one launch (start us, length us, event | category | flops | bytes accessed | tf_op | source)
XLA Modules:
  0.0 159.8 jit_solution(16707444173906067570)
XLA Ops:
  6.5 4.7 %collective-permute-start = (bf16[512,128]{1,0:T(8,128)(2,1)}, bf16[512,128]{1,0:T(8,128)(2,1)S(1)}, u32[]{:S(2)}, u32[]{:S(2)}) collective-permute-start(bf16[512,128]{1,0:T(8,128)(2,1)} %param.18), channel_id=1, source_target_pairs={{0,128},{1,96},{2,64},{3,32},{4,0},{5,224},{6,192},{7,160},{32,193... | collective-permute-start | bytes 393224 | tf_op jit(solution)/shard_map/ppermute | solution.py:334
  11.9 3.3 %attend.1 = bf16[128,512]{1,0:T(8,128)(2,1)} custom-call(s32[1]{0:T(128)S(6)} %copy.24.start_ref, bf16[128,512]{1,0:T(8,128)(2,1)} %queries_hbm.1, bf16[1152,128]{1,0:T(8,128)(2,1)} %keys_hbm.1, bf16[1152,128]{1,0:T(8,128)(2,1)} %values_hbm.1), custom_call_target="tpu_custom_call" | custom-call | flops 301989888 | bytes 1048576 | tf_op jit(solution)/shard_map/attend/pallas_call | solution.py:78
  15.2 3.4 %collective-permute-start.1 = (bf16[128,512]{1,0:T(8,128)(2,1)}, bf16[128,512]{1,0:T(8,128)(2,1)S(1)}, u32[]{:S(2)}, u32[]{:S(2)}) collective-permute-start(bf16[128,512]{1,0:T(8,128)(2,1)} %attend.1), channel_id=1, source_target_pairs={{0,256},{256,0},{1,257},{257,1},{2,258},{258,2},{3,259},{259,3},{4... | collective-permute-start | bytes 393224 | tf_op jit(solution)/shard_map/ppermute | solution.py:65
  18.6 1.7 %pack_gate_up.1.started_hbm = bf16[128,1280]{1,0:T(8,128)(2,1)} custom-call(bf16[128,384]{1,0:T(8,128)(2,1)} %gate_hbm.1, bf16[128,384]{1,0:T(8,128)(2,1)} %up_hbm.1), custom_call_target="tpu_custom_call" | custom-call | bytes 393216 | tf_op jit(solution)/shard_map/pack_gate_up/pallas_call | solution.py:78
  20.3 2.5 %collective-permute-done.swapped_ref = bf16[512,128]{1,0:T(8,128)(2,1)S(1)} collective-permute-done((bf16[512,128]{1,0:T(8,128)(2,1)}, bf16[512,128]{1,0:T(8,128)(2,1)S(1)}, u32[]{:S(2)}, u32[]{:S(2)}) %collective-permute-start) | collective-permute-done | bytes 131104 | tf_op jit(solution)/shard_map/ppermute | solution.py:334
  23.5 1.6 %pack_out.1 = bf16[128,1280]{1,0:T(8,128)(2,1)} custom-call(bf16[512,128]{1,0:T(8,128)(2,1)} %copy-done.1, bf16[128,1280]{1,0:T(8,128)(2,1)} %pack_gate_up.1.started_hbm), custom_call_target="tpu_custom_call", output_to_operand_aliasing={{}: (1, {})} | custom-call | bytes 262144 | tf_op jit(solution)/shard_map/pack_out/pallas_call | solution.py:78
  27.5 0.9 pad_maximum_fusion.refs_0_
  28.4 1.9 %collective-permute-start.2 = (bf16[256,512]{1,0:T(8,128)(2,1)S(1)}, bf16[256,512]{1,0:T(8,128)(2,1)S(1)}, u32[]{:S(2)}, u32[]{:S(2)}) collective-permute-start(bf16[256,512]{1,0:T(8,128)(2,1)S(1)} %pad_maximum_fusion.refs_0_), channel_id=1, source_target_pairs={{0,1},{1,2},{2,3},{3,4},{4,5},{5,6},{6,7},{7,0},{8,9},{9,10},{10,1... | collective-permute-start | bytes 786440 | tf_op jit(solution)/shard_map/ppermute | solution.py:69
  30.5 1.5 pad_maximum_fusion.1
  32.0 3.9 %collective-permute-start.3 = (bf16[256,512]{1,0:T(8,128)(2,1)S(1)}, bf16[256,512]{1,0:T(8,128)(2,1)S(1)}, u32[]{:S(2)}, u32[]{:S(2)}) collective-permute-start(bf16[256,512]{1,0:T(8,128)(2,1)S(1)} %pad_maximum_fusion.refs_0_), channel_id=1, source_target_pairs={{0,7},{1,0},{2,1},{3,2},{4,3},{5,4},{6,5},{7,6},{8,15},{9,8},{10,9... | collective-permute-start | bytes 786440 | tf_op jit(solution)/shard_map/ppermute | solution.py:69
  36.8 2.1 %collective-permute-start.4 = (bf16[256,512]{1,0:T(8,128)(2,1)S(1)}, bf16[256,512]{1,0:T(8,128)(2,1)S(1)}, u32[]{:S(2)}, u32[]{:S(2)}) collective-permute-start(bf16[256,512]{1,0:T(8,128)(2,1)S(1)} %collective-permute-done.2.refs_1_), channel_id=1, source_target_pairs={{0,1},{1,2},{2,3},{3,4},{4,5},{5,6},{6,7},{7,0},{8,9},{9,10},{10,1... | collective-permute-start | bytes 786440 | tf_op jit(solution)/shard_map/ppermute | solution.py:69
  39.2 1.1 collective-permute-done.3.refs_2_
  40.3 6.8 %collective-permute-start.5 = (bf16[256,512]{1,0:T(8,128)(2,1)S(1)}, bf16[256,512]{1,0:T(8,128)(2,1)S(1)}, u32[]{:S(2)}, u32[]{:S(2)}) collective-permute-start(bf16[256,512]{1,0:T(8,128)(2,1)S(1)} %collective-permute-done.3.refs_2_), channel_id=1, source_target_pairs={{0,7},{1,0},{2,1},{3,2},{4,3},{5,4},{6,5},{7,6},{8,15},{9,8},{10,9... | collective-permute-start | bytes 786440 | tf_op jit(solution)/shard_map/ppermute | solution.py:69
  47.1 1.7 %collective-permute-done.4.refs_3_ = bf16[256,512]{1,0:T(8,128)(2,1)S(1)} collective-permute-done((bf16[256,512]{1,0:T(8,128)(2,1)S(1)}, bf16[256,512]{1,0:T(8,128)(2,1)S(1)}, u32[]{:S(2)}, u32[]{:S(2)}) %collective-permute-start.4) | collective-permute-done | bytes 262176 | tf_op jit(solution)/shard_map/ppermute | solution.py:69
  48.8 1.9 %collective-permute-start.6 = (bf16[256,512]{1,0:T(8,128)(2,1)S(1)}, bf16[256,512]{1,0:T(8,128)(2,1)S(1)}, u32[]{:S(2)}, u32[]{:S(2)}) collective-permute-start(bf16[256,512]{1,0:T(8,128)(2,1)S(1)} %collective-permute-done.4.refs_3_), channel_id=1, source_target_pairs={{0,1},{1,2},{2,3},{3,4},{4,5},{5,6},{6,7},{7,0},{8,9},{9,10},{10,1... | collective-permute-start | bytes 786440 | tf_op jit(solution)/shard_map/ppermute | solution.py:69
  50.7 8.5 %all-to-all-start = ((bf16[16,16,256]{2,1,0:T(8,128)(2,1)}), bf16[16,16,256]{2,1,0:T(8,128)(2,1)S(1)}, u32[]{:S(2)}, u32[]{:S(2)}) async-start(bf16[16,16,256]{2,1,0:T(8,128)(2,1)} %pad_maximum_fusion.1), calls=%async_computation | async-start | bytes 262144 | tf_op jit(solution)/shard_map/all_to_all | solution.py:409
  59.2 2.0 %collective-permute-start.7 = (bf16[256,512]{1,0:T(8,128)(2,1)S(1)}, bf16[256,512]{1,0:T(8,128)(2,1)S(1)}, u32[]{:S(2)}, u32[]{:S(2)}) collective-permute-start(bf16[256,512]{1,0:T(8,128)(2,1)S(1)} %collective-permute-done.5.refs_4_), channel_id=1, source_target_pairs={{0,7},{1,0},{2,1},{3,2},{4,3},{5,4},{6,5},{7,6},{8,15},{9,8},{10,9... | collective-permute-start | bytes 786440 | tf_op jit(solution)/shard_map/ppermute | solution.py:69
  61.3 3.8 %collective-permute-start.8 = (bf16[256,512]{1,0:T(8,128)(2,1)S(1)}, bf16[256,512]{1,0:T(8,128)(2,1)S(1)}, u32[]{:S(2)}, u32[]{:S(2)}) collective-permute-start(bf16[256,512]{1,0:T(8,128)(2,1)S(1)} %collective-permute-done.6.refs_5_), channel_id=1, source_target_pairs={{0,1},{1,2},{2,3},{3,4},{4,5},{5,6},{6,7},{7,0},{8,9},{9,10},{10,1... | collective-permute-start | bytes 786440 | tf_op jit(solution)/shard_map/ppermute | solution.py:69
  66.1 1.5 all-to-all-done
  68.3 5.2 %all-gather.3.cloned.1.call-done.refs_8_.weights_hbm = bf16[2048,1280]{1,0:T(8,128)(2,1)} async-done(((bf16[128,1280]{1,0:T(8,128)(2,1)}), bf16[2048,1280]{1,0:T(8,128)(2,1)}) %all-gather.3.cloned.1.call-update) | async-done | bytes 5242896 | tf_op jit(solution)/shard_map/all_gather | solution.py:400
  73.5 2.8 %project.1 = (f32[256,256]{1,0:T(8,128)S(1)}, bf16[256,256]{1,0:T(8,128)(2,1)S(1)}) custom-call(s32[5]{0:T(128)S(1)} %stack.23.place_ref, bf16[128,256]{1,0:T(8,128)(2,1)S(1)} %get-tuple-element.26.hidden_ref, bf16[256,512]{1,0:T(8,128)(2,1)S(1)} %pad_maximum_fusion.refs_0_, bf16[256,512]{1,0:T(8,128)(2,1)S(1)} %collective-permute-done.2.refs_1_, ...), custom_call_target="tpu_custom_call" | custom-call | flops 536870912 | bytes 4194304 | tf_op jit(solution)/shard_map/project/pallas_call | solution.py:78
  76.4 4.9 %collective-permute-start.9 = (bf16[256,256]{1,0:T(8,128)(2,1)S(1)}, bf16[256,256]{1,0:T(8,128)(2,1)S(1)}, u32[]{:S(2)}, u32[]{:S(2)}) collective-permute-start(bf16[256,256]{1,0:T(8,128)(2,1)S(1)} %get-tuple-element.29), channel_id=1, source_target_pairs={{0,8},{8,0},{1,9},{9,1},{2,10},{10,2},{3,11},{11,3},{4,12},{12,4},... | collective-permute-start | bytes 393224 | tf_op jit(solution)/shard_map/ppermute | solution.py:65
  81.3 4.1 %collective-permute-done.9.recv_ref = bf16[256,256]{1,0:T(8,128)(2,1)S(1)} collective-permute-done((bf16[256,256]{1,0:T(8,128)(2,1)S(1)}, bf16[256,256]{1,0:T(8,128)(2,1)S(1)}, u32[]{:S(2)}, u32[]{:S(2)}) %collective-permute-start.9) | collective-permute-done | bytes 131104 | tf_op jit(solution)/shard_map/ppermute | solution.py:65
  86.2 23.2 %all_to_all.15 = bf16[8,128,256]{2,1,0:T(8,128)(2,1)S(1)} all-to-all(bf16[8,128,256]{2,1,0:T(8,128)(2,1)S(1)} %bitcast.19), channel_id=1, replica_groups=mesh['xl'=2,'y'=8,'core'=2,'xh'=2,'z'=8] {'z'}, dimensions={0} | all-to-all | bytes 1048576 | tf_op jit(solution)/shard_map/all_to_all | solution.py:459
  109.3 2.3 %gate_up.1 = (f32[128,896]{1,0:T(8,128)S(1)}, bf16[128,896]{1,0:T(8,128)(2,1)S(1)}) custom-call(bf16[1024,256]{1,0:T(8,128)(2,1)S(1)} %bitcast.18, bf16[1,2048]{1,0:T(2,128)(2,1)S(1)} %reshape.77.gain_ref, bf16[2048,1280]{1,0:T(8,128)(2,1)} %all-gather.3.cloned.1.call-done.refs_8_.weights_hbm), custom_call_target="tpu_custom_call" | custom-call | flops 402653184 | bytes 3145728 | tf_op jit(solution)/shard_map/gate_up/pallas_call | solution.py:78
  111.7 3.3 %collective-permute-start.10 = (bf16[128,896]{1,0:T(8,128)(2,1)S(1)}, bf16[128,896]{1,0:T(8,128)(2,1)S(1)}, u32[]{:S(2)}, u32[]{:S(2)}) collective-permute-start(bf16[128,896]{1,0:T(8,128)(2,1)S(1)} %get-tuple-element.34), channel_id=1, source_target_pairs={{0,256},{256,0},{1,257},{257,1},{2,258},{258,2},{3,259},{259,3},{4... | collective-permute-start | bytes 688136 | tf_op jit(solution)/shard_map/ppermute | solution.py:65
  114.9 1.0 all-gather.5.cloned.1.call-done.weights_hbm
  115.9 3.6 %collective-permute-done.10.recv_ref = bf16[128,896]{1,0:T(8,128)(2,1)S(1)} collective-permute-done((bf16[128,896]{1,0:T(8,128)(2,1)S(1)}, bf16[128,896]{1,0:T(8,128)(2,1)S(1)}, u32[]{:S(2)}, u32[]{:S(2)}) %collective-permute-start.10) | collective-permute-done | bytes 229408 | tf_op jit(solution)/shard_map/ppermute | solution.py:65
  119.6 3.8 %down.1 = bf16[256,1280]{1,0:T(8,128)(2,1)} custom-call(s32[5]{0:T(128)S(1)} %stack.23.place_ref, f32[128,896]{1,0:T(8,128)S(1)} %get-tuple-element.33.own_ref, bf16[128,896]{1,0:T(8,128)(2,1)S(1)} %collective-permute-done.10.recv_ref, bf16[128,256]{1,0:T(8,128)(2,1)S(1)} %get-tuple-element.35.residual_ref, ...), custom_call_target="tpu_custom_call" | custom-call | flops 402653184 | bytes 2097152 | tf_op jit(solution)/shard_map/down/pallas_call | solution.py:78
  123.4 6.9 %all-to-all-start.2 = ((bf16[32,8,1280]{2,1,0:T(8,128)(2,1)}), bf16[32,8,1280]{2,1,0:T(8,128)(2,1)S(1)}, u32[]{:S(2)}, u32[]{:S(2)}) async-start(bf16[32,8,1280]{2,1,0:T(8,128)(2,1)} %bitcast.11), calls=%async_computation.2 | async-start | bytes 1310720 | tf_op jit(solution)/shard_map/all_to_all | solution.py:483
  130.3 21.1 %all-to-all-done.2 = bf16[32,8,1280]{2,1,0:T(8,128)(2,1)S(1)} async-done(((bf16[32,8,1280]{2,1,0:T(8,128)(2,1)}), bf16[32,8,1280]{2,1,0:T(8,128)(2,1)S(1)}, u32[]{:S(2)}, u32[]{:S(2)}) %all-to-all-start.2) | async-done | bytes 655392 | tf_op jit(solution)/shard_map/all_to_all | solution.py:483
  151.3 1.6 %combine.1 = bf16[8,4096]{1,0:T(8,128)(2,1)} custom-call(s32[5]{0:T(128)S(1)} %stack.23.place_ref, f32[32,256]{1,0:T(8,128)S(1)} %copy.22.coefs_ref, bf16[256,1280]{1,0:T(8,128)(2,1)S(1)} %bitcast.17), custom_call_target="tpu_custom_call" | custom-call | flops 67108864 | bytes 1048576 | tf_op jit(solution)/shard_map/combine/pallas_call | solution.py:78
  (38 shorter events, 6.9 us)
Async XLA Ops:
  6.5 59.5 %copy-start.2 = (bf16[4096]{0:T(1024)(128)(2,1)S(1)}, bf16[4096]{0:T(1024)(128)(2,1)}, u32[]{:S(2)}) copy-start(bf16[4096]{0:T(1024)(128)(2,1)} %param.19) | copy-start | bytes 24580
  6.5 67.0 %all-gather.3.cloned.1.call-start = ((), (), s32[]{:S(2)}) async-start(), calls=%async_computation.3 | async-start | bytes 5570560 | tf_op jit(solution)/shard_map/all_gather | solution.py:400
  6.5 16.3 %collective-permute-start = (bf16[512,128]{1,0:T(8,128)(2,1)}, bf16[512,128]{1,0:T(8,128)(2,1)S(1)}, u32[]{:S(2)}, u32[]{:S(2)}) collective-permute-start(bf16[512,128]{1,0:T(8,128)(2,1)} %param.18), channel_id=1, source_target_pairs={{0,128},{1,96},{2,64},{3,32},{4,0},{5,224},{6,192},{7,160},{32,193... | collective-permute-start | bytes 393224 | tf_op jit(solution)/shard_map/ppermute | solution.py:334
  15.2 7.6 %collective-permute-start.1 = (bf16[128,512]{1,0:T(8,128)(2,1)}, bf16[128,512]{1,0:T(8,128)(2,1)S(1)}, u32[]{:S(2)}, u32[]{:S(2)}) collective-permute-start(bf16[128,512]{1,0:T(8,128)(2,1)} %attend.1), channel_id=1, source_target_pairs={{0,256},{256,0},{1,257},{257,1},{2,258},{258,2},{3,259},{259,3},{4... | collective-permute-start | bytes 393224 | tf_op jit(solution)/shard_map/ppermute | solution.py:65
  22.8 0.7 copy-start.1
  25.1 90.8 %all-gather.5.cloned.1.call-start = ((), (), s32[]{:S(2)}) async-start(), calls=%async_computation.4 | async-start | bytes 1671168 | tf_op jit(solution)/shard_map/all_gather | solution.py:402
  25.2 0.9 copy-start
  28.4 8.4 %collective-permute-start.2 = (bf16[256,512]{1,0:T(8,128)(2,1)S(1)}, bf16[256,512]{1,0:T(8,128)(2,1)S(1)}, u32[]{:S(2)}, u32[]{:S(2)}) collective-permute-start(bf16[256,512]{1,0:T(8,128)(2,1)S(1)} %pad_maximum_fusion.refs_0_), channel_id=1, source_target_pairs={{0,1},{1,2},{2,3},{3,4},{4,5},{5,6},{6,7},{7,0},{8,9},{9,10},{10,1... | collective-permute-start | bytes 786440 | tf_op jit(solution)/shard_map/ppermute | solution.py:69
  32.0 8.3 %collective-permute-start.3 = (bf16[256,512]{1,0:T(8,128)(2,1)S(1)}, bf16[256,512]{1,0:T(8,128)(2,1)S(1)}, u32[]{:S(2)}, u32[]{:S(2)}) collective-permute-start(bf16[256,512]{1,0:T(8,128)(2,1)S(1)} %pad_maximum_fusion.refs_0_), channel_id=1, source_target_pairs={{0,7},{1,0},{2,1},{3,2},{4,3},{5,4},{6,5},{7,6},{8,15},{9,8},{10,9... | collective-permute-start | bytes 786440 | tf_op jit(solution)/shard_map/ppermute | solution.py:69
  36.8 11.9 %collective-permute-start.4 = (bf16[256,512]{1,0:T(8,128)(2,1)S(1)}, bf16[256,512]{1,0:T(8,128)(2,1)S(1)}, u32[]{:S(2)}, u32[]{:S(2)}) collective-permute-start(bf16[256,512]{1,0:T(8,128)(2,1)S(1)} %collective-permute-done.2.refs_1_), channel_id=1, source_target_pairs={{0,1},{1,2},{2,3},{3,4},{4,5},{5,6},{6,7},{7,0},{8,9},{9,10},{10,1... | collective-permute-start | bytes 786440 | tf_op jit(solution)/shard_map/ppermute | solution.py:69
  40.3 18.9 %collective-permute-start.5 = (bf16[256,512]{1,0:T(8,128)(2,1)S(1)}, bf16[256,512]{1,0:T(8,128)(2,1)S(1)}, u32[]{:S(2)}, u32[]{:S(2)}) collective-permute-start(bf16[256,512]{1,0:T(8,128)(2,1)S(1)} %collective-permute-done.3.refs_2_), channel_id=1, source_target_pairs={{0,7},{1,0},{2,1},{3,2},{4,3},{5,4},{6,5},{7,6},{8,15},{9,8},{10,9... | collective-permute-start | bytes 786440 | tf_op jit(solution)/shard_map/ppermute | solution.py:69
  48.8 12.5 %collective-permute-start.6 = (bf16[256,512]{1,0:T(8,128)(2,1)S(1)}, bf16[256,512]{1,0:T(8,128)(2,1)S(1)}, u32[]{:S(2)}, u32[]{:S(2)}) collective-permute-start(bf16[256,512]{1,0:T(8,128)(2,1)S(1)} %collective-permute-done.4.refs_3_), channel_id=1, source_target_pairs={{0,1},{1,2},{2,3},{3,4},{4,5},{5,6},{6,7},{7,0},{8,9},{9,10},{10,1... | collective-permute-start | bytes 786440 | tf_op jit(solution)/shard_map/ppermute | solution.py:69
  50.7 16.9 %all-to-all-start = ((bf16[16,16,256]{2,1,0:T(8,128)(2,1)}), bf16[16,16,256]{2,1,0:T(8,128)(2,1)S(1)}, u32[]{:S(2)}, u32[]{:S(2)}) async-start(bf16[16,16,256]{2,1,0:T(8,128)(2,1)} %pad_maximum_fusion.1), calls=%async_computation | async-start | bytes 262144 | tf_op jit(solution)/shard_map/all_to_all | solution.py:409
  59.2 14.3 %collective-permute-start.7 = (bf16[256,512]{1,0:T(8,128)(2,1)S(1)}, bf16[256,512]{1,0:T(8,128)(2,1)S(1)}, u32[]{:S(2)}, u32[]{:S(2)}) collective-permute-start(bf16[256,512]{1,0:T(8,128)(2,1)S(1)} %collective-permute-done.5.refs_4_), channel_id=1, source_target_pairs={{0,7},{1,0},{2,1},{3,2},{4,3},{5,4},{6,5},{7,6},{8,15},{9,8},{10,9... | collective-permute-start | bytes 786440 | tf_op jit(solution)/shard_map/ppermute | solution.py:69
  61.3 12.2 %collective-permute-start.8 = (bf16[256,512]{1,0:T(8,128)(2,1)S(1)}, bf16[256,512]{1,0:T(8,128)(2,1)S(1)}, u32[]{:S(2)}, u32[]{:S(2)}) collective-permute-start(bf16[256,512]{1,0:T(8,128)(2,1)S(1)} %collective-permute-done.6.refs_5_), channel_id=1, source_target_pairs={{0,1},{1,2},{2,3},{3,4},{4,5},{5,6},{6,7},{7,0},{8,9},{9,10},{10,1... | collective-permute-start | bytes 786440 | tf_op jit(solution)/shard_map/ppermute | solution.py:69
  76.4 9.1 %collective-permute-start.9 = (bf16[256,256]{1,0:T(8,128)(2,1)S(1)}, bf16[256,256]{1,0:T(8,128)(2,1)S(1)}, u32[]{:S(2)}, u32[]{:S(2)}) collective-permute-start(bf16[256,256]{1,0:T(8,128)(2,1)S(1)} %get-tuple-element.29), channel_id=1, source_target_pairs={{0,8},{8,0},{1,9},{9,1},{2,10},{10,2},{3,11},{11,3},{4,12},{12,4},... | collective-permute-start | bytes 393224 | tf_op jit(solution)/shard_map/ppermute | solution.py:65
  111.7 7.9 %collective-permute-start.10 = (bf16[128,896]{1,0:T(8,128)(2,1)S(1)}, bf16[128,896]{1,0:T(8,128)(2,1)S(1)}, u32[]{:S(2)}, u32[]{:S(2)}) collective-permute-start(bf16[128,896]{1,0:T(8,128)(2,1)S(1)} %get-tuple-element.34), channel_id=1, source_target_pairs={{0,256},{256,0},{1,257},{257,1},{2,258},{258,2},{3,259},{259,3},{4... | collective-permute-start | bytes 688136 | tf_op jit(solution)/shard_map/ppermute | solution.py:65
  123.4 28.0 %all-to-all-start.2 = ((bf16[32,8,1280]{2,1,0:T(8,128)(2,1)}), bf16[32,8,1280]{2,1,0:T(8,128)(2,1)S(1)}, u32[]{:S(2)}, u32[]{:S(2)}) async-start(bf16[32,8,1280]{2,1,0:T(8,128)(2,1)} %bitcast.11), calls=%async_computation.2 | async-start | bytes 1310720 | tf_op jit(solution)/shard_map/all_to_all | solution.py:483
Sparse Core Ops, SparseCore 0:
  25.2 48.2 all-gather.2
  75.6 40.2 all-gather.4

commit v9 on v8

--- a/solution.py
+++ b/solution.py
@@ -252,11 +252,10 @@
     total = (own_ref[:, : 2 * HIDDEN] + recv_ref[:, : 2 * HIDDEN].astype(F32)) * inverse
     gate, up = total[:, :HIDDEN], total[:, HIDDEN:]
     activated = (gate / (1.0 + jnp.exp(-gate)) * up).astype(BF16)
-    to = lax.broadcasted_iota(jnp.int32, (2 * slots, slots), 0)
-    source = lax.broadcasted_iota(jnp.int32, (2 * slots, slots), 1)
-    twice = jnp.where(source == (to >> 3) * CAP + (to & 3), 1.0, 0.0).astype(BF16)
-    activated = jnp.dot(twice, activated, preferred_element_type=F32).astype(BF16)
-    first = (lax.broadcasted_iota(jnp.int32, (2 * slots, COLS), 0) & 4) == 0
+    to = lax.broadcasted_iota(jnp.int32, (2 * slots, 2 * slots), 0)
+    source = lax.broadcasted_iota(jnp.int32, (2 * slots, 2 * slots), 1)
+    wanted = ((to >> 2) & 1) * slots + (to >> 3) * CAP + (to & 3)
+    spread = jnp.where(source == wanted, 1.0, 0.0).astype(BF16)
 
     def columns(d):
         rhs = jnp.concatenate(
@@ -271,12 +270,13 @@
             ],
             axis=1,
         )
-        return jnp.dot(activated, rhs, preferred_element_type=F32)
+        return jnp.dot(activated, rhs, preferred_element_type=F32).astype(BF16)
 
     copy.wait()
     chunks = QUARTER // COLS
     for d in range(chunks):
-        out_ref[:, d * COLS : (d + 1) * COLS] = jnp.where(first, columns(d), columns(d + chunks)).astype(BF16)
+        both = jnp.concatenate([columns(d), columns(d + chunks)])
+        out_ref[:, d * COLS : (d + 1) * COLS] = jnp.dot(spread, both, preferred_element_type=F32).astype(BF16)
     residual = residual_ref[...].astype(F32)
     out_ref[:SLAB, QUARTER:] = jnp.where(xh == 0, residual, 0.0).astype(BF16)
     out_ref[SLAB:, QUARTER:] = jnp.where(xh == 1, residual, 0.0).astype(BF16)
@@ -289,23 +289,18 @@
     rest = coefs - high.astype(F32)
     middle = rest.astype(BF16)
     low = (rest - middle.astype(F32)).astype(BF16)
+    parts = jnp.concatenate([high, middle, low])
     rows, slots = 4 * ROWS, 2 * BLOCKS * ROWS
-    to = lax.broadcasted_iota(jnp.int32, (rows, slots), 0)
-    source = lax.broadcasted_iota(jnp.int32, (rows, slots), 1)
-    half, quarter, row = to >> 4, (to >> 3) & 1, to & 7
-    for k in range(QUARTER // COLS):
-        at = slice(k * COLS, (k + 1) * COLS)
-        wanted = (half * BLOCKS + xl * RING + quarter * (RING // 2) + k) * ROWS + row
-        picker = jnp.where(source == wanted, 1.0, 0.0).astype(BF16)
-        parts = returned_ref[:, at]
-        mixed = (
-            jnp.dot(picker, returned_ref[:, QUARTER:], preferred_element_type=F32)
-            + jnp.dot(high, parts, preferred_element_type=F32)
-            + (
-                jnp.dot(middle, parts, preferred_element_type=F32)
-                + jnp.dot(low, parts, preferred_element_type=F32)
-            )
-        )
+    chunks = QUARTER // COLS
+    to = lax.broadcasted_iota(jnp.int32, (chunks * rows, slots), 0)
+    source = lax.broadcasted_iota(jnp.int32, (chunks * rows, slots), 1)
+    chunk, half, quarter, row = to >> 5, (to >> 4) & 1, (to >> 3) & 1, to & 7
+    wanted = (half * BLOCKS + xl * RING + quarter * (RING // 2) + chunk) * ROWS + row
+    picker = jnp.where(source == wanted, 1.0, 0.0).astype(BF16)
+    residual = jnp.dot(picker, returned_ref[:, QUARTER:], preferred_element_type=F32)
+    for k in range(chunks):
+        sums = jnp.dot(parts, returned_ref[:, k * COLS : (k + 1) * COLS], preferred_element_type=F32)
+        mixed = residual[k * rows : (k + 1) * rows] + sums[:rows] + (sums[rows : 2 * rows] + sums[2 * rows :])
         for q in range(4):
             out_ref[:, q * QUARTER + k * COLS : q * QUARTER + (k + 1) * COLS] = mixed[
                 q * ROWS : (q + 1) * ROWS

time: 161 us -> 161 us (level)
  no operation moved by 1% of the time
where the time goes in v9:
time: 161 us; the launch traced here: 160 us
  starting transfers between devices  54.2 us (34%)
  waiting for transfers between devices  42.7 us (27%)
  blocking collectives  23.2 us (14%)
  Pallas kernels  19.5 us (12%)
  between operations  14.3 us (9%)
  other arithmetic  3.75 us (2%)
  local copies, waits for them, and re-layouts  2.41 us (1%)
    all_to_all x1, blocking collectives, per_device(): lax.all_to_all(rows_out.reshape(RING, 2 * BLOCKS * CAP, COLS), 'z', split...  23.2 us
    ppermute x7, starting transfers between devices, along_z(): lax.ppermute(block, 'z', [(i, (i + step) % RING) for i in range(RING)])  22.5 us
    all_to_all x1, waiting for transfers between devices, per_device(): lax.all_to_all(outward.reshape(2 * BLOCKS, 2 * CAP, QUARTER + COLS), PAIR...  21.1 us
    pallas_call x10, Pallas kernels, kernel_call(): pl.pallas_call(body, out_shape=[jax.ShapeDtypeStruct(shape, dtype) for sh...  19.5 us
    ppermute x3, starting transfers between devices, swap(): return lax.ppermute(block, axis, [(0, 1), (1, 0)])  11.6 us
    all_to_all x1, starting transfers between devices, per_device(): lax.all_to_all(outgoing, ('xl', 'z'), split_axis=0, concat_axis=0, tiled=...  8.53 us
    ppermute x3, waiting for transfers between devices, swap(): return lax.ppermute(block, axis, [(0, 1), (1, 0)])  7.76 us
    all_to_all x1, starting transfers between devices, per_device(): lax.all_to_all(outward.reshape(2 * BLOCKS, 2 * CAP, QUARTER + COLS), PAIR...  6.85 us
  transfers between devices with their start and end apart: 15, of which 10 were waited for; matrix products, arithmetic and copies ran while one was open for 3% of the time, Pallas kernels for 8%

profile of v9, /device:TPU:64, one launch (start us, length us, event | category | flops | bytes accessed | tf_op | source)
XLA Modules:
  0.0 160.0 jit_solution(8412777650925829496)
XLA Ops:
  6.5 4.7 %collective-permute-start = (bf16[512,128]{1,0:T(8,128)(2,1)}, bf16[512,128]{1,0:T(8,128)(2,1)S(1)}, u32[]{:S(2)}, u32[]{:S(2)}) collective-permute-start(bf16[512,128]{1,0:T(8,128)(2,1)} %param.18), channel_id=1, source_target_pairs={{0,128},{1,96},{2,64},{3,32},{4,0},{5,224},{6,192},{7,160},{32,193... | collective-permute-start | bytes 393224 | tf_op jit(solution)/shard_map/ppermute | solution.py:329
  11.9 3.3 %attend.1 = bf16[128,512]{1,0:T(8,128)(2,1)} custom-call(s32[1]{0:T(128)S(6)} %copy.24.start_ref, bf16[128,512]{1,0:T(8,128)(2,1)} %queries_hbm.1, bf16[1152,128]{1,0:T(8,128)(2,1)} %keys_hbm.1, bf16[1152,128]{1,0:T(8,128)(2,1)} %values_hbm.1), custom_call_target="tpu_custom_call" | custom-call | flops 301989888 | bytes 1048576 | tf_op jit(solution)/shard_map/attend/pallas_call | solution.py:78
  15.2 3.4 %collective-permute-start.1 = (bf16[128,512]{1,0:T(8,128)(2,1)}, bf16[128,512]{1,0:T(8,128)(2,1)S(1)}, u32[]{:S(2)}, u32[]{:S(2)}) collective-permute-start(bf16[128,512]{1,0:T(8,128)(2,1)} %attend.1), channel_id=1, source_target_pairs={{0,256},{256,0},{1,257},{257,1},{2,258},{258,2},{3,259},{259,3},{4... | collective-permute-start | bytes 393224 | tf_op jit(solution)/shard_map/ppermute | solution.py:65
  18.6 1.7 %pack_gate_up.1.started_hbm = bf16[128,1280]{1,0:T(8,128)(2,1)} custom-call(bf16[128,384]{1,0:T(8,128)(2,1)} %gate_hbm.1, bf16[128,384]{1,0:T(8,128)(2,1)} %up_hbm.1), custom_call_target="tpu_custom_call" | custom-call | bytes 393216 | tf_op jit(solution)/shard_map/pack_gate_up/pallas_call | solution.py:78
  20.3 2.5 %collective-permute-done.swapped_ref = bf16[512,128]{1,0:T(8,128)(2,1)S(1)} collective-permute-done((bf16[512,128]{1,0:T(8,128)(2,1)}, bf16[512,128]{1,0:T(8,128)(2,1)S(1)}, u32[]{:S(2)}, u32[]{:S(2)}) %collective-permute-start) | collective-permute-done | bytes 131104 | tf_op jit(solution)/shard_map/ppermute | solution.py:329
  23.5 1.6 %pack_out.1 = bf16[128,1280]{1,0:T(8,128)(2,1)} custom-call(bf16[512,128]{1,0:T(8,128)(2,1)} %copy-done.1, bf16[128,1280]{1,0:T(8,128)(2,1)} %pack_gate_up.1.started_hbm), custom_call_target="tpu_custom_call", output_to_operand_aliasing={{}: (1, {})} | custom-call | bytes 262144 | tf_op jit(solution)/shard_map/pack_out/pallas_call | solution.py:78
  27.5 0.9 pad_maximum_fusion.refs_0_
  28.4 1.9 %collective-permute-start.2 = (bf16[256,512]{1,0:T(8,128)(2,1)S(1)}, bf16[256,512]{1,0:T(8,128)(2,1)S(1)}, u32[]{:S(2)}, u32[]{:S(2)}) collective-permute-start(bf16[256,512]{1,0:T(8,128)(2,1)S(1)} %pad_maximum_fusion.refs_0_), channel_id=1, source_target_pairs={{0,1},{1,2},{2,3},{3,4},{4,5},{5,6},{6,7},{7,0},{8,9},{9,10},{10,1... | collective-permute-start | bytes 786440 | tf_op jit(solution)/shard_map/ppermute | solution.py:69
  30.5 1.5 pad_maximum_fusion.1
  32.0 3.9 %collective-permute-start.3 = (bf16[256,512]{1,0:T(8,128)(2,1)S(1)}, bf16[256,512]{1,0:T(8,128)(2,1)S(1)}, u32[]{:S(2)}, u32[]{:S(2)}) collective-permute-start(bf16[256,512]{1,0:T(8,128)(2,1)S(1)} %pad_maximum_fusion.refs_0_), channel_id=1, source_target_pairs={{0,7},{1,0},{2,1},{3,2},{4,3},{5,4},{6,5},{7,6},{8,15},{9,8},{10,9... | collective-permute-start | bytes 786440 | tf_op jit(solution)/shard_map/ppermute | solution.py:69
  36.8 2.1 %collective-permute-start.4 = (bf16[256,512]{1,0:T(8,128)(2,1)S(1)}, bf16[256,512]{1,0:T(8,128)(2,1)S(1)}, u32[]{:S(2)}, u32[]{:S(2)}) collective-permute-start(bf16[256,512]{1,0:T(8,128)(2,1)S(1)} %collective-permute-done.2.refs_1_), channel_id=1, source_target_pairs={{0,1},{1,2},{2,3},{3,4},{4,5},{5,6},{6,7},{7,0},{8,9},{9,10},{10,1... | collective-permute-start | bytes 786440 | tf_op jit(solution)/shard_map/ppermute | solution.py:69
  39.2 1.1 collective-permute-done.3.refs_2_
  40.3 6.8 %collective-permute-start.5 = (bf16[256,512]{1,0:T(8,128)(2,1)S(1)}, bf16[256,512]{1,0:T(8,128)(2,1)S(1)}, u32[]{:S(2)}, u32[]{:S(2)}) collective-permute-start(bf16[256,512]{1,0:T(8,128)(2,1)S(1)} %collective-permute-done.3.refs_2_), channel_id=1, source_target_pairs={{0,7},{1,0},{2,1},{3,2},{4,3},{5,4},{6,5},{7,6},{8,15},{9,8},{10,9... | collective-permute-start | bytes 786440 | tf_op jit(solution)/shard_map/ppermute | solution.py:69
  47.1 1.7 %collective-permute-done.4.refs_3_ = bf16[256,512]{1,0:T(8,128)(2,1)S(1)} collective-permute-done((bf16[256,512]{1,0:T(8,128)(2,1)S(1)}, bf16[256,512]{1,0:T(8,128)(2,1)S(1)}, u32[]{:S(2)}, u32[]{:S(2)}) %collective-permute-start.4) | collective-permute-done | bytes 262176 | tf_op jit(solution)/shard_map/ppermute | solution.py:69
  48.8 1.9 %collective-permute-start.6 = (bf16[256,512]{1,0:T(8,128)(2,1)S(1)}, bf16[256,512]{1,0:T(8,128)(2,1)S(1)}, u32[]{:S(2)}, u32[]{:S(2)}) collective-permute-start(bf16[256,512]{1,0:T(8,128)(2,1)S(1)} %collective-permute-done.4.refs_3_), channel_id=1, source_target_pairs={{0,1},{1,2},{2,3},{3,4},{4,5},{5,6},{6,7},{7,0},{8,9},{9,10},{10,1... | collective-permute-start | bytes 786440 | tf_op jit(solution)/shard_map/ppermute | solution.py:69
  50.7 8.5 %all-to-all-start = ((bf16[16,16,256]{2,1,0:T(8,128)(2,1)}), bf16[16,16,256]{2,1,0:T(8,128)(2,1)S(1)}, u32[]{:S(2)}, u32[]{:S(2)}) async-start(bf16[16,16,256]{2,1,0:T(8,128)(2,1)} %pad_maximum_fusion.1), calls=%async_computation | async-start | bytes 262144 | tf_op jit(solution)/shard_map/all_to_all | solution.py:404
  59.2 2.0 %collective-permute-start.7 = (bf16[256,512]{1,0:T(8,128)(2,1)S(1)}, bf16[256,512]{1,0:T(8,128)(2,1)S(1)}, u32[]{:S(2)}, u32[]{:S(2)}) collective-permute-start(bf16[256,512]{1,0:T(8,128)(2,1)S(1)} %collective-permute-done.5.refs_4_), channel_id=1, source_target_pairs={{0,7},{1,0},{2,1},{3,2},{4,3},{5,4},{6,5},{7,6},{8,15},{9,8},{10,9... | collective-permute-start | bytes 786440 | tf_op jit(solution)/shard_map/ppermute | solution.py:69
  61.3 3.8 %collective-permute-start.8 = (bf16[256,512]{1,0:T(8,128)(2,1)S(1)}, bf16[256,512]{1,0:T(8,128)(2,1)S(1)}, u32[]{:S(2)}, u32[]{:S(2)}) collective-permute-start(bf16[256,512]{1,0:T(8,128)(2,1)S(1)} %collective-permute-done.6.refs_5_), channel_id=1, source_target_pairs={{0,1},{1,2},{2,3},{3,4},{4,5},{5,6},{6,7},{7,0},{8,9},{9,10},{10,1... | collective-permute-start | bytes 786440 | tf_op jit(solution)/shard_map/ppermute | solution.py:69
  66.1 1.5 all-to-all-done
  68.3 5.2 %all-gather.3.cloned.1.call-done.refs_8_.weights_hbm = bf16[2048,1280]{1,0:T(8,128)(2,1)} async-done(((bf16[128,1280]{1,0:T(8,128)(2,1)}), bf16[2048,1280]{1,0:T(8,128)(2,1)}) %all-gather.3.cloned.1.call-update) | async-done | bytes 5242896 | tf_op jit(solution)/shard_map/all_gather | solution.py:395
  73.5 2.8 %project.1 = (f32[256,256]{1,0:T(8,128)S(1)}, bf16[256,256]{1,0:T(8,128)(2,1)S(1)}) custom-call(s32[5]{0:T(128)S(1)} %stack.23.place_ref, bf16[128,256]{1,0:T(8,128)(2,1)S(1)} %get-tuple-element.26.hidden_ref, bf16[256,512]{1,0:T(8,128)(2,1)S(1)} %pad_maximum_fusion.refs_0_, bf16[256,512]{1,0:T(8,128)(2,1)S(1)} %collective-permute-done.2.refs_1_, ...), custom_call_target="tpu_custom_call" | custom-call | flops 536870912 | bytes 4194304 | tf_op jit(solution)/shard_map/project/pallas_call | solution.py:78
  76.4 4.9 %collective-permute-start.9 = (bf16[256,256]{1,0:T(8,128)(2,1)S(1)}, bf16[256,256]{1,0:T(8,128)(2,1)S(1)}, u32[]{:S(2)}, u32[]{:S(2)}) collective-permute-start(bf16[256,256]{1,0:T(8,128)(2,1)S(1)} %get-tuple-element.29), channel_id=1, source_target_pairs={{0,8},{8,0},{1,9},{9,1},{2,10},{10,2},{3,11},{11,3},{4,12},{12,4},... | collective-permute-start | bytes 393224 | tf_op jit(solution)/shard_map/ppermute | solution.py:65
  81.3 4.1 %collective-permute-done.9.recv_ref = bf16[256,256]{1,0:T(8,128)(2,1)S(1)} collective-permute-done((bf16[256,256]{1,0:T(8,128)(2,1)S(1)}, bf16[256,256]{1,0:T(8,128)(2,1)S(1)}, u32[]{:S(2)}, u32[]{:S(2)}) %collective-permute-start.9) | collective-permute-done | bytes 131104 | tf_op jit(solution)/shard_map/ppermute | solution.py:65
  86.2 23.2 %all_to_all.15 = bf16[8,128,256]{2,1,0:T(8,128)(2,1)S(1)} all-to-all(bf16[8,128,256]{2,1,0:T(8,128)(2,1)S(1)} %bitcast.19), channel_id=1, replica_groups=mesh['xl'=2,'y'=8,'core'=2,'xh'=2,'z'=8] {'z'}, dimensions={0} | all-to-all | bytes 1048576 | tf_op jit(solution)/shard_map/all_to_all | solution.py:454
  109.3 2.3 %gate_up.1 = (f32[128,896]{1,0:T(8,128)S(1)}, bf16[128,896]{1,0:T(8,128)(2,1)S(1)}) custom-call(bf16[1024,256]{1,0:T(8,128)(2,1)S(1)} %bitcast.18, bf16[1,2048]{1,0:T(2,128)(2,1)S(1)} %reshape.77.gain_ref, bf16[2048,1280]{1,0:T(8,128)(2,1)} %all-gather.3.cloned.1.call-done.refs_8_.weights_hbm), custom_call_target="tpu_custom_call" | custom-call | flops 402653184 | bytes 3145728 | tf_op jit(solution)/shard_map/gate_up/pallas_call | solution.py:78
  111.7 3.3 %collective-permute-start.10 = (bf16[128,896]{1,0:T(8,128)(2,1)S(1)}, bf16[128,896]{1,0:T(8,128)(2,1)S(1)}, u32[]{:S(2)}, u32[]{:S(2)}) collective-permute-start(bf16[128,896]{1,0:T(8,128)(2,1)S(1)} %get-tuple-element.34), channel_id=1, source_target_pairs={{0,256},{256,0},{1,257},{257,1},{2,258},{258,2},{3,259},{259,3},{4... | collective-permute-start | bytes 688136 | tf_op jit(solution)/shard_map/ppermute | solution.py:65
  114.9 1.0 all-gather.5.cloned.1.call-done.weights_hbm
  115.9 3.6 %collective-permute-done.10.recv_ref = bf16[128,896]{1,0:T(8,128)(2,1)S(1)} collective-permute-done((bf16[128,896]{1,0:T(8,128)(2,1)S(1)}, bf16[128,896]{1,0:T(8,128)(2,1)S(1)}, u32[]{:S(2)}, u32[]{:S(2)}) %collective-permute-start.10) | collective-permute-done | bytes 229408 | tf_op jit(solution)/shard_map/ppermute | solution.py:65
  119.6 4.2 %down.1 = bf16[256,1280]{1,0:T(8,128)(2,1)} custom-call(s32[5]{0:T(128)S(1)} %stack.23.place_ref, f32[128,896]{1,0:T(8,128)S(1)} %get-tuple-element.33.own_ref, bf16[128,896]{1,0:T(8,128)(2,1)S(1)} %collective-permute-done.10.recv_ref, bf16[128,256]{1,0:T(8,128)(2,1)S(1)} %get-tuple-element.35.residual_ref, ...), custom_call_target="tpu_custom_call" | custom-call | flops 402653184 | bytes 2097152 | tf_op jit(solution)/shard_map/down/pallas_call | solution.py:78
  123.8 6.8 %all-to-all-start.2 = ((bf16[32,8,1280]{2,1,0:T(8,128)(2,1)}), bf16[32,8,1280]{2,1,0:T(8,128)(2,1)S(1)}, u32[]{:S(2)}, u32[]{:S(2)}) async-start(bf16[32,8,1280]{2,1,0:T(8,128)(2,1)} %bitcast.11), calls=%async_computation.2 | async-start | bytes 1310720 | tf_op jit(solution)/shard_map/all_to_all | solution.py:478
  130.7 21.1 %all-to-all-done.2 = bf16[32,8,1280]{2,1,0:T(8,128)(2,1)S(1)} async-done(((bf16[32,8,1280]{2,1,0:T(8,128)(2,1)}), bf16[32,8,1280]{2,1,0:T(8,128)(2,1)S(1)}, u32[]{:S(2)}, u32[]{:S(2)}) %all-to-all-start.2) | async-done | bytes 655392 | tf_op jit(solution)/shard_map/all_to_all | solution.py:478
  151.7 1.4 combine.1
  (38 shorter events, 6.9 us)
Async XLA Ops:
  6.5 59.5 %copy-start.2 = (bf16[4096]{0:T(1024)(128)(2,1)S(1)}, bf16[4096]{0:T(1024)(128)(2,1)}, u32[]{:S(2)}) copy-start(bf16[4096]{0:T(1024)(128)(2,1)} %param.19) | copy-start | bytes 24580
  6.5 67.0 %all-gather.3.cloned.1.call-start = ((), (), s32[]{:S(2)}) async-start(), calls=%async_computation.3 | async-start | bytes 5570560 | tf_op jit(solution)/shard_map/all_gather | solution.py:395
  6.5 16.3 %collective-permute-start = (bf16[512,128]{1,0:T(8,128)(2,1)}, bf16[512,128]{1,0:T(8,128)(2,1)S(1)}, u32[]{:S(2)}, u32[]{:S(2)}) collective-permute-start(bf16[512,128]{1,0:T(8,128)(2,1)} %param.18), channel_id=1, source_target_pairs={{0,128},{1,96},{2,64},{3,32},{4,0},{5,224},{6,192},{7,160},{32,193... | collective-permute-start | bytes 393224 | tf_op jit(solution)/shard_map/ppermute | solution.py:329
  15.2 7.6 %collective-permute-start.1 = (bf16[128,512]{1,0:T(8,128)(2,1)}, bf16[128,512]{1,0:T(8,128)(2,1)S(1)}, u32[]{:S(2)}, u32[]{:S(2)}) collective-permute-start(bf16[128,512]{1,0:T(8,128)(2,1)} %attend.1), channel_id=1, source_target_pairs={{0,256},{256,0},{1,257},{257,1},{2,258},{258,2},{3,259},{259,3},{4... | collective-permute-start | bytes 393224 | tf_op jit(solution)/shard_map/ppermute | solution.py:65
  22.8 0.7 copy-start.1
  25.1 90.8 %all-gather.5.cloned.1.call-start = ((), (), s32[]{:S(2)}) async-start(), calls=%async_computation.4 | async-start | bytes 1671168 | tf_op jit(solution)/shard_map/all_gather | solution.py:397
  25.2 0.9 copy-start
  28.4 8.4 %collective-permute-start.2 = (bf16[256,512]{1,0:T(8,128)(2,1)S(1)}, bf16[256,512]{1,0:T(8,128)(2,1)S(1)}, u32[]{:S(2)}, u32[]{:S(2)}) collective-permute-start(bf16[256,512]{1,0:T(8,128)(2,1)S(1)} %pad_maximum_fusion.refs_0_), channel_id=1, source_target_pairs={{0,1},{1,2},{2,3},{3,4},{4,5},{5,6},{6,7},{7,0},{8,9},{9,10},{10,1... | collective-permute-start | bytes 786440 | tf_op jit(solution)/shard_map/ppermute | solution.py:69
  32.0 8.3 %collective-permute-start.3 = (bf16[256,512]{1,0:T(8,128)(2,1)S(1)}, bf16[256,512]{1,0:T(8,128)(2,1)S(1)}, u32[]{:S(2)}, u32[]{:S(2)}) collective-permute-start(bf16[256,512]{1,0:T(8,128)(2,1)S(1)} %pad_maximum_fusion.refs_0_), channel_id=1, source_target_pairs={{0,7},{1,0},{2,1},{3,2},{4,3},{5,4},{6,5},{7,6},{8,15},{9,8},{10,9... | collective-permute-start | bytes 786440 | tf_op jit(solution)/shard_map/ppermute | solution.py:69
  36.8 11.9 %collective-permute-start.4 = (bf16[256,512]{1,0:T(8,128)(2,1)S(1)}, bf16[256,512]{1,0:T(8,128)(2,1)S(1)}, u32[]{:S(2)}, u32[]{:S(2)}) collective-permute-start(bf16[256,512]{1,0:T(8,128)(2,1)S(1)} %collective-permute-done.2.refs_1_), channel_id=1, source_target_pairs={{0,1},{1,2},{2,3},{3,4},{4,5},{5,6},{6,7},{7,0},{8,9},{9,10},{10,1... | collective-permute-start | bytes 786440 | tf_op jit(solution)/shard_map/ppermute | solution.py:69
  40.3 18.9 %collective-permute-start.5 = (bf16[256,512]{1,0:T(8,128)(2,1)S(1)}, bf16[256,512]{1,0:T(8,128)(2,1)S(1)}, u32[]{:S(2)}, u32[]{:S(2)}) collective-permute-start(bf16[256,512]{1,0:T(8,128)(2,1)S(1)} %collective-permute-done.3.refs_2_), channel_id=1, source_target_pairs={{0,7},{1,0},{2,1},{3,2},{4,3},{5,4},{6,5},{7,6},{8,15},{9,8},{10,9... | collective-permute-start | bytes 786440 | tf_op jit(solution)/shard_map/ppermute | solution.py:69
  48.8 12.5 %collective-permute-start.6 = (bf16[256,512]{1,0:T(8,128)(2,1)S(1)}, bf16[256,512]{1,0:T(8,128)(2,1)S(1)}, u32[]{:S(2)}, u32[]{:S(2)}) collective-permute-start(bf16[256,512]{1,0:T(8,128)(2,1)S(1)} %collective-permute-done.4.refs_3_), channel_id=1, source_target_pairs={{0,1},{1,2},{2,3},{3,4},{4,5},{5,6},{6,7},{7,0},{8,9},{9,10},{10,1... | collective-permute-start | bytes 786440 | tf_op jit(solution)/shard_map/ppermute | solution.py:69
  50.7 16.9 %all-to-all-start = ((bf16[16,16,256]{2,1,0:T(8,128)(2,1)}), bf16[16,16,256]{2,1,0:T(8,128)(2,1)S(1)}, u32[]{:S(2)}, u32[]{:S(2)}) async-start(bf16[16,16,256]{2,1,0:T(8,128)(2,1)} %pad_maximum_fusion.1), calls=%async_computation | async-start | bytes 262144 | tf_op jit(solution)/shard_map/all_to_all | solution.py:404
  59.2 14.3 %collective-permute-start.7 = (bf16[256,512]{1,0:T(8,128)(2,1)S(1)}, bf16[256,512]{1,0:T(8,128)(2,1)S(1)}, u32[]{:S(2)}, u32[]{:S(2)}) collective-permute-start(bf16[256,512]{1,0:T(8,128)(2,1)S(1)} %collective-permute-done.5.refs_4_), channel_id=1, source_target_pairs={{0,7},{1,0},{2,1},{3,2},{4,3},{5,4},{6,5},{7,6},{8,15},{9,8},{10,9... | collective-permute-start | bytes 786440 | tf_op jit(solution)/shard_map/ppermute | solution.py:69
  61.3 12.2 %collective-permute-start.8 = (bf16[256,512]{1,0:T(8,128)(2,1)S(1)}, bf16[256,512]{1,0:T(8,128)(2,1)S(1)}, u32[]{:S(2)}, u32[]{:S(2)}) collective-permute-start(bf16[256,512]{1,0:T(8,128)(2,1)S(1)} %collective-permute-done.6.refs_5_), channel_id=1, source_target_pairs={{0,1},{1,2},{2,3},{3,4},{4,5},{5,6},{6,7},{7,0},{8,9},{9,10},{10,1... | collective-permute-start | bytes 786440 | tf_op jit(solution)/shard_map/ppermute | solution.py:69
  76.4 9.1 %collective-permute-start.9 = (bf16[256,256]{1,0:T(8,128)(2,1)S(1)}, bf16[256,256]{1,0:T(8,128)(2,1)S(1)}, u32[]{:S(2)}, u32[]{:S(2)}) collective-permute-start(bf16[256,256]{1,0:T(8,128)(2,1)S(1)} %get-tuple-element.29), channel_id=1, source_target_pairs={{0,8},{8,0},{1,9},{9,1},{2,10},{10,2},{3,11},{11,3},{4,12},{12,4},... | collective-permute-start | bytes 393224 | tf_op jit(solution)/shard_map/ppermute | solution.py:65
  111.7 7.9 %collective-permute-start.10 = (bf16[128,896]{1,0:T(8,128)(2,1)S(1)}, bf16[128,896]{1,0:T(8,128)(2,1)S(1)}, u32[]{:S(2)}, u32[]{:S(2)}) collective-permute-start(bf16[128,896]{1,0:T(8,128)(2,1)S(1)} %get-tuple-element.34), channel_id=1, source_target_pairs={{0,256},{256,0},{1,257},{257,1},{2,258},{258,2},{3,259},{259,3},{4... | collective-permute-start | bytes 688136 | tf_op jit(solution)/shard_map/ppermute | solution.py:65
  123.8 28.0 %all-to-all-start.2 = ((bf16[32,8,1280]{2,1,0:T(8,128)(2,1)}), bf16[32,8,1280]{2,1,0:T(8,128)(2,1)S(1)}, u32[]{:S(2)}, u32[]{:S(2)}) async-start(bf16[32,8,1280]{2,1,0:T(8,128)(2,1)} %bitcast.11), calls=%async_computation.2 | async-start | bytes 1310720 | tf_op jit(solution)/shard_map/all_to_all | solution.py:478
Sparse Core Ops, SparseCore 0:
  25.2 48.2 all-gather.2
  75.6 40.2 all-gather.4

commit v10 on v9

--- a/solution.py
+++ b/solution.py
@@ -40,9 +40,9 @@
     ]
     for copy in copies:
         copy.start()
-    for copy in copies:
+    for copy in copies[:2]:
         copy.wait()
-    keys, values = keys_ref[...], values_ref[...]
+    keys = keys_ref[...]
     size = keys.shape[1]
     shape = (2 * SLAB, keys.shape[0])
     position = start_ref[0] + (lax.broadcasted_iota(jnp.int32, shape, 0) & (SLAB - 1))
@@ -56,6 +56,9 @@
         scores = jnp.where(visible, scores, -1e30)
         exp_scores = jnp.exp(scores - jnp.max(scores, axis=1, keepdims=True))
         totals = jnp.sum(exp_scores, axis=1, keepdims=True)
+        if pair == 0:
+            copies[2].wait()
+        values = values_ref[...]
         context = (jnp.dot(exp_scores.astype(BF16), values, preferred_element_type=F32) / totals).astype(BF16)
         out_ref[:, first] = context[:SLAB]
         out_ref[:, second] = context[SLAB:]
@@ -102,18 +105,19 @@
     whole.wait()
 
 
-def pack_out_kernel(swapped_ref, started_hbm, packed_hbm, sems):
-    copies = [
-        pltpu.make_async_copy(
-            swapped_ref.at[pl.ds(j * 128, 128)],
-            packed_hbm.at[:, pl.ds(2 * HIDDEN + j * 128, 128)],
-            sems.at[j],
-        )
-        for j in range(HEADS_WIDE // 128)
-    ]
-    for copy in copies:
+def pack_out_kernel(swapped_hbm, started_hbm, packed_hbm, held, in_sems, out_sems):
+    arriving, leaving = [], []
+    for j in range(HEADS_WIDE // 128):
+        at = pl.ds(j * 128, 128)
+        to = packed_hbm.at[:, pl.ds(2 * HIDDEN + j * 128, 128)]
+        arriving.append(pltpu.make_async_copy(swapped_hbm.at[at], held.at[at], in_sems.at[j]))
+        leaving.append(pltpu.make_async_copy(held.at[at], to, out_sems.at[j]))
+    for copy in arriving:
         copy.start()
-    for copy in copies:
+    for arrived, copy in zip(arriving, leaving):
+        arrived.wait()
+        copy.start()
+    for copy in leaving:
         copy.wait()
 
 
@@ -252,10 +256,11 @@
     total = (own_ref[:, : 2 * HIDDEN] + recv_ref[:, : 2 * HIDDEN].astype(F32)) * inverse
     gate, up = total[:, :HIDDEN], total[:, HIDDEN:]
     activated = (gate / (1.0 + jnp.exp(-gate)) * up).astype(BF16)
-    to = lax.broadcasted_iota(jnp.int32, (2 * slots, 2 * slots), 0)
-    source = lax.broadcasted_iota(jnp.int32, (2 * slots, 2 * slots), 1)
-    wanted = ((to >> 2) & 1) * slots + (to >> 3) * CAP + (to & 3)
-    spread = jnp.where(source == wanted, 1.0, 0.0).astype(BF16)
+    to = lax.broadcasted_iota(jnp.int32, (2 * slots, slots), 0)
+    source = lax.broadcasted_iota(jnp.int32, (2 * slots, slots), 1)
+    twice = jnp.where(source == (to >> 3) * CAP + (to & 3), 1.0, 0.0).astype(BF16)
+    activated = jnp.dot(twice, activated, preferred_element_type=F32).astype(BF16)
+    first = (lax.broadcasted_iota(jnp.int32, (2 * slots, COLS), 0) & 4) == 0
 
     def columns(d):
         rhs = jnp.concatenate(
@@ -270,13 +275,12 @@
             ],
             axis=1,
         )
-        return jnp.dot(activated, rhs, preferred_element_type=F32).astype(BF16)
+        return jnp.dot(activated, rhs, preferred_element_type=F32)
 
     copy.wait()
     chunks = QUARTER // COLS
     for d in range(chunks):
-        both = jnp.concatenate([columns(d), columns(d + chunks)])
-        out_ref[:, d * COLS : (d + 1) * COLS] = jnp.dot(spread, both, preferred_element_type=F32).astype(BF16)
+        out_ref[:, d * COLS : (d + 1) * COLS] = jnp.where(first, columns(d), columns(d + chunks)).astype(BF16)
     residual = residual_ref[...].astype(F32)
     out_ref[:SLAB, QUARTER:] = jnp.where(xh == 0, residual, 0.0).astype(BF16)
     out_ref[SLAB:, QUARTER:] = jnp.where(xh == 1, residual, 0.0).astype(BF16)
@@ -383,11 +387,11 @@
         pack_out_kernel,
         [((128, 2 * HIDDEN + HEADS_WIDE), BF16)],
         (swapped, started),
-        "vh",
+        "hh",
         0,
         4 * 128 * 512,
         "pack_out",
-        [pltpu.SemaphoreType.DMA((HEADS_WIDE // 128,))],
+        [pltpu.VMEM((HEADS_WIDE, 128), BF16)] + [pltpu.SemaphoreType.DMA((HEADS_WIDE // 128,))] * 2,
         "h",
         vmem=MOST_VMEM_BYTES,
         aliases={1: 0},

time: 161 us -> 161 us (level)
  no operation moved by 1% of the time
where the time goes in v10:
time: 161 us; the launch traced here: 160 us
  starting transfers between devices  54 us (34%)
  waiting for transfers between devices  42.9 us (27%)
  blocking collectives  23.1 us (14%)
  Pallas kernels  19.1 us (12%)
  between operations  14.3 us (9%)
  other arithmetic  3.75 us (2%)
  local copies, waits for them, and re-layouts  2.41 us (1%)
    all_to_all x1, blocking collectives, per_device(): lax.all_to_all(rows_out.reshape(RING, 2 * BLOCKS * CAP, COLS), 'z', split...  23.1 us
    ppermute x7, starting transfers between devices, along_z(): lax.ppermute(block, 'z', [(i, (i + step) % RING) for i in range(RING)])  22.4 us
    all_to_all x1, waiting for transfers between devices, per_device(): lax.all_to_all(outward.reshape(2 * BLOCKS, 2 * CAP, QUARTER + COLS), PAIR...  21.1 us
    pallas_call x10, Pallas kernels, kernel_call(): pl.pallas_call(body, out_shape=[jax.ShapeDtypeStruct(shape, dtype) for sh...  19.1 us
    ppermute x3, starting transfers between devices, swap(): return lax.ppermute(block, axis, [(0, 1), (1, 0)])  11.5 us
    all_to_all x1, starting transfers between devices, per_device(): lax.all_to_all(outgoing, ('xl', 'z'), split_axis=0, concat_axis=0, tiled=...  8.53 us
    ppermute x3, waiting for transfers between devices, swap(): return lax.ppermute(block, axis, [(0, 1), (1, 0)])  7.89 us
    all_to_all x1, starting transfers between devices, per_device(): lax.all_to_all(outward.reshape(2 * BLOCKS, 2 * CAP, QUARTER + COLS), PAIR...  6.81 us
  transfers between devices with their start and end apart: 15, of which 10 were waited for; matrix products, arithmetic and copies ran while one was open for 3% of the time, Pallas kernels for 8%

profile of v10, /device:TPU:64, one launch (start us, length us, event | category | flops | bytes accessed | tf_op | source)
XLA Modules:
  0.0 159.6 jit_solution(2716112913810796317)
XLA Ops:
  6.5 4.7 %collective-permute-start = (bf16[512,128]{1,0:T(8,128)(2,1)}, bf16[512,128]{1,0:T(8,128)(2,1)S(1)}, u32[]{:S(2)}, u32[]{:S(2)}) collective-permute-start(bf16[512,128]{1,0:T(8,128)(2,1)} %param.18), channel_id=1, source_target_pairs={{0,128},{1,96},{2,64},{3,32},{4,0},{5,224},{6,192},{7,160},{32,193... | collective-permute-start | bytes 393224 | tf_op jit(solution)/shard_map/ppermute | solution.py:333
  11.9 3.4 %attend.1 = bf16[128,512]{1,0:T(8,128)(2,1)} custom-call(s32[1]{0:T(128)S(6)} %copy.24.start_ref, bf16[128,512]{1,0:T(8,128)(2,1)} %queries_hbm.1, bf16[1152,128]{1,0:T(8,128)(2,1)} %keys_hbm.1, bf16[1152,128]{1,0:T(8,128)(2,1)} %values_hbm.1), custom_call_target="tpu_custom_call" | custom-call | flops 301989888 | bytes 1048576 | tf_op jit(solution)/shard_map/attend/pallas_call | solution.py:81
  15.3 3.4 %collective-permute-start.1 = (bf16[128,512]{1,0:T(8,128)(2,1)}, bf16[128,512]{1,0:T(8,128)(2,1)S(1)}, u32[]{:S(2)}, u32[]{:S(2)}) collective-permute-start(bf16[128,512]{1,0:T(8,128)(2,1)} %attend.1), channel_id=1, source_target_pairs={{0,256},{256,0},{1,257},{257,1},{2,258},{258,2},{3,259},{259,3},{4... | collective-permute-start | bytes 393224 | tf_op jit(solution)/shard_map/ppermute | solution.py:68
  18.7 1.7 %pack_gate_up.1.started_hbm = bf16[128,1280]{1,0:T(8,128)(2,1)} custom-call(bf16[128,384]{1,0:T(8,128)(2,1)} %gate_hbm.1, bf16[128,384]{1,0:T(8,128)(2,1)} %up_hbm.1), custom_call_target="tpu_custom_call" | custom-call | bytes 393216 | tf_op jit(solution)/shard_map/pack_gate_up/pallas_call | solution.py:81
  20.4 2.4 %collective-permute-done.swapped_hbm = bf16[512,128]{1,0:T(8,128)(2,1)S(1)} collective-permute-done((bf16[512,128]{1,0:T(8,128)(2,1)}, bf16[512,128]{1,0:T(8,128)(2,1)S(1)}, u32[]{:S(2)}, u32[]{:S(2)}) %collective-permute-start) | collective-permute-done | bytes 131104 | tf_op jit(solution)/shard_map/ppermute | solution.py:333
  23.5 1.5 pack_out.1
  28.3 1.9 %collective-permute-start.2 = (bf16[256,512]{1,0:T(8,128)(2,1)S(1)}, bf16[256,512]{1,0:T(8,128)(2,1)S(1)}, u32[]{:S(2)}, u32[]{:S(2)}) collective-permute-start(bf16[256,512]{1,0:T(8,128)(2,1)S(1)} %pad_maximum_fusion.refs_0_), channel_id=1, source_target_pairs={{0,1},{1,2},{2,3},{3,4},{4,5},{5,6},{6,7},{7,0},{8,9},{9,10},{10,1... | collective-permute-start | bytes 786440 | tf_op jit(solution)/shard_map/ppermute | solution.py:72
  30.4 1.5 pad_maximum_fusion.1
  31.9 3.9 %collective-permute-start.3 = (bf16[256,512]{1,0:T(8,128)(2,1)S(1)}, bf16[256,512]{1,0:T(8,128)(2,1)S(1)}, u32[]{:S(2)}, u32[]{:S(2)}) collective-permute-start(bf16[256,512]{1,0:T(8,128)(2,1)S(1)} %pad_maximum_fusion.refs_0_), channel_id=1, source_target_pairs={{0,7},{1,0},{2,1},{3,2},{4,3},{5,4},{6,5},{7,6},{8,15},{9,8},{10,9... | collective-permute-start | bytes 786440 | tf_op jit(solution)/shard_map/ppermute | solution.py:72
  35.8 1.0 collective-permute-done.2.refs_1_
  36.8 2.0 %collective-permute-start.4 = (bf16[256,512]{1,0:T(8,128)(2,1)S(1)}, bf16[256,512]{1,0:T(8,128)(2,1)S(1)}, u32[]{:S(2)}, u32[]{:S(2)}) collective-permute-start(bf16[256,512]{1,0:T(8,128)(2,1)S(1)} %collective-permute-done.2.refs_1_), channel_id=1, source_target_pairs={{0,1},{1,2},{2,3},{3,4},{4,5},{5,6},{6,7},{7,0},{8,9},{9,10},{10,1... | collective-permute-start | bytes 786440 | tf_op jit(solution)/shard_map/ppermute | solution.py:72
  39.1 1.1 collective-permute-done.3.refs_2_
  40.2 6.8 %collective-permute-start.5 = (bf16[256,512]{1,0:T(8,128)(2,1)S(1)}, bf16[256,512]{1,0:T(8,128)(2,1)S(1)}, u32[]{:S(2)}, u32[]{:S(2)}) collective-permute-start(bf16[256,512]{1,0:T(8,128)(2,1)S(1)} %collective-permute-done.3.refs_2_), channel_id=1, source_target_pairs={{0,7},{1,0},{2,1},{3,2},{4,3},{5,4},{6,5},{7,6},{8,15},{9,8},{10,9... | collective-permute-start | bytes 786440 | tf_op jit(solution)/shard_map/ppermute | solution.py:72
  47.0 1.7 %collective-permute-done.4.refs_3_ = bf16[256,512]{1,0:T(8,128)(2,1)S(1)} collective-permute-done((bf16[256,512]{1,0:T(8,128)(2,1)S(1)}, bf16[256,512]{1,0:T(8,128)(2,1)S(1)}, u32[]{:S(2)}, u32[]{:S(2)}) %collective-permute-start.4) | collective-permute-done | bytes 262176 | tf_op jit(solution)/shard_map/ppermute | solution.py:72
  48.6 1.9 %collective-permute-start.6 = (bf16[256,512]{1,0:T(8,128)(2,1)S(1)}, bf16[256,512]{1,0:T(8,128)(2,1)S(1)}, u32[]{:S(2)}, u32[]{:S(2)}) collective-permute-start(bf16[256,512]{1,0:T(8,128)(2,1)S(1)} %collective-permute-done.4.refs_3_), channel_id=1, source_target_pairs={{0,1},{1,2},{2,3},{3,4},{4,5},{5,6},{6,7},{7,0},{8,9},{9,10},{10,1... | collective-permute-start | bytes 786440 | tf_op jit(solution)/shard_map/ppermute | solution.py:72
  50.6 8.5 %all-to-all-start = ((bf16[16,16,256]{2,1,0:T(8,128)(2,1)}), bf16[16,16,256]{2,1,0:T(8,128)(2,1)S(1)}, u32[]{:S(2)}, u32[]{:S(2)}) async-start(bf16[16,16,256]{2,1,0:T(8,128)(2,1)} %pad_maximum_fusion.1), calls=%async_computation | async-start | bytes 262144 | tf_op jit(solution)/shard_map/all_to_all | solution.py:408
  59.1 2.0 %collective-permute-start.7 = (bf16[256,512]{1,0:T(8,128)(2,1)S(1)}, bf16[256,512]{1,0:T(8,128)(2,1)S(1)}, u32[]{:S(2)}, u32[]{:S(2)}) collective-permute-start(bf16[256,512]{1,0:T(8,128)(2,1)S(1)} %collective-permute-done.5.refs_4_), channel_id=1, source_target_pairs={{0,7},{1,0},{2,1},{3,2},{4,3},{5,4},{6,5},{7,6},{8,15},{9,8},{10,9... | collective-permute-start | bytes 786440 | tf_op jit(solution)/shard_map/ppermute | solution.py:72
  61.2 3.8 %collective-permute-start.8 = (bf16[256,512]{1,0:T(8,128)(2,1)S(1)}, bf16[256,512]{1,0:T(8,128)(2,1)S(1)}, u32[]{:S(2)}, u32[]{:S(2)}) collective-permute-start(bf16[256,512]{1,0:T(8,128)(2,1)S(1)} %collective-permute-done.6.refs_5_), channel_id=1, source_target_pairs={{0,1},{1,2},{2,3},{3,4},{4,5},{5,6},{6,7},{7,0},{8,9},{9,10},{10,1... | collective-permute-start | bytes 786440 | tf_op jit(solution)/shard_map/ppermute | solution.py:72
  66.0 1.5 all-to-all-done
  68.2 5.4 %all-gather.3.cloned.1.call-done.refs_8_.weights_hbm = bf16[2048,1280]{1,0:T(8,128)(2,1)} async-done(((bf16[128,1280]{1,0:T(8,128)(2,1)}), bf16[2048,1280]{1,0:T(8,128)(2,1)}) %all-gather.3.cloned.1.call-update) | async-done | bytes 5242896 | tf_op jit(solution)/shard_map/all_gather | solution.py:399
  73.6 2.8 %project.1 = (f32[256,256]{1,0:T(8,128)S(1)}, bf16[256,256]{1,0:T(8,128)(2,1)S(1)}) custom-call(s32[5]{0:T(128)S(1)} %stack.23.place_ref, bf16[128,256]{1,0:T(8,128)(2,1)S(1)} %get-tuple-element.26.hidden_ref, bf16[256,512]{1,0:T(8,128)(2,1)S(1)} %pad_maximum_fusion.refs_0_, bf16[256,512]{1,0:T(8,128)(2,1)S(1)} %collective-permute-done.2.refs_1_, ...), custom_call_target="tpu_custom_call" | custom-call | flops 536870912 | bytes 4194304 | tf_op jit(solution)/shard_map/project/pallas_call | solution.py:81
  76.4 4.8 %collective-permute-start.9 = (bf16[256,256]{1,0:T(8,128)(2,1)S(1)}, bf16[256,256]{1,0:T(8,128)(2,1)S(1)}, u32[]{:S(2)}, u32[]{:S(2)}) collective-permute-start(bf16[256,256]{1,0:T(8,128)(2,1)S(1)} %get-tuple-element.29), channel_id=1, source_target_pairs={{0,8},{8,0},{1,9},{9,1},{2,10},{10,2},{3,11},{11,3},{4,12},{12,4},... | collective-permute-start | bytes 393224 | tf_op jit(solution)/shard_map/ppermute | solution.py:68
  81.3 4.2 %collective-permute-done.9.recv_ref = bf16[256,256]{1,0:T(8,128)(2,1)S(1)} collective-permute-done((bf16[256,256]{1,0:T(8,128)(2,1)S(1)}, bf16[256,256]{1,0:T(8,128)(2,1)S(1)}, u32[]{:S(2)}, u32[]{:S(2)}) %collective-permute-start.9) | collective-permute-done | bytes 131104 | tf_op jit(solution)/shard_map/ppermute | solution.py:68
  86.2 23.1 %all_to_all.15 = bf16[8,128,256]{2,1,0:T(8,128)(2,1)S(1)} all-to-all(bf16[8,128,256]{2,1,0:T(8,128)(2,1)S(1)} %bitcast.19), channel_id=1, replica_groups=mesh['xl'=2,'y'=8,'core'=2,'xh'=2,'z'=8] {'z'}, dimensions={0} | all-to-all | bytes 1048576 | tf_op jit(solution)/shard_map/all_to_all | solution.py:458
  109.3 2.3 %gate_up.1 = (f32[128,896]{1,0:T(8,128)S(1)}, bf16[128,896]{1,0:T(8,128)(2,1)S(1)}) custom-call(bf16[1024,256]{1,0:T(8,128)(2,1)S(1)} %bitcast.18, bf16[1,2048]{1,0:T(2,128)(2,1)S(1)} %reshape.77.gain_ref, bf16[2048,1280]{1,0:T(8,128)(2,1)} %all-gather.3.cloned.1.call-done.refs_8_.weights_hbm), custom_call_target="tpu_custom_call" | custom-call | flops 402653184 | bytes 3145728 | tf_op jit(solution)/shard_map/gate_up/pallas_call | solution.py:81
  111.7 3.3 %collective-permute-start.10 = (bf16[128,896]{1,0:T(8,128)(2,1)S(1)}, bf16[128,896]{1,0:T(8,128)(2,1)S(1)}, u32[]{:S(2)}, u32[]{:S(2)}) collective-permute-start(bf16[128,896]{1,0:T(8,128)(2,1)S(1)} %get-tuple-element.34), channel_id=1, source_target_pairs={{0,256},{256,0},{1,257},{257,1},{2,258},{258,2},{3,259},{259,3},{4... | collective-permute-start | bytes 688136 | tf_op jit(solution)/shard_map/ppermute | solution.py:68
  115.0 0.9 all-gather.5.cloned.1.call-done.weights_hbm
  115.9 3.7 %collective-permute-done.10.recv_ref = bf16[128,896]{1,0:T(8,128)(2,1)S(1)} collective-permute-done((bf16[128,896]{1,0:T(8,128)(2,1)S(1)}, bf16[128,896]{1,0:T(8,128)(2,1)S(1)}, u32[]{:S(2)}, u32[]{:S(2)}) %collective-permute-start.10) | collective-permute-done | bytes 229408 | tf_op jit(solution)/shard_map/ppermute | solution.py:68
  119.6 3.8 %down.1 = bf16[256,1280]{1,0:T(8,128)(2,1)} custom-call(s32[5]{0:T(128)S(1)} %stack.23.place_ref, f32[128,896]{1,0:T(8,128)S(1)} %get-tuple-element.33.own_ref, bf16[128,896]{1,0:T(8,128)(2,1)S(1)} %collective-permute-done.10.recv_ref, bf16[128,256]{1,0:T(8,128)(2,1)S(1)} %get-tuple-element.35.residual_ref, ...), custom_call_target="tpu_custom_call" | custom-call | flops 402653184 | bytes 2097152 | tf_op jit(solution)/shard_map/down/pallas_call | solution.py:81
  123.4 6.8 %all-to-all-start.2 = ((bf16[32,8,1280]{2,1,0:T(8,128)(2,1)}), bf16[32,8,1280]{2,1,0:T(8,128)(2,1)S(1)}, u32[]{:S(2)}, u32[]{:S(2)}) async-start(bf16[32,8,1280]{2,1,0:T(8,128)(2,1)} %bitcast.11), calls=%async_computation.2 | async-start | bytes 1310720 | tf_op jit(solution)/shard_map/all_to_all | solution.py:482
  130.3 21.1 %all-to-all-done.2 = bf16[32,8,1280]{2,1,0:T(8,128)(2,1)S(1)} async-done(((bf16[32,8,1280]{2,1,0:T(8,128)(2,1)}), bf16[32,8,1280]{2,1,0:T(8,128)(2,1)S(1)}, u32[]{:S(2)}, u32[]{:S(2)}) %all-to-all-start.2) | async-done | bytes 655392 | tf_op jit(solution)/shard_map/all_to_all | solution.py:482
  151.3 1.4 combine.1
  (38 shorter events, 6.9 us)
Async XLA Ops:
  6.5 59.4 %copy-start.2 = (bf16[4096]{0:T(1024)(128)(2,1)S(1)}, bf16[4096]{0:T(1024)(128)(2,1)}, u32[]{:S(2)}) copy-start(bf16[4096]{0:T(1024)(128)(2,1)} %param.19) | copy-start | bytes 24580
  6.5 67.0 %all-gather.3.cloned.1.call-start = ((), (), s32[]{:S(2)}) async-start(), calls=%async_computation.3 | async-start | bytes 5570560 | tf_op jit(solution)/shard_map/all_gather | solution.py:399
  6.5 16.3 %collective-permute-start = (bf16[512,128]{1,0:T(8,128)(2,1)}, bf16[512,128]{1,0:T(8,128)(2,1)S(1)}, u32[]{:S(2)}, u32[]{:S(2)}) collective-permute-start(bf16[512,128]{1,0:T(8,128)(2,1)} %param.18), channel_id=1, source_target_pairs={{0,128},{1,96},{2,64},{3,32},{4,0},{5,224},{6,192},{7,160},{32,193... | collective-permute-start | bytes 393224 | tf_op jit(solution)/shard_map/ppermute | solution.py:333
  15.3 7.5 %collective-permute-start.1 = (bf16[128,512]{1,0:T(8,128)(2,1)}, bf16[128,512]{1,0:T(8,128)(2,1)S(1)}, u32[]{:S(2)}, u32[]{:S(2)}) collective-permute-start(bf16[128,512]{1,0:T(8,128)(2,1)} %attend.1), channel_id=1, source_target_pairs={{0,256},{256,0},{1,257},{257,1},{2,258},{258,2},{3,259},{259,3},{4... | collective-permute-start | bytes 393224 | tf_op jit(solution)/shard_map/ppermute | solution.py:68
  22.8 0.7 copy-start.1
  25.0 90.9 %all-gather.5.cloned.1.call-start = ((), (), s32[]{:S(2)}) async-start(), calls=%async_computation.4 | async-start | bytes 1671168 | tf_op jit(solution)/shard_map/all_gather | solution.py:401
  25.0 0.9 copy-start
  28.3 8.5 %collective-permute-start.2 = (bf16[256,512]{1,0:T(8,128)(2,1)S(1)}, bf16[256,512]{1,0:T(8,128)(2,1)S(1)}, u32[]{:S(2)}, u32[]{:S(2)}) collective-permute-start(bf16[256,512]{1,0:T(8,128)(2,1)S(1)} %pad_maximum_fusion.refs_0_), channel_id=1, source_target_pairs={{0,1},{1,2},{2,3},{3,4},{4,5},{5,6},{6,7},{7,0},{8,9},{9,10},{10,1... | collective-permute-start | bytes 786440 | tf_op jit(solution)/shard_map/ppermute | solution.py:72
  31.9 8.3 %collective-permute-start.3 = (bf16[256,512]{1,0:T(8,128)(2,1)S(1)}, bf16[256,512]{1,0:T(8,128)(2,1)S(1)}, u32[]{:S(2)}, u32[]{:S(2)}) collective-permute-start(bf16[256,512]{1,0:T(8,128)(2,1)S(1)} %pad_maximum_fusion.refs_0_), channel_id=1, source_target_pairs={{0,7},{1,0},{2,1},{3,2},{4,3},{5,4},{6,5},{7,6},{8,15},{9,8},{10,9... | collective-permute-start | bytes 786440 | tf_op jit(solution)/shard_map/ppermute | solution.py:72
  36.8 11.8 %collective-permute-start.4 = (bf16[256,512]{1,0:T(8,128)(2,1)S(1)}, bf16[256,512]{1,0:T(8,128)(2,1)S(1)}, u32[]{:S(2)}, u32[]{:S(2)}) collective-permute-start(bf16[256,512]{1,0:T(8,128)(2,1)S(1)} %collective-permute-done.2.refs_1_), channel_id=1, source_target_pairs={{0,1},{1,2},{2,3},{3,4},{4,5},{5,6},{6,7},{7,0},{8,9},{9,10},{10,1... | collective-permute-start | bytes 786440 | tf_op jit(solution)/shard_map/ppermute | solution.py:72
  40.2 18.9 %collective-permute-start.5 = (bf16[256,512]{1,0:T(8,128)(2,1)S(1)}, bf16[256,512]{1,0:T(8,128)(2,1)S(1)}, u32[]{:S(2)}, u32[]{:S(2)}) collective-permute-start(bf16[256,512]{1,0:T(8,128)(2,1)S(1)} %collective-permute-done.3.refs_2_), channel_id=1, source_target_pairs={{0,7},{1,0},{2,1},{3,2},{4,3},{5,4},{6,5},{7,6},{8,15},{9,8},{10,9... | collective-permute-start | bytes 786440 | tf_op jit(solution)/shard_map/ppermute | solution.py:72
  48.6 12.5 %collective-permute-start.6 = (bf16[256,512]{1,0:T(8,128)(2,1)S(1)}, bf16[256,512]{1,0:T(8,128)(2,1)S(1)}, u32[]{:S(2)}, u32[]{:S(2)}) collective-permute-start(bf16[256,512]{1,0:T(8,128)(2,1)S(1)} %collective-permute-done.4.refs_3_), channel_id=1, source_target_pairs={{0,1},{1,2},{2,3},{3,4},{4,5},{5,6},{6,7},{7,0},{8,9},{9,10},{10,1... | collective-permute-start | bytes 786440 | tf_op jit(solution)/shard_map/ppermute | solution.py:72
  50.6 16.9 %all-to-all-start = ((bf16[16,16,256]{2,1,0:T(8,128)(2,1)}), bf16[16,16,256]{2,1,0:T(8,128)(2,1)S(1)}, u32[]{:S(2)}, u32[]{:S(2)}) async-start(bf16[16,16,256]{2,1,0:T(8,128)(2,1)} %pad_maximum_fusion.1), calls=%async_computation | async-start | bytes 262144 | tf_op jit(solution)/shard_map/all_to_all | solution.py:408
  59.1 14.4 %collective-permute-start.7 = (bf16[256,512]{1,0:T(8,128)(2,1)S(1)}, bf16[256,512]{1,0:T(8,128)(2,1)S(1)}, u32[]{:S(2)}, u32[]{:S(2)}) collective-permute-start(bf16[256,512]{1,0:T(8,128)(2,1)S(1)} %collective-permute-done.5.refs_4_), channel_id=1, source_target_pairs={{0,7},{1,0},{2,1},{3,2},{4,3},{5,4},{6,5},{7,6},{8,15},{9,8},{10,9... | collective-permute-start | bytes 786440 | tf_op jit(solution)/shard_map/ppermute | solution.py:72
  61.2 12.4 %collective-permute-start.8 = (bf16[256,512]{1,0:T(8,128)(2,1)S(1)}, bf16[256,512]{1,0:T(8,128)(2,1)S(1)}, u32[]{:S(2)}, u32[]{:S(2)}) collective-permute-start(bf16[256,512]{1,0:T(8,128)(2,1)S(1)} %collective-permute-done.6.refs_5_), channel_id=1, source_target_pairs={{0,1},{1,2},{2,3},{3,4},{4,5},{5,6},{6,7},{7,0},{8,9},{9,10},{10,1... | collective-permute-start | bytes 786440 | tf_op jit(solution)/shard_map/ppermute | solution.py:72
  76.4 9.1 %collective-permute-start.9 = (bf16[256,256]{1,0:T(8,128)(2,1)S(1)}, bf16[256,256]{1,0:T(8,128)(2,1)S(1)}, u32[]{:S(2)}, u32[]{:S(2)}) collective-permute-start(bf16[256,256]{1,0:T(8,128)(2,1)S(1)} %get-tuple-element.29), channel_id=1, source_target_pairs={{0,8},{8,0},{1,9},{9,1},{2,10},{10,2},{3,11},{11,3},{4,12},{12,4},... | collective-permute-start | bytes 393224 | tf_op jit(solution)/shard_map/ppermute | solution.py:68
  111.7 7.9 %collective-permute-start.10 = (bf16[128,896]{1,0:T(8,128)(2,1)S(1)}, bf16[128,896]{1,0:T(8,128)(2,1)S(1)}, u32[]{:S(2)}, u32[]{:S(2)}) collective-permute-start(bf16[128,896]{1,0:T(8,128)(2,1)S(1)} %get-tuple-element.34), channel_id=1, source_target_pairs={{0,256},{256,0},{1,257},{257,1},{2,258},{258,2},{3,259},{259,3},{4... | collective-permute-start | bytes 688136 | tf_op jit(solution)/shard_map/ppermute | solution.py:68
  123.4 27.9 %all-to-all-start.2 = ((bf16[32,8,1280]{2,1,0:T(8,128)(2,1)}), bf16[32,8,1280]{2,1,0:T(8,128)(2,1)S(1)}, u32[]{:S(2)}, u32[]{:S(2)}) async-start(bf16[32,8,1280]{2,1,0:T(8,128)(2,1)} %bitcast.11), calls=%async_computation.2 | async-start | bytes 1310720 | tf_op jit(solution)/shard_map/all_to_all | solution.py:482
Sparse Core Ops, SparseCore 0:
  25.1 48.3 all-gather.2
  75.7 40.2 all-gather.4

commit v11 on v10

--- a/solution.py
+++ b/solution.py
@@ -13,6 +13,7 @@
 STEPS = (0, -1, 1, -2, 2, -3, 3, 4)
 SLAB = 128
 HALF = 2048
+LEAST_START = 512
 QUARTER = 1024
 COLS = 256
 HIDDEN = 384
@@ -44,24 +45,23 @@
         copy.wait()
     keys = keys_ref[...]
     size = keys.shape[1]
-    shape = (2 * SLAB, keys.shape[0])
-    position = start_ref[0] + (lax.broadcasted_iota(jnp.int32, shape, 0) & (SLAB - 1))
+    heads = HEADS_WIDE // size
+    shape = (heads * SLAB, keys.shape[0] - LEAST_START)
+    position = start_ref[0] - LEAST_START + (lax.broadcasted_iota(jnp.int32, shape, 0) & (SLAB - 1))
     visible = lax.broadcasted_iota(jnp.int32, shape, 1) <= position
-    for pair in range(HEADS_WIDE // size // 2):
-        first, second = (slice((2 * pair + i) * size, (2 * pair + i + 1) * size) for i in range(2))
-        block = jnp.concatenate([queries_ref[:, first], queries_ref[:, second]])
-        scores = lax.dot_general(
-            block, keys, (((1,), (1,)), ((), ())), preferred_element_type=F32
-        ) * size ** (-0.5)
-        scores = jnp.where(visible, scores, -1e30)
-        exp_scores = jnp.exp(scores - jnp.max(scores, axis=1, keepdims=True))
-        totals = jnp.sum(exp_scores, axis=1, keepdims=True)
-        if pair == 0:
-            copies[2].wait()
-        values = values_ref[...]
-        context = (jnp.dot(exp_scores.astype(BF16), values, preferred_element_type=F32) / totals).astype(BF16)
-        out_ref[:, first] = context[:SLAB]
-        out_ref[:, second] = context[SLAB:]
+    block = jnp.concatenate([queries_ref[:, h * size : (h + 1) * size] for h in range(heads)])
+    scores = lax.dot_general(
+        block, keys, (((1,), (1,)), ((), ())), preferred_element_type=F32
+    ) * size ** (-0.5)
+    scores = jnp.concatenate(
+        [scores[:, :LEAST_START], jnp.where(visible, scores[:, LEAST_START:], -1e30)], axis=1
+    )
+    exp_scores = jnp.exp(scores - jnp.max(scores, axis=1, keepdims=True))
+    totals = jnp.sum(exp_scores, axis=1, keepdims=True)
+    copies[2].wait()
+    context = (jnp.dot(exp_scores.astype(BF16), values_ref[...], preferred_element_type=F32) / totals).astype(BF16)
+    for h in range(heads):
+        out_ref[:, h * size : (h + 1) * size] = context[h * SLAB : (h + 1) * SLAB]
 
 
 def swap(block, axis):

time: 161 us -> 161 us (level)
  no operation moved by 1% of the time
where the time goes in v11:
time: 161 us; the launch traced here: 160 us
  starting transfers between devices  53.8 us (33%)
  waiting for transfers between devices  43.2 us (27%)
  blocking collectives  23.2 us (14%)
  Pallas kernels  19.3 us (12%)
  between operations  14.3 us (9%)
  other arithmetic  3.75 us (2%)
  local copies, waits for them, and re-layouts  2.41 us (1%)
    all_to_all x1, blocking collectives, per_device(): lax.all_to_all(rows_out.reshape(RING, 2 * BLOCKS * CAP, COLS), 'z', split...  23.2 us
    ppermute x7, starting transfers between devices, along_z(): lax.ppermute(block, 'z', [(i, (i + step) % RING) for i in range(RING)])  22 us
    all_to_all x1, waiting for transfers between devices, per_device(): lax.all_to_all(outward.reshape(2 * BLOCKS, 2 * CAP, QUARTER + COLS), PAIR...  21.1 us
    pallas_call x10, Pallas kernels, kernel_call(): pl.pallas_call(body, out_shape=[jax.ShapeDtypeStruct(shape, dtype) for sh...  19.3 us
    ppermute x3, starting transfers between devices, swap(): return lax.ppermute(block, axis, [(0, 1), (1, 0)])  11.5 us
    all_to_all x1, starting transfers between devices, per_device(): lax.all_to_all(outgoing, ('xl', 'z'), split_axis=0, concat_axis=0, tiled=...  8.53 us
    ppermute x3, waiting for transfers between devices, swap(): return lax.ppermute(block, axis, [(0, 1), (1, 0)])  7.74 us
    all_to_all x1, starting transfers between devices, per_device(): lax.all_to_all(outward.reshape(2 * BLOCKS, 2 * CAP, QUARTER + COLS), PAIR...  6.89 us
  transfers between devices with their start and end apart: 15, of which 10 were waited for; matrix products, arithmetic and copies ran while one was open for 3% of the time, Pallas kernels for 8%

profile of v11, /device:TPU:64, one launch (start us, length us, event | category | flops | bytes accessed | tf_op | source)
XLA Modules:
  0.0 159.9 jit_solution(1612501907492966090)
XLA Ops:
  6.5 4.7 %collective-permute-start = (bf16[512,128]{1,0:T(8,128)(2,1)}, bf16[512,128]{1,0:T(8,128)(2,1)S(1)}, u32[]{:S(2)}, u32[]{:S(2)}) collective-permute-start(bf16[512,128]{1,0:T(8,128)(2,1)} %param.18), channel_id=1, source_target_pairs={{0,128},{1,96},{2,64},{3,32},{4,0},{5,224},{6,192},{7,160},{32,193... | collective-permute-start | bytes 393224 | tf_op jit(solution)/shard_map/ppermute | solution.py:333
  11.9 3.6 %attend.1 = bf16[128,512]{1,0:T(8,128)(2,1)} custom-call(s32[1]{0:T(128)S(6)} %copy.24.start_ref, bf16[128,512]{1,0:T(8,128)(2,1)} %queries_hbm.1, bf16[1152,128]{1,0:T(8,128)(2,1)} %keys_hbm.1, bf16[1152,128]{1,0:T(8,128)(2,1)} %values_hbm.1), custom_call_target="tpu_custom_call" | custom-call | flops 301989888 | bytes 1048576 | tf_op jit(solution)/shard_map/attend/pallas_call | solution.py:81
  15.5 3.4 %collective-permute-start.1 = (bf16[128,512]{1,0:T(8,128)(2,1)}, bf16[128,512]{1,0:T(8,128)(2,1)S(1)}, u32[]{:S(2)}, u32[]{:S(2)}) collective-permute-start(bf16[128,512]{1,0:T(8,128)(2,1)} %attend.1), channel_id=1, source_target_pairs={{0,256},{256,0},{1,257},{257,1},{2,258},{258,2},{3,259},{259,3},{4... | collective-permute-start | bytes 393224 | tf_op jit(solution)/shard_map/ppermute | solution.py:68
  18.9 1.7 %pack_gate_up.1.started_hbm = bf16[128,1280]{1,0:T(8,128)(2,1)} custom-call(bf16[128,384]{1,0:T(8,128)(2,1)} %gate_hbm.1, bf16[128,384]{1,0:T(8,128)(2,1)} %up_hbm.1), custom_call_target="tpu_custom_call" | custom-call | bytes 393216 | tf_op jit(solution)/shard_map/pack_gate_up/pallas_call | solution.py:81
  20.6 2.2 %collective-permute-done.swapped_hbm = bf16[512,128]{1,0:T(8,128)(2,1)S(1)} collective-permute-done((bf16[512,128]{1,0:T(8,128)(2,1)}, bf16[512,128]{1,0:T(8,128)(2,1)S(1)}, u32[]{:S(2)}, u32[]{:S(2)}) %collective-permute-start) | collective-permute-done | bytes 131104 | tf_op jit(solution)/shard_map/ppermute | solution.py:333
  23.5 1.5 pack_out.1
  28.3 1.9 %collective-permute-start.2 = (bf16[256,512]{1,0:T(8,128)(2,1)S(1)}, bf16[256,512]{1,0:T(8,128)(2,1)S(1)}, u32[]{:S(2)}, u32[]{:S(2)}) collective-permute-start(bf16[256,512]{1,0:T(8,128)(2,1)S(1)} %pad_maximum_fusion.refs_0_), channel_id=1, source_target_pairs={{0,1},{1,2},{2,3},{3,4},{4,5},{5,6},{6,7},{7,0},{8,9},{9,10},{10,1... | collective-permute-start | bytes 786440 | tf_op jit(solution)/shard_map/ppermute | solution.py:72
  30.4 1.5 pad_maximum_fusion.1
  31.9 3.9 %collective-permute-start.3 = (bf16[256,512]{1,0:T(8,128)(2,1)S(1)}, bf16[256,512]{1,0:T(8,128)(2,1)S(1)}, u32[]{:S(2)}, u32[]{:S(2)}) collective-permute-start(bf16[256,512]{1,0:T(8,128)(2,1)S(1)} %pad_maximum_fusion.refs_0_), channel_id=1, source_target_pairs={{0,7},{1,0},{2,1},{3,2},{4,3},{5,4},{6,5},{7,6},{8,15},{9,8},{10,9... | collective-permute-start | bytes 786440 | tf_op jit(solution)/shard_map/ppermute | solution.py:72
  35.8 1.2 collective-permute-done.2.refs_1_
  37.0 1.9 %collective-permute-start.4 = (bf16[256,512]{1,0:T(8,128)(2,1)S(1)}, bf16[256,512]{1,0:T(8,128)(2,1)S(1)}, u32[]{:S(2)}, u32[]{:S(2)}) collective-permute-start(bf16[256,512]{1,0:T(8,128)(2,1)S(1)} %collective-permute-done.2.refs_1_), channel_id=1, source_target_pairs={{0,1},{1,2},{2,3},{3,4},{4,5},{5,6},{6,7},{7,0},{8,9},{9,10},{10,1... | collective-permute-start | bytes 786440 | tf_op jit(solution)/shard_map/ppermute | solution.py:72
  39.2 1.2 collective-permute-done.3.refs_2_
  40.4 6.6 %collective-permute-start.5 = (bf16[256,512]{1,0:T(8,128)(2,1)S(1)}, bf16[256,512]{1,0:T(8,128)(2,1)S(1)}, u32[]{:S(2)}, u32[]{:S(2)}) collective-permute-start(bf16[256,512]{1,0:T(8,128)(2,1)S(1)} %collective-permute-done.3.refs_2_), channel_id=1, source_target_pairs={{0,7},{1,0},{2,1},{3,2},{4,3},{5,4},{6,5},{7,6},{8,15},{9,8},{10,9... | collective-permute-start | bytes 786440 | tf_op jit(solution)/shard_map/ppermute | solution.py:72
  47.0 1.7 %collective-permute-done.4.refs_3_ = bf16[256,512]{1,0:T(8,128)(2,1)S(1)} collective-permute-done((bf16[256,512]{1,0:T(8,128)(2,1)S(1)}, bf16[256,512]{1,0:T(8,128)(2,1)S(1)}, u32[]{:S(2)}, u32[]{:S(2)}) %collective-permute-start.4) | collective-permute-done | bytes 262176 | tf_op jit(solution)/shard_map/ppermute | solution.py:72
  48.6 1.9 %collective-permute-start.6 = (bf16[256,512]{1,0:T(8,128)(2,1)S(1)}, bf16[256,512]{1,0:T(8,128)(2,1)S(1)}, u32[]{:S(2)}, u32[]{:S(2)}) collective-permute-start(bf16[256,512]{1,0:T(8,128)(2,1)S(1)} %collective-permute-done.4.refs_3_), channel_id=1, source_target_pairs={{0,1},{1,2},{2,3},{3,4},{4,5},{5,6},{6,7},{7,0},{8,9},{9,10},{10,1... | collective-permute-start | bytes 786440 | tf_op jit(solution)/shard_map/ppermute | solution.py:72
  50.6 8.5 %all-to-all-start = ((bf16[16,16,256]{2,1,0:T(8,128)(2,1)}), bf16[16,16,256]{2,1,0:T(8,128)(2,1)S(1)}, u32[]{:S(2)}, u32[]{:S(2)}) async-start(bf16[16,16,256]{2,1,0:T(8,128)(2,1)} %pad_maximum_fusion.1), calls=%async_computation | async-start | bytes 262144 | tf_op jit(solution)/shard_map/all_to_all | solution.py:408
  59.1 2.0 %collective-permute-start.7 = (bf16[256,512]{1,0:T(8,128)(2,1)S(1)}, bf16[256,512]{1,0:T(8,128)(2,1)S(1)}, u32[]{:S(2)}, u32[]{:S(2)}) collective-permute-start(bf16[256,512]{1,0:T(8,128)(2,1)S(1)} %collective-permute-done.5.refs_4_), channel_id=1, source_target_pairs={{0,7},{1,0},{2,1},{3,2},{4,3},{5,4},{6,5},{7,6},{8,15},{9,8},{10,9... | collective-permute-start | bytes 786440 | tf_op jit(solution)/shard_map/ppermute | solution.py:72
  61.2 3.8 %collective-permute-start.8 = (bf16[256,512]{1,0:T(8,128)(2,1)S(1)}, bf16[256,512]{1,0:T(8,128)(2,1)S(1)}, u32[]{:S(2)}, u32[]{:S(2)}) collective-permute-start(bf16[256,512]{1,0:T(8,128)(2,1)S(1)} %collective-permute-done.6.refs_5_), channel_id=1, source_target_pairs={{0,1},{1,2},{2,3},{3,4},{4,5},{5,6},{6,7},{7,0},{8,9},{9,10},{10,1... | collective-permute-start | bytes 786440 | tf_op jit(solution)/shard_map/ppermute | solution.py:72
  66.0 1.5 all-to-all-done
  68.2 5.5 %all-gather.3.cloned.1.call-done.refs_8_.weights_hbm = bf16[2048,1280]{1,0:T(8,128)(2,1)} async-done(((bf16[128,1280]{1,0:T(8,128)(2,1)}), bf16[2048,1280]{1,0:T(8,128)(2,1)}) %all-gather.3.cloned.1.call-update) | async-done | bytes 5242896 | tf_op jit(solution)/shard_map/all_gather | solution.py:399
  73.7 2.8 %project.1 = (f32[256,256]{1,0:T(8,128)S(1)}, bf16[256,256]{1,0:T(8,128)(2,1)S(1)}) custom-call(s32[5]{0:T(128)S(1)} %stack.23.place_ref, bf16[128,256]{1,0:T(8,128)(2,1)S(1)} %get-tuple-element.26.hidden_ref, bf16[256,512]{1,0:T(8,128)(2,1)S(1)} %pad_maximum_fusion.refs_0_, bf16[256,512]{1,0:T(8,128)(2,1)S(1)} %collective-permute-done.2.refs_1_, ...), custom_call_target="tpu_custom_call" | custom-call | flops 536870912 | bytes 4194304 | tf_op jit(solution)/shard_map/project/pallas_call | solution.py:81
  76.6 4.9 %collective-permute-start.9 = (bf16[256,256]{1,0:T(8,128)(2,1)S(1)}, bf16[256,256]{1,0:T(8,128)(2,1)S(1)}, u32[]{:S(2)}, u32[]{:S(2)}) collective-permute-start(bf16[256,256]{1,0:T(8,128)(2,1)S(1)} %get-tuple-element.29), channel_id=1, source_target_pairs={{0,8},{8,0},{1,9},{9,1},{2,10},{10,2},{3,11},{11,3},{4,12},{12,4},... | collective-permute-start | bytes 393224 | tf_op jit(solution)/shard_map/ppermute | solution.py:68
  81.5 4.1 %collective-permute-done.9.recv_ref = bf16[256,256]{1,0:T(8,128)(2,1)S(1)} collective-permute-done((bf16[256,256]{1,0:T(8,128)(2,1)S(1)}, bf16[256,256]{1,0:T(8,128)(2,1)S(1)}, u32[]{:S(2)}, u32[]{:S(2)}) %collective-permute-start.9) | collective-permute-done | bytes 131104 | tf_op jit(solution)/shard_map/ppermute | solution.py:68
  86.4 23.2 %all_to_all.15 = bf16[8,128,256]{2,1,0:T(8,128)(2,1)S(1)} all-to-all(bf16[8,128,256]{2,1,0:T(8,128)(2,1)S(1)} %bitcast.19), channel_id=1, replica_groups=mesh['xl'=2,'y'=8,'core'=2,'xh'=2,'z'=8] {'z'}, dimensions={0} | all-to-all | bytes 1048576 | tf_op jit(solution)/shard_map/all_to_all | solution.py:458
  109.6 2.3 %gate_up.1 = (f32[128,896]{1,0:T(8,128)S(1)}, bf16[128,896]{1,0:T(8,128)(2,1)S(1)}) custom-call(bf16[1024,256]{1,0:T(8,128)(2,1)S(1)} %bitcast.18, bf16[1,2048]{1,0:T(2,128)(2,1)S(1)} %reshape.77.gain_ref, bf16[2048,1280]{1,0:T(8,128)(2,1)} %all-gather.3.cloned.1.call-done.refs_8_.weights_hbm), custom_call_target="tpu_custom_call" | custom-call | flops 402653184 | bytes 3145728 | tf_op jit(solution)/shard_map/gate_up/pallas_call | solution.py:81
  111.9 3.2 %collective-permute-start.10 = (bf16[128,896]{1,0:T(8,128)(2,1)S(1)}, bf16[128,896]{1,0:T(8,128)(2,1)S(1)}, u32[]{:S(2)}, u32[]{:S(2)}) collective-permute-start(bf16[128,896]{1,0:T(8,128)(2,1)S(1)} %get-tuple-element.34), channel_id=1, source_target_pairs={{0,256},{256,0},{1,257},{257,1},{2,258},{258,2},{3,259},{259,3},{4... | collective-permute-start | bytes 688136 | tf_op jit(solution)/shard_map/ppermute | solution.py:68
  115.1 1.1 all-gather.5.cloned.1.call-done.weights_hbm
  116.2 3.6 %collective-permute-done.10.recv_ref = bf16[128,896]{1,0:T(8,128)(2,1)S(1)} collective-permute-done((bf16[128,896]{1,0:T(8,128)(2,1)S(1)}, bf16[128,896]{1,0:T(8,128)(2,1)S(1)}, u32[]{:S(2)}, u32[]{:S(2)}) %collective-permute-start.10) | collective-permute-done | bytes 229408 | tf_op jit(solution)/shard_map/ppermute | solution.py:68
  119.8 3.8 %down.1 = bf16[256,1280]{1,0:T(8,128)(2,1)} custom-call(s32[5]{0:T(128)S(1)} %stack.23.place_ref, f32[128,896]{1,0:T(8,128)S(1)} %get-tuple-element.33.own_ref, bf16[128,896]{1,0:T(8,128)(2,1)S(1)} %collective-permute-done.10.recv_ref, bf16[128,256]{1,0:T(8,128)(2,1)S(1)} %get-tuple-element.35.residual_ref, ...), custom_call_target="tpu_custom_call" | custom-call | flops 402653184 | bytes 2097152 | tf_op jit(solution)/shard_map/down/pallas_call | solution.py:81
  123.6 6.9 %all-to-all-start.2 = ((bf16[32,8,1280]{2,1,0:T(8,128)(2,1)}), bf16[32,8,1280]{2,1,0:T(8,128)(2,1)S(1)}, u32[]{:S(2)}, u32[]{:S(2)}) async-start(bf16[32,8,1280]{2,1,0:T(8,128)(2,1)} %bitcast.11), calls=%async_computation.2 | async-start | bytes 1310720 | tf_op jit(solution)/shard_map/all_to_all | solution.py:482
  130.6 21.1 %all-to-all-done.2 = bf16[32,8,1280]{2,1,0:T(8,128)(2,1)S(1)} async-done(((bf16[32,8,1280]{2,1,0:T(8,128)(2,1)}), bf16[32,8,1280]{2,1,0:T(8,128)(2,1)S(1)}, u32[]{:S(2)}, u32[]{:S(2)}) %all-to-all-start.2) | async-done | bytes 655392 | tf_op jit(solution)/shard_map/all_to_all | solution.py:482
  151.6 1.4 combine.1
  (38 shorter events, 6.9 us)
Async XLA Ops:
  6.5 59.4 %copy-start.2 = (bf16[4096]{0:T(1024)(128)(2,1)S(1)}, bf16[4096]{0:T(1024)(128)(2,1)}, u32[]{:S(2)}) copy-start(bf16[4096]{0:T(1024)(128)(2,1)} %param.19) | copy-start | bytes 24580
  6.5 67.2 %all-gather.3.cloned.1.call-start = ((), (), s32[]{:S(2)}) async-start(), calls=%async_computation.3 | async-start | bytes 5570560 | tf_op jit(solution)/shard_map/all_gather | solution.py:399
  6.5 16.3 %collective-permute-start = (bf16[512,128]{1,0:T(8,128)(2,1)}, bf16[512,128]{1,0:T(8,128)(2,1)S(1)}, u32[]{:S(2)}, u32[]{:S(2)}) collective-permute-start(bf16[512,128]{1,0:T(8,128)(2,1)} %param.18), channel_id=1, source_target_pairs={{0,128},{1,96},{2,64},{3,32},{4,0},{5,224},{6,192},{7,160},{32,193... | collective-permute-start | bytes 393224 | tf_op jit(solution)/shard_map/ppermute | solution.py:333
  15.5 7.3 %collective-permute-start.1 = (bf16[128,512]{1,0:T(8,128)(2,1)}, bf16[128,512]{1,0:T(8,128)(2,1)S(1)}, u32[]{:S(2)}, u32[]{:S(2)}) collective-permute-start(bf16[128,512]{1,0:T(8,128)(2,1)} %attend.1), channel_id=1, source_target_pairs={{0,256},{256,0},{1,257},{257,1},{2,258},{258,2},{3,259},{259,3},{4... | collective-permute-start | bytes 393224 | tf_op jit(solution)/shard_map/ppermute | solution.py:68
  22.8 0.7 copy-start.1
  25.0 91.2 %all-gather.5.cloned.1.call-start = ((), (), s32[]{:S(2)}) async-start(), calls=%async_computation.4 | async-start | bytes 1671168 | tf_op jit(solution)/shard_map/all_gather | solution.py:401
  25.0 0.9 copy-start
  28.3 8.7 %collective-permute-start.2 = (bf16[256,512]{1,0:T(8,128)(2,1)S(1)}, bf16[256,512]{1,0:T(8,128)(2,1)S(1)}, u32[]{:S(2)}, u32[]{:S(2)}) collective-permute-start(bf16[256,512]{1,0:T(8,128)(2,1)S(1)} %pad_maximum_fusion.refs_0_), channel_id=1, source_target_pairs={{0,1},{1,2},{2,3},{3,4},{4,5},{5,6},{6,7},{7,0},{8,9},{9,10},{10,1... | collective-permute-start | bytes 786440 | tf_op jit(solution)/shard_map/ppermute | solution.py:72
  31.9 8.5 %collective-permute-start.3 = (bf16[256,512]{1,0:T(8,128)(2,1)S(1)}, bf16[256,512]{1,0:T(8,128)(2,1)S(1)}, u32[]{:S(2)}, u32[]{:S(2)}) collective-permute-start(bf16[256,512]{1,0:T(8,128)(2,1)S(1)} %pad_maximum_fusion.refs_0_), channel_id=1, source_target_pairs={{0,7},{1,0},{2,1},{3,2},{4,3},{5,4},{6,5},{7,6},{8,15},{9,8},{10,9... | collective-permute-start | bytes 786440 | tf_op jit(solution)/shard_map/ppermute | solution.py:72
  37.0 11.6 %collective-permute-start.4 = (bf16[256,512]{1,0:T(8,128)(2,1)S(1)}, bf16[256,512]{1,0:T(8,128)(2,1)S(1)}, u32[]{:S(2)}, u32[]{:S(2)}) collective-permute-start(bf16[256,512]{1,0:T(8,128)(2,1)S(1)} %collective-permute-done.2.refs_1_), channel_id=1, source_target_pairs={{0,1},{1,2},{2,3},{3,4},{4,5},{5,6},{6,7},{7,0},{8,9},{9,10},{10,1... | collective-permute-start | bytes 786440 | tf_op jit(solution)/shard_map/ppermute | solution.py:72
  40.4 18.7 %collective-permute-start.5 = (bf16[256,512]{1,0:T(8,128)(2,1)S(1)}, bf16[256,512]{1,0:T(8,128)(2,1)S(1)}, u32[]{:S(2)}, u32[]{:S(2)}) collective-permute-start(bf16[256,512]{1,0:T(8,128)(2,1)S(1)} %collective-permute-done.3.refs_2_), channel_id=1, source_target_pairs={{0,7},{1,0},{2,1},{3,2},{4,3},{5,4},{6,5},{7,6},{8,15},{9,8},{10,9... | collective-permute-start | bytes 786440 | tf_op jit(solution)/shard_map/ppermute | solution.py:72
  48.6 12.5 %collective-permute-start.6 = (bf16[256,512]{1,0:T(8,128)(2,1)S(1)}, bf16[256,512]{1,0:T(8,128)(2,1)S(1)}, u32[]{:S(2)}, u32[]{:S(2)}) collective-permute-start(bf16[256,512]{1,0:T(8,128)(2,1)S(1)} %collective-permute-done.4.refs_3_), channel_id=1, source_target_pairs={{0,1},{1,2},{2,3},{3,4},{4,5},{5,6},{6,7},{7,0},{8,9},{9,10},{10,1... | collective-permute-start | bytes 786440 | tf_op jit(solution)/shard_map/ppermute | solution.py:72
  50.6 16.9 %all-to-all-start = ((bf16[16,16,256]{2,1,0:T(8,128)(2,1)}), bf16[16,16,256]{2,1,0:T(8,128)(2,1)S(1)}, u32[]{:S(2)}, u32[]{:S(2)}) async-start(bf16[16,16,256]{2,1,0:T(8,128)(2,1)} %pad_maximum_fusion.1), calls=%async_computation | async-start | bytes 262144 | tf_op jit(solution)/shard_map/all_to_all | solution.py:408
  59.1 14.6 %collective-permute-start.7 = (bf16[256,512]{1,0:T(8,128)(2,1)S(1)}, bf16[256,512]{1,0:T(8,128)(2,1)S(1)}, u32[]{:S(2)}, u32[]{:S(2)}) collective-permute-start(bf16[256,512]{1,0:T(8,128)(2,1)S(1)} %collective-permute-done.5.refs_4_), channel_id=1, source_target_pairs={{0,7},{1,0},{2,1},{3,2},{4,3},{5,4},{6,5},{7,6},{8,15},{9,8},{10,9... | collective-permute-start | bytes 786440 | tf_op jit(solution)/shard_map/ppermute | solution.py:72
  61.2 12.6 %collective-permute-start.8 = (bf16[256,512]{1,0:T(8,128)(2,1)S(1)}, bf16[256,512]{1,0:T(8,128)(2,1)S(1)}, u32[]{:S(2)}, u32[]{:S(2)}) collective-permute-start(bf16[256,512]{1,0:T(8,128)(2,1)S(1)} %collective-permute-done.6.refs_5_), channel_id=1, source_target_pairs={{0,1},{1,2},{2,3},{3,4},{4,5},{5,6},{6,7},{7,0},{8,9},{9,10},{10,1... | collective-permute-start | bytes 786440 | tf_op jit(solution)/shard_map/ppermute | solution.py:72
  76.6 9.1 %collective-permute-start.9 = (bf16[256,256]{1,0:T(8,128)(2,1)S(1)}, bf16[256,256]{1,0:T(8,128)(2,1)S(1)}, u32[]{:S(2)}, u32[]{:S(2)}) collective-permute-start(bf16[256,256]{1,0:T(8,128)(2,1)S(1)} %get-tuple-element.29), channel_id=1, source_target_pairs={{0,8},{8,0},{1,9},{9,1},{2,10},{10,2},{3,11},{11,3},{4,12},{12,4},... | collective-permute-start | bytes 393224 | tf_op jit(solution)/shard_map/ppermute | solution.py:68
  111.9 7.9 %collective-permute-start.10 = (bf16[128,896]{1,0:T(8,128)(2,1)S(1)}, bf16[128,896]{1,0:T(8,128)(2,1)S(1)}, u32[]{:S(2)}, u32[]{:S(2)}) collective-permute-start(bf16[128,896]{1,0:T(8,128)(2,1)S(1)} %get-tuple-element.34), channel_id=1, source_target_pairs={{0,256},{256,0},{1,257},{257,1},{2,258},{258,2},{3,259},{259,3},{4... | collective-permute-start | bytes 688136 | tf_op jit(solution)/shard_map/ppermute | solution.py:68
  123.6 28.0 %all-to-all-start.2 = ((bf16[32,8,1280]{2,1,0:T(8,128)(2,1)}), bf16[32,8,1280]{2,1,0:T(8,128)(2,1)S(1)}, u32[]{:S(2)}, u32[]{:S(2)}) async-start(bf16[32,8,1280]{2,1,0:T(8,128)(2,1)} %bitcast.11), calls=%async_computation.2 | async-start | bytes 1310720 | tf_op jit(solution)/shard_map/all_to_all | solution.py:482
Sparse Core Ops, SparseCore 0:
  25.1 48.5 all-gather.2
  75.8 40.3 all-gather.4
